TPU v7x, 32 devices: a whole 2x2x4 slice. The times are simulated.
32 devices in a mesh: seq: 4 (over z), fsdp: 8 (over y, x, core).
Axes of the slice: x: 2, y: 2, z: 4, core: 2. Of those that a mesh axis runs over, the one named last changes fastest.
Arguments:
- hidden_in: bfloat16 [8, 2048, 1024], P('fsdp', 'seq'), may hold values from -6 to 6
- cotangent: bfloat16 [8, 2048, 1024], P('fsdp', 'seq'), may hold values from -6 to 6
- norm_gain: bfloat16 [2, 1024], P(None, 'fsdp'), may hold values from 0.25 to 1.75
- input_projection_weight: bfloat16 [2, 1024, 4384], P(None, 'fsdp'), may hold values from -0.1875 to 0.1875
- conv_weight: bfloat16 [2, 4, 2304], P(None, None, 'fsdp'), may hold values from -3 to 3
- conv_bias: bfloat16 [2, 2304], P(None, 'fsdp'), may hold values from -1 to 1
- dt_bias: bfloat16 [2, 32], P(None, 'fsdp'), may hold values from -9 to -4
- a_log: bfloat16 [2, 32], P(None, 'fsdp'), may hold values from 0 to 2.5
- skip: bfloat16 [2, 32], P(None, 'fsdp'), may hold values from 0.5 to 1.5
- gate_gain: bfloat16 [2, 2048], P(None, 'fsdp'), may hold values from 0.25 to 1.75
- output_projection_weight: bfloat16 [2, 2048, 1024], P(None, 'fsdp'), may hold values from -0.125 to 0.125
Outputs:
- block_out: bfloat16 [8, 2048, 1024], P('fsdp', 'seq')
- input_grad: float32 [8, 2048, 1024], P('fsdp', 'seq')
- norm_gain_grad: float32 [2, 1024], P(None, 'fsdp')
- in_weight_grad: float32 [2, 1024, 4384], P(None, 'fsdp')
- conv_weight_grad: float32 [2, 4, 2304], P(None, None, 'fsdp')
- conv_bias_grad: float32 [2, 2304], P(None, 'fsdp')
- dt_bias_grad: float32 [2, 32], P(None, 'fsdp')
- a_log_grad: float32 [2, 32], P(None, 'fsdp')
- skip_grad: float32 [2, 32], P(None, 'fsdp')
- gate_gain_grad: float32 [2, 2048], P(None, 'fsdp')
- out_weight_grad: float32 [2, 2048, 1024], P(None, 'fsdp')
All inputs are finite; a program needn't handle non-finite values.
Results may differ from a plain program's by a relative error of at most 0.019.
Values may be sent and summed in bfloat16 or wider, within the bound.
No kernel may reach another device: no remote copies, remote signals or barrier semaphores. Data moves between devices by JAX's collectives and lax.ppermute only.
A program may use at most 320 MiB of HBM per device.

v0:
```python
import jax
import jax.numpy as jnp
from jax import lax
from jax.sharding import PartitionSpec as P

H = 32
P_SIZE = 64
N = 128
GROUP = 256
DI = 2048


epsilon = 1e-05
highest_precision = lax.Precision.HIGHEST


def rms_scale(values):
    return lax.rsqrt(jnp.mean(values * values, axis=-1, keepdims=True) + epsilon)


def scaled_norm(values, gain):
    return values * rms_scale(values) * gain[None, :]


def gated_norm(mixed, gate_part, gain):
    gated = mixed * jax.nn.silu(gate_part)
    return gated * rms_scale(gated) * gain[None, :]


def contract(left, right, left_dim, right_dim):
    return lax.dot_general(
        left, right, (((left_dim,), (right_dim,)), ((), ())), preferred_element_type=jnp.float32
    )


def place_slice(piece, rank, parts, axis_dim):
    width = piece.shape[axis_dim]
    reps = [1] * piece.ndim
    reps[axis_dim] = parts
    tiled = jnp.tile(piece, tuple(reps))
    owner = lax.broadcasted_iota(jnp.int32, tiled.shape, axis_dim) // width
    return jnp.where(owner == rank, tiled, 0.0)


def causal_conv(values, taps, shift):
    length = values.shape[0]
    reach = taps.shape[0]
    padded = jnp.pad(values, ((reach - 1, 0), (0, 0)))
    total = shift[None, :] + jnp.zeros_like(values)
    for offset in range(reach):
        total = total + taps[offset][None, :] * padded[offset : offset + length]
    return total


def block_scan(values, steps_dt, decay_rate, bmatrix, cmatrix):
    length, width = values.shape
    head_count = steps_dt.shape[1]
    head_width = width // head_count
    blocks = length // GROUP
    states = bmatrix.shape[1]
    causal_mask = jnp.tril(jnp.ones((GROUP, GROUP), jnp.float32))
    xblocks = values.reshape(blocks, GROUP, head_count, head_width)
    dblocks = steps_dt.reshape(blocks, GROUP, head_count)
    bblocks = bmatrix.reshape(blocks, GROUP, states)
    cblocks = cmatrix.reshape(blocks, GROUP, states)
    cumulative = jnp.cumsum(dblocks * decay_rate[None, None, :], axis=1)
    across = jnp.swapaxes(cumulative, 1, 2)
    scores = (
        jnp.einsum("btn,bsn->bts", cblocks, bblocks, precision=highest_precision)
        * causal_mask[None]
    )
    decays = jnp.exp(jnp.minimum(across[:, :, :, None] - across[:, :, None, :], 0.0))
    weights = decays * scores[:, None, :, :] * jnp.swapaxes(dblocks, 1, 2)[:, :, None, :]
    inside = jnp.einsum("bhts,bshp->bthp", weights, xblocks, precision=highest_precision)
    tail_weight = jnp.exp(cumulative[:, -1:, :] - cumulative) * dblocks
    fresh = jnp.einsum(
        "bsh,bshp,bsn->bhpn", tail_weight, xblocks, bblocks, precision=highest_precision
    )
    whole_decay = jnp.exp(cumulative[:, -1, :])

    def carry_step(state, pieces):
        fresh_one, decay_one = pieces
        return (state * decay_one[:, None, None] + fresh_one, state)

    initial = jnp.zeros((head_count, head_width, states), jnp.float32)
    final_state, before = lax.scan(carry_step, initial, (fresh, whole_decay))
    carried = (
        jnp.einsum("btn,bhpn->bthp", cblocks, before, precision=highest_precision)
        * jnp.exp(cumulative)[:, :, :, None]
    )
    return (inside + carried).reshape(length, width)


def mix_layer(
    x_part, dt_part, bc_part, x_taps, bc_taps, x_shift, bc_shift, bias_dt, log_rate, skip_gain
):
    length, width = x_part.shape
    head_count = dt_part.shape[1]
    states = bc_part.shape[1] // 2
    xs_act = jax.nn.silu(causal_conv(x_part, x_taps, x_shift))
    bc_act = jax.nn.silu(causal_conv(bc_part, bc_taps, bc_shift))
    steps_dt = jax.nn.softplus(dt_part + bias_dt[None, :])
    decay_rate = -jnp.exp(log_rate)
    scanned = block_scan(xs_act, steps_dt, decay_rate, bc_act[:, :states], bc_act[:, states:])
    return scanned + jnp.repeat(skip_gain, width // head_count)[None, :] * xs_act


def fetch_weights(
    norm_gain,
    input_projection_weight,
    conv_weight,
    conv_bias,
    dt_bias,
    a_log,
    skip,
    gate_gain,
    output_projection_weight,
    current_layer_index,
):
    return (
        lax.all_gather(norm_gain[current_layer_index], "fsdp", axis=0, tiled=True),
        lax.all_gather(input_projection_weight[current_layer_index], "fsdp", axis=0, tiled=True),
        lax.all_gather(conv_weight[current_layer_index], "fsdp", axis=1, tiled=True),
        lax.all_gather(conv_bias[current_layer_index], "fsdp", axis=0, tiled=True),
        lax.all_gather(dt_bias[current_layer_index], "fsdp", axis=0, tiled=True),
        lax.all_gather(a_log[current_layer_index], "fsdp", axis=0, tiled=True),
        lax.all_gather(skip[current_layer_index], "fsdp", axis=0, tiled=True),
        lax.all_gather(gate_gain[current_layer_index], "fsdp", axis=0, tiled=True),
        lax.all_gather(output_projection_weight[current_layer_index], "fsdp", axis=0, tiled=True),
    )


def fetch_again(
    norm_gain,
    input_projection_weight,
    conv_weight,
    conv_bias,
    dt_bias,
    a_log,
    skip,
    gate_gain,
    output_projection_weight,
    current_layer_index,
):
    return (
        lax.all_gather(norm_gain[current_layer_index], "fsdp", axis=0, tiled=True),
        lax.all_gather(input_projection_weight[current_layer_index], "fsdp", axis=0, tiled=True),
        lax.all_gather(conv_weight[current_layer_index], "fsdp", axis=1, tiled=True),
        lax.all_gather(conv_bias[current_layer_index], "fsdp", axis=0, tiled=True),
        lax.all_gather(dt_bias[current_layer_index], "fsdp", axis=0, tiled=True),
        lax.all_gather(a_log[current_layer_index], "fsdp", axis=0, tiled=True),
        lax.all_gather(skip[current_layer_index], "fsdp", axis=0, tiled=True),
        lax.all_gather(gate_gain[current_layer_index], "fsdp", axis=0, tiled=True),
        lax.all_gather(output_projection_weight[current_layer_index], "fsdp", axis=0, tiled=True),
    )


def on_device(
    hidden_in,
    cotangent,
    norm_gain,
    input_projection_weight,
    conv_weight,
    conv_bias,
    dt_bias,
    a_log,
    skip,
    gate_gain,
    output_projection_weight,
):
    layer_count = input_projection_weight.shape[0]
    seq_parts = lax.axis_size("seq")
    seq_rank = lax.axis_index("seq")
    head_local = H // seq_parts
    chan_start = seq_rank * (head_local * P_SIZE)
    head_start = seq_rank * head_local
    hidden = hidden_in[0].astype(jnp.float32)
    stored = []
    for current_layer_index in range(layer_count):
        gathered = fetch_weights(
            norm_gain,
            input_projection_weight,
            conv_weight,
            conv_bias,
            dt_bias,
            a_log,
            skip,
            gate_gain,
            output_projection_weight,
            current_layer_index,
        )
        (
            gain_in,
            proj_weight,
            conv_taps,
            conv_shift,
            bias_dt,
            log_rate,
            skip_gain,
            gain_out,
            down_weight,
        ) = gathered
        normed_layer_input, norm_pull = jax.vjp(scaled_norm, hidden, gain_in.astype(jnp.float32))
        normed_low = normed_layer_input.astype(jnp.bfloat16)
        projected_input = jnp.dot(normed_low, proj_weight, preferred_element_type=jnp.float32)
        gate_part = projected_input[:, :DI]
        x_low = projected_input[:, DI : 2 * DI].astype(jnp.bfloat16)
        bc_low = projected_input[:, 2 * DI : 2 * DI + 2 * N].astype(jnp.bfloat16)
        dt_low = projected_input[:, 2 * DI + 2 * N :].astype(jnp.bfloat16)
        x_seq, dt_seq = (
            lax.all_to_all(x_low, "seq", split_axis=1, concat_axis=0, tiled=True),
            lax.all_to_all(dt_low, "seq", split_axis=1, concat_axis=0, tiled=True),
        )
        bc_seq = lax.all_gather(bc_low, "seq", axis=0, tiled=True)
        taps_float = conv_taps.astype(jnp.float32)
        shift_float = conv_shift.astype(jnp.float32)
        mixed_seq, mixer_pull = jax.vjp(
            mix_layer,
            x_seq.astype(jnp.float32),
            dt_seq.astype(jnp.float32),
            bc_seq.astype(jnp.float32),
            lax.dynamic_slice_in_dim(taps_float, chan_start, head_local * P_SIZE, 1),
            taps_float[:, DI:],
            lax.dynamic_slice_in_dim(shift_float, chan_start, head_local * P_SIZE, 0),
            shift_float[DI:],
            lax.dynamic_slice_in_dim(bias_dt.astype(jnp.float32), head_start, head_local, 0),
            lax.dynamic_slice_in_dim(log_rate.astype(jnp.float32), head_start, head_local, 0),
            lax.dynamic_slice_in_dim(skip_gain.astype(jnp.float32), head_start, head_local, 0),
        )
        mixed_tok = lax.all_to_all(
            mixed_seq.astype(jnp.bfloat16), "seq", split_axis=0, concat_axis=1, tiled=True
        )
        normed_gate_value, gate_pull = jax.vjp(
            gated_norm, mixed_tok.astype(jnp.float32), gate_part, gain_out.astype(jnp.float32)
        )
        gate_low = normed_gate_value.astype(jnp.bfloat16)
        hidden = hidden + jnp.dot(gate_low, down_weight, preferred_element_type=jnp.float32)
        stored.append((norm_pull, normed_low, mixer_pull, gate_pull, gate_low, gathered))
    block_out = hidden.astype(jnp.bfloat16)[None]
    grad_hidden = cotangent[0].astype(jnp.float32)
    results = [None] * layer_count
    for current_layer_index in reversed(range(layer_count)):
        norm_pull, normed_low, mixer_pull, gate_pull, gate_low, gathered = stored[
            current_layer_index
        ]
        weights_now = fetch_again(
            norm_gain,
            input_projection_weight,
            conv_weight,
            conv_bias,
            dt_bias,
            a_log,
            skip,
            gate_gain,
            output_projection_weight,
            current_layer_index,
        )
        proj_weight = weights_now[1]
        down_weight = weights_now[8]
        d_branch = grad_hidden.astype(jnp.bfloat16)
        down_grad = contract(gate_low, d_branch, 0, 0)
        d_gate_normed = contract(d_branch, down_weight, 1, 1)
        d_mixed, d_gate_part, gain_out_grad = gate_pull(d_gate_normed)
        d_mixed_seq = lax.all_to_all(
            d_mixed.astype(jnp.bfloat16), "seq", split_axis=1, concat_axis=0, tiled=True
        )
        d_x, d_dt, d_bc, g_xtaps, g_bctaps, g_xshift, g_bcshift, g_dtbias, g_lograte, g_skip = (
            mixer_pull(d_mixed_seq.astype(jnp.float32))
        )
        d_x_tok, d_dt_tok = (
            lax.all_to_all(
                d_x.astype(jnp.bfloat16), "seq", split_axis=0, concat_axis=1, tiled=True
            ),
            lax.all_to_all(
                d_dt.astype(jnp.bfloat16), "seq", split_axis=0, concat_axis=1, tiled=True
            ),
        )
        d_bc_tok = lax.psum_scatter(
            d_bc.astype(jnp.bfloat16), "seq", scatter_dimension=0, tiled=True
        )
        d_projected = jnp.concatenate(
            [d_gate_part.astype(jnp.bfloat16), d_x_tok, d_bc_tok, d_dt_tok], axis=1
        )
        proj_grad = contract(normed_low, d_projected, 0, 0)
        d_normed = contract(d_projected, proj_weight, 1, 1)
        d_hidden, gain_in_grad = norm_pull(d_normed)
        grad_hidden = grad_hidden + d_hidden
        taps_grad = jnp.concatenate(
            [place_slice(g_xtaps, seq_rank, seq_parts, 1), g_bctaps], axis=1
        )
        shift_grad = jnp.concatenate(
            [place_slice(g_xshift, seq_rank, seq_parts, 0), g_bcshift], axis=0
        )
        bias_grad = place_slice(g_dtbias, seq_rank, seq_parts, 0)
        rate_grad = place_slice(g_lograte, seq_rank, seq_parts, 0)
        skip_part = place_slice(g_skip, seq_rank, seq_parts, 0)
        shares = (
            lax.psum_scatter(
                gain_in_grad.astype(jnp.bfloat16), "fsdp", scatter_dimension=0, tiled=True
            ).astype(jnp.float32),
            lax.psum_scatter(
                proj_grad.astype(jnp.bfloat16), "fsdp", scatter_dimension=0, tiled=True
            ).astype(jnp.float32),
            lax.psum_scatter(
                taps_grad.astype(jnp.bfloat16), "fsdp", scatter_dimension=1, tiled=True
            ).astype(jnp.float32),
            lax.psum_scatter(
                shift_grad.astype(jnp.bfloat16), "fsdp", scatter_dimension=0, tiled=True
            ).astype(jnp.float32),
            lax.psum_scatter(
                bias_grad.astype(jnp.bfloat16), "fsdp", scatter_dimension=0, tiled=True
            ).astype(jnp.float32),
            lax.psum_scatter(
                rate_grad.astype(jnp.bfloat16), "fsdp", scatter_dimension=0, tiled=True
            ).astype(jnp.float32),
            lax.psum_scatter(
                skip_part.astype(jnp.bfloat16), "fsdp", scatter_dimension=0, tiled=True
            ).astype(jnp.float32),
            lax.psum_scatter(
                gain_out_grad.astype(jnp.bfloat16), "fsdp", scatter_dimension=0, tiled=True
            ).astype(jnp.float32),
            lax.psum_scatter(
                down_grad.astype(jnp.bfloat16), "fsdp", scatter_dimension=0, tiled=True
            ).astype(jnp.float32),
        )
        results[current_layer_index] = (
            lax.psum(shares[0].astype(jnp.bfloat16), "seq").astype(jnp.float32),
            lax.psum(shares[1].astype(jnp.bfloat16), "seq").astype(jnp.float32),
            lax.psum(shares[2].astype(jnp.bfloat16), "seq").astype(jnp.float32),
            lax.psum(shares[3].astype(jnp.bfloat16), "seq").astype(jnp.float32),
            lax.psum(shares[4].astype(jnp.bfloat16), "seq").astype(jnp.float32),
            lax.psum(shares[5].astype(jnp.bfloat16), "seq").astype(jnp.float32),
            lax.psum(shares[6].astype(jnp.bfloat16), "seq").astype(jnp.float32),
            lax.psum(shares[7].astype(jnp.bfloat16), "seq").astype(jnp.float32),
            lax.psum(shares[8].astype(jnp.bfloat16), "seq").astype(jnp.float32),
        )
    stacked = [
        jnp.stack(
            [results[current_layer_index][member] for current_layer_index in range(layer_count)]
        )
        for member in range(9)
    ]
    return (
        block_out,
        grad_hidden[None],
        stacked[0],
        stacked[1],
        stacked[2],
        stacked[3],
        stacked[4],
        stacked[5],
        stacked[6],
        stacked[7],
        stacked[8],
    )


def solution(mesh):
    return jax.shard_map(
        on_device,
        mesh=mesh,
        in_specs=(
            P("fsdp", "seq", None),
            P("fsdp", "seq", None),
            P(None, "fsdp"),
            P(None, "fsdp", None),
            P(None, None, "fsdp"),
            P(None, "fsdp"),
            P(None, "fsdp"),
            P(None, "fsdp"),
            P(None, "fsdp"),
            P(None, "fsdp"),
            P(None, "fsdp", None),
        ),
        out_specs=(
            P("fsdp", "seq", None),
            P("fsdp", "seq", None),
            P(None, "fsdp"),
            P(None, "fsdp", None),
            P(None, None, "fsdp"),
            P(None, "fsdp"),
            P(None, "fsdp"),
            P(None, "fsdp"),
            P(None, "fsdp"),
            P(None, "fsdp"),
            P(None, "fsdp", None),
        ),
        check_vma=False,
    )
```

profile of v0, /device:TPU:0, one launch (start us, length us, event | category | flops | bytes accessed | tf_op | source)
XLA Modules:
  0.0 1594.4 jit_solution(10734870499665015965)
XLA Ops:
  10.5 10.2 all-gather.2
  21.6 50.2 %all-gather.29.cloned.1.call-done = bf16[1,1024,4384]{1,2,0:T(8,128)(2,1)} async-done(((bf16[1,128,4384]{1,2,0:T(8,128)(2,1)}), bf16[1,1024,4384]{1,2,0:T(8,128)(2,1)}) %all-gather.29.cloned.1.call-update) | async-done | bytes 8978448 | tf_op jit(solution)/shard_map/all_gather | solution.py:122
  71.9 11.1 fusion.264
  87.9 11.6 all-gather.1
  105.1 24.2 %all-reduce.65 = (bf16[2304]{0:T(1024)(128)(2,1)S(1)}, bf16[32]{0:T(256)(128)(2,1)S(1)}, bf16[32]{0:T(256)(128)(2,1)S(1)}, bf16[32]{0:T(256)(128)(2,1)S(1)}, bf1...) all-reduce(bf16[2304]{0:T(1024)(128)(2,1)S(1)} %dynamic-update-slic, ...), channel_id=2, replica_groups=mesh['seq'=4,'fsdp'=8] {'fsdp'}, use_global_device_ids=true, to_apply=%add.44 | all-reduce | flops 4800 | bytes 19200
  135.6 7.7 dynamic-slice_reduce_fusion.7
  184.5 13.7 all-to-all-done
  220.4 9.1 while.68
  237.4 21.3 %bitcast_add_fusion.7 = f32[8,256,8,64]{1,3,2,0:T(8,128)} fusion(f32[8,256,8,64]{1,3,2,0:T(8,128)S(1)} %fusion.266, f32[8,256,8]{1,2,0:T(8,128)S(1)} %get-tuple-element.633, f32[8,8,256]{2,1,0:T(8,128)S(1)} %bitcast.533, f32[8,256,256]{2,1,0:T(8,128)S(1)} %copy-done.42, f32[8,8,256]{2,1,0:T(8,128)S(1)} %add_bitcast_fusion.3, ...), kind=kOutput, calls=%fused_computation.139 | convolution fusion | flops 3240099840 | bytes 14876672 | tf_op jit(solution)/shard_map/jvp(bhts,bshp->bthp)/dot_general | solution.py:74
  265.6 7.5 reshape.711
  282.8 8.9 all-gather.7
  291.7 8.7 all-gather.11
  300.4 30.2 %all-to-all-done.2 = bf16[4,512,512]{2,1,0:T(8,128)(2,1)S(1)} async-done(((bf16[4,512,512]{2,1,0:T(8,128)(2,1)}), bf16[4,512,512]{2,1,0:T(8,128)(2,1)S(1)}, u32[]{:S(2)}, u32[]{:S(2)}) %all-to-all-start.2) | async-done | bytes 2097184 | tf_op jit(solution)/shard_map/all_to_all | solution.py:230
  338.5 7.0 multiply_reduce_fusion.15
  351.9 11.7 fusion.265
  367.2 11.4 all-gather.10
  385.0 7.7 dynamic-slice_reduce_fusion.3
  434.3 17.0 %all-to-all-done.3 = bf16[512,4,512]{2,0,1:T(8,128)(2,1)S(1)} async-done(((bf16[512,4,512]{2,0,1:T(8,128)(2,1)}), bf16[512,4,512]{2,0,1:T(8,128)(2,1)S(1)}, u32[]{:S(2)}, u32[]{:S(2)}) %all-to-all-start.3) | async-done | bytes 2097184 | tf_op jit(solution)/shard_map/all_to_all | solution.py:211
  472.8 9.1 while.69
  489.9 21.3 %bitcast_add_fusion.6 = f32[8,256,8,64]{1,3,2,0:T(8,128)} fusion(f32[8,256,8,64]{1,3,2,0:T(8,128)S(1)} %fusion.267, f32[8,256,8]{1,2,0:T(8,128)S(1)} %get-tuple-element.625, f32[8,8,256]{2,1,0:T(8,128)S(1)} %bitcast.540, f32[8,256,256]{2,1,0:T(8,128)S(1)} %copy-done.43, f32[8,8,256]{2,1,0:T(8,128)S(1)} %add_bitcast_fusion.1, ...), kind=kOutput, calls=%fused_computation.132 | convolution fusion | flops 3240099840 | bytes 14876672 | tf_op jit(solution)/shard_map/jvp(bhts,bshp->bthp)/dot_general | solution.py:74
  518.1 7.5 reshape.712
  535.1 8.5 all-gather.16
  543.7 39.1 %all-to-all-done.5 = bf16[4,512,512]{2,1,0:T(8,128)(2,1)S(1)} async-done(((bf16[4,512,512]{2,1,0:T(8,128)(2,1)}), bf16[4,512,512]{2,1,0:T(8,128)(2,1)S(1)}, u32[]{:S(2)}, u32[]{:S(2)}) %all-to-all-start.5) | async-done | bytes 2097184 | tf_op jit(solution)/shard_map/all_to_all | solution.py:230
  597.6 7.4 multiply_reduce_fusion.2
  617.1 47.6 %all-to-all-done.6 = bf16[512,4,512]{2,0,1:T(8,128)(2,1)S(1)} async-done(((bf16[512,4,512]{2,0,1:T(8,128)(2,1)}), bf16[512,4,512]{2,0,1:T(8,128)(2,1)S(1)}, u32[]{:S(2)}, u32[]{:S(2)}) %all-to-all-start.6) | async-done | bytes 2097184 | tf_op jit(solution)/shard_map/all_to_all | solution.py:264
  673.7 22.4 %fusion.113 = (f32[8,8,256]{2,1,0:T(8,128)S(1)}, f32[8,8,256]{2,1,0:T(8,128)S(1)}, f32[8,8,256]{2,1,0:T(8,128)S(1)}, f32[8,256,256]{2,1,0:T(8,128)}) fusion(f32[8,8,256]{2,1,0:T(8,128)S(1)} %add_bitcast_fusion.1, f32[8,256,256]{2,1,0:T(8,128)} %convolution_multiply_fusion, f32[8,8,256]{2,1,0:T(8,128)S(1)} %bitcast.541, f32[8,256,8,64]{1,0,3,2:T(8,128)} %bitcast.485, ...), kind=kOutput, calls=%fused_computation.208 | convolution fusion | flops 3291955200 | bytes 10813440 | tf_op jit(solution)/shard_map/transpose(jvp(bhts,bshp->bthp))/dot_general | solution.py:74
  703.0 15.9 while.70
  718.9 7.5 fusion.268
  726.4 7.3 fusion.189
  733.8 7.9 fusion.170
  756.5 13.3 bitcast_add_fusion.5
  769.8 7.0 copy.456
  776.8 7.5 reshape.713
  784.3 12.3 multiply_reduce_fusion.6
  802.2 8.2 fusion.81
  834.8 19.8 %reduce-window.34 = f32[8,8,2,128]{3,1,2,0:T(8,128)S(1)} reduce-window(f32[8,8,2,128]{3,1,2,0:T(8,128)S(1)} %fusion.214, f32[]{:T(128)} %constant.232.clone.1), window={size=1x1x1x128 pad=0_0x0_0x0_0x0_127}, to_apply=%region_23.25 | reduce-window | flops 2080768 | bytes 131076 | tf_op jit(solution)/shard_map/reduce-window.4
  857.0 22.5 %all-to-all-done.7 = bf16[4,512,512]{2,1,0:T(8,128)(2,1)} async-done(((bf16[4,512,512]{2,1,0:T(8,128)(2,1)}), bf16[4,512,512]{2,1,0:T(8,128)(2,1)}, u32[]{:S(2)}, u32[]{:S(2)}) %all-to-all-start.7) | async-done | bytes 2097184 | tf_op jit(solution)/shard_map/all_to_all | solution.py:271
  888.6 10.6 multiply_reduce_fusion.24
  917.1 47.0 %all-to-all-done.9 = bf16[512,4,512]{2,0,1:T(8,128)(2,1)S(1)} async-done(((bf16[512,4,512]{2,0,1:T(8,128)(2,1)}), bf16[512,4,512]{2,0,1:T(8,128)(2,1)S(1)}, u32[]{:S(2)}, u32[]{:S(2)}) %all-to-all-start.9) | async-done | bytes 2097184 | tf_op jit(solution)/shard_map/all_to_all | solution.py:264
  973.5 22.4 %fusion.115 = (f32[8,8,256]{2,1,0:T(8,128)}, f32[8,8,256]{2,1,0:T(8,128)}, f32[8,8,256]{2,1,0:T(8,128)}, f32[8,256,256]{2,1,0:T(8,128)}) fusion(f32[8,8,256]{2,1,0:T(8,128)S(1)} %copy-done.76, f32[8,256,256]{2,1,0:T(8,128)} %convolution_multiply_fusion.1, f32[8,8,256]{2,1,0:T(8,128)S(1)} %bitcast.534, f32[8,256,8,64]{1,0,3,2:T(8,128)} %bitcast.480, ...), kind=kOutput, calls=%fused_computation.210 | convolution fusion | flops 3291955200 | bytes 10813440 | tf_op jit(solution)/shard_map/transpose(jvp(bhts,bshp->bthp))/dot_general | solution.py:74
  1002.7 20.9 %while.71 = (s32[]{:T(128)}, f32[8,64,128]{2,1,0:T(8,128)S(1)}, f32[8,8,64,128]{3,2,1,0:T(8,128)}, f32[8,8]{1,0:T(8,128)S(1)}, f32[8,8,64,128]{3,2,1,0:T(8,128)}...) while((s32[]{:T(128)}, f32[8,64,128]{2,1,0:T(8,128)S(1)}, ...), condition=%wide.region_29.31_spmd.clone, body=%wide.region_27.30_spmd.clone.sunk | while | flops 393212 | bytes 1573204 | solution.py:86
  1023.7 7.5 fusion.269
  1031.2 7.4 fusion.186
  1038.6 7.9 fusion.169
  1060.4 7.0 multiply_reduce_fusion.22
  1070.8 13.0 bitcast_add_fusion.4
  1090.7 7.5 reshape.714
  1098.2 14.3 multiply_reduce_fusion.10
  1115.3 11.3 convolution_convert_fusion
  1126.6 11.9 copy.468
  1139.1 7.7 broadcast_multiply_fusion.4
  1146.8 7.0 fusion.80
  1169.2 19.8 %reduce-window.36 = f32[8,8,2,128]{3,1,2,0:T(8,128)S(1)} reduce-window(f32[8,8,2,128]{3,1,2,0:T(8,128)S(1)} %fusion.213, f32[]{:T(128)} %constant.232.clone.1), window={size=1x1x1x128 pad=0_0x0_0x0_0x0_127}, to_apply=%region_37.39 | reduce-window | flops 2080768 | bytes 131076 | tf_op jit(solution)/shard_map/reduce-window.6
  1191.8 14.4 all-to-all-done.10
  1215.0 13.5 convolution_convert_fusion.1
  1228.5 12.2 copy.466
  1259.7 7.0 fusion.183
  1272.4 69.2 %reduce-scatter.25.cloned.1.call-done = bf16[128,4384]{1,0:T(8,128)(2,1)} async-done(((bf16[1024,4384]{1,0:T(8,128)(2,1)}), bf16[128,4384]{1,0:T(8,128)(2,1)}) %reduce-scatter.25.cloned.1.call-update) | async-done | bytes 1122320
  1344.0 52.9 %reduce-scatter.23.cloned.1.call-done = bf16[256,1024]{1,0:T(8,128)(2,1)} async-done(((bf16[2048,1024]{1,0:T(8,128)(2,1)}), bf16[256,1024]{1,0:T(8,128)(2,1)}) %reduce-scatter.23.cloned.1.call-update) | async-done | bytes 524304 | tf_op jit(solution)/shard_map/reduce_scatter | solution.py:322
  1396.9 54.9 %reduce-scatter.21.cloned.1.call-done = bf16[256,1024]{1,0:T(8,128)(2,1)} async-done(((bf16[2048,1024]{1,0:T(8,128)(2,1)}), bf16[256,1024]{1,0:T(8,128)(2,1)}) %reduce-scatter.21.cloned.1.call-update) | async-done | bytes 524304 | tf_op jit(solution)/shard_map/reduce_scatter | solution.py:322
  1451.9 10.9 fusion.123
  1462.8 24.8 %all-reduce.64 = (bf16[1024]{0:T(1024)(128)(2,1)S(1)}, bf16[1024]{0:T(1024)(128)(2,1)S(1)}, bf16[2304]{0:T(1024)(128)(2,1)S(1)}, bf16[2304]{0:T(1024)(128)(2,1)S...) all-reduce(bf16[1024]{0:T(1024)(128)(2,1)S(1)} %copy-done.135, ...), channel_id=23, replica_groups=mesh['seq'=4,'fsdp'=8] {'fsdp'}, use_global_device_ids=true, to_apply=%region_44.46.clone | all-reduce | flops 10944 | bytes 43776
  1488.6 20.3 %all-reduce.66 = (bf16[1,128]{1,0:T(2,128)(2,1)S(1)}, bf16[1,128]{1,0:T(2,128)(2,1)S(1)}, bf16[1,4,288]{2,1,0:T(4,128)(2,1)S(1)}, bf16[1,4,288]{2,1,0:T(4,128)(2...) all-reduce(bf16[1,128]{1,0:T(2,128)(2,1)S(1)} %dynamic-slice_bitcas, ...), channel_id=1, replica_groups=mesh['seq'=4,'fsdp'=8] {'seq'}, use_global_device_ids=true, to_apply=%region_45.47 | all-reduce | flops 3672 | bytes 14688 | tf_op jit(solution)/shard_map/psum | solution.py:327
  1516.5 65.5 %all-reduce.70.cloned.1.call-done = (bf16[1,128,4384]{1,2,0:T(8,128)(2,1)}, bf16[1,128,4384]{1,2,0:T(8,128)(2,1)}, bf16[1,256,1024]{2,1,0:T(8,128)(2,1)}, bf16[1,256,1024]{2,1,0:T(8,128)(2,1)}) async-done(((bf16[1,128,4384]{1,2,0:T(8,128)(2,1)}, bf16[1,128,4384]{1,2,0:T(8,128)(2,1)}, bf16[1,256,1024]{2,1,0:T(8,128)(2,1)}, bf16[1,256,1024]{2,1,0:T(8,128)(2,1)}), (bf16[1,128,4384]{1,2,0:T(8,128)(2,1)}, ...) | async-done | bytes 3293200 | tf_op jit(solution)/shard_map/psum | solution.py:328
  (768 shorter events, 496.8 us)
Async XLA Ops:
  7.2 64.7 %all-gather.29.cloned.1.call-start = ((), (), s32[]{:S(2)}) async-start(), calls=%async_computation.26 | async-start | bytes 10100736 | tf_op jit(solution)/shard_map/all_gather | solution.py:122
  10.4 149.5 %all-gather.25.cloned.1.call-start = ((), (), s32[]{:S(2)}) async-start(), calls=%async_computation.20 | async-start | bytes 1310720 | tf_op jit(solution)/shard_map/all_gather | solution.py:214
  20.7 62.3 %copy-start.93 = (f32[1,1024]{1,0:T(1,128)}, f32[1,1024]{1,0:T(1,128)S(1)}, u32[]{:S(2)}) copy-start(f32[1,1024]{1,0:T(1,128)S(1)} %convert_element_type.376) | copy-start | bytes 12292
  21.6 61.4 %copy-start.109 = (f32[512]{0:T(512)}, f32[512]{0:T(512)S(1)}, u32[]{:S(2)}) copy-start(f32[512]{0:T(512)S(1)} %fusion.229) | copy-start | bytes 6148
  85.9 259.6 %all-gather.31.cloned.1.call-start = ((), (), s32[]{:S(2)}) async-start(), calls=%async_computation.27 | async-start | bytes 4718592 | tf_op jit(solution)/shard_map/all_gather | solution.py:129
  87.1 264.8 %all-gather.33.cloned.1.call-start = ((), (), s32[]{:S(2)}) async-start(), calls=%async_computation.28 | async-start | bytes 10100736 | tf_op jit(solution)/shard_map/all_gather | solution.py:122
  101.1 60.4 %copy-start.99 = (f32[256]{0:T(256)}, f32[256]{0:T(256)S(1)}, u32[]{:S(2)}) copy-start(f32[256]{0:T(256)S(1)} %get-tuple-element.515) | copy-start | bytes 3076
  101.1 60.4 %copy-start.101 = (f32[256]{0:T(256)}, f32[256]{0:T(256)S(1)}, u32[]{:S(2)}) copy-start(f32[256]{0:T(256)S(1)} %get-tuple-element.516) | copy-start | bytes 3076
  101.1 60.4 %copy-start.103 = (f32[256]{0:T(256)}, f32[256]{0:T(256)S(1)}, u32[]{:S(2)}) copy-start(f32[256]{0:T(256)S(1)} %get-tuple-element.517) | copy-start | bytes 3076
  101.2 60.4 %copy-start.105 = (f32[256]{0:T(256)}, f32[256]{0:T(256)S(1)}, u32[]{:S(2)}) copy-start(f32[256]{0:T(256)S(1)} %get-tuple-element.518) | copy-start | bytes 3076
  129.4 24.2 %copy-start.126 = (f32[8]{0:T(128)}, f32[8]{0:T(128)S(1)}, u32[]{:S(2)}) copy-start(f32[8]{0:T(128)S(1)} %fusion.242) | copy-start | bytes 100
  130.8 17.1 %all-to-all-start.1 = ((bf16[512,4,8]{0,2,1:T(8,128)(2,1)}), bf16[512,4,8]{0,2,1:T(8,128)(2,1)S(1)}, u32[]{:S(2)}, u32[]{:S(2)}) async-start(bf16[512,4,8]{0,2,1:T(8,128)(2,1)} %slice_bitcast_fusion.1), calls=%async_computation.1 | async-start | bytes 65536 | tf_op jit(solution)/shard_map/all_to_all | solution.py:212
  143.3 55.6 %copy-start.79 = (f32[512]{0:T(512)}, f32[512]{0:T(512)S(1)}, u32[]{:S(2)}) copy-start(f32[512]{0:T(512)S(1)} %get-tuple-element.511) | copy-start | bytes 6148
  143.3 55.6 %copy-start.81 = (f32[512]{0:T(512)}, f32[512]{0:T(512)S(1)}, u32[]{:S(2)}) copy-start(f32[512]{0:T(512)S(1)} %get-tuple-element.512) | copy-start | bytes 6148
  143.3 55.6 %copy-start.83 = (f32[512]{0:T(512)}, f32[512]{0:T(512)S(1)}, u32[]{:S(2)}) copy-start(f32[512]{0:T(512)S(1)} %get-tuple-element.513) | copy-start | bytes 6148
  143.3 55.6 %copy-start.85 = (f32[512]{0:T(512)}, f32[512]{0:T(512)S(1)}, u32[]{:S(2)}) copy-start(f32[512]{0:T(512)S(1)} %get-tuple-element.514) | copy-start | bytes 6148
  143.8 129.3 %copy-start.89 = (f32[512]{0:T(512)}, f32[512]{0:T(512)S(1)}, u32[]{:S(2)}) copy-start(f32[512]{0:T(512)S(1)} %mul.1050) | copy-start | bytes 6148
  147.9 50.4 %all-to-all-start = ((bf16[512,4,512]{2,0,1:T(8,128)(2,1)}), bf16[512,4,512]{2,0,1:T(8,128)(2,1)S(1)}, u32[]{:S(2)}, u32[]{:S(2)}) async-start(bf16[512,4,512]{2,0,1:T(8,128)(2,1)} %copy.347), calls=%async_computation | async-start | bytes 4194304 | tf_op jit(solution)/shard_map/all_to_all | solution.py:211
  153.5 81.8 %copy-start.49 = (f32[2048,8]{0,1:T(8,128)}, f32[2048,8]{0,1:T(8,128)S(1)}, u32[]{:S(2)}) copy-start(f32[2048,8]{0,1:T(8,128)S(1)} %compare_select_fusion.5) | copy-start | bytes 196612
  159.0 76.3 %copy-start.63 = (f32[8,256,8]{1,2,0:T(8,128)}, f32[8,256,8]{1,2,0:T(8,128)S(1)}, u32[]{:S(2)}) copy-start(f32[8,256,8]{1,2,0:T(8,128)S(1)} %get-tuple-element.633) | copy-start | bytes 196612
  159.8 75.6 %copy-start.75 = (f32[8,8,256]{2,1,0:T(8,128)}, f32[8,8,256]{2,1,0:T(8,128)S(1)}, u32[]{:S(2)}) copy-start(f32[8,8,256]{2,1,0:T(8,128)S(1)} %add_bitcast_fusion.3) | copy-start | bytes 196612
  159.9 54.1 %copy-start.57 = (f32[8,256,8]{1,2,0:T(8,128)}, f32[8,256,8]{1,2,0:T(8,128)S(1)}, u32[]{:S(2)}) copy-start(f32[8,256,8]{1,2,0:T(8,128)S(1)} %fusion.215) | copy-start | bytes 196612
  229.5 29.1 %copy-start.11 = (f32[8,8,64,128]{3,2,1,0:T(8,128)}, f32[8,8,64,128]{3,2,1,0:T(8,128)S(1)}, u32[]{:S(2)}) copy-start(f32[8,8,64,128]{3,2,1,0:T(8,128)S(1)} %get-tuple-element.965) | copy-start | bytes 6291460
  229.5 29.1 %copy-start.124 = (f32[8,8,1,1]{1,3,2,0:T(1,128)}, f32[8,8,1,1]{1,3,2,0:T(1,128)S(1)}, u32[]{:S(2)}) copy-start(f32[8,8,1,1]{1,3,2,0:T(1,128)S(1)} %get-tuple-element.964) | copy-start | bytes 772
  279.0 51.7 %all-to-all-start.2 = ((bf16[4,512,512]{2,1,0:T(8,128)(2,1)}), bf16[4,512,512]{2,1,0:T(8,128)(2,1)S(1)}, u32[]{:S(2)}, u32[]{:S(2)}) async-start(bf16[4,512,512]{2,1,0:T(8,128)(2,1)} %bitcast.509), calls=%async_computation.2 | async-start | bytes 4194304 | tf_op jit(solution)/shard_map/all_to_all | solution.py:230
  282.7 126.7 %all-gather.27.cloned.1.call-start = ((), (), s32[]{:S(2)}) async-start(), calls=%async_computation.21 | async-start | bytes 1310720 | tf_op jit(solution)/shard_map/all_gather | solution.py:214
  291.7 53.8 %copy-start.77 = (f32[1,2048]{1,0:T(1,128)}, f32[1,2048]{1,0:T(1,128)S(1)}, u32[]{:S(2)}) copy-start(f32[1,2048]{1,0:T(1,128)S(1)} %convert_element_type.380) | copy-start | bytes 24580
  300.4 51.4 %copy-start.95 = (f32[1,1024]{1,0:T(1,128)}, f32[1,1024]{1,0:T(1,128)S(1)}, u32[]{:S(2)}) copy-start(f32[1,1024]{1,0:T(1,128)S(1)} %convert_element_type.383) | copy-start | bytes 12292
  366.4 231.2 %all-gather.35.cloned.1.call-start = ((), (), s32[]{:S(2)}) async-start(), calls=%async_computation.29 | async-start | bytes 4718592 | tf_op jit(solution)/shard_map/all_gather | solution.py:129
  380.3 22.7 %copy-start.128 = (f32[8]{0:T(128)}, f32[8]{0:T(128)S(1)}, u32[]{:S(2)}) copy-start(f32[8]{0:T(128)S(1)} %fusion.243) | copy-start | bytes 100
  381.7 15.5 all-to-all-start.4
  397.2 54.0 %all-to-all-start.3 = ((bf16[512,4,512]{2,0,1:T(8,128)(2,1)}), bf16[512,4,512]{2,0,1:T(8,128)(2,1)S(1)}, u32[]{:S(2)}, u32[]{:S(2)}) async-start(bf16[512,4,512]{2,0,1:T(8,128)(2,1)} %copy.361), calls=%async_computation.3 | async-start | bytes 4194304 | tf_op jit(solution)/shard_map/all_to_all | solution.py:211
  481.9 29.3 %copy-start.13 = (f32[8,8,64,128]{3,2,1,0:T(8,128)}, f32[8,8,64,128]{3,2,1,0:T(8,128)S(1)}, u32[]{:S(2)}) copy-start(f32[8,8,64,128]{3,2,1,0:T(8,128)S(1)} %get-tuple-element.935) | copy-start | bytes 6291460
  531.5 51.3 %all-to-all-start.5 = ((bf16[4,512,512]{2,1,0:T(8,128)(2,1)}), bf16[4,512,512]{2,1,0:T(8,128)(2,1)S(1)}, u32[]{:S(2)}, u32[]{:S(2)}) async-start(bf16[4,512,512]{2,1,0:T(8,128)(2,1)} %bitcast.510), calls=%async_computation.5 | async-start | bytes 4194304 | tf_op jit(solution)/shard_map/all_to_all | solution.py:230
  543.7 61.4 %copy-start.67 = (f32[1,2048]{1,0:T(1,128)}, f32[1,2048]{1,0:T(1,128)S(1)}, u32[]{:S(2)}) copy-start(f32[1,2048]{1,0:T(1,128)S(1)} %convert_element_type.387) | copy-start | bytes 24580
  613.1 51.7 %all-to-all-start.6 = ((bf16[512,4,512]{2,0,1:T(8,128)(2,1)}), bf16[512,4,512]{2,0,1:T(8,128)(2,1)S(1)}, u32[]{:S(2)}, u32[]{:S(2)}) async-start(bf16[512,4,512]{2,0,1:T(8,128)(2,1)} %copy.375), calls=%async_computation.6 | async-start | bytes 4194304 | tf_op jit(solution)/shard_map/all_to_all | solution.py:264
  810.4 69.1 %all-to-all-start.7 = ((bf16[4,512,512]{2,1,0:T(8,128)(2,1)}), bf16[4,512,512]{2,1,0:T(8,128)(2,1)}, u32[]{:S(2)}, u32[]{:S(2)}) async-start(bf16[4,512,512]{2,1,0:T(8,128)(2,1)} %bitcast.505), calls=%async_computation.7 | async-start | bytes 4194304 | tf_op jit(solution)/shard_map/all_to_all | solution.py:271
  814.8 73.7 %reduce-scatter.17.cloned.1.call-start = ((), (), s32[]{:S(2)}) async-start(), calls=%async_computation.22 | async-start | bytes 1310720 | tf_op jit(solution)/shard_map/reduce_scatter | solution.py:278
  831.1 23.7 %copy-start.129 = (f32[8]{0:T(128)S(1)}, f32[8]{0:T(128)}, u32[]{:S(2)}) copy-start(f32[8]{0:T(128)} %copy-done.128) | copy-start | bytes 100
  831.1 24.4 %copy-start.62 = (f32[512,4,8]{0,2,1:T(8,128)S(1)}, f32[512,4,8]{0,2,1:T(8,128)}, u32[]{:S(2)}) copy-start(f32[512,4,8]{0,2,1:T(8,128)} %copy-done.61) | copy-start | bytes 196612
  831.1 24.4 %copy-start.131 = (f32[8]{0:T(128)S(1)}, f32[8]{0:T(128)}, u32[]{:S(2)}) copy-start(f32[8]{0:T(128)} %copy-done.130) | copy-start | bytes 100
  834.6 53.9 %copy-start.33 = (f32[512,1024]{1,0:T(8,128)S(1)}, f32[512,1024]{1,0:T(8,128)}, u32[]{:S(2)}) copy-start(f32[512,1024]{1,0:T(8,128)} %copy-done.32) | copy-start | bytes 6291460
  834.7 53.9 %copy-start.96 = (f32[1,1024]{1,0:T(1,128)S(1)}, f32[1,1024]{1,0:T(1,128)}, u32[]{:S(2)}) copy-start(f32[1,1024]{1,0:T(1,128)} %copy-done.95) | copy-start | bytes 12292
  834.7 53.9 %copy-start.112 = (f32[512]{0:T(512)S(1)}, f32[512]{0:T(512)}, u32[]{:S(2)}) copy-start(f32[512]{0:T(512)} %copy-done.111) | copy-start | bytes 6148
  879.4 9.1 all-to-all-start.8
  913.3 50.8 %all-to-all-start.9 = ((bf16[512,4,512]{2,0,1:T(8,128)(2,1)}), bf16[512,4,512]{2,0,1:T(8,128)(2,1)S(1)}, u32[]{:S(2)}, u32[]{:S(2)}) async-start(bf16[512,4,512]{2,0,1:T(8,128)(2,1)} %copy.395), calls=%async_computation.10 | async-start | bytes 4194304 | tf_op jit(solution)/shard_map/all_to_all | solution.py:264
  916.9 298.1 %reduce-scatter.19.cloned.1.call-start = ((), (), s32[]{:S(2)}) async-start(), calls=%async_computation.23 | async-start | bytes 1310720 | tf_op jit(solution)/shard_map/reduce_scatter | solution.py:278
  973.4 22.4 %copy-start.29 = (f32[8,256,128,1]{2,1,3,0:T(8,128)S(1)}, f32[8,256,128,1]{2,1,3,0:T(8,128)}, u32[]{:S(2)}) copy-start(f32[8,256,128,1]{2,1,3,0:T(8,128)} %copy.417) | copy-start | bytes 3145732
  973.4 22.4 %copy-start.64 = (f32[8,256,8]{1,2,0:T(8,128)S(1)}, f32[8,256,8]{1,2,0:T(8,128)}, u32[]{:S(2)}) copy-start(f32[8,256,8]{1,2,0:T(8,128)} %copy-done.63) | copy-start | bytes 196612
  1070.7 197.3 %reduce-scatter.31.cloned.1.call-start = ((), (), s32[]{:S(2)}) async-start(), calls=%async_computation.33 | async-start | bytes 663552
  1113.8 155.2 %reduce-scatter.29.cloned.1.call-start = ((), (), s32[]{:S(2)}) async-start(), calls=%async_computation.32 | async-start | bytes 663552
  1115.0 155.0 %reduce-scatter.27.cloned.1.call-start = ((), (), s32[]{:S(2)}) async-start(), calls=%async_computation.31 | async-start | bytes 10321920
  1153.8 52.3 %all-to-all-start.10 = ((bf16[4,512,512]{2,1,0:T(8,128)(2,1)}), bf16[4,512,512]{2,1,0:T(8,128)(2,1)}, u32[]{:S(2)}, u32[]{:S(2)}) async-start(bf16[4,512,512]{2,1,0:T(8,128)(2,1)} %bitcast.506), calls=%async_computation.11 | async-start | bytes 4194304 | tf_op jit(solution)/shard_map/all_to_all | solution.py:271
  1164.7 25.7 %copy-start.60 = (f32[512,4,8]{0,2,1:T(8,128)S(1)}, f32[512,4,8]{0,2,1:T(8,128)}, u32[]{:S(2)}) copy-start(f32[512,4,8]{0,2,1:T(8,128)} %copy-done.59) | copy-start | bytes 196612
  1168.1 46.9 %copy-start.41 = (bf16[1,512,1024]{2,1,0:T(8,128)(2,1)S(1)}, bf16[1,512,1024]{2,1,0:T(8,128)(2,1)}, u32[]{:S(2)}) copy-start(bf16[1,512,1024]{2,1,0:T(8,128)(2,1)} %param.20) | copy-start | bytes 3145732
  1168.2 46.9 %copy-start.94 = (f32[1,1024]{1,0:T(1,128)S(1)}, f32[1,1024]{1,0:T(1,128)}, u32[]{:S(2)}) copy-start(f32[1,1024]{1,0:T(1,128)} %copy-done.93) | copy-start | bytes 12292
  1206.1 8.9 all-to-all-start.11
  1209.4 132.2 %reduce-scatter.25.cloned.1.call-start = ((), (), s32[]{:S(2)}) async-start(), calls=%async_computation.30 | async-start | bytes 10321920
  1240.7 156.2 %reduce-scatter.23.cloned.1.call-start = ((), (), s32[]{:S(2)}) async-start(), calls=%async_computation.25 | async-start | bytes 4718592 | tf_op jit(solution)/shard_map/reduce_scatter | solution.py:322
  1248.6 203.2 %reduce-scatter.21.cloned.1.call-start = ((), (), s32[]{:S(2)}) async-start(), calls=%async_computation.24 | async-start | bytes 4718592 | tf_op jit(solution)/shard_map/reduce_scatter | solution.py:322
  1256.7 325.2 %all-reduce.70.cloned.1.call-start = ((), (), s32[]{:S(2)}) async-start(), calls=%async_computation.34 | async-start | bytes 6586368 | tf_op jit(solution)/shard_map/psum | solution.py:328
  1266.7 185.1 %copy-start.110 = (f32[512]{0:T(512)S(1)}, f32[512]{0:T(512)}, u32[]{:S(2)}) copy-start(f32[512]{0:T(512)} %copy-done.109) | copy-start | bytes 6148
  1451.9 61.1 %copy-start.88 = (f32[512]{0:T(512)S(1)}, f32[512]{0:T(512)}, u32[]{:S(2)}) copy-start(f32[512]{0:T(512)} %copy-done.87) | copy-start | bytes 6148
  1451.9 61.1 %copy-start.39 = (f32[512,1024]{1,0:T(8,128)S(1)}, f32[512,1024]{1,0:T(8,128)}, u32[]{:S(2)}) copy-start(f32[512,1024]{1,0:T(8,128)} %copy-done.37) | copy-start | bytes 6291460
  (113 other events, 765.7 us)
Sparse Core Ops, SparseCore 0:
  10.6 61.2 all-gather.28
  86.0 27.9 all-gather.24
  115.9 36.2 all-gather.30
  153.9 58.6 all-gather.32
  366.5 28.0 all-gather.26
  396.4 35.7 all-gather.34
  825.2 48.6 reduce-scatter.16
  1070.9 25.2 reduce-scatter.18
  1114.0 32.4 reduce-scatter.30
  1149.4 34.3 reduce-scatter.28
  1187.4 75.0 reduce-scatter.26
  1266.5 75.0 reduce-scatter.24
  1345.5 51.2 reduce-scatter.22
  1400.4 51.3 reduce-scatter.20
  1454.3 127.5 all-reduce.69
where the time goes:
time: 1610 us; the launch traced here: 1590 us
  waiting for transfers between devices  530 us (33%)
  matrix products  329 us (20%)
  other arithmetic  277 us (17%)
  local copies, waits for them, and re-layouts  257 us (16%)
  blocking collectives  129 us (8%)
  starting transfers between devices  51.2 us (3%)
  between operations  21 us (1%)
    dot_general x6, matrix products, block_scan(): jnp.einsum('bhts,bshp->bthp', weights, xblocks, precision=highest_precision)  114 us
    reduce_scatter x2, waiting for transfers between devices, on_device(): lax.psum_scatter(down_grad.astype(jnp.bfloat16), 'fsdp', scatter_dimensio...  108 us
    all_to_all x2, waiting for transfers between devices, on_device(): lax.all_to_all(d_mixed.astype(jnp.bfloat16), 'seq', split_axis=1, concat_...  94.6 us
    unnamed x350, local copies, waits for them, and re-layouts  71.9 us
    another operation x22, other arithmetic  70.8 us
    dot_general x8, matrix products, contract(): lax.dot_general(left, right, (((left_dim,), (right_dim,)), ((), ())), pre...  70.7 us
    unnamed x19, waiting for transfers between devices  70.3 us
    all_to_all x2, waiting for transfers between devices, on_device(): lax.all_to_all(mixed_seq.astype(jnp.bfloat16), 'seq', split_axis=0, conca...  69.3 us
  transfers between devices with their start and end apart: 27, of which 15 were waited for; matrix products, arithmetic and copies ran while one was open for 33% of the time, Pallas kernels for 0%

commit v1 on v0

v1 whole, which is shorter than its diff:
```python
import jax
import jax.numpy as jnp
from jax import lax
from jax.experimental import pallas as pl
from jax.experimental.pallas import tpu as pltpu
from jax.sharding import PartitionSpec as P

H = 32
P_SIZE = 64
N = 128
DI = 2048
CC = DI + 2 * N
T = 128
WB = 256
HB = WB // P_SIZE
STEPS = DI // WB
HALO = 16
F32 = jnp.float32
BF16 = jnp.bfloat16
EPS = 1e-05
VMEM_LIMIT = 50 * 1024 * 1024

L_STEP, L_CUM, L_CUMF, L_SIG = 0, 32, 64, 96


def dot(a, b):
    return jnp.dot(a, b, preferred_element_type=F32)


def dot_nt(a, b):
    return lax.dot_general(a, b, (((1,), (1,)), ((), ())), preferred_element_type=F32)


def dot_tn(a, b):
    return lax.dot_general(a, b, (((0,), (0,)), ((), ())), preferred_element_type=F32)


def sigmoid(v):
    return 1.0 / (1.0 + jnp.exp(-v))


def lane_iota(rows, lanes=128):
    return lax.broadcasted_iota(jnp.int32, (rows, lanes), 1)


def row_iota(rows, lanes=128):
    return lax.broadcasted_iota(jnp.int32, (rows, lanes), 0)


def column(cols, lane):
    return jnp.broadcast_to(cols[:, lane : lane + 1], (cols.shape[0], 128))


def widen(columns):
    left = lane_iota(columns[0].shape[0]) < P_SIZE
    tiles = [
        jnp.where(left, columns[2 * p], columns[2 * p + 1]) for p in range(len(columns) // 2)
    ]
    return jnp.concatenate(tiles, axis=1)


def spread(cols, lane, heads):
    return widen([column(cols, lane + h) for h in range(heads)])


def halves(tile, axis_rows=True):
    left = lane_iota(tile.shape[0]) < P_SIZE
    zero = jnp.zeros_like(tile)
    return jnp.concatenate([jnp.where(left, tile, zero), jnp.where(left, zero, tile)], axis=0)


def head_columns(cols, i):
    return pltpu.roll(cols, lax.rem(128 - HB * i, 128), 1)


def head_row(pt_ref, i, h, tokens):
    eight = pl.multiple_of(L_CUM + 8 * lax.shift_right_logical(i, 1), 8)
    block = pt_ref[pl.ds(eight, 8), tokens]
    odd = jnp.full((1, T), lax.rem(i, 2), jnp.int32) == 1
    return jnp.where(odd, block[HB + h : HB + h + 1, :], block[h : h + 1, :])


def fill(ext, halo_ref, v_ref):
    ext[0:HALO, :] = halo_ref[...].astype(F32)
    ext[HALO:, :] = v_ref[...].astype(F32)


def conv_block(ext, taps_ref, shift_ref, c):
    total = shift_ref[0:1, :] + taps_ref[0:1, :] * ext[pl.ds(HALO - 3 + c * T, T), :]
    for k in range(1, 4):
        total = total + taps_ref[k : k + 1, :] * ext[pl.ds(HALO - 3 + k + c * T, T), :]
    return total


def state_kernel(
    v_ref, halo_ref, bc_ref, bchalo_ref, dt_ref, taps_ref, shift_ref, bctaps_ref, bcshift_ref,
    prm_ref, f_ref, tot_ref, p_ref, pt_ref, b_ref, c_ref, bt_ref, ct_ref, ext,
):
    i = pl.program_id(0)
    blocks = v_ref.shape[0] // T

    @pl.when(i == 0)
    def _():
        fill(ext, bchalo_ref, bc_ref)
        lane = lane_iota(T)
        tril = (row_iota(T) >= lane).astype(F32)
        offset = jnp.zeros((1, 128), F32)
        for c in range(blocks):
            rows = pl.ds(c * T, T)
            conv = conv_block(ext, bctaps_ref, bcshift_ref, c)
            act = conv * sigmoid(conv)
            b_ref[rows, :] = act[:, :N].astype(BF16)
            c_ref[rows, :] = act[:, N:].astype(BF16)
            bt_ref[:, rows] = act[:, :N].T.astype(BF16)
            ct_ref[:, rows] = act[:, N:].T.astype(BF16)
            z = dt_ref[rows, :].astype(F32) + prm_ref[0:1, :]
            step = jnp.maximum(z, 0.0) + jnp.log1p(jnp.exp(-jnp.abs(z)))
            decay = step * prm_ref[1:2, :]
            cum = lax.dot_general(
                tril, decay, (((1,), (0,)), ((), ())),
                precision=lax.Precision.HIGHEST, preferred_element_type=F32,
            )
            cumf = cum + offset
            offset = cumf[T - 1 : T, :]
            packed = jnp.where(
                lane < L_CUM, step,
                jnp.where(lane < L_CUMF, cum, jnp.where(lane < L_SIG, cumf, sigmoid(z))),
            )
            p_ref[rows, :] = packed
            pt_ref[:, rows] = packed.T

    fill(ext, halo_ref, v_ref)
    last = head_columns(p_ref[pl.ds(blocks * T - 8, 8), :], i)
    tot = spread(last, L_CUMF, HB)[7:8, :]
    total = jnp.zeros((N, WB), F32)
    for c in range(blocks):
        rows = pl.ds(c * T, T)
        conv = conv_block(ext, taps_ref, shift_ref, c)
        cols = head_columns(p_ref[rows, :], i)
        w = jnp.exp(tot - spread(cols, L_CUMF, HB)) * spread(cols, L_STEP, HB)
        wx = (conv * sigmoid(conv) * w).astype(BF16)
        total = total + dot(bt_ref[:, rows], wx)
    f_ref[...] = total.astype(BF16)
    tot_ref[...] = jnp.broadcast_to(jnp.exp(tot), (8, WB))


def scan_kernel(
    v_ref, halo_ref, taps_ref, shift_ref, skip_ref, p_ref, pt_ref, b_ref, c_ref, bt_ref,
    y_ref, ext, cb,
):
    i = pl.program_id(0)
    blocks = v_ref.shape[0] // T

    @pl.when(i == 0)
    def _():
        causal = row_iota(T) >= lane_iota(T)
        for c in range(blocks):
            rows = pl.ds(c * T, T)
            cb[c] = jnp.where(causal, dot_nt(c_ref[rows, :], b_ref[rows, :]), 0.0)

    fill(ext, halo_ref, v_ref)
    state = None
    for c in range(blocks):
        rows = pl.ds(c * T, T)
        conv = conv_block(ext, taps_ref, shift_ref, c)
        x = conv * sigmoid(conv)
        cols = head_columns(p_ref[rows, :], i)
        cums = [column(cols, L_CUM + h) for h in range(HB)]
        xd = x * spread(cols, L_STEP, HB)
        parts = []
        for p in range(HB // 2):
            weights = []
            for h in (2 * p, 2 * p + 1):
                across = head_row(pt_ref, i, h, rows)
                weights.append(
                    (jnp.exp(jnp.minimum(cums[h] - across, 0.0)) * cb[c]).astype(BF16)
                )
            parts.append(
                dot(
                    jnp.concatenate(weights, axis=1),
                    halves(xd[:, p * 128 : (p + 1) * 128]).astype(BF16),
                )
            )
        y = jnp.concatenate(parts, axis=1) + skip_ref[0:1, :] * x
        cumx = widen(cums)
        if state is not None:
            y = y + jnp.exp(cumx) * dot(c_ref[rows, :], state.astype(BF16))
        y_ref[rows, :] = y
        if c < blocks - 1:
            tot = cumx[T - 1 : T, :]
            fresh = dot(bt_ref[:, rows], (jnp.exp(tot - cumx) * xd).astype(BF16))
            state = fresh if state is None else state * jnp.exp(tot) + fresh


def gate_kernel(y_ref, gate_ref, p_ref, c_ref, s_ref, gain_ref, out_y_ref, out_ref):
    grow = spread(jnp.exp(p_ref[...]), L_CUMF, H)
    y = y_ref[...] + grow * dot(c_ref[...], s_ref[...])
    out_y_ref[...] = y
    mixed = y.astype(BF16).astype(F32)
    gate = gate_ref[...]
    gated = mixed * (gate * sigmoid(gate))
    r = lax.rsqrt(jnp.mean(gated * gated, axis=1, keepdims=True) + EPS)
    out_ref[...] = (gated * r * gain_ref[0:1, :]).astype(BF16)


def gate_back_kernel(
    y_ref, gate_ref, dgn_ref, p_ref, ct_ref, gain_ref, dgate_ref, dmix_ref, gg_ref, g_ref, acc
):
    i = pl.program_id(0)

    @pl.when(i == 0)
    def _():
        acc[...] = jnp.zeros_like(acc)
        gg_ref[...] = jnp.zeros_like(gg_ref)

    mixed = y_ref[...].astype(BF16).astype(F32)
    gate = gate_ref[...]
    sig = sigmoid(gate)
    silu = gate * sig
    gated = mixed * silu
    r = lax.rsqrt(jnp.mean(gated * gated, axis=1, keepdims=True) + EPS)
    q = gated * r
    dgn = dgn_ref[...]
    gg_ref[...] += jnp.broadcast_to(jnp.sum(dgn * q, axis=0, keepdims=True), gg_ref.shape)
    dq = dgn * gain_ref[0:1, :]
    dgated = r * (dq - q * jnp.mean(dq * q, axis=1, keepdims=True))
    dgate_ref[...] = (dgated * mixed * (sig * (1.0 + gate * (1.0 - sig)))).astype(BF16)
    dmix = (dgated * silu).astype(BF16)
    dmix_ref[...] = dmix
    grow = spread(jnp.exp(p_ref[...]), L_CUMF, H)
    acc[...] += dot(ct_ref[...], (grow * dmix.astype(F32)).astype(BF16))

    @pl.when(i == pl.num_programs(0) - 1)
    def _():
        g_ref[...] = acc[...].astype(BF16)


def conv_back(ext, dext, taps_ref, dv_ref, tail_ref, head_ref, stats_ref, blocks):
    sums = [jnp.zeros((1, WB), F32) for _ in range(5)]
    for c in range(blocks):
        d = dext[pl.ds(c * T, T), :]
        total = taps_ref[3:4, :] * d
        for k in range(3):
            total = total + taps_ref[k : k + 1, :] * dext[pl.ds(c * T + 3 - k, T), :]
        dv_ref[pl.ds(c * T, T), :] = total.astype(BF16)
        if c == blocks - 1:
            tail_ref[...] = total[T - 8 :, :]
        for k in range(4):
            v = ext[pl.ds(HALO - 3 + k + c * T, T), :]
            sums[k] = sums[k] + jnp.sum(d * v, axis=0, keepdims=True)
        sums[4] = sums[4] + jnp.sum(d, axis=0, keepdims=True)
    head_ref[...] = dext[0:8, :]
    for k in range(5):
        stats_ref[k : k + 1, :] = sums[k]


def back_kernel(
    v_ref, halo_ref, bc_ref, bchalo_ref, taps_ref, shift_ref, bctaps_ref, bcshift_ref, skip_ref,
    prm_ref, p_ref, pt_ref, b_ref, c_ref, bt_ref, ct_ref, s_ref, gin_ref, dy_ref, y_ref,
    dv_ref, tail_ref, head_ref, stats_ref, bdv_ref, btail_ref, bhead_ref, bstats_ref,
    ddt_ref, dtstats_ref,
    ext, dext, convs, sigs, cbt, dcbt, acc, dbacc, dcacc,
):
    i = pl.program_id(0)
    blocks = v_ref.shape[0] // T
    length = blocks * T

    @pl.when(i == 0)
    def _():
        causal = row_iota(T) <= lane_iota(T)
        for c in range(blocks):
            rows = pl.ds(c * T, T)
            cbt[c] = jnp.where(causal, dot_nt(b_ref[rows, :], c_ref[rows, :]), 0.0)
        dcbt[...] = jnp.zeros_like(dcbt)
        acc[...] = jnp.zeros_like(acc)
        dbacc[...] = jnp.zeros_like(dbacc)
        dcacc[...] = jnp.zeros_like(dcacc)

    fill(ext, halo_ref, v_ref)
    dext[length:, :] = jnp.zeros((8, WB), F32)
    states = [s_ref[...].astype(F32)]
    for c in range(blocks):
        rows = pl.ds(c * T, T)
        conv = conv_block(ext, taps_ref, shift_ref, c)
        sig = sigmoid(conv)
        convs[rows, :] = conv
        sigs[rows, :] = sig
        cols = head_columns(p_ref[rows, :], i)
        cumx = spread(cols, L_CUM, HB)
        tot = cumx[T - 1 : T, :]
        wx = (jnp.exp(tot - cumx) * (conv * sig * spread(cols, L_STEP, HB))).astype(BF16)
        states.append(states[-1] * jnp.exp(tot) + dot(bt_ref[:, rows], wx))

    ch = lax.shift_right_logical(row_iota(WB), 6)
    seg1 = (lane_iota(WB) == HB * i + ch).astype(BF16)
    seg2 = (lane_iota(WB) == 32 + HB * i + ch).astype(BF16)
    final = row_iota(T, WB) == T - 1
    grad = gin_ref[...].astype(F32)
    skip_sum = jnp.zeros((1, WB), F32)
    for c in reversed(range(blocks)):
        rows = pl.ds(c * T, T)
        conv, sig = convs[rows, :], sigs[rows, :]
        x = conv * sig
        cols = head_columns(p_ref[rows, :], i)
        cums = [column(cols, L_CUM + h) for h in range(HB)]
        cumx = widen(cums)
        dt = spread(cols, L_STEP, HB)
        tot = cumx[T - 1 : T, :]
        xd = x * dt
        xdb = xd.astype(BF16)
        dyb = dy_ref[rows, :]
        dy = dyb.astype(F32)
        parts = []
        for p in range(HB // 2):
            lanes = slice(p * 128, (p + 1) * 128)
            dm = dot_nt(halves(xd[:, lanes]).astype(BF16), dyb[:, lanes])
            weights = []
            for j in range(2):
                h = 2 * p + j
                across = head_row(pt_ref, i, h, rows)
                e = jnp.exp(jnp.minimum(across - cums[h], 0.0))
                weights.append((e * cbt[c]).astype(BF16))
                dcbt[c] += dm[j * T : (j + 1) * T, :] * e
            parts.append(
                dot(jnp.concatenate(weights, axis=1), halves(dy[:, lanes]).astype(BF16))
            )
        gb = grad.astype(BF16)
        w = jnp.exp(tot - cumx)
        dxd = jnp.concatenate(parts, axis=1) + w * dot(b_ref[rows, :], gb)
        ey = (jnp.exp(cumx) * dy).astype(BF16)
        wx = (w * xd).astype(BF16)
        dcacc[rows, :] += dot_nt(ey, states[c].astype(BF16))
        dbacc[rows, :] += dot_nt(wx, gb)
        bound = jnp.sum(grad * states[c + 1], axis=0, keepdims=True)
        skip = skip_ref[0:1, :]
        p1 = dy * (y_ref[rows, :] - skip * x) - xdb.astype(F32) * dxd
        p1 = p1 + jnp.where(final, bound, 0.0)
        p2 = x * dxd
        p1h = p1.astype(BF16)
        p2h = p2.astype(BF16)
        acc[rows, :] += (
            dot(p1h, seg1) + dot((p1 - p1h.astype(F32)).astype(BF16), seg1)
        ) + (dot(p2h, seg2) + dot((p2 - p2h.astype(F32)).astype(BF16), seg2))
        skip_sum = skip_sum + jnp.sum(x * dy, axis=0, keepdims=True)
        dx = dt * dxd + skip * dy
        dext[rows, :] = dx * (sig * (1.0 + conv * (1.0 - sig)))
        grad = grad * jnp.exp(tot) + dot(ct_ref[:, rows], ey)
    conv_back(ext, dext, taps_ref, dv_ref, tail_ref, head_ref, stats_ref, blocks)
    stats_ref[5:6, :] = skip_sum

    @pl.when(i == pl.num_programs(0) - 1)
    def _():
        fill(ext, bchalo_ref, bc_ref)
        triu = (row_iota(T) <= lane_iota(T)).astype(F32)
        rate = prm_ref[1:2, :]
        rate_sum = jnp.zeros((1, 128), F32)
        bias_sum = jnp.zeros((1, 128), F32)
        for c in range(blocks):
            rows = pl.ds(c * T, T)
            causal = row_iota(T) <= lane_iota(T)
            m = jnp.where(causal, dcbt[c], 0.0).astype(BF16)
            db = dbacc[rows, :] + dot(m, c_ref[rows, :])
            dc = dcacc[rows, :] + dot_tn(m, b_ref[rows, :])
            conv = conv_block(ext, bctaps_ref, bcshift_ref, c)
            sig = sigmoid(conv)
            dext[rows, :] = jnp.concatenate([db, dc], axis=1) * (
                sig * (1.0 + conv * (1.0 - sig))
            )
            a = acc[rows, :]
            ddecay = lax.dot_general(
                triu, a, (((1,), (0,)), ((), ())),
                precision=lax.Precision.HIGHEST, preferred_element_type=F32,
            )
            packed = p_ref[rows, :]
            rate_sum = rate_sum + jnp.sum(packed * ddecay, axis=0, keepdims=True)
            dz = (pltpu.roll(a, 96, 1) + rate * ddecay) * pltpu.roll(packed, 32, 1)
            ddt_ref[rows, :] = dz.astype(BF16)
            bias_sum = bias_sum + jnp.sum(dz, axis=0, keepdims=True)
        conv_back(ext, dext, bctaps_ref, bdv_ref, btail_ref, bhead_ref, bstats_ref, blocks)
        dtstats_ref[0:1, :] = rate_sum * rate
        dtstats_ref[1:2, :] = bias_sum


def whole(shape):
    return pl.BlockSpec(shape, lambda i: (0,) * len(shape))


def wide(rows):
    return pl.BlockSpec((rows, WB), lambda i: (0, i))


def bc_block(rows):
    return pl.BlockSpec((rows, WB), lambda i: (0, STEPS))


def shape_of(shape, dtype):
    return jax.ShapeDtypeStruct(shape, dtype)


def params():
    return pltpu.CompilerParams(vmem_limit_bytes=VMEM_LIMIT)


def cost(flops, moved):
    return pl.CostEstimate(flops=int(flops), bytes_accessed=int(moved), transcendentals=0)


def local_state(r_low, halo, dt_low, taps, shift, prm):
    length = r_low.shape[0]
    return pl.pallas_call(
        state_kernel,
        name="local_state",
        grid=(STEPS,),
        in_specs=[
            wide(length), wide(HALO), bc_block(length), bc_block(HALO), whole((length, 128)),
            wide(4), wide(1), bc_block(4), bc_block(1), whole((8, 128)),
        ],
        out_specs=[
            wide(N), wide(8), whole((length, 128)), whole((128, length)),
            whole((length, N)), whole((length, N)), whole((N, length)), whole((N, length)),
        ],
        out_shape=[
            shape_of((N, DI), BF16), shape_of((8, DI), F32), shape_of((length, 128), F32),
            shape_of((128, length), F32), shape_of((length, N), BF16),
            shape_of((length, N), BF16), shape_of((N, length), BF16), shape_of((N, length), BF16),
        ],
        scratch_shapes=[pltpu.VMEM((HALO + length, WB), F32)],
        compiler_params=params(),
        cost_estimate=cost(4e9, 8e6),
    )(r_low, halo, r_low, halo, dt_low, taps, shift, taps, shift, prm)


def local_scan(r_low, halo, taps, shift, skip, p, pt, b, c, bt):
    length = r_low.shape[0]
    return pl.pallas_call(
        scan_kernel,
        name="local_scan",
        grid=(STEPS,),
        in_specs=[
            wide(length), wide(HALO), wide(4), wide(1), wide(1), whole((length, 128)),
            whole((128, length)), whole((length, N)), whole((length, N)), whole((N, length)),
        ],
        out_specs=wide(length),
        out_shape=shape_of((length, DI), F32),
        scratch_shapes=[
            pltpu.VMEM((HALO + length, WB), F32), pltpu.VMEM((length // T, T, T), F32)
        ],
        compiler_params=params(),
        cost_estimate=cost(1.5e10, 8e6),
    )(r_low, halo, taps, shift, skip, p, pt, b, c, bt)


def gate_forward(y, gate, p, c, s_in, gain):
    length = y.shape[0]
    rows = lambda width: pl.BlockSpec((T, width), lambda i: (i, 0))
    return pl.pallas_call(
        gate_kernel,
        name="gate_forward",
        grid=(length // T,),
        in_specs=[rows(DI), rows(DI), rows(128), rows(N), whole((N, DI)), whole((1, DI))],
        out_specs=[rows(DI), rows(DI)],
        out_shape=[shape_of((length, DI), F32), shape_of((length, DI), BF16)],
        compiler_params=params(),
        cost_estimate=cost(5e9, 15e6),
    )(y, gate, p, c, s_in, gain)


def gate_backward(y, gate, dgn, p, ct, gain):
    length = y.shape[0]
    rows = lambda width: pl.BlockSpec((T, width), lambda i: (i, 0))
    return pl.pallas_call(
        gate_back_kernel,
        name="gate_backward",
        grid=(length // T,),
        in_specs=[
            rows(DI), rows(DI), rows(DI), rows(128),
            pl.BlockSpec((N, T), lambda i: (0, i)), whole((1, DI)),
        ],
        out_specs=[rows(DI), rows(DI), whole((8, DI)), whole((N, DI))],
        out_shape=[
            shape_of((length, DI), BF16), shape_of((length, DI), BF16),
            shape_of((8, DI), F32), shape_of((N, DI), BF16),
        ],
        scratch_shapes=[pltpu.VMEM((N, DI), F32)],
        compiler_params=params(),
        cost_estimate=cost(1e10, 17e6),
    )(y, gate, dgn, p, ct, gain)


def scan_backward(
    r_low, halo, taps, shift, skip, prm, p, pt, b, c, bt, ct, s_in, g_in, dy, y
):
    length = r_low.shape[0]
    blocks = length // T
    return pl.pallas_call(
        back_kernel,
        name="scan_backward",
        grid=(STEPS,),
        in_specs=[
            wide(length), wide(HALO), bc_block(length), bc_block(HALO),
            wide(4), wide(1), bc_block(4), bc_block(1), wide(1), whole((8, 128)),
            whole((length, 128)), whole((128, length)), whole((length, N)), whole((length, N)),
            whole((N, length)), whole((N, length)), wide(N), wide(N), wide(length), wide(length),
        ],
        out_specs=[
            wide(length), wide(8), wide(8), wide(8),
            whole((length, WB)), whole((8, WB)), whole((8, WB)), whole((8, WB)),
            whole((length, 128)), whole((8, 128)),
        ],
        out_shape=[
            shape_of((length, DI), BF16), shape_of((8, DI), F32), shape_of((8, DI), F32),
            shape_of((8, DI), F32),
            shape_of((length, WB), BF16), shape_of((8, WB), F32), shape_of((8, WB), F32),
            shape_of((8, WB), F32),
            shape_of((length, 128), BF16), shape_of((8, 128), F32),
        ],
        scratch_shapes=[
            pltpu.VMEM((HALO + length, WB), F32),
            pltpu.VMEM((length + 8, WB), F32),
            pltpu.VMEM((length, WB), F32),
            pltpu.VMEM((length, WB), F32),
            pltpu.VMEM((blocks, T, T), F32),
            pltpu.VMEM((blocks, T, T), F32),
            pltpu.VMEM((length, 128), F32),
            pltpu.VMEM((length, 128), F32),
            pltpu.VMEM((length, 128), F32),
        ],
        compiler_params=params(),
        cost_estimate=cost(3e10, 16e6),
    )(
        r_low, halo, r_low, halo, taps, shift, taps, shift, skip, prm, p, pt, b, c, bt, ct,
        s_in, g_in, dy, y,
    )


def pass_along(local, decay, order):
    hops = lax.axis_size("seq") - 1
    state = jnp.zeros_like(local)
    message = local
    for hop in range(hops):
        state = lax.ppermute(message, "seq", order)
        if hop < hops - 1:
            message = (local.astype(F32) + decay * state.astype(F32)).astype(BF16)
    return state


def on_device(
    hidden_in, cotangent, norm_gain, input_projection_weight, conv_weight, conv_bias, dt_bias,
    a_log, skip, gate_gain, output_projection_weight,
):
    layers = input_projection_weight.shape[0]
    seq_parts = lax.axis_size("seq")
    up = [(z, z + 1) for z in range(seq_parts - 1)]
    down = [(z + 1, z) for z in range(seq_parts - 1)]

    small = [norm_gain, conv_weight, conv_bias, dt_bias, a_log, skip, gate_gain]
    flat = jnp.concatenate([a.reshape(layers, -1) for a in small], axis=1)
    packed = lax.all_gather(flat, "fsdp", axis=0).astype(F32)
    shards = packed.shape[0]
    unpacked = []
    start = 0
    for a in small:
        width = a[0].size
        piece = packed[:, :, start : start + width].reshape((shards,) + a.shape)
        start += width
        piece = jnp.moveaxis(piece, 0, -2)
        unpacked.append(piece.reshape(a.shape[:-1] + (shards * a.shape[-1],)))
    gains, taps_all, shift_all, bias_all, rate_all, skip_all, gate_all = unpacked

    weights = []
    for layer in range(layers):
        w = input_projection_weight[layer]
        weights.append(
            (
                lax.all_gather(w[:, DI:], "fsdp", axis=0, tiled=True),
                lax.all_gather(w[:, :DI], "fsdp", axis=0, tiled=True),
                lax.all_gather(output_projection_weight[layer], "fsdp", axis=0, tiled=True),
            )
        )

    hidden = hidden_in[0].astype(F32)
    stored = []
    for layer in range(layers):
        w_rest, w_gate, w_out = weights[layer]
        r_in = lax.rsqrt(jnp.mean(hidden * hidden, axis=1, keepdims=True) + EPS)
        normed = (hidden * r_in * gains[layer][None, :]).astype(BF16)
        r_low = dot(normed, w_rest).astype(BF16)
        halo = lax.ppermute(r_low[-HALO:, :CC], "seq", up)
        gate = dot(normed, w_gate)
        taps = taps_all[layer]
        shift = shift_all[layer][None, :]
        skip_wide = jnp.repeat(skip_all[layer], P_SIZE)[None, :]
        prm = jnp.zeros((8, 128), F32)
        prm = prm.at[0].set(jnp.tile(bias_all[layer], 4))
        prm = prm.at[1].set(jnp.tile(-jnp.exp(rate_all[layer]), 4))
        dt_low = jnp.tile(r_low[:, CC:], (1, 4))
        f, decay, p, pt, b, c, bt, ct = local_state(r_low, halo, dt_low, taps, shift, prm)
        s_in = pass_along(f, decay[0:1], up)
        y = local_scan(r_low, halo, taps, shift, skip_wide, p, pt, b, c, bt)
        y, gate_low = gate_forward(y, gate, p, c, s_in, gate_all[layer][None, :])
        stored.append(
            (
                hidden, r_in, normed, r_low, halo, gate, taps, shift, skip_wide, prm, decay, p,
                pt, b, c, bt, ct, s_in, y, gate_low,
            )
        )
        hidden = hidden + dot(gate_low, w_out)
    block_out = hidden.astype(BF16)[None]

    grad = cotangent[0].astype(F32)
    big = [None] * layers
    vectors = [None] * layers
    for layer in reversed(range(layers)):
        (
            hidden, r_in, normed, r_low, halo, gate, taps, shift, skip_wide, prm, decay, p,
            pt, b, c, bt, ct, s_in, y, gate_low,
        ) = stored[layer]
        w_rest, w_gate, w_out = weights[layer]
        d_branch = grad.astype(BF16)
        dgn = dot_nt(d_branch, w_out)
        dgate, dmix, gain_out_grad, g_local = gate_backward(
            y, gate, dgn, p, ct, gate_all[layer][None, :]
        )
        g_in = pass_along(g_local, decay[0:1], down)
        out_grad = dot_tn(gate_low, d_branch).astype(BF16)
        gate_w_grad = dot_tn(normed, dgate).astype(BF16)
        dv, tail, head, stats, bdv, btail, bhead, bstats, ddt, dtstats = scan_backward(
            r_low, halo, taps, shift, skip_wide, prm, p, pt, b, c, bt, ct, s_in, g_in, dmix, y
        )
        heads_in = lax.ppermute(jnp.concatenate([head, bhead], axis=1), "seq", down)
        tail = jnp.concatenate([tail, btail], axis=1)
        fix = [tail[j : j + 1] for j in range(8)]
        for j in range(3):
            for k in range(j + 1):
                fix[5 + j] = fix[5 + j] + taps[k : k + 1] * heads_in[j - k : j - k + 1]
        d_rest = jnp.concatenate([dv, bdv, ddt[:, :H]], axis=1)
        d_rest = lax.dynamic_update_slice(
            d_rest, jnp.concatenate(fix, axis=0).astype(BF16), (d_rest.shape[0] - 8, 0)
        )
        rest_w_grad = dot_tn(normed, d_rest).astype(BF16)
        d_normed = dot_nt(dgate, w_gate) + dot_nt(d_rest, w_rest)
        q = hidden * r_in
        dq = d_normed * gains[layer][None, :]
        gain_in_grad = jnp.sum(d_normed * q, axis=0)
        grad = grad + r_in * (dq - q * jnp.mean(dq * q, axis=1, keepdims=True))
        big[layer] = [
            lax.psum(lax.psum_scatter(a, "fsdp", scatter_dimension=0, tiled=True), "seq")
            for a in (out_grad, gate_w_grad, rest_w_grad)
        ]
        stats = jnp.concatenate([stats, bstats], axis=1)
        vectors[layer] = [
            gain_in_grad,
            stats[0:4],
            stats[4],
            dtstats[1, :H],
            dtstats[0, :H],
            stats[5, :DI].reshape(H, P_SIZE).sum(axis=1),
            gain_out_grad[0],
        ]

    rows = []
    for a, member in zip(small, range(len(small))):
        full = jnp.stack([vectors[layer][member] for layer in range(layers)])
        full = full.reshape(a.shape[:-1] + (shards, a.shape[-1]))
        rows.append(jnp.moveaxis(full, -2, 0).reshape(shards, -1))
    summed = lax.psum(jnp.concatenate(rows, axis=1), ("fsdp", "seq"))
    mine = lax.dynamic_index_in_dim(summed, lax.axis_index("fsdp"), 0, keepdims=False)
    outs = []
    start = 0
    for a in small:
        outs.append(mine[start : start + a.size].reshape(a.shape))
        start += a.size
    in_w = jnp.stack(
        [jnp.concatenate([big[k][1], big[k][2]], axis=1) for k in range(layers)]
    ).astype(F32)
    out_w = jnp.stack([big[k][0] for k in range(layers)]).astype(F32)
    return (
        block_out, grad[None], outs[0], in_w, outs[1], outs[2], outs[3], outs[4], outs[5],
        outs[6], out_w,
    )


def solution(mesh):
    tokens = P("fsdp", "seq", None)
    vector = P(None, "fsdp")
    matrix = P(None, "fsdp", None)
    channels = P(None, None, "fsdp")
    return jax.shard_map(
        on_device,
        mesh=mesh,
        in_specs=(
            tokens, tokens, vector, matrix, channels, vector, vector, vector, vector, vector,
            matrix,
        ),
        out_specs=(
            tokens, tokens, vector, matrix, channels, vector, vector, vector, vector, vector,
            matrix,
        ),
        check_vma=False,
    )
```

time: 1610 us -> 1010 us (0.63)
  other arithmetic: 277 us -> 25.2 us
  matrix products: 329 us -> 102 us
  local copies, waits for them, and re-layouts: 257 us -> 70.1 us
  Pallas kernels: 0 us -> 163 us
  blocking collectives: 129 us -> 10.7 us
  waiting for transfers between devices: 530 us -> 565 us
    all_to_all x12 -> x0, waiting for transfers between devices: 236 us -> none  [the longest x2 94.6 us: on_device(): lax.all_to_all(d_mixed.astype(jnp.bfloat16), 'seq', split_axis=1, concat_...]
    dot_general x36 -> x18, matrix products: 329 us -> 102 us  [the longest x6 38.2 us: dot(): return jnp.dot(a, b, preferred_element_type=F32)]
    psum x1 -> x2, waiting for transfers between devices: 65.5 us -> 241 us  [the longest x1 122 us: on_device(): lax.psum(lax.psum_scatter(a, 'fsdp', scatter_dimension=0, tiled=True), 's...]
    pallas_call x0 -> x10, Pallas kernels: none -> 163 us  [the longest x2 68.5 us: scan_backward(): pl.pallas_call(back_kernel, name='scan_backward', grid=(STEPS,), in_specs...]
    reduce_sum x33 -> x3, other arithmetic: 84.9 us -> 0.51 us  [the longest x1 0.28 us: on_device(): r_in = lax.rsqrt(jnp.mean(hidden * hidden, axis=1, keepdims=True) + EPS)]
    reshape x24 -> x17, local copies, waits for them, and re-layouts: 88.1 us -> 4.77 us  [the longest x6 3.86 us: on_device(): outs.append(mine[start:start + a.size].reshape(a.shape))]
    another operation x31 -> x8, other arithmetic: 80.4 us -> 1.65 us  [the longest x2 1.46 us: on_device(): jnp.stack([jnp.concatenate([big[k][1], big[k][2]], axis=1) for k in range...]
    ppermute x0 -> x16, waiting for transfers between devices: none -> 74.6 us  [the longest x12 66.8 us: pass_along(): state = lax.ppermute(message, 'seq', order)]
  transfers between devices with their start and end apart: 27 -> 30, of which waited for: 15 -> 22; matrix products, arithmetic and copies ran while one was open for 33% -> 16% of each run, Pallas kernels for 0% -> 15%
where the time goes in v1:
time: 1010 us; the launch traced here: 998 us
  waiting for transfers between devices  565 us (56%)
  Pallas kernels  163 us (16%)
  matrix products  102 us (10%)
  local copies, waits for them, and re-layouts  70.1 us (7%)
  starting transfers between devices  46.9 us (5%)
  other arithmetic  25.2 us (2%)
  between operations  15.6 us (2%)
  blocking collectives  10.7 us (1%)
    reduce_scatter x3, waiting for transfers between devices, on_device(): lax.psum_scatter(a, 'fsdp', scatter_dimension=0, tiled=True)  163 us
    psum x1, waiting for transfers between devices, on_device(): lax.psum(lax.psum_scatter(a, 'fsdp', scatter_dimension=0, tiled=True), 's...  122 us
    psum x1, waiting for transfers between devices, on_device(): summed = lax.psum(jnp.concatenate(rows, axis=1), ('fsdp', 'seq'))  119 us
    pallas_call x2, Pallas kernels, scan_backward(): pl.pallas_call(back_kernel, name='scan_backward', grid=(STEPS,), in_specs...  68.5 us
    ppermute x12, waiting for transfers between devices, pass_along(): state = lax.ppermute(message, 'seq', order)  66.8 us
    unnamed x192, local copies, waits for them, and re-layouts  44.6 us
    all_gather x2, waiting for transfers between devices, on_device(): lax.all_gather(w[:, DI:], 'fsdp', axis=0, tiled=True)  43.4 us
    dot_general x6, matrix products, dot(): return jnp.dot(a, b, preferred_element_type=F32)  38.2 us
  transfers between devices with their start and end apart: 30, of which 22 were waited for; matrix products, arithmetic and copies ran while one was open for 16% of the time, Pallas kernels for 15%

profile of v1, /device:TPU:0, one launch (start us, length us, event | category | flops | bytes accessed | tf_op | source)
XLA Modules:
  0.0 997.6 jit_solution(5649296117953814716)
XLA Ops:
  14.7 10.7 %all-gather.3 = bf16[8,2,1836]{2,1,0:T(2,128)(2,1)S(1)} all-gather(bf16[1,2,1836]{2,1,0:T(2,128)(2,1)S(1)} %bitcast.171), channel_id=2, replica_groups=mesh['seq'=4,'fsdp'=8] {'fsdp'}, dimensions={0}, use_global_device_ids=true | all-gather | bytes 66096 | tf_op jit(solution)/shard_map/all_gather | solution.py:558
  28.9 24.4 %all-gather.11.cloned.1.call-done = bf16[1024,2336]{0,1:T(8,128)(2,1)} async-done(((bf16[128,2336]{0,1:T(8,128)(2,1)}), bf16[1024,2336]{0,1:T(8,128)(2,1)}) %all-gather.11.cloned.1.call-update) | async-done | bytes 4784144 | tf_op jit(solution)/shard_map/all_gather | solution.py:575
  53.3 5.6 convolution_convert_fusion.3.v_ref.bc_ref
  59.0 3.4 collective-permute-start
  64.4 16.1 %local_state.2 = (bf16[128,2048]{1,0:T(8,128)(2,1)S(1)}, f32[8,2048]{1,0:T(8,128)S(1)}, f32[512,128]{1,0:T(8,128)S(1)}, f32[128,512]{1,0:T(8,128)S(1)}, bf16[512...) custom-call(bf16[512,2336]{1,0:T(8,128)(2,1)} %copy-done, ...), custom_call_target="tpu_custom_call" | custom-call | flops 4000000000 | bytes 8000000 | tf_op jit(solution)/shard_map/local_state/pallas_call | solution.py:410
  83.8 4.4 collective-permute-start.1
  89.9 9.0 collective-permute-done.1
  99.9 5.4 collective-permute-start.2
  105.3 6.9 fusion.55.gate_ref
  112.2 2.5 collective-permute-done.2
  115.9 4.6 collective-permute-start.3
  123.4 13.8 %local_scan.2.y_ref = f32[512,2048]{1,0:T(8,128)} custom-call(bf16[512,2336]{1,0:T(8,128)(2,1)S(1)} %copy-done.1, bf16[16,2304]{1,0:T(8,128)(2,1)S(1)} %collective-permute-done.halo_ref.bchalo_ref, f32[4,2304]{1,0:T(4,128)S(1)} %squeeze.33.taps_ref.bctaps_ref, f32[1,2304]{1,0:T(1,128)S(1)} %slice.378.shift_ref.bcshift_ref, ...), custom_call_target="tpu_custom_call" | custom-call | flops 15000000512 | bytes 8000000 | tf_op jit(solution)/shard_map/local_scan/pallas_call | solution.py:435
  137.2 7.4 gate_forward.2
  145.4 6.9 multiply_reduce_fusion.2
  152.4 2.8 multiply_convert_fusion
  155.2 19.0 %all-gather.15.cloned.1.call-done = bf16[1024,2336]{0,1:T(8,128)(2,1)} async-done(((bf16[128,2336]{0,1:T(8,128)(2,1)}), bf16[1024,2336]{0,1:T(8,128)(2,1)}) %all-gather.15.cloned.1.call-update) | async-done | bytes 4784144 | tf_op jit(solution)/shard_map/all_gather | solution.py:575
  174.2 5.6 convolution_convert_fusion.2.v_ref.bc_ref
  179.9 3.4 collective-permute-start.4
  185.2 16.1 %local_state.3 = (bf16[128,2048]{1,0:T(8,128)(2,1)S(1)}, f32[8,2048]{1,0:T(8,128)S(1)}, f32[512,128]{1,0:T(8,128)S(1)}, f32[128,512]{1,0:T(8,128)S(1)}, bf16[512...) custom-call(bf16[512,2336]{1,0:T(8,128)(2,1)} %copy-done.2, ...), custom_call_target="tpu_custom_call" | custom-call | flops 4000000000 | bytes 8000000 | tf_op jit(solution)/shard_map/local_state/pallas_call | solution.py:410
  205.3 4.8 collective-permute-start.5
  210.1 2.7 all-gather.21.cloned.1.call-done
  212.7 6.9 fusion.dgn_ref
  221.4 5.5 collective-permute-start.6
  226.8 25.1 %all-gather.17.cloned.1.call-done = bf16[1024,2048]{0,1:T(8,128)(2,1)} async-done(((bf16[128,2048]{0,1:T(8,128)(2,1)}), bf16[1024,2048]{0,1:T(8,128)(2,1)}) %all-gather.17.cloned.1.call-update) | async-done | bytes 4194320 | tf_op jit(solution)/shard_map/all_gather | solution.py:576
  251.9 6.8 fusion.65.gate_ref
  260.0 3.4 collective-permute-start.7
  267.1 13.8 %local_scan.3.y_ref = f32[512,2048]{1,0:T(8,128)} custom-call(bf16[512,2336]{1,0:T(8,128)(2,1)S(1)} %copy-done.3, bf16[16,2304]{1,0:T(8,128)(2,1)S(1)} %collective-permute-done.4.halo_ref.bchalo_ref, f32[4,2304]{1,0:T(4,128)S(1)} %squeeze.37.taps_ref.bctaps_ref, f32[1,2304]{1,0:T(1,128)S(1)} %slice.398.shift_ref.bcshift_ref, ...), custom_call_target="tpu_custom_call" | custom-call | flops 15000000512 | bytes 8000000 | tf_op jit(solution)/shard_map/local_scan/pallas_call | solution.py:435
  280.9 7.1 gate_forward.3
  289.4 10.0 %gate_backward.2 = (bf16[512,2048]{1,0:T(8,128)(2,1)S(1)}, bf16[512,2048]{1,0:T(8,128)(2,1)}, f32[8,2048]{1,0:T(8,128)S(1)}, bf16[128,2048]{1,0:T(8,128)(2,1)S(1)}) custom-call(f32[512,2048]{1,0:T(8,128)} %get-tuple-element.123.y_ref, f32[512,2048]{1,0:T(8,128)} %fusion.65.gate_ref, f32[512,2048]{1,0:T(8,128)} %fusion.dgn_ref, f32[512,128]{1,0:T(8,128)S(1)} %copy-done.21, ...), custom_call_target="tpu_custom_call" | custom-call | flops 10000000000 | bytes 17000000 | tf_op jit(solution)/shard_map/gate_backward/pallas_call | solution.py:471
  301.0 14.4 %collective-permute-done.8 = bf16[128,2048]{1,0:T(8,128)(2,1)S(1)} collective-permute-done((bf16[128,2048]{1,0:T(8,128)(2,1)S(1)}, bf16[128,2048]{1,0:T(8,128)(2,1)S(1)}, u32[]{:S(2)}, u32[]{:S(2)}) %collective-permute-start.8) | collective-permute-done | bytes 524320 | tf_op jit(solution)/shard_map/ppermute | solution.py:541
  316.8 13.6 %collective-permute-done.9 = bf16[128,2048]{1,0:T(8,128)(2,1)S(1)} collective-permute-done((bf16[128,2048]{1,0:T(8,128)(2,1)S(1)}, bf16[128,2048]{1,0:T(8,128)(2,1)S(1)}, u32[]{:S(2)}, u32[]{:S(2)}) %collective-permute-start.9) | collective-permute-done | bytes 524320 | tf_op jit(solution)/shard_map/ppermute | solution.py:541
  333.5 6.0 convolution_convert_fusion.6
  339.8 5.7 collective-permute-done.10.gin_ref
  345.5 34.3 %scan_backward.2 = (bf16[512,2048]{1,0:T(8,128)(2,1)}, f32[8,2048]{1,0:T(8,128)S(1)}, f32[8,2048]{1,0:T(8,128)S(1)}, f32[8,2048]{1,0:T(8,128)S(1)}, bf16[512,256...) custom-call(bf16[512,2336]{1,0:T(8,128)(2,1)} %copy-done.2, ...), custom_call_target="tpu_custom_call" | custom-call | flops 30000001024 | bytes 16000000 | tf_op jit(solution)/shard_map/scan_backward/pallas_call | solution.py:495
  383.0 3.1 collective-permute-done.11
  386.2 4.9 fusion.66
  391.2 4.5 multiply_reduce_fusion
  395.7 2.3 multiply_add_fusion
  398.5 4.4 fusion.4.dgn_ref
  403.0 10.1 %gate_backward.3 = (bf16[512,2048]{1,0:T(8,128)(2,1)S(1)}, bf16[512,2048]{1,0:T(8,128)(2,1)}, f32[8,2048]{1,0:T(8,128)S(1)}, bf16[128,2048]{1,0:T(8,128)(2,1)S(1)}) custom-call(f32[512,2048]{1,0:T(8,128)} %get-tuple-element.135.y_ref, f32[512,2048]{1,0:T(8,128)} %fusion.55.gate_ref, f32[512,2048]{1,0:T(8,128)} %fusion.4.dgn_ref, f32[512,128]{1,0:T(8,128)S(1)} %copy-done.19, ...), custom_call_target="tpu_custom_call" | custom-call | flops 10000000000 | bytes 17000000 | tf_op jit(solution)/shard_map/gate_backward/pallas_call | solution.py:471
  414.4 4.6 convolution_convert_fusion
  419.0 7.3 copy.75
  429.5 11.3 %collective-permute-done.13 = bf16[128,2048]{1,0:T(8,128)(2,1)S(1)} collective-permute-done((bf16[128,2048]{1,0:T(8,128)(2,1)S(1)}, bf16[128,2048]{1,0:T(8,128)(2,1)S(1)}, u32[]{:S(2)}, u32[]{:S(2)}) %collective-permute-start.13) | collective-permute-done | bytes 524320 | tf_op jit(solution)/shard_map/ppermute | solution.py:541
  443.6 9.5 collective-permute-done.14.gin_ref
  453.1 34.2 %scan_backward.3 = (bf16[512,2048]{1,0:T(8,128)(2,1)}, f32[8,2048]{1,0:T(8,128)S(1)}, f32[8,2048]{1,0:T(8,128)S(1)}, f32[8,2048]{1,0:T(8,128)S(1)}, bf16[512,256...) custom-call(bf16[512,2336]{1,0:T(8,128)(2,1)} %copy-done, ...), custom_call_target="tpu_custom_call" | custom-call | flops 30000001024 | bytes 16000000 | tf_op jit(solution)/shard_map/scan_backward/pallas_call | solution.py:495
  490.6 3.0 collective-permute-done.15
  495.2 4.6 convolution_convert_fusion.1
  499.8 7.2 copy.71
  508.6 5.6 convolution_convert_fusion.4
  516.0 6.2 convolution_convert_fusion.5
  523.9 6.0 convolution_convert_fusion.7
  532.0 5.6 fusion.67
  537.7 4.1 fusion.18
  542.8 2.0 copy.74
  544.8 2.2 copy.76
  547.0 14.4 %reduce-scatter.19.cloned.1.call-done = bf16[128,2336]{1,0:T(8,128)(2,1)} async-done(((bf16[1024,2336]{1,0:T(8,128)(2,1)}), bf16[128,2336]{1,0:T(8,128)(2,1)}) %reduce-scatter.19.cloned.1.call-update) | async-done | bytes 598032
  561.4 2.1 copy.72
  563.5 52.8 %reduce-scatter.17.cloned.1.call-done = bf16[256,1024]{1,0:T(8,128)(2,1)} async-done(((bf16[2048,1024]{1,0:T(8,128)(2,1)}), bf16[256,1024]{1,0:T(8,128)(2,1)}) %reduce-scatter.17.cloned.1.call-update) | async-done | bytes 524304 | tf_op jit(solution)/shard_map/reduce_scatter | solution.py:647
  616.3 54.7 %reduce-scatter.15.cloned.1.call-done = bf16[256,1024]{1,0:T(8,128)(2,1)} async-done(((bf16[2048,1024]{1,0:T(8,128)(2,1)}), bf16[256,1024]{1,0:T(8,128)(2,1)}) %reduce-scatter.15.cloned.1.call-update) | async-done | bytes 524304 | tf_op jit(solution)/shard_map/reduce_scatter | solution.py:647
  671.0 55.5 %reduce-scatter.13.cloned.1.call-done = bf16[128,2048]{1,0:T(8,128)(2,1)} async-done(((bf16[1024,2048]{1,0:T(8,128)(2,1)}), bf16[128,2048]{1,0:T(8,128)(2,1)}) %reduce-scatter.13.cloned.1.call-update) | async-done | bytes 524304 | tf_op jit(solution)/shard_map/reduce_scatter | solution.py:647
  726.6 6.3 fusion.24
  734.8 118.6 %all-reduce.6.cloned.1.call-done = f32[8,3672]{1,0:T(8,128)} async-done(((f32[8,3672]{1,0:T(8,128)}), f32[8,3672]{1,0:T(8,128)}) %all-reduce.6.cloned.1.call-update) | async-done | bytes 117520 | tf_op jit(solution)/shard_map/psum | solution.py:666
  862.0 122.1 %all-reduce.8.cloned.1.call-done = (bf16[128,2336]{0,1:T(8,128)(2,1)}, bf16[128,2048]{0,1:T(8,128)(2,1)}, bf16[128,2336]{0,1:T(8,128)(2,1)}, bf16[128,2048]{1,0:...) async-done(((bf16[128,2336]{0,1:T(8,128)(2,1)}, bf16[128,2048]{0,1:T(8,128)(2,1)}, bf16[128,2336]{0,1:T(8,128)(2,1)}, ...) | async-done | bytes 3293200 | tf_op jit(solution)/shard_map/psum | solution.py:647
  988.5 2.4 maximum_convert_fusion
  (383 shorter events, 82.1 us)
Async XLA Ops:
  7.2 46.1 %all-gather.11.cloned.1.call-start = ((), (), s32[]{:S(2)}) async-start(), calls=%async_computation.6 | async-start | bytes 5382144 | tf_op jit(solution)/shard_map/all_gather | solution.py:575
  9.9 95.5 %all-gather.13.cloned.1.call-start = ((), (), s32[]{:S(2)}) async-start(), calls=%async_computation.7 | async-start | bytes 4718592 | tf_op jit(solution)/shard_map/all_gather | solution.py:576
  10.8 134.7 %all-gather.19.cloned.1.call-start = ((), (), s32[]{:S(2)}) async-start(), calls=%async_computation.14 | async-start | bytes 4718592 | tf_op jit(solution)/shard_map/all_gather | solution.py:577
  11.9 162.3 %all-gather.15.cloned.1.call-start = ((), (), s32[]{:S(2)}) async-start(), calls=%async_computation.8 | async-start | bytes 5382144 | tf_op jit(solution)/shard_map/all_gather | solution.py:575
  12.0 14.8 %copy-start.52 = (bf16[1,512,1024]{2,1,0:T(8,128)(2,1)S(1)}, bf16[1,512,1024]{2,1,0:T(8,128)(2,1)}, u32[]{:S(2)}) copy-start(bf16[1,512,1024]{2,1,0:T(8,128)(2,1)} %param.19) | copy-start | bytes 3145732
  12.9 199.9 %all-gather.21.cloned.1.call-start = ((), (), s32[]{:S(2)}) async-start(), calls=%async_computation.15 | async-start | bytes 4718592 | tf_op jit(solution)/shard_map/all_gather | solution.py:577
  13.5 238.5 %all-gather.17.cloned.1.call-start = ((), (), s32[]{:S(2)}) async-start(), calls=%async_computation.9 | async-start | bytes 4718592 | tf_op jit(solution)/shard_map/all_gather | solution.py:576
  14.4 528.4 %reduce-scatter.21.cloned.1.call-start = ((), (), s32[]{:S(2)}) async-start(), calls=%async_computation.17 | async-start | bytes 4718592
  27.1 31.9 %copy-start.79 = (f32[512]{0:T(512)}, f32[512]{0:T(512)S(1)}, u32[]{:S(2)}) copy-start(f32[512]{0:T(512)S(1)} %add_rsqrt_fusion.1) | copy-start | bytes 6148
  27.3 31.7 %copy-start.62 = (f32[8,2,4,288]{3,0,2,1:T(8,128)}, f32[8,2,4,288]{3,0,2,1:T(8,128)S(1)}, u32[]{:S(2)}) copy-start(f32[8,2,4,288]{3,0,2,1:T(8,128)S(1)} %copy.80) | copy-start | bytes 221188
  27.3 78.0 %copy-start.74 = (f32[1,8,128]{2,0,1:T(1,128)}, f32[1,8,128]{2,0,1:T(1,128)S(1)}, u32[]{:S(2)}) copy-start(f32[1,8,128]{2,0,1:T(1,128)S(1)} %get-tuple-element.200) | copy-start | bytes 12292
  59.0 5.4 collective-permute-start
  63.3 17.2 %copy-start.4 = (f32[8,128]{1,0:T(8,128)}, f32[8,128]{1,0:T(8,128)S(1)}, u32[]{:S(2)}) copy-start(f32[8,128]{1,0:T(8,128)S(1)} %scatter.15.prm_ref) | copy-start | bytes 12292
  63.5 24.6 %copy-start.73 = (f32[2,8,4]{2,0,1:T(2,128)S(1)}, f32[2,8,4]{2,0,1:T(2,128)}, u32[]{:S(2)}) copy-start(f32[2,8,4]{2,0,1:T(2,128)} %get-tuple-element.188) | copy-start | bytes 772
  83.8 53.4 %copy-start.29 = (bf16[512,128]{1,0:T(8,128)(2,1)}, bf16[512,128]{1,0:T(8,128)(2,1)S(1)}, u32[]{:S(2)}) copy-start(bf16[512,128]{1,0:T(8,128)(2,1)S(1)} %get-tuple-element.110.c_ref) | copy-start | bytes 393220
  83.8 15.1 %collective-permute-start.1 = (bf16[128,2048]{1,0:T(8,128)(2,1)S(1)}, bf16[128,2048]{1,0:T(8,128)(2,1)S(1)}, u32[]{:S(2)}, u32[]{:S(2)}) collective-permute-start(bf16[128,2048]{1,0:T(8,128)(2,1)S(1)} %get-tuple-element.112), channel_id=1, source_target_pairs={{0,8},{8,16},{16,24},{1,9},{9,17},{17,25},{2,10},{10,18},{18,26},{... | collective-permute-start | bytes 1572872 | tf_op jit(solution)/shard_map/ppermute | solution.py:541
  89.9 24.9 %copy-start.68 = (f32[1,2048]{1,0:T(1,128)}, f32[1,2048]{1,0:T(1,128)S(1)}, u32[]{:S(2)}) copy-start(f32[1,2048]{1,0:T(1,128)S(1)} %slice.387) | copy-start | bytes 24580
  99.9 20.7 %copy-start.1 = (bf16[512,2336]{1,0:T(8,128)(2,1)S(1)}, bf16[512,2336]{1,0:T(8,128)(2,1)}, u32[]{:S(2)}) copy-start(bf16[512,2336]{1,0:T(8,128)(2,1)} %copy-done) | copy-start | bytes 7176196
  99.9 20.7 %copy-start.35 = (bf16[512,128]{1,0:T(8,128)(2,1)S(1)}, bf16[512,128]{1,0:T(8,128)(2,1)}, u32[]{:S(2)}) copy-start(bf16[512,128]{1,0:T(8,128)(2,1)} %copy-done.34) | copy-start | bytes 393220
  99.9 14.8 %collective-permute-start.2 = (bf16[128,2048]{1,0:T(8,128)(2,1)}, bf16[128,2048]{1,0:T(8,128)(2,1)}, u32[]{:S(2)}, u32[]{:S(2)}) collective-permute-start(bf16[128,2048]{1,0:T(8,128)(2,1)} %fusion.27), channel_id=1, source_target_pairs={{0,8},{8,16},{16,24},{1,9},{9,17},{17,25},{2,10},{10,18},{18,26},{... | collective-permute-start | bytes 1572872 | tf_op jit(solution)/shard_map/ppermute | solution.py:541
  115.9 21.2 %collective-permute-start.3 = (bf16[128,2048]{1,0:T(8,128)(2,1)S(1)}, bf16[128,2048]{1,0:T(8,128)(2,1)S(1)}, u32[]{:S(2)}, u32[]{:S(2)}) collective-permute-start(bf16[128,2048]{1,0:T(8,128)(2,1)S(1)} %fusion.28), channel_id=1, source_target_pairs={{0,8},{8,16},{16,24},{1,9},{9,17},{17,25},{2,10},{10,18},{18,26},{... | collective-permute-start | bytes 1572872 | tf_op jit(solution)/shard_map/ppermute | solution.py:541
  145.4 7.0 copy-start.10
  155.2 28.1 %copy-start.78 = (f32[8,4]{1,0:T(8,128)S(1)}, f32[8,4]{1,0:T(8,128)}, u32[]{:S(2)}) copy-start(f32[8,4]{1,0:T(8,128)} %get-tuple-element.164) | copy-start | bytes 388
  155.2 28.2 %copy-start.72 = (f32[8,288]{1,0:T(8,128)S(1)}, f32[8,288]{1,0:T(8,128)}, u32[]{:S(2)}) copy-start(f32[8,288]{1,0:T(8,128)} %get-tuple-element.162) | copy-start | bytes 27652
  155.2 28.3 %copy-start.77 = (f32[8,4]{1,0:T(8,128)S(1)}, f32[8,4]{1,0:T(8,128)}, u32[]{:S(2)}) copy-start(f32[8,4]{1,0:T(8,128)} %get-tuple-element.210) | copy-start | bytes 388
  155.2 28.5 %copy-start.76 = (f32[8,4]{1,0:T(8,128)S(1)}, f32[8,4]{1,0:T(8,128)}, u32[]{:S(2)}) copy-start(f32[8,4]{1,0:T(8,128)} %get-tuple-element.168) | copy-start | bytes 388
  155.2 28.8 %copy-start.70 = (f32[1,4,8,288]{3,2,1,0:T(8,128)S(1)}, f32[1,4,8,288]{3,2,1,0:T(8,128)}, u32[]{:S(2)}) copy-start(f32[1,4,8,288]{3,2,1,0:T(8,128)} %get-tuple-element.195) | copy-start | bytes 110596
  179.9 5.4 collective-permute-start.4
  205.3 15.1 %collective-permute-start.5 = (bf16[128,2048]{1,0:T(8,128)(2,1)S(1)}, bf16[128,2048]{1,0:T(8,128)(2,1)S(1)}, u32[]{:S(2)}, u32[]{:S(2)}) collective-permute-start(bf16[128,2048]{1,0:T(8,128)(2,1)S(1)} %get-tuple-element.120), channel_id=1, source_target_pairs={{0,8},{8,16},{16,24},{1,9},{9,17},{17,25},{2,10},{10,18},{18,26},{... | collective-permute-start | bytes 1572872 | tf_op jit(solution)/shard_map/ppermute | solution.py:541
  221.4 42.0 %copy-start.3 = (bf16[512,2336]{1,0:T(8,128)(2,1)S(1)}, bf16[512,2336]{1,0:T(8,128)(2,1)}, u32[]{:S(2)}) copy-start(bf16[512,2336]{1,0:T(8,128)(2,1)} %copy-done.2) | copy-start | bytes 7176196
  221.4 42.0 %copy-start.32 = (bf16[512,128]{1,0:T(8,128)(2,1)S(1)}, bf16[512,128]{1,0:T(8,128)(2,1)}, u32[]{:S(2)}) copy-start(bf16[512,128]{1,0:T(8,128)(2,1)} %copy-done.31) | copy-start | bytes 393220
  221.4 37.4 %collective-permute-start.6 = (bf16[128,2048]{1,0:T(8,128)(2,1)}, bf16[128,2048]{1,0:T(8,128)(2,1)}, u32[]{:S(2)}, u32[]{:S(2)}) collective-permute-start(bf16[128,2048]{1,0:T(8,128)(2,1)} %fusion.29), channel_id=1, source_target_pairs={{0,8},{8,16},{16,24},{1,9},{9,17},{17,25},{2,10},{10,18},{18,26},{... | collective-permute-start | bytes 1572872 | tf_op jit(solution)/shard_map/ppermute | solution.py:541
  260.0 21.0 %collective-permute-start.7 = (bf16[128,2048]{1,0:T(8,128)(2,1)S(1)}, bf16[128,2048]{1,0:T(8,128)(2,1)S(1)}, u32[]{:S(2)}, u32[]{:S(2)}) collective-permute-start(bf16[128,2048]{1,0:T(8,128)(2,1)S(1)} %fusion.30), channel_id=1, source_target_pairs={{0,8},{8,16},{16,24},{1,9},{9,17},{17,25},{2,10},{10,18},{18,26},{... | collective-permute-start | bytes 1572872 | tf_op jit(solution)/shard_map/ppermute | solution.py:541
  280.9 8.5 copy-start.49
  299.4 32.0 %copy-start.8 = (bf16[512,2048]{1,0:T(8,128)(2,1)}, bf16[512,2048]{1,0:T(8,128)(2,1)S(1)}, u32[]{:S(2)}) copy-start(bf16[512,2048]{1,0:T(8,128)(2,1)S(1)} %get-tuple-element.125) | copy-start | bytes 6291460
  299.4 33.3 %copy-start.63 = (f32[8,2,4,288]{3,0,2,1:T(8,128)S(1)}, f32[8,2,4,288]{3,0,2,1:T(8,128)}, u32[]{:S(2)}) copy-start(f32[8,2,4,288]{3,0,2,1:T(8,128)} %copy-done.62) | copy-start | bytes 221188
  299.4 34.1 %copy-start.59 = (bf16[512,1024]{1,0:T(8,128)(2,1)S(1)}, bf16[512,1024]{1,0:T(8,128)(2,1)}, u32[]{:S(2)}) copy-start(bf16[512,1024]{1,0:T(8,128)(2,1)} %multiply_convert_fusion) | copy-start | bytes 3145732
  299.4 16.0 %collective-permute-start.8 = (bf16[128,2048]{1,0:T(8,128)(2,1)S(1)}, bf16[128,2048]{1,0:T(8,128)(2,1)S(1)}, u32[]{:S(2)}, u32[]{:S(2)}) collective-permute-start(bf16[128,2048]{1,0:T(8,128)(2,1)S(1)} %get-tuple-element.126), channel_id=1, source_target_pairs={{8,0},{16,8},{24,16},{9,1},{17,9},{25,17},{10,2},{18,10},{26,18},{... | collective-permute-start | bytes 1572872 | tf_op jit(solution)/shard_map/ppermute | solution.py:541
  315.5 14.9 %collective-permute-start.9 = (bf16[128,2048]{1,0:T(8,128)(2,1)S(1)}, bf16[128,2048]{1,0:T(8,128)(2,1)S(1)}, u32[]{:S(2)}, u32[]{:S(2)}) collective-permute-start(bf16[128,2048]{1,0:T(8,128)(2,1)S(1)} %fusion.31), channel_id=1, source_target_pairs={{8,0},{16,8},{24,16},{9,1},{17,9},{25,17},{10,2},{18,10},{26,18},{... | collective-permute-start | bytes 1572872 | tf_op jit(solution)/shard_map/ppermute | solution.py:541
  331.4 14.1 %collective-permute-start.10 = (bf16[128,2048]{1,0:T(8,128)(2,1)}, bf16[128,2048]{1,0:T(8,128)(2,1)S(1)}, u32[]{:S(2)}, u32[]{:S(2)}) collective-permute-start(bf16[128,2048]{1,0:T(8,128)(2,1)} %fusion.32), channel_id=1, source_target_pairs={{8,0},{16,8},{24,16},{9,1},{17,9},{25,17},{10,2},{18,10},{26,18},{... | collective-permute-start | bytes 1572872 | tf_op jit(solution)/shard_map/ppermute | solution.py:541
  339.6 205.2 %reduce-scatter.23.cloned.1.call-start = ((), (), s32[]{:S(2)}) async-start(), calls=%async_computation.18 | async-start | bytes 5603328
  379.8 6.2 collective-permute-start.11
  403.0 11.4 %copy-start.60 = (bf16[512,1024]{1,0:T(8,128)(2,1)S(1)}, bf16[512,1024]{1,0:T(8,128)(2,1)}, u32[]{:S(2)}) copy-start(bf16[512,1024]{1,0:T(8,128)(2,1)} %multiply_convert_fusion) | copy-start | bytes 3145732
  413.1 13.4 %collective-permute-start.12 = (bf16[128,2048]{1,0:T(8,128)(2,1)S(1)}, bf16[128,2048]{1,0:T(8,128)(2,1)}, u32[]{:S(2)}, u32[]{:S(2)}) collective-permute-start(bf16[128,2048]{1,0:T(8,128)(2,1)S(1)} %get-tuple-element.138), channel_id=1, source_target_pairs={{8,0},{16,8},{24,16},{9,1},{17,9},{25,17},{10,2},{18,10},{26,18},{... | collective-permute-start | bytes 1572872 | tf_op jit(solution)/shard_map/ppermute | solution.py:541
  426.3 17.0 %copy-start.71 = (f32[1,1,8,288]{3,2,1,0:T(8,128)S(1)}, f32[1,1,8,288]{3,2,1,0:T(8,128)}, u32[]{:S(2)}) copy-start(f32[1,1,8,288]{3,2,1,0:T(8,128)} %get-tuple-element.189) | copy-start | bytes 27652
  426.3 26.8 %copy-start.5 = (f32[8,128]{1,0:T(8,128)S(1)}, f32[8,128]{1,0:T(8,128)}, u32[]{:S(2)}) copy-start(f32[8,128]{1,0:T(8,128)} %copy-done.4) | copy-start | bytes 12292
  426.3 26.8 %copy-start.7 = (bf16[128,2048]{1,0:T(8,128)(2,1)S(1)}, bf16[128,2048]{1,0:T(8,128)(2,1)}, u32[]{:S(2)}) copy-start(bf16[128,2048]{1,0:T(8,128)(2,1)} %copy-done.6) | copy-start | bytes 1572868
  426.4 26.7 %copy-start.25 = (f32[128,512]{1,0:T(8,128)S(1)}, f32[128,512]{1,0:T(8,128)}, u32[]{:S(2)}) copy-start(f32[128,512]{1,0:T(8,128)} %copy-done.23) | copy-start | bytes 786436
  426.4 26.7 %copy-start.30 = (bf16[512,128]{1,0:T(8,128)(2,1)S(1)}, bf16[512,128]{1,0:T(8,128)(2,1)}, u32[]{:S(2)}) copy-start(bf16[512,128]{1,0:T(8,128)(2,1)} %copy-done.29) | copy-start | bytes 393220
  426.4 26.7 %copy-start.36 = (bf16[512,128]{1,0:T(8,128)(2,1)S(1)}, bf16[512,128]{1,0:T(8,128)(2,1)}, u32[]{:S(2)}) copy-start(bf16[512,128]{1,0:T(8,128)(2,1)} %copy-done.34) | copy-start | bytes 393220
  426.4 26.7 %copy-start.39 = (bf16[128,512]{1,0:T(8,128)(2,1)S(1)}, bf16[128,512]{1,0:T(8,128)(2,1)}, u32[]{:S(2)}) copy-start(bf16[128,512]{1,0:T(8,128)(2,1)} %copy-done.37) | copy-start | bytes 393220
  426.4 135.0 %reduce-scatter.19.cloned.1.call-start = ((), (), s32[]{:S(2)}) async-start(), calls=%async_computation.16 | async-start | bytes 5603328
  428.2 12.6 %collective-permute-start.13 = (bf16[128,2048]{1,0:T(8,128)(2,1)S(1)}, bf16[128,2048]{1,0:T(8,128)(2,1)S(1)}, u32[]{:S(2)}, u32[]{:S(2)}) collective-permute-start(bf16[128,2048]{1,0:T(8,128)(2,1)S(1)} %fusion.33), channel_id=1, source_target_pairs={{8,0},{16,8},{24,16},{9,1},{17,9},{25,17},{10,2},{18,10},{26,18},{... | collective-permute-start | bytes 1572872 | tf_op jit(solution)/shard_map/ppermute | solution.py:541
  441.8 11.3 %collective-permute-start.14 = (bf16[128,2048]{1,0:T(8,128)(2,1)}, bf16[128,2048]{1,0:T(8,128)(2,1)S(1)}, u32[]{:S(2)}, u32[]{:S(2)}) collective-permute-start(bf16[128,2048]{1,0:T(8,128)(2,1)} %fusion.34), channel_id=1, source_target_pairs={{8,0},{16,8},{24,16},{9,1},{17,9},{25,17},{10,2},{18,10},{26,18},{... | collective-permute-start | bytes 1572872 | tf_op jit(solution)/shard_map/ppermute | solution.py:541
  487.4 6.2 collective-permute-start.15
  488.7 6.5 copy-start.53
  488.7 6.5 copy-start.75
  488.7 6.5 copy-start.80
  507.0 109.3 %reduce-scatter.17.cloned.1.call-start = ((), (), s32[]{:S(2)}) async-start(), calls=%async_computation.13 | async-start | bytes 4718592 | tf_op jit(solution)/shard_map/reduce_scatter | solution.py:647
  514.2 156.8 %reduce-scatter.15.cloned.1.call-start = ((), (), s32[]{:S(2)}) async-start(), calls=%async_computation.12 | async-start | bytes 4718592 | tf_op jit(solution)/shard_map/reduce_scatter | solution.py:647
  522.3 204.2 %reduce-scatter.13.cloned.1.call-start = ((), (), s32[]{:S(2)}) async-start(), calls=%async_computation.11 | async-start | bytes 4718592 | tf_op jit(solution)/shard_map/reduce_scatter | solution.py:647
  529.8 323.5 %all-reduce.6.cloned.1.call-start = ((), (), s32[]{:S(2)}) async-start(), calls=%async_computation.10 | async-start | bytes 237568 | tf_op jit(solution)/shard_map/psum | solution.py:666
  542.5 441.6 %all-reduce.8.cloned.1.call-start = ((), (), s32[]{:S(2)}) async-start(), calls=%async_computation.19 | async-start | bytes 6586368 | tf_op jit(solution)/shard_map/psum | solution.py:647
  547.0 179.5 %copy-start.14 = (bf16[512,2048]{1,0:T(8,128)(2,1)S(1)}, bf16[512,2048]{1,0:T(8,128)(2,1)}, u32[]{:S(2)}) copy-start(bf16[512,2048]{1,0:T(8,128)(2,1)} %copy-done.12) | copy-start | bytes 6291460
  (57 other events, 157.4 us)
Sparse Core Ops, SparseCore 0:
  10.5 42.7 all-gather.10
  55.8 37.4 all-gather.12
  95.1 36.7 all-gather.18
  134.2 40.0 all-gather.14
  176.0 36.7 all-gather.20
  214.5 37.4 all-gather.16
  339.7 52.4 reduce-scatter.20
  426.4 57.1 reduce-scatter.22
  507.1 54.1 reduce-scatter.18
  565.0 51.2 reduce-scatter.16
  619.7 51.3 reduce-scatter.14
  675.2 51.2 reduce-scatter.12
  732.1 121.2 all-reduce.5
  856.1 127.9 all-reduce.7

commit v2 on v1

--- a/solution.py
+++ b/solution.py
@@ -1,3 +1,5 @@
+import functools
+
 import jax
 import jax.numpy as jnp
 from jax import lax
@@ -8,6 +10,7 @@
 H = 32
 P_SIZE = 64
 N = 128
+D = 1024
 DI = 2048
 CC = DI + 2 * N
 T = 128
@@ -36,7 +39,7 @@
 
 
 def sigmoid(v):
-    return 1.0 / (1.0 + jnp.exp(-v))
+    return 0.5 * jnp.tanh(0.5 * v) + 0.5
 
 
 def lane_iota(rows, lanes=128):
@@ -47,20 +50,33 @@
     return lax.broadcasted_iota(jnp.int32, (rows, lanes), 0)
 
 
-def column(cols, lane):
-    return jnp.broadcast_to(cols[:, lane : lane + 1], (cols.shape[0], 128))
-
-
-def widen(columns):
-    left = lane_iota(columns[0].shape[0]) < P_SIZE
-    tiles = [
-        jnp.where(left, columns[2 * p], columns[2 * p + 1]) for p in range(len(columns) // 2)
-    ]
-    return jnp.concatenate(tiles, axis=1)
-
-
-def spread(cols, lane, heads):
-    return widen([column(cols, lane + h) for h in range(heads)])
+def parts_of(packed):
+    high = packed.astype(BF16)
+    rest = packed - high.astype(F32)
+    middle = rest.astype(BF16)
+    return jnp.concatenate([high, middle, (rest - middle.astype(F32)).astype(BF16)], axis=1)
+
+
+def pick(first, rows, lanes, shift):
+    row = jnp.bitwise_and(row_iota(rows, lanes), 127)
+    head = lax.shift_right_logical(lane_iota(rows, lanes), shift)
+    return jnp.where(row == first + head, 1.0, 0.0).astype(BF16)
+
+
+def head_lanes(first, i):
+    return pick(first + HB * i, 384, WB, 6)
+
+
+def head_tiles(first, i):
+    return pick(first + HB * i, 384, HB * 128, 7)
+
+
+def widen(tiles):
+    left = lane_iota(tiles.shape[0]) < P_SIZE
+    tile = lambda h: tiles[:, h * 128 : (h + 1) * 128]
+    return jnp.concatenate(
+        [jnp.where(left, tile(2 * p), tile(2 * p + 1)) for p in range(HB // 2)], axis=1
+    )
 
 
 def halves(tile, axis_rows=True):
@@ -69,15 +85,10 @@
     return jnp.concatenate([jnp.where(left, tile, zero), jnp.where(left, zero, tile)], axis=0)
 
 
-def head_columns(cols, i):
-    return pltpu.roll(cols, lax.rem(128 - HB * i, 128), 1)
-
-
-def head_row(pt_ref, i, h, tokens):
-    eight = pl.multiple_of(L_CUM + 8 * lax.shift_right_logical(i, 1), 8)
-    block = pt_ref[pl.ds(eight, 8), tokens]
-    odd = jnp.full((1, T), lax.rem(i, 2), jnp.int32) == 1
-    return jnp.where(odd, block[HB + h : HB + h + 1, :], block[h : h + 1, :])
+def head_rows(heads, i):
+    lane = jnp.bitwise_and(lane_iota(16, 384), 127)
+    sel = jnp.where(lane == L_CUM + HB * i + row_iota(16, 384), 1.0, 0.0).astype(BF16)
+    return dot_nt(sel, heads)
 
 
 def fill(ext, halo_ref, v_ref):
@@ -94,7 +105,7 @@
 
 def state_kernel(
     v_ref, halo_ref, bc_ref, bchalo_ref, dt_ref, taps_ref, shift_ref, bctaps_ref, bcshift_ref,
-    prm_ref, f_ref, tot_ref, p_ref, pt_ref, b_ref, c_ref, bt_ref, ct_ref, ext,
+    prm_ref, f_ref, tot_ref, x_ref, p_ref, p3_ref, b_ref, c_ref, bt_ref, ct_ref, ext,
 ):
     i = pl.program_id(0)
     blocks = v_ref.shape[0] // T
@@ -124,32 +135,33 @@
             offset = cumf[T - 1 : T, :]
             packed = jnp.where(
                 lane < L_CUM, step,
-                jnp.where(lane < L_CUMF, cum, jnp.where(lane < L_SIG, cumf, sigmoid(z))),
+                jnp.where(lane < L_CUMF, cum, jnp.where(lane < L_SIG, cumf, 1.0 / (1.0 + jnp.exp(-z)))),
             )
             p_ref[rows, :] = packed
-            pt_ref[:, rows] = packed.T
+            p3_ref[rows, :] = parts_of(packed)
 
     fill(ext, halo_ref, v_ref)
-    last = head_columns(p_ref[pl.ds(blocks * T - 8, 8), :], i)
-    tot = spread(last, L_CUMF, HB)[7:8, :]
+    steps = head_lanes(L_STEP, i)
+    sums = head_lanes(L_CUMF, i)
+    tot = dot(p3_ref[pl.ds(blocks * T - 16, 16), :], sums)[15:16, :]
     total = jnp.zeros((N, WB), F32)
     for c in range(blocks):
         rows = pl.ds(c * T, T)
         conv = conv_block(ext, taps_ref, shift_ref, c)
-        cols = head_columns(p_ref[rows, :], i)
-        w = jnp.exp(tot - spread(cols, L_CUMF, HB)) * spread(cols, L_STEP, HB)
-        wx = (conv * sigmoid(conv) * w).astype(BF16)
+        x = conv * sigmoid(conv)
+        x_ref[rows, :] = x
+        heads = p3_ref[rows, :]
+        wx = (x * (jnp.exp(tot - dot(heads, sums)) * dot(heads, steps))).astype(BF16)
         total = total + dot(bt_ref[:, rows], wx)
     f_ref[...] = total.astype(BF16)
     tot_ref[...] = jnp.broadcast_to(jnp.exp(tot), (8, WB))
 
 
 def scan_kernel(
-    v_ref, halo_ref, taps_ref, shift_ref, skip_ref, p_ref, pt_ref, b_ref, c_ref, bt_ref,
-    y_ref, ext, cb,
+    x_ref, skip_ref, p3_ref, b_ref, c_ref, bt_ref, y_ref, cb,
 ):
     i = pl.program_id(0)
-    blocks = v_ref.shape[0] // T
+    blocks = x_ref.shape[0] // T
 
     @pl.when(i == 0)
     def _():
@@ -158,23 +170,23 @@
             rows = pl.ds(c * T, T)
             cb[c] = jnp.where(causal, dot_nt(c_ref[rows, :], b_ref[rows, :]), 0.0)
 
-    fill(ext, halo_ref, v_ref)
+    steps = head_lanes(L_STEP, i)
+    sums = head_tiles(L_CUM, i)
     state = None
     for c in range(blocks):
         rows = pl.ds(c * T, T)
-        conv = conv_block(ext, taps_ref, shift_ref, c)
-        x = conv * sigmoid(conv)
-        cols = head_columns(p_ref[rows, :], i)
-        cums = [column(cols, L_CUM + h) for h in range(HB)]
-        xd = x * spread(cols, L_STEP, HB)
+        x = x_ref[rows, :]
+        heads = p3_ref[rows, :]
+        cums = dot(heads, sums)
+        turned = head_rows(heads, i)
+        xd = x * dot(heads, steps)
         parts = []
         for p in range(HB // 2):
             weights = []
             for h in (2 * p, 2 * p + 1):
-                across = head_row(pt_ref, i, h, rows)
-                weights.append(
-                    (jnp.exp(jnp.minimum(cums[h] - across, 0.0)) * cb[c]).astype(BF16)
-                )
+                across = turned[h : h + 1, :]
+                e = jnp.exp(jnp.minimum(cums[:, h * 128 : (h + 1) * 128] - across, 0.0))
+                weights.append((e * cb[c]).astype(BF16))
             parts.append(
                 dot(
                     jnp.concatenate(weights, axis=1),
@@ -192,8 +204,21 @@
             state = fresh if state is None else state * jnp.exp(tot) + fresh
 
 
-def gate_kernel(y_ref, gate_ref, p_ref, c_ref, s_ref, gain_ref, out_y_ref, out_ref):
-    grow = spread(jnp.exp(p_ref[...]), L_CUMF, H)
+def grow_factors(p_ref, sel):
+    lane = lane_iota(p_ref.shape[0])
+    inside = jnp.logical_and(lane >= L_CUMF, lane < L_SIG)
+    grow = jnp.where(inside, jnp.exp(jnp.where(inside, p_ref[...], 0.0)), 0.0)
+    high = grow.astype(BF16)
+    low = (grow - high.astype(F32)).astype(BF16)
+    return dot(jnp.concatenate([high, low], axis=1), sel[...])
+
+
+def gate_kernel(y_ref, gate_ref, p_ref, c_ref, s_ref, gain_ref, out_y_ref, out_ref, sel):
+    @pl.when(pl.program_id(0) == 0)
+    def _():
+        sel[...] = pick(L_CUMF, 256, DI, 6)
+
+    grow = grow_factors(p_ref, sel)
     y = y_ref[...] + grow * dot(c_ref[...], s_ref[...])
     out_y_ref[...] = y
     mixed = y.astype(BF16).astype(F32)
@@ -204,12 +229,14 @@
 
 
 def gate_back_kernel(
-    y_ref, gate_ref, dgn_ref, p_ref, ct_ref, gain_ref, dgate_ref, dmix_ref, gg_ref, g_ref, acc
+    y_ref, gate_ref, dgn_ref, p_ref, ct_ref, gain_ref, dgate_ref, dmix_ref, gg_ref, g_ref, acc,
+    sel,
 ):
     i = pl.program_id(0)
 
     @pl.when(i == 0)
     def _():
+        sel[...] = pick(L_CUMF, 256, DI, 6)
         acc[...] = jnp.zeros_like(acc)
         gg_ref[...] = jnp.zeros_like(gg_ref)
 
@@ -227,7 +254,7 @@
     dgate_ref[...] = (dgated * mixed * (sig * (1.0 + gate * (1.0 - sig)))).astype(BF16)
     dmix = (dgated * silu).astype(BF16)
     dmix_ref[...] = dmix
-    grow = spread(jnp.exp(p_ref[...]), L_CUMF, H)
+    grow = grow_factors(p_ref, sel)
     acc[...] += dot(ct_ref[...], (grow * dmix.astype(F32)).astype(BF16))
 
     @pl.when(i == pl.num_programs(0) - 1)
@@ -254,30 +281,70 @@
         stats_ref[k : k + 1, :] = sums[k]
 
 
-def back_kernel(
-    v_ref, halo_ref, bc_ref, bchalo_ref, taps_ref, shift_ref, bctaps_ref, bcshift_ref, skip_ref,
-    prm_ref, p_ref, pt_ref, b_ref, c_ref, bt_ref, ct_ref, s_ref, gin_ref, dy_ref, y_ref,
-    dv_ref, tail_ref, head_ref, stats_ref, bdv_ref, btail_ref, bhead_ref, bstats_ref,
-    ddt_ref, dtstats_ref,
-    ext, dext, convs, sigs, cbt, dcbt, acc, dbacc, dcacc,
+def back_inside_kernel(
+    x_ref, p3_ref, b_ref, c_ref, dy_ref, dxd_ref, dcbt_ref, cbt, first,
 ):
-    i = pl.program_id(0)
-    blocks = v_ref.shape[0] // T
-    length = blocks * T
-
-    @pl.when(i == 0)
+    i = pl.program_id(0) + first
+    blocks = x_ref.shape[0] // T
+
+    @pl.when(pl.program_id(0) == 0)
     def _():
         causal = row_iota(T) <= lane_iota(T)
         for c in range(blocks):
             rows = pl.ds(c * T, T)
             cbt[c] = jnp.where(causal, dot_nt(b_ref[rows, :], c_ref[rows, :]), 0.0)
-        dcbt[...] = jnp.zeros_like(dcbt)
+        dcbt_ref[...] = jnp.zeros_like(dcbt_ref)
+
+    steps = head_lanes(L_STEP, i)
+    sums = head_tiles(L_CUM, i)
+    for c in range(blocks):
+        rows = pl.ds(c * T, T)
+        heads = p3_ref[rows, :]
+        cums = dot(heads, sums)
+        turned = head_rows(heads, i)
+        xd = x_ref[rows, :] * dot(heads, steps)
+        dyb = dy_ref[rows, :]
+        dy = dyb.astype(F32)
+        dcb = jnp.zeros((T, T), F32)
+        for p in range(HB // 2):
+            lanes = slice(p * 128, (p + 1) * 128)
+            dm = dot_nt(halves(xd[:, lanes]).astype(BF16), dyb[:, lanes])
+            weights = []
+            for j in range(2):
+                h = 2 * p + j
+                across = turned[h : h + 1, :]
+                e = jnp.exp(jnp.minimum(across - cums[:, h * 128 : (h + 1) * 128], 0.0))
+                weights.append((e * cbt[c]).astype(BF16))
+                dcb = dcb + dm[j * T : (j + 1) * T, :] * e
+            dxd_ref[rows, lanes] = dot(
+                jnp.concatenate(weights, axis=1), halves(dy[:, lanes]).astype(BF16)
+            )
+        dcbt_ref[c] += dcb
+
+
+def back_kernel(
+    v_ref, halo_ref, bc_ref, bchalo_ref, taps_ref, shift_ref, bctaps_ref, bcshift_ref, skip_ref,
+    prm_ref, p_ref, p3_ref, b_ref, c_ref, bt_ref, ct_ref, s_ref, gin_ref, dy_ref, y_ref,
+    inside_ref,
+    low_ref, high_ref,
+    dv_ref, tail_ref, head_ref, stats_ref, bdv_ref, btail_ref, bhead_ref, bstats_ref,
+    ddt_ref, dtstats_ref,
+    ext, dext, convs, sigs, cumw, dtw, acc, dbacc, dcacc,
+):
+    i = pl.program_id(0)
+    blocks = v_ref.shape[0] // T
+    length = blocks * T
+
+    @pl.when(i == 0)
+    def _():
         acc[...] = jnp.zeros_like(acc)
         dbacc[...] = jnp.zeros_like(dbacc)
         dcacc[...] = jnp.zeros_like(dcacc)
 
     fill(ext, halo_ref, v_ref)
     dext[length:, :] = jnp.zeros((8, WB), F32)
+    steps = head_lanes(L_STEP, i)
+    sums = head_lanes(L_CUM, i)
     states = [s_ref[...].astype(F32)]
     for c in range(blocks):
         rows = pl.ds(c * T, T)
@@ -285,10 +352,13 @@
         sig = sigmoid(conv)
         convs[rows, :] = conv
         sigs[rows, :] = sig
-        cols = head_columns(p_ref[rows, :], i)
-        cumx = spread(cols, L_CUM, HB)
+        heads = p3_ref[rows, :]
+        cumx = dot(heads, sums)
+        dt = dot(heads, steps)
+        cumw[rows, :] = cumx
+        dtw[rows, :] = dt
         tot = cumx[T - 1 : T, :]
-        wx = (jnp.exp(tot - cumx) * (conv * sig * spread(cols, L_STEP, HB))).astype(BF16)
+        wx = (jnp.exp(tot - cumx) * (conv * sig * dt)).astype(BF16)
         states.append(states[-1] * jnp.exp(tot) + dot(bt_ref[:, rows], wx))
 
     ch = lax.shift_right_logical(row_iota(WB), 6)
@@ -301,32 +371,15 @@
         rows = pl.ds(c * T, T)
         conv, sig = convs[rows, :], sigs[rows, :]
         x = conv * sig
-        cols = head_columns(p_ref[rows, :], i)
-        cums = [column(cols, L_CUM + h) for h in range(HB)]
-        cumx = widen(cums)
-        dt = spread(cols, L_STEP, HB)
+        cumx, dt = cumw[rows, :], dtw[rows, :]
         tot = cumx[T - 1 : T, :]
         xd = x * dt
         xdb = xd.astype(BF16)
         dyb = dy_ref[rows, :]
         dy = dyb.astype(F32)
-        parts = []
-        for p in range(HB // 2):
-            lanes = slice(p * 128, (p + 1) * 128)
-            dm = dot_nt(halves(xd[:, lanes]).astype(BF16), dyb[:, lanes])
-            weights = []
-            for j in range(2):
-                h = 2 * p + j
-                across = head_row(pt_ref, i, h, rows)
-                e = jnp.exp(jnp.minimum(across - cums[h], 0.0))
-                weights.append((e * cbt[c]).astype(BF16))
-                dcbt[c] += dm[j * T : (j + 1) * T, :] * e
-            parts.append(
-                dot(jnp.concatenate(weights, axis=1), halves(dy[:, lanes]).astype(BF16))
-            )
         gb = grad.astype(BF16)
         w = jnp.exp(tot - cumx)
-        dxd = jnp.concatenate(parts, axis=1) + w * dot(b_ref[rows, :], gb)
+        dxd = inside_ref[rows, :] + w * dot(b_ref[rows, :], gb)
         ey = (jnp.exp(cumx) * dy).astype(BF16)
         wx = (w * xd).astype(BF16)
         dcacc[rows, :] += dot_nt(ey, states[c].astype(BF16))
@@ -358,7 +411,7 @@
         for c in range(blocks):
             rows = pl.ds(c * T, T)
             causal = row_iota(T) <= lane_iota(T)
-            m = jnp.where(causal, dcbt[c], 0.0).astype(BF16)
+            m = jnp.where(causal, low_ref[c] + high_ref[c], 0.0).astype(BF16)
             db = dbacc[rows, :] + dot(m, c_ref[rows, :])
             dc = dcacc[rows, :] + dot_tn(m, b_ref[rows, :])
             conv = conv_block(ext, bctaps_ref, bcshift_ref, c)
@@ -374,7 +427,7 @@
             packed = p_ref[rows, :]
             rate_sum = rate_sum + jnp.sum(packed * ddecay, axis=0, keepdims=True)
             dz = (pltpu.roll(a, 96, 1) + rate * ddecay) * pltpu.roll(packed, 32, 1)
-            ddt_ref[rows, :] = dz.astype(BF16)
+            ddt_ref[rows, :] = jnp.where(lane_iota(T) < H, dz, 0.0).astype(BF16)
             bias_sum = bias_sum + jnp.sum(dz, axis=0, keepdims=True)
         conv_back(ext, dext, bctaps_ref, bdv_ref, btail_ref, bhead_ref, bstats_ref, blocks)
         dtstats_ref[0:1, :] = rate_sum * rate
@@ -405,49 +458,49 @@
     return pl.CostEstimate(flops=int(flops), bytes_accessed=int(moved), transcendentals=0)
 
 
-def local_state(r_low, halo, dt_low, taps, shift, prm):
+def local_state(r_low, halo, taps, shift, prm):
     length = r_low.shape[0]
     return pl.pallas_call(
         state_kernel,
         name="local_state",
         grid=(STEPS,),
         in_specs=[
-            wide(length), wide(HALO), bc_block(length), bc_block(HALO), whole((length, 128)),
+            wide(length), wide(HALO), bc_block(length), bc_block(HALO),
+            pl.BlockSpec((length, 128), lambda i: (0, CC // 128)),
             wide(4), wide(1), bc_block(4), bc_block(1), whole((8, 128)),
         ],
         out_specs=[
-            wide(N), wide(8), whole((length, 128)), whole((128, length)),
+            wide(N), wide(8), wide(length), whole((length, 128)), whole((length, 384)),
             whole((length, N)), whole((length, N)), whole((N, length)), whole((N, length)),
         ],
         out_shape=[
-            shape_of((N, DI), BF16), shape_of((8, DI), F32), shape_of((length, 128), F32),
-            shape_of((128, length), F32), shape_of((length, N), BF16),
-            shape_of((length, N), BF16), shape_of((N, length), BF16), shape_of((N, length), BF16),
+            shape_of((N, DI), BF16), shape_of((8, DI), F32), shape_of((length, DI), F32),
+            shape_of((length, 128), F32), shape_of((length, 384), BF16),
+            shape_of((length, N), BF16), shape_of((length, N), BF16),
+            shape_of((N, length), BF16), shape_of((N, length), BF16),
         ],
         scratch_shapes=[pltpu.VMEM((HALO + length, WB), F32)],
         compiler_params=params(),
         cost_estimate=cost(4e9, 8e6),
-    )(r_low, halo, r_low, halo, dt_low, taps, shift, taps, shift, prm)
-
-
-def local_scan(r_low, halo, taps, shift, skip, p, pt, b, c, bt):
-    length = r_low.shape[0]
+    )(r_low, halo, r_low, halo, r_low, taps, shift, taps, shift, prm)
+
+
+def local_scan(x, skip, p3, b, c, bt):
+    length = x.shape[0]
     return pl.pallas_call(
         scan_kernel,
         name="local_scan",
         grid=(STEPS,),
         in_specs=[
-            wide(length), wide(HALO), wide(4), wide(1), wide(1), whole((length, 128)),
-            whole((128, length)), whole((length, N)), whole((length, N)), whole((N, length)),
+            wide(length), wide(1), whole((length, 384)),
+            whole((length, N)), whole((length, N)), whole((N, length)),
         ],
         out_specs=wide(length),
         out_shape=shape_of((length, DI), F32),
-        scratch_shapes=[
-            pltpu.VMEM((HALO + length, WB), F32), pltpu.VMEM((length // T, T, T), F32)
-        ],
+        scratch_shapes=[pltpu.VMEM((length // T, T, T), F32)],
         compiler_params=params(),
         cost_estimate=cost(1.5e10, 8e6),
-    )(r_low, halo, taps, shift, skip, p, pt, b, c, bt)
+    )(x, skip, p3, b, c, bt)
 
 
 def gate_forward(y, gate, p, c, s_in, gain):
@@ -460,6 +513,7 @@
         in_specs=[rows(DI), rows(DI), rows(128), rows(N), whole((N, DI)), whole((1, DI))],
         out_specs=[rows(DI), rows(DI)],
         out_shape=[shape_of((length, DI), F32), shape_of((length, DI), BF16)],
+        scratch_shapes=[pltpu.VMEM((256, DI), BF16)],
         compiler_params=params(),
         cost_estimate=cost(5e9, 15e6),
     )(y, gate, p, c, s_in, gain)
@@ -481,17 +535,38 @@
             shape_of((length, DI), BF16), shape_of((length, DI), BF16),
             shape_of((8, DI), F32), shape_of((N, DI), BF16),
         ],
-        scratch_shapes=[pltpu.VMEM((N, DI), F32)],
+        scratch_shapes=[pltpu.VMEM((N, DI), F32), pltpu.VMEM((256, DI), BF16)],
         compiler_params=params(),
         cost_estimate=cost(1e10, 17e6),
     )(y, gate, dgn, p, ct, gain)
 
 
+def scan_inside(x, p3, b, c, dy, first):
+    length = x.shape[0]
+    blocks = length // T
+    wide_from = lambda rows: pl.BlockSpec((rows, WB), lambda i: (0, i + first))
+    return pl.pallas_call(
+        functools.partial(back_inside_kernel, first=first),
+        name="scan_inside",
+        grid=(STEPS // 2,),
+        in_specs=[
+            wide_from(length), whole((length, 384)), whole((length, N)),
+            whole((length, N)), wide_from(length),
+        ],
+        out_specs=[wide(length), whole((blocks, T, T))],
+        out_shape=[shape_of((length, DI // 2), F32), shape_of((blocks, T, T), F32)],
+        scratch_shapes=[pltpu.VMEM((blocks, T, T), F32)],
+        compiler_params=params(),
+        cost_estimate=cost(1e10, 6e6),
+    )(x, p3, b, c, dy)
+
+
 def scan_backward(
-    r_low, halo, taps, shift, skip, prm, p, pt, b, c, bt, ct, s_in, g_in, dy, y
+    r_low, halo, taps, shift, skip, prm, p, p3, b, c, bt, ct, s_in, g_in, dy, y, low, high
 ):
     length = r_low.shape[0]
     blocks = length // T
+    inside = jnp.concatenate([low[0], high[0]], axis=1)
     return pl.pallas_call(
         back_kernel,
         name="scan_backward",
@@ -499,8 +574,9 @@
         in_specs=[
             wide(length), wide(HALO), bc_block(length), bc_block(HALO),
             wide(4), wide(1), bc_block(4), bc_block(1), wide(1), whole((8, 128)),
-            whole((length, 128)), whole((128, length)), whole((length, N)), whole((length, N)),
+            whole((length, 128)), whole((length, 384)), whole((length, N)), whole((length, N)),
             whole((N, length)), whole((N, length)), wide(N), wide(N), wide(length), wide(length),
+            wide(length), whole((blocks, T, T)), whole((blocks, T, T)),
         ],
         out_specs=[
             wide(length), wide(8), wide(8), wide(8),
@@ -519,8 +595,8 @@
             pltpu.VMEM((length + 8, WB), F32),
             pltpu.VMEM((length, WB), F32),
             pltpu.VMEM((length, WB), F32),
-            pltpu.VMEM((blocks, T, T), F32),
-            pltpu.VMEM((blocks, T, T), F32),
+            pltpu.VMEM((length, WB), F32),
+            pltpu.VMEM((length, WB), F32),
             pltpu.VMEM((length, 128), F32),
             pltpu.VMEM((length, 128), F32),
             pltpu.VMEM((length, 128), F32),
@@ -528,35 +604,249 @@
         compiler_params=params(),
         cost_estimate=cost(3e10, 16e6),
     )(
-        r_low, halo, r_low, halo, taps, shift, taps, shift, skip, prm, p, pt, b, c, bt, ct,
-        s_in, g_in, dy, y,
+        r_low, halo, r_low, halo, taps, shift, taps, shift, skip, prm, p, p3, b, c, bt, ct,
+        s_in, g_in, dy, y, inside, low[1], high[1],
     )
 
 
-def pass_along(local, decay, order):
+def add(a, b):
+    return (a.astype(F32) + b.astype(F32)).astype(BF16)
+
+
+def swap(a, axis, bit):
+    return lax.ppermute(a, axis, [(k, k ^ bit) for k in range(lax.axis_size(axis))])
+
+
+def hop_to(message, state, hop, upward):
+    last = lax.axis_size("seq") - 1
+    pair = (hop, hop + 1) if upward else (last - hop, last - hop - 1)
+    got = lax.ppermute(message, "seq", [pair])
+    return got if state is None else got + state
+
+
+def message_of(local, decay, state):
+    return (local.astype(F32) + decay * state.astype(F32)).astype(BF16)
+
+
+def pass_along(local, decay, upward, work):
     hops = lax.axis_size("seq") - 1
-    state = jnp.zeros_like(local)
-    message = local
+    state = None
+    done = []
     for hop in range(hops):
-        state = lax.ppermute(message, "seq", order)
-        if hop < hops - 1:
-            message = (local.astype(F32) + decay * state.astype(F32)).astype(BF16)
-    return state
+        message = local if hop == 0 else message_of(local, decay, state)
+        state = hop_to(message, state, hop, upward)
+        if work:
+            item = work[0]()
+            work = work[1:]
+            state, item = lax.optimization_barrier((state, item))
+            done.append(item)
+    for item in work:
+        done.append(item())
+    return state, done
+
+
+def gather_pieces(w):
+    n = lax.axis_size("fsdp")
+    pieces = [w, swap(w, "fsdp", 1)]
+    for piece in [swap(w, "fsdp", 2 * d) for d in range(1, n // 2)]:
+        pieces += [piece, swap(piece, "fsdp", 1)]
+    return pieces
+
+
+def pieces_kernel(order_ref, left_ref, base_ref, *refs):
+    del order_ref
+    for m, piece in enumerate(refs[:-1]):
+
+        @pl.when(pl.program_id(0) == m)
+        def _(m=m, piece=piece):
+            total = base_ref[...] if m == 0 else refs[-1][...]
+            refs[-1][...] = total + dot(left_ref[...], piece[...])
+
+
+def pieces_back_kernel(order_ref, left_ref, *refs):
+    del order_ref
+    for m, piece in enumerate(refs[:-1]):
+
+        @pl.when(pl.program_id(0) == m)
+        def _(piece=piece):
+            refs[-1][...] = dot_nt(left_ref[...], piece[...])
+
+
+def xor_order():
+    n = lax.axis_size("fsdp")
+    return jnp.bitwise_xor(lax.axis_index("fsdp"), jnp.arange(n)).astype(jnp.int32)
+
+
+def fixed(shape):
+    return pl.BlockSpec(shape, lambda i, order: (0,) * len(shape))
+
+
+def add_product(base, left, w):
+    if not isinstance(w, list):
+        return base + dot(left, w)
+    return pl.pallas_call(
+        pieces_kernel,
+        name="add_product",
+        grid_spec=pltpu.PrefetchScalarGridSpec(
+            num_scalar_prefetch=1,
+            grid=(len(w),),
+            in_specs=[
+                pl.BlockSpec((left.shape[0], w[0].shape[0]), lambda i, order: (0, order[i])),
+                fixed(base.shape),
+            ]
+            + [fixed(w[0].shape)] * len(w),
+            out_specs=fixed(base.shape),
+        ),
+        out_shape=shape_of(base.shape, F32),
+        compiler_params=params(),
+        cost_estimate=cost(2e9, 10e6),
+    )(xor_order(), left, base, *w)
+
+
+def product_back(left, w):
+    if not isinstance(w, list):
+        return dot_nt(left, w)
+    length = left.shape[0]
+    return pl.pallas_call(
+        pieces_back_kernel,
+        name="product_back",
+        grid_spec=pltpu.PrefetchScalarGridSpec(
+            num_scalar_prefetch=1,
+            grid=(len(w),),
+            in_specs=[fixed(left.shape)] + [fixed(w[0].shape)] * len(w),
+            out_specs=pl.BlockSpec((length, w[0].shape[0]), lambda i, order: (0, order[i])),
+        ),
+        out_shape=shape_of((length, len(w) * w[0].shape[0]), F32),
+        compiler_params=params(),
+        cost_estimate=cost(2e9, 10e6),
+    )(xor_order(), left, *w)
+
+
+def give_kernel(left_ref, right_ref, out_ref):
+    out_ref[...] = dot_tn(left_ref[...], right_ref[...]).astype(BF16)
+
+
+def own_kernel(left_ref, right_ref, got_ref, *out_refs):
+    value = dot_tn(left_ref[...], right_ref[...]) + got_ref[...].astype(F32)
+    rows = out_refs[0].shape[0]
+    for d, out_ref in enumerate(out_refs):
+        out_ref[...] = value[d * rows : (d + 1) * rows].astype(BF16)
+
+
+def shard_columns(left, core):
+    n = lax.axis_size("fsdp")
+    me = lax.axis_index("fsdp")
+    width = left.shape[1] // n
+    return jnp.concatenate(
+        [
+            lax.dynamic_slice_in_dim(left, jnp.bitwise_xor(me, 2 * d + core) * width, width, 1)
+            for d in range(n // 2)
+        ],
+        axis=1,
+    )
+
+
+def product_give(left, right):
+    length, rows = left.shape
+    columns = right.shape[1]
+    block = columns // 2 if columns % 256 == 0 else columns
+    return pl.pallas_call(
+        give_kernel,
+        name="product_give",
+        grid=(columns // block,),
+        in_specs=[whole((length, rows)), pl.BlockSpec((length, block), lambda i: (0, i))],
+        out_specs=pl.BlockSpec((rows, block), lambda i: (0, i)),
+        out_shape=shape_of((rows, columns), BF16),
+        compiler_params=params(),
+        cost_estimate=cost(3e9, 8e6),
+    )(left, right)
+
+
+def product_own(left, right, got):
+    chips = lax.axis_size("fsdp") // 2
+    length, rows = left.shape
+    columns = right.shape[1]
+    block = columns // 2 if columns % 256 == 0 else columns
+    blocks = lambda height: pl.BlockSpec((height, block), lambda i: (0, i))
+    return pl.pallas_call(
+        own_kernel,
+        name="product_own",
+        grid=(columns // block,),
+        in_specs=[whole((length, rows)), blocks(length), blocks(rows)],
+        out_specs=[blocks(rows // chips)] * chips,
+        out_shape=[shape_of((rows // chips, columns), BF16)] * chips,
+        compiler_params=params(),
+        cost_estimate=cost(3e9, 10e6),
+    )(left, right, got)
+
+
+def send_chips(parts):
+    return parts[0], [swap(part, "fsdp", 2 * d) for d, part in enumerate(parts) if d]
+
+
+def gather_sum(own, got):
+    total = own.astype(F32)
+    for piece in got:
+        total = total + piece.astype(F32)
+    return total.astype(BF16)
+
+
+def tie(*values):
+    return lax.optimization_barrier(values)
+
+
+def seq_first(a):
+    odd = lax.axis_index("seq") % 2
+    half = a.shape[0] // 2
+    keep = lax.dynamic_slice_in_dim(a, odd * half, half, 0)
+    give = lax.dynamic_slice_in_dim(a, (1 - odd) * half, half, 0)
+    return keep, swap(give, "seq", 1)
+
+
+def seq_across(keep, got):
+    keep = add(keep, got)
+    bit = 2
+    while 2 * bit < lax.axis_size("seq"):
+        keep = add(keep, swap(keep, "seq", bit))
+        bit *= 2
+    return keep, swap(keep, "seq", bit)
+
+
+def seq_back(keep, got):
+    keep = add(keep, got)
+    return keep, swap(keep, "seq", 1)
+
+
+def seq_join(keep, other):
+    odd = lax.axis_index("seq") % 2
+    return jnp.where(
+        odd == 0, jnp.concatenate([keep, other]), jnp.concatenate([other, keep])
+    )
+
+
+def sum_over(a, *axes):
+    for axis in axes:
+        bit = 1
+        while bit < lax.axis_size(axis):
+            a = a + swap(a, axis, bit)
+            bit *= 2
+    return a
 
 
 def on_device(
     hidden_in, cotangent, norm_gain, input_projection_weight, conv_weight, conv_bias, dt_bias,
     a_log, skip, gate_gain, output_projection_weight,
 ):
-    layers = input_projection_weight.shape[0]
+    layers, _, in_width = input_projection_weight.shape
     seq_parts = lax.axis_size("seq")
     up = [(z, z + 1) for z in range(seq_parts - 1)]
     down = [(z + 1, z) for z in range(seq_parts - 1)]
 
     small = [norm_gain, conv_weight, conv_bias, dt_bias, a_log, skip, gate_gain]
     flat = jnp.concatenate([a.reshape(layers, -1) for a in small], axis=1)
-    packed = lax.all_gather(flat, "fsdp", axis=0).astype(F32)
-    shards = packed.shape[0]
+    shards = lax.axis_size("fsdp")
+    packed = lax.all_gather(flat, "fsdp", axis=0)
+    packed = packed.astype(F32)
     unpacked = []
     start = 0
     for a in small:
@@ -570,11 +860,17 @@
     weights = []
     for layer in range(layers):
         w = input_projection_weight[layer]
+        rest = jnp.concatenate([w[:, DI : DI + CC]] + [w[:, DI + CC :]] * 4, axis=1)
+        rest = lax.all_gather(rest, "fsdp", axis=0, tiled=True)
+        if layer == 0:
+            rest, first_out = tie(rest, output_projection_weight[0])
         weights.append(
             (
-                lax.all_gather(w[:, DI:], "fsdp", axis=0, tiled=True),
+                rest,
                 lax.all_gather(w[:, :DI], "fsdp", axis=0, tiled=True),
-                lax.all_gather(output_projection_weight[layer], "fsdp", axis=0, tiled=True),
+                gather_pieces(first_out)
+                if layer == 0 and first_out.shape[0] % 128 == 0
+                else lax.all_gather(output_projection_weight[layer], "fsdp", axis=0, tiled=True),
             )
         )
 
@@ -586,67 +882,145 @@
         normed = (hidden * r_in * gains[layer][None, :]).astype(BF16)
         r_low = dot(normed, w_rest).astype(BF16)
         halo = lax.ppermute(r_low[-HALO:, :CC], "seq", up)
-        gate = dot(normed, w_gate)
         taps = taps_all[layer]
         shift = shift_all[layer][None, :]
         skip_wide = jnp.repeat(skip_all[layer], P_SIZE)[None, :]
         prm = jnp.zeros((8, 128), F32)
         prm = prm.at[0].set(jnp.tile(bias_all[layer], 4))
         prm = prm.at[1].set(jnp.tile(-jnp.exp(rate_all[layer]), 4))
-        dt_low = jnp.tile(r_low[:, CC:], (1, 4))
-        f, decay, p, pt, b, c, bt, ct = local_state(r_low, halo, dt_low, taps, shift, prm)
-        s_in = pass_along(f, decay[0:1], up)
-        y = local_scan(r_low, halo, taps, shift, skip_wide, p, pt, b, c, bt)
+        f, decay, x, p, p3, b, c, bt, ct = local_state(r_low, halo, taps, shift, prm)
+        s_in, (y, gate) = pass_along(
+            f,
+            decay[0:1],
+            True,
+            [
+                lambda: local_scan(x, skip_wide, p3, b, c, bt),
+                lambda: dot(normed, w_gate),
+            ],
+        )
         y, gate_low = gate_forward(y, gate, p, c, s_in, gate_all[layer][None, :])
         stored.append(
             (
-                hidden, r_in, normed, r_low, halo, gate, taps, shift, skip_wide, prm, decay, p,
-                pt, b, c, bt, ct, s_in, y, gate_low,
+                hidden, r_in, normed, r_low, halo, gate, taps, shift, skip_wide, prm, decay, x, p,
+                p3, b, c, bt, ct, s_in, y, gate_low,
             )
         )
-        hidden = hidden + dot(gate_low, w_out)
+        hidden = add_product(hidden, gate_low, w_out)
     block_out = hidden.astype(BF16)[None]
 
+    block_out, cotangent = tie(block_out, cotangent)
     grad = cotangent[0].astype(F32)
     big = [None] * layers
     vectors = [None] * layers
+    waiting = None
     for layer in reversed(range(layers)):
         (
-            hidden, r_in, normed, r_low, halo, gate, taps, shift, skip_wide, prm, decay, p,
-            pt, b, c, bt, ct, s_in, y, gate_low,
+            hidden, r_in, normed, r_low, halo, gate, taps, shift, skip_wide, prm, decay, x, p,
+            p3, b, c, bt, ct, s_in, y, gate_low,
         ) = stored[layer]
         w_rest, w_gate, w_out = weights[layer]
         d_branch = grad.astype(BF16)
-        dgn = dot_nt(d_branch, w_out)
+        dgn = product_back(d_branch, w_out)
         dgate, dmix, gain_out_grad, g_local = gate_backward(
             y, gate, dgn, p, ct, gate_all[layer][None, :]
         )
-        g_in = pass_along(g_local, decay[0:1], down)
-        out_grad = dot_tn(gate_low, d_branch).astype(BF16)
-        gate_w_grad = dot_tn(normed, dgate).astype(BF16)
-        dv, tail, head, stats, bdv, btail, bhead, bstats, ddt, dtstats = scan_backward(
-            r_low, halo, taps, shift, skip_wide, prm, p, pt, b, c, bt, ct, s_in, g_in, dmix, y
+
+        if waiting is not None:
+            scattered, g_local = tie(scattered, g_local)
+            big[layer + 1] = [lax.psum(a, "seq") for a in scattered]
+
+        normed_give, normed_own = shard_columns(normed, 1), shard_columns(normed, 0)
+        inside = lambda first: scan_inside(x, p3, b, c, dmix, first)
+        if layer == 0:
+            out_give = product_give(shard_columns(gate_low, 1), d_branch)
+            state = hop_to(g_local, None, 0, False)
+            low = inside(0)
+            state, out_give, low, rest_sent = tie(state, out_give, low, rest_sent)
+            above = seq_first(gather_sum(rest_mine, rest_sent))
+            for hop in range(1, seq_parts - 1):
+                state = hop_to(message_of(g_local, decay[0:1], state), state, hop, False)
+                if hop == 1:
+                    out_got = swap(out_give, "fsdp", 1)
+                    gate_give = product_give(normed_give, dgate)
+                    high = inside(STEPS // 2)
+                    state, out_got, gate_give, high, above = tie(
+                        state, out_got, gate_give, high, above
+                    )
+                    above = seq_across(*above)
+                    gate_got = swap(gate_give, "fsdp", 1)
+                    out_parts = product_own(shard_columns(gate_low, 0), d_branch, out_got)
+                elif hop == 2:
+                    out_parts, state = tie(out_parts, state)
+                    out_mine, out_sent = send_chips(out_parts)
+                    state, gate_got, above = tie(state, gate_got, above)
+                    above = seq_back(*above)
+                    gate_parts = product_own(normed_own, dgate, gate_got)
+                    state, gate_parts = tie(state, gate_parts)
+                    gate_mine, gate_sent = send_chips(gate_parts)
+        else:
+            state, ((out_grad, gate_w_grad), low, high) = pass_along(
+                g_local,
+                decay[0:1],
+                False,
+                [
+                    lambda: (
+                        dot_tn(gate_low, d_branch).astype(BF16),
+                        dot_tn(normed, dgate).astype(BF16),
+                    ),
+                    lambda: inside(0),
+                    lambda: inside(STEPS // 2),
+                ],
+            )
+            scattered = [
+                lax.psum_scatter(a, "fsdp", scatter_dimension=0, tiled=True)
+                for a in (out_grad, gate_w_grad)
+            ]
+        back = scan_backward(
+            r_low, halo, taps, shift, skip_wide, prm, p, p3, b, c, bt, ct, s_in, state, dmix, y,
+            low, high,
         )
+        if layer == 0:
+            back, out_sent, above = tie(back, out_sent, above)
+            big[layer + 1].append(seq_join(*above))
+            out_seq = seq_first(gather_sum(out_mine, out_sent))
+        dv, tail, head, stats, bdv, btail, bhead, bstats, ddt, dtstats = back
         heads_in = lax.ppermute(jnp.concatenate([head, bhead], axis=1), "seq", down)
         tail = jnp.concatenate([tail, btail], axis=1)
         fix = [tail[j : j + 1] for j in range(8)]
         for j in range(3):
             for k in range(j + 1):
                 fix[5 + j] = fix[5 + j] + taps[k : k + 1] * heads_in[j - k : j - k + 1]
-        d_rest = jnp.concatenate([dv, bdv, ddt[:, :H]], axis=1)
+        d_rest = jnp.concatenate([dv, bdv, ddt], axis=1)
         d_rest = lax.dynamic_update_slice(
             d_rest, jnp.concatenate(fix, axis=0).astype(BF16), (d_rest.shape[0] - 8, 0)
         )
-        rest_w_grad = dot_tn(normed, d_rest).astype(BF16)
-        d_normed = dot_nt(dgate, w_gate) + dot_nt(d_rest, w_rest)
+        got = swap(product_give(normed_give, d_rest), "fsdp", 1)
+        d_normed = dot_nt(dgate, w_gate)
+        got, d_normed = tie(got, d_normed)
+        if layer == 0:
+            got, out_seq, gate_sent = tie(got, out_seq, gate_sent)
+            out_seq = seq_across(*out_seq)
+            gate_seq = seq_first(gather_sum(gate_mine, gate_sent))
+        parts = product_own(normed_own, d_rest, got)
+        parts, d_rest = tie(parts, d_rest)
+        rest_mine, rest_sent = send_chips(parts)
+        d_normed = d_normed + dot_nt(d_rest, w_rest)
         q = hidden * r_in
         dq = d_normed * gains[layer][None, :]
         gain_in_grad = jnp.sum(d_normed * q, axis=0)
         grad = grad + r_in * (dq - q * jnp.mean(dq * q, axis=1, keepdims=True))
-        big[layer] = [
-            lax.psum(lax.psum_scatter(a, "fsdp", scatter_dimension=0, tiled=True), "seq")
-            for a in (out_grad, gate_w_grad, rest_w_grad)
-        ]
+        if layer == 0:
+            grad, gain_in_grad, out_seq, gate_seq, rest_sent = tie(
+                grad, gain_in_grad, out_seq, gate_seq, rest_sent
+            )
+            out_seq = seq_back(*out_seq)
+            gate_seq = seq_across(*gate_seq)
+            rest_seq = seq_first(gather_sum(rest_mine, rest_sent))
+            out_seq, gate_seq, rest_seq = tie(out_seq, gate_seq, rest_seq)
+            gate_seq = seq_back(*gate_seq)
+            rest_seq = seq_back(*seq_across(*rest_seq))
+            big[layer] = [seq_join(*out_seq), seq_join(*gate_seq), seq_join(*rest_seq)]
+        waiting = layer
         stats = jnp.concatenate([stats, bstats], axis=1)
         vectors[layer] = [
             gain_in_grad,
@@ -663,15 +1037,16 @@
         full = jnp.stack([vectors[layer][member] for layer in range(layers)])
         full = full.reshape(a.shape[:-1] + (shards, a.shape[-1]))
         rows.append(jnp.moveaxis(full, -2, 0).reshape(shards, -1))
-    summed = lax.psum(jnp.concatenate(rows, axis=1), ("fsdp", "seq"))
+    summed = sum_over(jnp.concatenate(rows, axis=1), "fsdp", "seq")
     mine = lax.dynamic_index_in_dim(summed, lax.axis_index("fsdp"), 0, keepdims=False)
     outs = []
     start = 0
     for a in small:
         outs.append(mine[start : start + a.size].reshape(a.shape))
         start += a.size
+    rest_width = in_width - DI
     in_w = jnp.stack(
-        [jnp.concatenate([big[k][1], big[k][2]], axis=1) for k in range(layers)]
+        [jnp.concatenate([big[k][1], big[k][2][:, :rest_width]], axis=1) for k in range(layers)]
     ).astype(F32)
     out_w = jnp.stack([big[k][0] for k in range(layers)]).astype(F32)
     return (

time: 1010 us -> 674 us (0.67)
  waiting for transfers between devices: 565 us -> 146 us
  Pallas kernels: 163 us -> 233 us
  matrix products: 102 us -> 64.8 us
  other arithmetic: 25.2 us -> 60.9 us
  starting transfers between devices: 46.9 us -> 71.8 us
  local copies, waits for them, and re-layouts: 70.1 us -> 59.7 us
    psum x2 -> x1, waiting for transfers between devices: 241 us -> 0.01 us  [on_device(): big[layer + 1] = [lax.psum(a, 'seq') for a in scattered]]
    reduce_scatter x3 -> x2, waiting for transfers between devices: 163 us -> 0.01 us  [on_device(): lax.psum_scatter(a, 'fsdp', scatter_dimension=0, tiled=True)]
    pallas_call x0 -> x14, Pallas kernels: none -> 78.7 us  [the longest x4 29.9 us: scan_inside(): pl.pallas_call(functools.partial(back_inside_kernel, first=first), name='...]
    ppermute x12 -> x52, waiting for transfers between devices: 66.8 us -> 105 us  [the longest x40 78.8 us: swap(): lax.ppermute(a, axis, [(k, k ^ bit) for k in range(lax.axis_size(axis))])]
    all_gather x2, waiting for transfers between devices: 25.1 us -> 0.02 us  [on_device(): lax.all_gather(w[:, :DI], 'fsdp', axis=0, tiled=True)]
    ppermute x12 -> x52, starting transfers between devices: 36.2 us -> 61.2 us  [the longest x40 39.9 us: swap(): lax.ppermute(a, axis, [(k, k ^ bit) for k in range(lax.axis_size(axis))])]
    dot_general x6 -> x2, matrix products: 33 us -> 10.1 us  [dot_tn(): lax.dot_general(a, b, (((0,), (0,)), ((), ())), preferred_element_type=F32)]
    all_gather x2, waiting for transfers between devices: 43.4 us -> 24.7 us  [on_device(): rest = lax.all_gather(rest, 'fsdp', axis=0, tiled=True)]
  transfers between devices with their start and end apart: 30 -> 64, of which waited for: 22 -> 23; matrix products, arithmetic and copies ran while one was open for 16% -> 21% of each run, Pallas kernels for 15% -> 33%
where the time goes in v2:
time: 674 us; the launch traced here: 664 us
  Pallas kernels  233 us (35%)
  waiting for transfers between devices  146 us (22%)
  starting transfers between devices  71.8 us (11%)
  matrix products  64.8 us (10%)
  other arithmetic  60.9 us (9%)
  local copies, waits for them, and re-layouts  59.7 us (9%)
  between operations  17.2 us (3%)
  blocking collectives  10.7 us (2%)
    ppermute x40, waiting for transfers between devices, swap(): lax.ppermute(a, axis, [(k, k ^ bit) for k in range(lax.axis_size(axis))])  78.8 us
    pallas_call x2, Pallas kernels, scan_backward(): pl.pallas_call(back_kernel, name='scan_backward', grid=(STEPS,), in_specs...  63.2 us
    ppermute x40, starting transfers between devices, swap(): lax.ppermute(a, axis, [(k, k ^ bit) for k in range(lax.axis_size(axis))])  39.9 us
    unnamed x346, local copies, waits for them, and re-layouts  31.2 us
    dot_general x5, matrix products, dot(): return jnp.dot(a, b, preferred_element_type=F32)  31.2 us
    pallas_call x4, Pallas kernels, scan_inside(): pl.pallas_call(functools.partial(back_inside_kernel, first=first), name='...  29.9 us
    pallas_call x2, Pallas kernels, local_scan(): pl.pallas_call(scan_kernel, name='local_scan', grid=(STEPS,), in_specs=[w...  29.3 us
    pallas_call x2, Pallas kernels, local_state(): pl.pallas_call(state_kernel, name='local_state', grid=(STEPS,), in_specs=...  27.2 us
  transfers between devices with their start and end apart: 64, of which 23 were waited for; matrix products, arithmetic and copies ran while one was open for 21% of the time, Pallas kernels for 33%

profile of v2, /device:TPU:0, one launch (start us, length us, event | category | flops | bytes accessed | tf_op | source)
XLA Modules:
  0.0 664.2 jit_solution(6983531834067977419)
XLA Ops:
  14.2 10.7 %all-gather.2 = bf16[8,2,1836]{2,1,0:T(2,128)(2,1)S(1)} all-gather(bf16[1,2,1836]{2,1,0:T(2,128)(2,1)S(1)} %bitcast.150), channel_id=2, replica_groups=mesh['seq'=4,'fsdp'=8] {'fsdp'}, dimensions={0}, use_global_device_ids=true | all-gather | bytes 66096 | tf_op jit(solution)/shard_map/all_gather | solution.py:848
  29.5 24.7 %all-gather.9.cloned.1.call-done = bf16[1024,2432]{0,1:T(8,128)(2,1)} async-done(((bf16[128,2432]{0,1:T(8,128)(2,1)}), bf16[1024,2432]{0,1:T(8,128)(2,1)}) %all-gather.9.cloned.1.call-update) | async-done | bytes 4980752 | tf_op jit(solution)/shard_map/all_gather | solution.py:864
  54.2 5.5 convolution_convert_fusion.1.v_ref.bc_ref.dt_ref
  59.8 3.4 collective-permute-start
  65.1 13.6 %local_state.2 = (bf16[128,2048]{1,0:T(8,128)(2,1)S(1)}, f32[8,2048]{1,0:T(8,128)S(1)}, f32[512,2048]{1,0:T(8,128)}, f32[512,128]{1,0:T(8,128)S(1)}, bf16[512,38...) custom-call(bf16[512,2432]{1,0:T(8,128)(2,1)} %copy-done.159, ...), custom_call_target="tpu_custom_call" | custom-call | flops 4000000000 | bytes 8000000 | tf_op jit(solution)/shard_map/local_state/pallas_call | solution.py:463
  78.9 4.4 collective-permute-start.1
  83.2 14.6 %local_scan.2.y_ref = f32[512,2048]{1,0:T(8,128)} custom-call(f32[512,2048]{1,0:T(8,128)} %get-tuple-element.237.x_ref, f32[1,2048]{1,0:T(1,128)S(1)} %broadcast_in_dim_reshape.6.skip_ref, bf16[512,384]{1,0:T(8,128)(2,1)S(1)} %get-tuple-element.238.p3_ref, bf16[512,128]{1,0:T(8,128)(2,1)S(1)} %get-tuple-element.239.b_ref, ...), custom_call_target="tpu_custom_call" | custom-call | flops 15000000512 | bytes 8000000 | tf_op jit(solution)/shard_map/local_scan/pallas_call | solution.py:490
  100.4 6.7 %fusion.43.gate_ref = f32[512,2048]{1,0:T(8,128)} fusion(bf16[512,1024]{1,0:T(8,128)(2,1)S(1)} %multiply_convert_fusion.1, bf16[1024,2048]{0,1:T(8,128)(2,1)} %all-gather.11.cloned.1.call-done), kind=kOutput, calls=%fused_computation.191 | convolution fusion | flops 2147483648 | bytes 9437184 | tf_op jit(solution)/shard_map/dot_general | solution.py:30
  114.5 2.8 bitcast_convert_fusion.base_ref
  117.2 8.4 %collective-permute-done.9.refs_6_ = bf16[256,1024]{1,0:T(8,128)(2,1)S(1)} collective-permute-done((bf16[256,1024]{1,0:T(8,128)(2,1)S(1)}, bf16[256,1024]{1,0:T(8,128)(2,1)S(1)}, u32[]{:S(2)}, u32[]{:S(2)}) %collective-permute-start.9) | collective-permute-done | bytes 524320 | tf_op jit(solution)/shard_map/ppermute | solution.py:617
  125.7 10.0 %collective-permute-done.7.refs_4_ = bf16[256,1024]{1,0:T(8,128)(2,1)S(1)} collective-permute-done((bf16[256,1024]{1,0:T(8,128)(2,1)S(1)}, bf16[256,1024]{1,0:T(8,128)(2,1)S(1)}, u32[]{:S(2)}, u32[]{:S(2)}) %collective-permute-start.7) | collective-permute-done | bytes 524320 | tf_op jit(solution)/shard_map/ppermute | solution.py:617
  137.5 7.2 %gate_forward.2 = (f32[512,2048]{1,0:T(8,128)}, bf16[512,2048]{1,0:T(8,128)(2,1)S(1)}) custom-call(f32[512,2048]{1,0:T(8,128)} %local_scan.2.y_ref, f32[512,2048]{1,0:T(8,128)} %fusion.43.gate_ref, f32[512,128]{1,0:T(8,128)S(1)} %get-tuple-element.246.p_ref, bf16[512,128]{1,0:T(8,128)(2,1)S(1)} %get-tuple-element.240.c_ref, ...), custom_call_target="tpu_custom_call" | custom-call | flops 5000000000 | bytes 15000000 | tf_op jit(solution)/shard_map/gate_forward/pallas_call | solution.py:509
  146.9 9.0 %add_product.1 = f32[512,1024]{1,0:T(8,128)} custom-call(s32[8]{0:T(128)S(1)} %iota_xor_fusion.order_ref, bf16[512,2048]{1,0:T(8,128)(2,1)} %copy-done, f32[512,1024]{1,0:T(8,128)} %bitcast_convert_fusion.base_ref, bf16[256,1024]{1,0:T(8,128)(2,1)S(1)} %get-tuple-element.249.refs_0_, bf16[256,1024]{1,0:T(8,128)(2,1)S(1)} %collective-permute-done.4.refs_1_, ...), custom_call_target="tpu_custom_call" | custom-call | flops 2000000000 | bytes 10000000 | tf_op jit(solution)/shard_map/add_product/pallas_call | solution.py:687
  158.5 5.9 convolution_convert_fusion.v_ref.bc_ref.dt_ref
  164.4 3.6 collective-permute-start.11
  169.9 13.6 %local_state.3 = (bf16[128,2048]{1,0:T(8,128)(2,1)S(1)}, f32[8,2048]{1,0:T(8,128)S(1)}, f32[512,2048]{1,0:T(8,128)}, f32[512,128]{1,0:T(8,128)S(1)}, bf16[512,38...) custom-call(bf16[512,2432]{1,0:T(8,128)(2,1)} %copy-done.160, ...), custom_call_target="tpu_custom_call" | custom-call | flops 4000000000 | bytes 8000000 | tf_op jit(solution)/shard_map/local_state/pallas_call | solution.py:463
  183.6 4.3 collective-permute-start.12
  187.9 14.6 %local_scan.3.y_ref = f32[512,2048]{1,0:T(8,128)} custom-call(f32[512,2048]{1,0:T(8,128)} %get-tuple-element.251.x_ref, f32[1,2048]{1,0:T(1,128)S(1)} %broadcast_in_dim_reshape.7.skip_ref, bf16[512,384]{1,0:T(8,128)(2,1)S(1)} %get-tuple-element.252.p3_ref, bf16[512,128]{1,0:T(8,128)(2,1)S(1)} %get-tuple-element.253.b_ref, ...), custom_call_target="tpu_custom_call" | custom-call | flops 15000000512 | bytes 8000000 | tf_op jit(solution)/shard_map/local_scan/pallas_call | solution.py:490
  206.2 6.7 %fusion.44.gate_ref = f32[512,2048]{1,0:T(8,128)} fusion(bf16[512,1024]{1,0:T(8,128)(2,1)S(1)} %multiply_convert_fusion, bf16[1024,2048]{0,1:T(8,128)(2,1)} %all-gather.15.cloned.1.call-done), kind=kOutput, calls=%fused_computation.192 | convolution fusion | flops 2147483648 | bytes 9437184 | tf_op jit(solution)/shard_map/dot_general | solution.py:30
  215.1 7.0 %gate_forward.3 = (f32[512,2048]{1,0:T(8,128)}, bf16[512,2048]{1,0:T(8,128)(2,1)S(1)}) custom-call(f32[512,2048]{1,0:T(8,128)} %local_scan.3.y_ref, f32[512,2048]{1,0:T(8,128)} %fusion.44.gate_ref, f32[512,128]{1,0:T(8,128)S(1)} %get-tuple-element.260.p_ref, bf16[512,128]{1,0:T(8,128)(2,1)S(1)} %get-tuple-element.254.c_ref, ...), custom_call_target="tpu_custom_call" | custom-call | flops 5000000000 | bytes 15000000 | tf_op jit(solution)/shard_map/gate_forward/pallas_call | solution.py:509
  223.0 9.1 %all-gather.17.cloned.1.call-done = bf16[1,2048,1024]{2,1,0:T(8,128)(2,1)} async-done(((bf16[1,256,1024]{2,1,0:T(8,128)(2,1)}), bf16[1,2048,1024]{2,1,0:T(8,128)(2,1)}) %all-gather.17.cloned.1.call-update) | async-done | bytes 4194320 | tf_op jit(solution)/shard_map/all_gather | solution.py:873
  232.0 6.3 fusion.6
  238.4 4.3 fusion.dgn_ref
  242.7 10.0 %gate_backward.2 = (bf16[512,2048]{1,0:T(8,128)(2,1)S(1)}, bf16[512,2048]{1,0:T(8,128)(2,1)}, f32[8,2048]{1,0:T(8,128)S(1)}, bf16[128,2048]{1,0:T(8,128)(2,1)S(1)}) custom-call(f32[512,2048]{1,0:T(8,128)} %get-tuple-element.266.y_ref, f32[512,2048]{1,0:T(8,128)} %fusion.44.gate_ref, f32[512,2048]{1,0:T(8,128)} %fusion.dgn_ref, ...), custom_call_target="tpu_custom_call" | custom-call | flops 10000000000 | bytes 17000000 | tf_op jit(solution)/shard_map/gate_backward/pallas_call | solution.py:525
  255.9 4.5 convolution_convert_fusion.3
  260.4 5.6 convolution_convert_fusion.2
  271.1 7.4 %scan_inside.4 = (f32[512,1024]{1,0:T(8,128)S(1)}, f32[4,128,128]{2,1,0:T(8,128)S(1)}) custom-call(f32[512,2048]{1,0:T(8,128)} %get-tuple-element.251.x_ref, bf16[512,384]{1,0:T(8,128)(2,1)S(1)} %copy-done.57, bf16[512,128]{1,0:T(8,128)(2,1)S(1)} %copy-done.75, bf16[512,128]{1,0:T(8,128)(2,1)S(1)} %copy-done.78, bf16[512,2048]{1,0:T(8,128)(2,1)} %get-tuple-element.270.dy_ref), custom_call_target="tpu_custom_call" | custom-call | flops 10000000000 | bytes 6000000 | tf_op jit(solution)/shard_map/scan_inside/pallas_call | solution.py:548
  282.1 7.5 %scan_inside.5 = (f32[512,1024]{1,0:T(8,128)S(1)}, f32[4,128,128]{2,1,0:T(8,128)S(1)}) custom-call(f32[512,2048]{1,0:T(8,128)} %get-tuple-element.251.x_ref, bf16[512,384]{1,0:T(8,128)(2,1)S(1)} %copy-done.57, bf16[512,128]{1,0:T(8,128)(2,1)S(1)} %copy-done.75, bf16[512,128]{1,0:T(8,128)(2,1)S(1)} %copy-done.78, bf16[512,2048]{1,0:T(8,128)(2,1)} %get-tuple-element.270.dy_ref), custom_call_target="tpu_custom_call" | custom-call | flops 10000000000 | bytes 6000000 | tf_op jit(solution)/shard_map/scan_inside/pallas_call | solution.py:548
  291.0 12.6 %collective-permute-done.17 = bf16[128,2048]{1,0:T(8,128)(2,1)} collective-permute-done((bf16[128,2048]{1,0:T(8,128)(2,1)}, bf16[128,2048]{1,0:T(8,128)(2,1)}, u32[]{:S(2)}, u32[]{:S(2)}) %collective-permute-start.17) | collective-permute-done | bytes 524320 | tf_op jit(solution)/shard_map/ppermute | solution.py:623
  305.0 4.2 pad_maximum_fusion.inside_ref
  309.3 31.6 %scan_backward.2 = (bf16[512,2048]{1,0:T(8,128)(2,1)}, f32[8,2048]{1,0:T(8,128)S(1)}, f32[8,2048]{1,0:T(8,128)S(1)}, f32[8,2048]{1,0:T(8,128)S(1)}, bf16[512,256...) custom-call(bf16[512,2432]{1,0:T(8,128)(2,1)} %copy-done.160, ...), custom_call_target="tpu_custom_call" | custom-call | flops 30000001024 | bytes 16000000 | tf_op jit(solution)/shard_map/scan_backward/pallas_call | solution.py:570
  344.6 2.6 collective-permute-done.18
  348.7 4.8 product_give.4
  364.1 5.4 product_own.4
  373.9 5.8 multiply_reduce_fusion
  382.3 7.9 %product_back.1.dgn_ref = f32[512,2048]{1,0:T(8,128)} custom-call(s32[8]{0:T(128)S(1)} %copy-done.39, bf16[512,1024]{1,0:T(8,128)(2,1)} %get-tuple-element.461.left_ref.right_ref, bf16[256,1024]{1,0:T(8,128)(2,1)S(1)} %get-tuple-element.249.refs_0_, bf16[256,1024]{1,0:T(8,128)(2,1)S(1)} %copy-done.15, bf16[256,1024]{1,0:T(8,128)(2,1)S(1)} %copy-done.13, ...), custom_call_target="tpu_custom_call" | custom-call | flops 2000000000 | bytes 10000000 | tf_op jit(solution)/shard_map/product_back/pallas_call | solution.py:710
  390.2 9.9 %gate_backward.3 = (bf16[512,2048]{1,0:T(8,128)(2,1)S(1)}, bf16[512,2048]{1,0:T(8,128)(2,1)}, f32[8,2048]{1,0:T(8,128)S(1)}, bf16[128,2048]{1,0:T(8,128)(2,1)S(1)}) custom-call(f32[512,2048]{1,0:T(8,128)} %get-tuple-element.298.y_ref, f32[512,2048]{1,0:T(8,128)} %fusion.43.gate_ref, f32[512,2048]{1,0:T(8,128)} %product_back.1.dgn_ref, ...), custom_call_target="tpu_custom_call" | custom-call | flops 10000000000 | bytes 17000000 | tf_op jit(solution)/shard_map/gate_backward/pallas_call | solution.py:525
  404.3 7.5 %scan_inside.6 = (f32[512,1024]{1,0:T(8,128)S(1)}, f32[4,128,128]{2,1,0:T(8,128)S(1)}) custom-call(f32[512,2048]{1,0:T(8,128)} %get-tuple-element.237.x_ref, bf16[512,384]{1,0:T(8,128)(2,1)S(1)} %copy-done.54, bf16[512,128]{1,0:T(8,128)(2,1)S(1)} %copy-done.65, bf16[512,128]{1,0:T(8,128)(2,1)S(1)} %copy-done.67, bf16[512,2048]{1,0:T(8,128)(2,1)} %get-tuple-element.301.dy_ref), custom_call_target="tpu_custom_call" | custom-call | flops 10000000000 | bytes 6000000 | tf_op jit(solution)/shard_map/scan_inside/pallas_call | solution.py:548
  419.2 7.4 %scan_inside.7 = (f32[512,1024]{1,0:T(8,128)S(1)}, f32[4,128,128]{2,1,0:T(8,128)S(1)}) custom-call(f32[512,2048]{1,0:T(8,128)} %get-tuple-element.237.x_ref, bf16[512,384]{1,0:T(8,128)(2,1)S(1)} %copy-done.54, bf16[512,128]{1,0:T(8,128)(2,1)S(1)} %copy-done.65, bf16[512,128]{1,0:T(8,128)(2,1)S(1)} %copy-done.67, bf16[512,2048]{1,0:T(8,128)(2,1)} %get-tuple-element.301.dy_ref), custom_call_target="tpu_custom_call" | custom-call | flops 10000000000 | bytes 6000000 | tf_op jit(solution)/shard_map/scan_inside/pallas_call | solution.py:548
  427.9 3.9 product_give.6
  436.5 4.4 collective-permute-start.29
  442.6 3.1 product_own.5
  448.2 13.6 %collective-permute-done.27 = bf16[128,2048]{1,0:T(8,128)(2,1)S(1)} collective-permute-done((bf16[128,2048]{1,0:T(8,128)(2,1)S(1)}, bf16[128,2048]{1,0:T(8,128)(2,1)S(1)}, u32[]{:S(2)}, u32[]{:S(2)}) %collective-permute-start.27) | collective-permute-done | bytes 524320 | tf_op jit(solution)/shard_map/ppermute | solution.py:623
  465.7 3.2 product_own.6
  470.7 31.5 %scan_backward.3 = (bf16[512,2048]{1,0:T(8,128)(2,1)}, f32[8,2048]{1,0:T(8,128)S(1)}, f32[8,2048]{1,0:T(8,128)S(1)}, f32[8,2048]{1,0:T(8,128)S(1)}, bf16[512,256...) custom-call(bf16[512,2432]{1,0:T(8,128)(2,1)} %copy-done.159, ...), custom_call_target="tpu_custom_call" | custom-call | flops 30000001024 | bytes 16000000 | tf_op jit(solution)/shard_map/scan_backward/pallas_call | solution.py:570
  507.0 2.9 collective-permute-done.34
  511.5 4.9 product_give.7
  516.5 5.9 fusion.46
  528.9 2.6 add_convert_fusion.4
  543.4 4.9 collective-permute-done.38
  552.5 4.2 product_own.7
  565.2 5.2 multiply_reduce_fusion.1
  572.4 12.3 %collective-permute-done.40 = bf16[128,1024]{1,0:T(8,128)(2,1)S(1)} collective-permute-done((bf16[128,1024]{1,0:T(8,128)(2,1)S(1)}, bf16[128,1024]{1,0:T(8,128)(2,1)S(1)}, u32[]{:S(2)}, u32[]{:S(2)}) %collective-permute-start.40) | collective-permute-done | bytes 262176 | tf_op jit(solution)/shard_map/ppermute | solution.py:617
  586.7 4.9 collective-permute-done.43
  599.1 3.3 collective-permute-done.46
  604.0 3.7 collective-permute-done.51
  607.7 2.7 collective-permute-done.50
  610.4 5.4 collective-permute-done.52
  617.9 2.8 collective-permute-start.54
  623.5 8.3 %collective-permute-done.48 = f32[8,3672]{1,0:T(8,128)S(1)} collective-permute-done((f32[8,3672]{1,0:T(8,128)S(1)}, f32[8,3672]{1,0:T(8,128)S(1)}, u32[]{:S(2)}, u32[]{:S(2)}) %collective-permute-start.48) | collective-permute-done | bytes 117536 | tf_op jit(solution)/shard_map/ppermute | solution.py:617
  631.8 2.6 collective-permute-start.49
  634.5 4.4 collective-permute-done.49
  644.2 4.4 collective-permute-done.55
  651.1 5.9 copy.51
  (650 shorter events, 165.0 us)
Async XLA Ops:
  7.2 47.0 %all-gather.9.cloned.1.call-start = ((), (), s32[]{:S(2)}) async-start(), calls=%async_computation.2 | async-start | bytes 5603328 | tf_op jit(solution)/shard_map/all_gather | solution.py:864
  9.9 90.5 %all-gather.11.cloned.1.call-start = ((), (), s32[]{:S(2)}) async-start(), calls=%async_computation.3 | async-start | bytes 4718592 | tf_op jit(solution)/shard_map/all_gather | solution.py:870
  10.8 147.6 %all-gather.13.cloned.1.call-start = ((), (), s32[]{:S(2)}) async-start(), calls=%async_computation.4 | async-start | bytes 5603328 | tf_op jit(solution)/shard_map/all_gather | solution.py:864
  11.9 194.2 %all-gather.15.cloned.1.call-start = ((), (), s32[]{:S(2)}) async-start(), calls=%async_computation.5 | async-start | bytes 4718592 | tf_op jit(solution)/shard_map/all_gather | solution.py:870
  12.9 219.1 %all-gather.17.cloned.1.call-start = ((), (), s32[]{:S(2)}) async-start(), calls=%async_computation.8 | async-start | bytes 4718592 | tf_op jit(solution)/shard_map/all_gather | solution.py:873
  13.9 387.6 %reduce-scatter.3.cloned.1.call-start = ((), (), s32[]{:S(2)}) async-start(), calls=%async_computation.6 | async-start | bytes 4718592 | tf_op jit(solution)/shard_map/reduce_scatter | solution.py:975
  59.8 5.4 collective-permute-start
  78.9 19.1 %collective-permute-start.1 = (bf16[128,2048]{1,0:T(8,128)(2,1)S(1)}, bf16[128,2048]{1,0:T(8,128)(2,1)S(1)}, u32[]{:S(2)}, u32[]{:S(2)}) collective-permute-start(bf16[128,2048]{1,0:T(8,128)(2,1)S(1)} %get-tuple-element.236), channel_id=1, source_target_pairs={{0,8},{1,9},{2,10},{3,11},{4,12},{5,13},{6,14},{7,15}} | collective-permute-start | bytes 1572872 | tf_op jit(solution)/shard_map/ppermute | solution.py:623
  98.9 11.7 %collective-permute-start.2 = (bf16[128,2048]{1,0:T(8,128)(2,1)S(1)}, bf16[128,2048]{1,0:T(8,128)(2,1)}, u32[]{:S(2)}, u32[]{:S(2)}) collective-permute-start(bf16[128,2048]{1,0:T(8,128)(2,1)S(1)} %fusion.9), channel_id=1, source_target_pairs={{8,16},{9,17},{10,18},{11,19},{12,20},{13,21},{14,22},{15,23}} | collective-permute-start | bytes 1572872 | tf_op jit(solution)/shard_map/ppermute | solution.py:623
  107.1 18.5 %collective-permute-start.9 = (bf16[256,1024]{1,0:T(8,128)(2,1)S(1)}, bf16[256,1024]{1,0:T(8,128)(2,1)S(1)}, u32[]{:S(2)}, u32[]{:S(2)}) collective-permute-start(bf16[256,1024]{1,0:T(8,128)(2,1)S(1)} %get-tuple-element.249.refs_0_), channel_id=1, source_target_pairs={{0,6},{1,7},{2,4},{3,5},{4,2},{5,3},{6,0},{7,1},{8,14},{9,15},{10,... | collective-permute-start | bytes 1572872 | tf_op jit(solution)/shard_map/ppermute | solution.py:617
  108.5 27.2 %collective-permute-start.7 = (bf16[256,1024]{1,0:T(8,128)(2,1)S(1)}, bf16[256,1024]{1,0:T(8,128)(2,1)S(1)}, u32[]{:S(2)}, u32[]{:S(2)}) collective-permute-start(bf16[256,1024]{1,0:T(8,128)(2,1)S(1)} %get-tuple-element.249.refs_0_), channel_id=1, source_target_pairs={{0,4},{1,5},{2,6},{3,7},{4,0},{5,1},{6,2},{7,3},{8,12},{9,13},{10,... | collective-permute-start | bytes 1572872 | tf_op jit(solution)/shard_map/ppermute | solution.py:617
  110.0 25.7 %collective-permute-start.5 = (bf16[256,1024]{1,0:T(8,128)(2,1)S(1)}, bf16[256,1024]{1,0:T(8,128)(2,1)S(1)}, u32[]{:S(2)}, u32[]{:S(2)}) collective-permute-start(bf16[256,1024]{1,0:T(8,128)(2,1)S(1)} %get-tuple-element.249.refs_0_), channel_id=1, source_target_pairs={{0,2},{1,3},{2,0},{3,1},{4,6},{5,7},{6,4},{7,5},{8,10},{9,11},{10,... | collective-permute-start | bytes 1572872 | tf_op jit(solution)/shard_map/ppermute | solution.py:617
  112.8 23.5 %collective-permute-start.3 = (bf16[128,2048]{1,0:T(8,128)(2,1)}, bf16[128,2048]{1,0:T(8,128)(2,1)}, u32[]{:S(2)}, u32[]{:S(2)}) collective-permute-start(bf16[128,2048]{1,0:T(8,128)(2,1)} %fusion.10), channel_id=1, source_target_pairs={{16,24},{17,25},{18,26},{19,27},{20,28},{21,29},{22,30},{23,31}} | collective-permute-start | bytes 1572872 | tf_op jit(solution)/shard_map/ppermute | solution.py:623
  117.2 28.8 %collective-permute-start.4 = (bf16[256,1024]{1,0:T(8,128)(2,1)S(1)}, bf16[256,1024]{1,0:T(8,128)(2,1)S(1)}, u32[]{:S(2)}, u32[]{:S(2)}) collective-permute-start(bf16[256,1024]{1,0:T(8,128)(2,1)S(1)} %get-tuple-element.249.refs_0_), channel_id=1, source_target_pairs={{0,1},{1,0},{2,3},{3,2},{4,5},{5,4},{6,7},{7,6},{8,9},{9,8},{10,11... | collective-permute-start | bytes 1572872 | tf_op jit(solution)/shard_map/ppermute | solution.py:617
  125.7 20.4 %collective-permute-start.10 = (bf16[256,1024]{1,0:T(8,128)(2,1)S(1)}, bf16[256,1024]{1,0:T(8,128)(2,1)S(1)}, u32[]{:S(2)}, u32[]{:S(2)}) collective-permute-start(bf16[256,1024]{1,0:T(8,128)(2,1)S(1)} %collective-permute-done.9.refs_6_), channel_id=1, source_target_pairs={{0,1},{1,0},{2,3},{3,2},{4,5},{5,4},{6,7},{7,6},{8,9},{9,8},{10,11... | collective-permute-start | bytes 1572872 | tf_op jit(solution)/shard_map/ppermute | solution.py:617
  135.7 10.4 %collective-permute-start.8 = (bf16[256,1024]{1,0:T(8,128)(2,1)S(1)}, bf16[256,1024]{1,0:T(8,128)(2,1)S(1)}, u32[]{:S(2)}, u32[]{:S(2)}) collective-permute-start(bf16[256,1024]{1,0:T(8,128)(2,1)S(1)} %collective-permute-done.7.refs_4_), channel_id=1, source_target_pairs={{0,1},{1,0},{2,3},{3,2},{4,5},{5,4},{6,7},{7,6},{8,9},{9,8},{10,11... | collective-permute-start | bytes 1572872 | tf_op jit(solution)/shard_map/ppermute | solution.py:617
  135.7 10.4 %collective-permute-start.6 = (bf16[256,1024]{1,0:T(8,128)(2,1)S(1)}, bf16[256,1024]{1,0:T(8,128)(2,1)S(1)}, u32[]{:S(2)}, u32[]{:S(2)}) collective-permute-start(bf16[256,1024]{1,0:T(8,128)(2,1)S(1)} %collective-permute-done.5.refs_2_), channel_id=1, source_target_pairs={{0,1},{1,0},{2,3},{3,2},{4,5},{5,4},{6,7},{7,6},{8,9},{9,8},{10,11... | collective-permute-start | bytes 1572872 | tf_op jit(solution)/shard_map/ppermute | solution.py:617
  164.4 5.5 collective-permute-start.11
  183.6 19.0 %collective-permute-start.12 = (bf16[128,2048]{1,0:T(8,128)(2,1)S(1)}, bf16[128,2048]{1,0:T(8,128)(2,1)S(1)}, u32[]{:S(2)}, u32[]{:S(2)}) collective-permute-start(bf16[128,2048]{1,0:T(8,128)(2,1)S(1)} %get-tuple-element.250), channel_id=1, source_target_pairs={{0,8},{1,9},{2,10},{3,11},{4,12},{5,13},{6,14},{7,15}} | collective-permute-start | bytes 1572872 | tf_op jit(solution)/shard_map/ppermute | solution.py:623
  204.3 8.6 %collective-permute-start.13 = (bf16[128,2048]{1,0:T(8,128)(2,1)}, bf16[128,2048]{1,0:T(8,128)(2,1)}, u32[]{:S(2)}, u32[]{:S(2)}) collective-permute-start(bf16[128,2048]{1,0:T(8,128)(2,1)} %fusion.11), channel_id=1, source_target_pairs={{8,16},{9,17},{10,18},{11,19},{12,20},{13,21},{14,22},{15,23}} | collective-permute-start | bytes 1572872 | tf_op jit(solution)/shard_map/ppermute | solution.py:623
  214.3 0.7 collective-permute-start.14
  254.1 11.9 %collective-permute-start.15 = (bf16[128,2048]{1,0:T(8,128)(2,1)S(1)}, bf16[128,2048]{1,0:T(8,128)(2,1)}, u32[]{:S(2)}, u32[]{:S(2)}) collective-permute-start(bf16[128,2048]{1,0:T(8,128)(2,1)S(1)} %get-tuple-element.267), channel_id=1, source_target_pairs={{24,16},{25,17},{26,18},{27,19},{28,20},{29,21},{30,22},{31,23}} | collective-permute-start | bytes 1572872 | tf_op jit(solution)/shard_map/ppermute | solution.py:623
  266.0 135.5 %reduce-scatter.5.cloned.1.call-start = ((), (), s32[]{:S(2)}) async-start(), calls=%async_computation.7 | async-start | bytes 4718592 | tf_op jit(solution)/shard_map/reduce_scatter | solution.py:975
  270.3 8.2 %collective-permute-start.16 = (bf16[128,2048]{1,0:T(8,128)(2,1)S(1)}, bf16[128,2048]{1,0:T(8,128)(2,1)S(1)}, u32[]{:S(2)}, u32[]{:S(2)}) collective-permute-start(bf16[128,2048]{1,0:T(8,128)(2,1)S(1)} %fusion.13), channel_id=1, source_target_pairs={{16,8},{17,9},{18,10},{19,11},{20,12},{21,13},{22,14},{23,15}} | collective-permute-start | bytes 1572872 | tf_op jit(solution)/shard_map/ppermute | solution.py:623
  280.8 22.8 %collective-permute-start.17 = (bf16[128,2048]{1,0:T(8,128)(2,1)}, bf16[128,2048]{1,0:T(8,128)(2,1)}, u32[]{:S(2)}, u32[]{:S(2)}) collective-permute-start(bf16[128,2048]{1,0:T(8,128)(2,1)} %fusion.14), channel_id=1, source_target_pairs={{8,0},{9,1},{10,2},{11,3},{12,4},{13,5},{14,6},{15,7}} | collective-permute-start | bytes 1572872 | tf_op jit(solution)/shard_map/ppermute | solution.py:623
  291.0 307.0 %all-reduce.5.cloned.1.call-start = ((), (), s32[]{:S(2)}) async-start(), calls=%async_computation.9 | async-start | bytes 2097152 | tf_op jit(solution)/shard_map/psum | solution.py:930
  340.9 6.2 collective-permute-start.18
  353.5 10.6 %collective-permute-start.19 = (bf16[512,2432]{1,0:T(8,128)(2,1)}, bf16[512,2432]{1,0:T(8,128)(2,1)}, u32[]{:S(2)}, u32[]{:S(2)}) collective-permute-start(bf16[512,2432]{1,0:T(8,128)(2,1)} %product_give.4), channel_id=1, source_target_pairs={{0,1},{1,0},{2,3},{3,2},{4,5},{5,4},{6,7},{7,6},{8,9},{9,8},{10,11... | collective-permute-start | bytes 7471112 | tf_op jit(solution)/shard_map/ppermute | solution.py:617
  369.4 46.3 %collective-permute-start.21 = (bf16[128,2432]{1,0:T(8,128)(2,1)}, bf16[128,2432]{1,0:T(8,128)(2,1)}, u32[]{:S(2)}, u32[]{:S(2)}) collective-permute-start(bf16[128,2432]{1,0:T(8,128)(2,1)} %get-tuple-element.304), channel_id=1, source_target_pairs={{0,2},{1,3},{2,0},{3,1},{4,6},{5,7},{6,4},{7,5},{8,10},{9,11},{10,... | collective-permute-start | bytes 1867784 | tf_op jit(solution)/shard_map/ppermute | solution.py:617
  370.9 44.9 %collective-permute-start.22 = (bf16[128,2432]{1,0:T(8,128)(2,1)}, bf16[128,2432]{1,0:T(8,128)(2,1)}, u32[]{:S(2)}, u32[]{:S(2)}) collective-permute-start(bf16[128,2432]{1,0:T(8,128)(2,1)} %get-tuple-element.305), channel_id=1, source_target_pairs={{0,4},{1,5},{2,6},{3,7},{4,0},{5,1},{6,2},{7,3},{8,12},{9,13},{10,... | collective-permute-start | bytes 1867784 | tf_op jit(solution)/shard_map/ppermute | solution.py:617
  372.6 43.2 %collective-permute-start.23 = (bf16[128,2432]{1,0:T(8,128)(2,1)}, bf16[128,2432]{1,0:T(8,128)(2,1)}, u32[]{:S(2)}, u32[]{:S(2)}) collective-permute-start(bf16[128,2432]{1,0:T(8,128)(2,1)} %get-tuple-element.306), channel_id=1, source_target_pairs={{0,6},{1,7},{2,4},{3,5},{4,2},{5,3},{6,0},{7,1},{8,14},{9,15},{10,... | collective-permute-start | bytes 1867784 | tf_op jit(solution)/shard_map/ppermute | solution.py:617
  401.5 14.3 %collective-permute-start.20 = (bf16[128,2048]{1,0:T(8,128)(2,1)S(1)}, bf16[128,2048]{1,0:T(8,128)(2,1)S(1)}, u32[]{:S(2)}, u32[]{:S(2)}) collective-permute-start(bf16[128,2048]{1,0:T(8,128)(2,1)S(1)} %get-tuple-element.300), channel_id=1, source_target_pairs={{24,16},{25,17},{26,18},{27,19},{28,20},{29,21},{30,22},{31,23}} | collective-permute-start | bytes 1572872 | tf_op jit(solution)/shard_map/ppermute | solution.py:623
  415.8 16.2 %collective-permute-start.25 = (bf16[1024,1024]{1,0:T(8,128)(2,1)}, bf16[1024,1024]{1,0:T(8,128)(2,1)S(1)}, u32[]{:S(2)}, u32[]{:S(2)}) collective-permute-start(bf16[1024,1024]{1,0:T(8,128)(2,1)} %product_give.5), channel_id=1, source_target_pairs={{0,1},{1,0},{2,3},{3,2},{4,5},{5,4},{6,7},{7,6},{8,9},{9,8},{10,11... | collective-permute-start | bytes 6291464 | tf_op jit(solution)/shard_map/ppermute | solution.py:617
  417.7 14.3 %collective-permute-start.26 = (bf16[64,2432]{1,0:T(8,128)(2,1)S(1)}, bf16[64,2432]{1,0:T(8,128)(2,1)}, u32[]{:S(2)}, u32[]{:S(2)}) collective-permute-start(bf16[64,2432]{1,0:T(8,128)(2,1)S(1)} %get-tuple-element.493), channel_id=1, source_target_pairs={{0,8},{8,0},{16,24},{24,16},{1,9},{9,1},{17,25},{25,17},{2,10},{10... | collective-permute-start | bytes 933896 | tf_op jit(solution)/shard_map/ppermute | solution.py:617
  418.4 13.5 %collective-permute-start.24 = (bf16[128,2048]{1,0:T(8,128)(2,1)S(1)}, bf16[128,2048]{1,0:T(8,128)(2,1)S(1)}, u32[]{:S(2)}, u32[]{:S(2)}) collective-permute-start(bf16[128,2048]{1,0:T(8,128)(2,1)S(1)} %fusion.15), channel_id=1, source_target_pairs={{16,8},{17,9},{18,10},{19,11},{20,12},{21,13},{22,14},{23,15}} | collective-permute-start | bytes 1572872 | tf_op jit(solution)/shard_map/ppermute | solution.py:623
  432.0 33.7 %collective-permute-start.28 = (bf16[512,2048]{1,0:T(8,128)(2,1)}, bf16[512,2048]{1,0:T(8,128)(2,1)}, u32[]{:S(2)}, u32[]{:S(2)}) collective-permute-start(bf16[512,2048]{1,0:T(8,128)(2,1)} %product_give.6), channel_id=1, source_target_pairs={{0,1},{1,0},{2,3},{3,2},{4,5},{5,4},{6,7},{7,6},{8,9},{9,8},{10,11... | collective-permute-start | bytes 6291464 | tf_op jit(solution)/shard_map/ppermute | solution.py:617
  436.5 29.2 %collective-permute-start.29 = (bf16[64,2432]{1,0:T(8,128)(2,1)S(1)}, bf16[64,2432]{1,0:T(8,128)(2,1)S(1)}, u32[]{:S(2)}, u32[]{:S(2)}) collective-permute-start(bf16[64,2432]{1,0:T(8,128)(2,1)S(1)} %add_convert_fusion.8), channel_id=1, source_target_pairs={{0,16},{8,24},{16,0},{24,8},{1,17},{9,25},{17,1},{25,9},{2,18},{10... | collective-permute-start | bytes 933896 | tf_op jit(solution)/shard_map/ppermute | solution.py:617
  441.0 20.8 %collective-permute-start.27 = (bf16[128,2048]{1,0:T(8,128)(2,1)S(1)}, bf16[128,2048]{1,0:T(8,128)(2,1)S(1)}, u32[]{:S(2)}, u32[]{:S(2)}) collective-permute-start(bf16[128,2048]{1,0:T(8,128)(2,1)S(1)} %fusion.16), channel_id=1, source_target_pairs={{8,0},{9,1},{10,2},{11,3},{12,4},{13,5},{14,6},{15,7}} | collective-permute-start | bytes 1572872 | tf_op jit(solution)/shard_map/ppermute | solution.py:623
  462.1 40.1 %collective-permute-start.30 = (bf16[256,1024]{1,0:T(8,128)(2,1)S(1)}, bf16[256,1024]{1,0:T(8,128)(2,1)S(1)}, u32[]{:S(2)}, u32[]{:S(2)}) collective-permute-start(bf16[256,1024]{1,0:T(8,128)(2,1)S(1)} %get-tuple-element.347), channel_id=1, source_target_pairs={{0,2},{1,3},{2,0},{3,1},{4,6},{5,7},{6,4},{7,5},{8,10},{9,11},{10,... | collective-permute-start | bytes 1572872 | tf_op jit(solution)/shard_map/ppermute | solution.py:617
  462.7 39.6 %collective-permute-start.31 = (bf16[256,1024]{1,0:T(8,128)(2,1)S(1)}, bf16[256,1024]{1,0:T(8,128)(2,1)S(1)}, u32[]{:S(2)}, u32[]{:S(2)}) collective-permute-start(bf16[256,1024]{1,0:T(8,128)(2,1)S(1)} %get-tuple-element.348), channel_id=1, source_target_pairs={{0,4},{1,5},{2,6},{3,7},{4,0},{5,1},{6,2},{7,3},{8,12},{9,13},{10,... | collective-permute-start | bytes 1572872 | tf_op jit(solution)/shard_map/ppermute | solution.py:617
  464.4 37.9 %collective-permute-start.32 = (bf16[256,1024]{1,0:T(8,128)(2,1)S(1)}, bf16[256,1024]{1,0:T(8,128)(2,1)S(1)}, u32[]{:S(2)}, u32[]{:S(2)}) collective-permute-start(bf16[256,1024]{1,0:T(8,128)(2,1)S(1)} %get-tuple-element.349), channel_id=1, source_target_pairs={{0,6},{1,7},{2,4},{3,5},{4,2},{5,3},{6,0},{7,1},{8,14},{9,15},{10,... | collective-permute-start | bytes 1572872 | tf_op jit(solution)/shard_map/ppermute | solution.py:617
  470.5 31.7 %collective-permute-start.33 = (bf16[64,2432]{1,0:T(8,128)(2,1)S(1)}, bf16[64,2432]{1,0:T(8,128)(2,1)S(1)}, u32[]{:S(2)}, u32[]{:S(2)}) collective-permute-start(bf16[64,2432]{1,0:T(8,128)(2,1)S(1)} %add_convert_fusion.7), channel_id=1, source_target_pairs={{0,8},{8,0},{16,24},{24,16},{1,9},{9,1},{17,25},{25,17},{2,10},{10... | collective-permute-start | bytes 933896 | tf_op jit(solution)/shard_map/ppermute | solution.py:617
  503.5 6.4 collective-permute-start.34
  516.4 27.0 %collective-permute-start.35 = (bf16[512,2432]{1,0:T(8,128)(2,1)}, bf16[512,2432]{1,0:T(8,128)(2,1)}, u32[]{:S(2)}, u32[]{:S(2)}) collective-permute-start(bf16[512,2432]{1,0:T(8,128)(2,1)} %product_give.7), channel_id=1, source_target_pairs={{0,1},{1,0},{2,3},{3,2},{4,5},{5,4},{6,7},{7,6},{8,9},{9,8},{10,11... | collective-permute-start | bytes 7471112 | tf_op jit(solution)/shard_map/ppermute | solution.py:617
  523.1 20.3 %collective-permute-start.37 = (bf16[128,2048]{1,0:T(8,128)(2,1)S(1)}, bf16[128,2048]{1,0:T(8,128)(2,1)}, u32[]{:S(2)}, u32[]{:S(2)}) collective-permute-start(bf16[128,2048]{1,0:T(8,128)(2,1)S(1)} %copy-done.43), channel_id=1, source_target_pairs={{0,2},{1,3},{2,0},{3,1},{4,6},{5,7},{6,4},{7,5},{8,10},{9,11},{10,... | collective-permute-start | bytes 1572872 | tf_op jit(solution)/shard_map/ppermute | solution.py:617
  523.7 24.6 %collective-permute-start.38 = (bf16[128,2048]{1,0:T(8,128)(2,1)S(1)}, bf16[128,2048]{1,0:T(8,128)(2,1)}, u32[]{:S(2)}, u32[]{:S(2)}) collective-permute-start(bf16[128,2048]{1,0:T(8,128)(2,1)S(1)} %copy-done.41), channel_id=1, source_target_pairs={{0,4},{1,5},{2,6},{3,7},{4,0},{5,1},{6,2},{7,3},{8,12},{9,13},{10,... | collective-permute-start | bytes 1572872 | tf_op jit(solution)/shard_map/ppermute | solution.py:617
  525.3 24.9 %collective-permute-start.39 = (bf16[128,2048]{1,0:T(8,128)(2,1)S(1)}, bf16[128,2048]{1,0:T(8,128)(2,1)}, u32[]{:S(2)}, u32[]{:S(2)}) collective-permute-start(bf16[128,2048]{1,0:T(8,128)(2,1)S(1)} %get-tuple-element.367), channel_id=1, source_target_pairs={{0,6},{1,7},{2,4},{3,5},{4,2},{5,3},{6,0},{7,1},{8,14},{9,15},{10,... | collective-permute-start | bytes 1572872 | tf_op jit(solution)/shard_map/ppermute | solution.py:617
  539.3 13.2 %collective-permute-start.36 = (bf16[128,1024]{1,0:T(8,128)(2,1)S(1)}, bf16[128,1024]{1,0:T(8,128)(2,1)S(1)}, u32[]{:S(2)}, u32[]{:S(2)}) collective-permute-start(bf16[128,1024]{1,0:T(8,128)(2,1)S(1)} %get-tuple-element.497), channel_id=1, source_target_pairs={{0,8},{8,0},{16,24},{24,16},{1,9},{9,1},{17,25},{25,17},{2,10},{10... | collective-permute-start | bytes 786440 | tf_op jit(solution)/shard_map/ppermute | solution.py:617
  558.6 26.1 %collective-permute-start.40 = (bf16[128,1024]{1,0:T(8,128)(2,1)S(1)}, bf16[128,1024]{1,0:T(8,128)(2,1)S(1)}, u32[]{:S(2)}, u32[]{:S(2)}) collective-permute-start(bf16[128,1024]{1,0:T(8,128)(2,1)S(1)} %add_convert_fusion.12), channel_id=1, source_target_pairs={{0,16},{8,24},{16,0},{24,8},{1,17},{9,25},{17,1},{25,9},{2,18},{10... | collective-permute-start | bytes 786440 | tf_op jit(solution)/shard_map/ppermute | solution.py:617
  561.1 25.5 %collective-permute-start.41 = (bf16[64,2048]{1,0:T(8,128)(2,1)S(1)}, bf16[64,2048]{1,0:T(8,128)(2,1)S(1)}, u32[]{:S(2)}, u32[]{:S(2)}) collective-permute-start(bf16[64,2048]{1,0:T(8,128)(2,1)S(1)} %get-tuple-element.495), channel_id=1, source_target_pairs={{0,8},{8,0},{16,24},{24,16},{1,9},{9,1},{17,25},{25,17},{2,10},{10... | collective-permute-start | bytes 786440 | tf_op jit(solution)/shard_map/ppermute | solution.py:617
  561.6 25.0 %collective-permute-start.42 = (bf16[128,2432]{1,0:T(8,128)(2,1)S(1)}, bf16[128,2432]{1,0:T(8,128)(2,1)S(1)}, u32[]{:S(2)}, u32[]{:S(2)}) collective-permute-start(bf16[128,2432]{1,0:T(8,128)(2,1)S(1)} %get-tuple-element.380), channel_id=1, source_target_pairs={{0,2},{1,3},{2,0},{3,1},{4,6},{5,7},{6,4},{7,5},{8,10},{9,11},{10,... | collective-permute-start | bytes 1867784 | tf_op jit(solution)/shard_map/ppermute | solution.py:617
  563.1 28.4 %collective-permute-start.43 = (bf16[128,2432]{1,0:T(8,128)(2,1)S(1)}, bf16[128,2432]{1,0:T(8,128)(2,1)S(1)}, u32[]{:S(2)}, u32[]{:S(2)}) collective-permute-start(bf16[128,2432]{1,0:T(8,128)(2,1)S(1)} %get-tuple-element.381), channel_id=1, source_target_pairs={{0,4},{1,5},{2,6},{3,7},{4,0},{5,1},{6,2},{7,3},{8,12},{9,13},{10,... | collective-permute-start | bytes 1867784 | tf_op jit(solution)/shard_map/ppermute | solution.py:617
  564.6 27.0 %collective-permute-start.44 = (bf16[128,2432]{1,0:T(8,128)(2,1)S(1)}, bf16[128,2432]{1,0:T(8,128)(2,1)S(1)}, u32[]{:S(2)}, u32[]{:S(2)}) collective-permute-start(bf16[128,2432]{1,0:T(8,128)(2,1)S(1)} %get-tuple-element.382), channel_id=1, source_target_pairs={{0,6},{1,7},{2,4},{3,5},{4,2},{5,3},{6,0},{7,1},{8,14},{9,15},{10,... | collective-permute-start | bytes 1867784 | tf_op jit(solution)/shard_map/ppermute | solution.py:617
  592.6 5.0 collective-permute-start.45
  593.3 14.4 %collective-permute-start.51 = (bf16[64,2048]{1,0:T(8,128)(2,1)S(1)}, bf16[64,2048]{1,0:T(8,128)(2,1)}, u32[]{:S(2)}, u32[]{:S(2)}) collective-permute-start(bf16[64,2048]{1,0:T(8,128)(2,1)S(1)} %add_convert_fusion.10), channel_id=1, source_target_pairs={{0,16},{8,24},{16,0},{24,8},{1,17},{9,25},{17,1},{25,9},{2,18},{10... | collective-permute-start | bytes 786440 | tf_op jit(solution)/shard_map/ppermute | solution.py:617
  595.5 14.9 %collective-permute-start.50 = (bf16[128,1024]{1,0:T(8,128)(2,1)S(1)}, bf16[128,1024]{1,0:T(8,128)(2,1)}, u32[]{:S(2)}, u32[]{:S(2)}) collective-permute-start(bf16[128,1024]{1,0:T(8,128)(2,1)S(1)} %add_convert_fusion.11), channel_id=1, source_target_pairs={{0,8},{8,0},{16,24},{24,16},{1,9},{9,1},{17,25},{25,17},{2,10},{10... | collective-permute-start | bytes 786440 | tf_op jit(solution)/shard_map/ppermute | solution.py:617
  597.2 18.5 %collective-permute-start.52 = (bf16[64,2432]{1,0:T(8,128)(2,1)S(1)}, bf16[64,2432]{1,0:T(8,128)(2,1)}, u32[]{:S(2)}, u32[]{:S(2)}) collective-permute-start(bf16[64,2432]{1,0:T(8,128)(2,1)S(1)} %get-tuple-element.491), channel_id=1, source_target_pairs={{0,8},{8,0},{16,24},{24,16},{1,9},{9,1},{17,25},{25,17},{2,10},{10... | collective-permute-start | bytes 933896 | tf_op jit(solution)/shard_map/ppermute | solution.py:617
  597.6 4.9 collective-permute-start.46
  602.5 19.5 %collective-permute-start.47 = (f32[8,3672]{1,0:T(8,128)S(1)}, f32[8,3672]{1,0:T(8,128)S(1)}, u32[]{:S(2)}, u32[]{:S(2)}) collective-permute-start(f32[8,3672]{1,0:T(8,128)S(1)} %add.366), channel_id=1, source_target_pairs={{0,4},{1,5},{2,6},{3,7},{4,0},{5,1},{6,2},{7,3},{8,12},{9,13},{10,... | collective-permute-start | bytes 352520 | tf_op jit(solution)/shard_map/ppermute | solution.py:617
  616.8 17.7 %collective-permute-start.53 = (bf16[64,2048]{1,0:T(8,128)(2,1)S(1)}, bf16[64,2048]{1,0:T(8,128)(2,1)S(1)}, u32[]{:S(2)}, u32[]{:S(2)}) collective-permute-start(bf16[64,2048]{1,0:T(8,128)(2,1)S(1)} %add_convert_fusion.9), channel_id=1, source_target_pairs={{0,8},{8,0},{16,24},{24,16},{1,9},{9,1},{17,25},{25,17},{2,10},{10... | collective-permute-start | bytes 786440 | tf_op jit(solution)/shard_map/ppermute | solution.py:617
  617.9 23.6 %collective-permute-start.54 = (bf16[64,2432]{1,0:T(8,128)(2,1)S(1)}, bf16[64,2432]{1,0:T(8,128)(2,1)S(1)}, u32[]{:S(2)}, u32[]{:S(2)}) collective-permute-start(bf16[64,2432]{1,0:T(8,128)(2,1)S(1)} %add_convert_fusion.6), channel_id=1, source_target_pairs={{0,16},{8,24},{16,0},{24,8},{1,17},{9,25},{17,1},{25,9},{2,18},{10... | collective-permute-start | bytes 933896 | tf_op jit(solution)/shard_map/ppermute | solution.py:617
  622.0 9.8 %collective-permute-start.48 = (f32[8,3672]{1,0:T(8,128)S(1)}, f32[8,3672]{1,0:T(8,128)S(1)}, u32[]{:S(2)}, u32[]{:S(2)}) collective-permute-start(f32[8,3672]{1,0:T(8,128)S(1)} %add.367), channel_id=1, source_target_pairs={{0,8},{8,0},{16,24},{24,16},{1,9},{9,1},{17,25},{25,17},{2,10},{10... | collective-permute-start | bytes 352520 | tf_op jit(solution)/shard_map/ppermute | solution.py:617
  631.8 7.1 %collective-permute-start.49 = (f32[8,3672]{1,0:T(8,128)S(1)}, f32[8,3672]{1,0:T(8,128)S(1)}, u32[]{:S(2)}, u32[]{:S(2)}) collective-permute-start(f32[8,3672]{1,0:T(8,128)S(1)} %add.368), channel_id=1, source_target_pairs={{0,16},{8,24},{16,0},{24,8},{1,17},{9,25},{17,1},{25,9},{2,18},{10... | collective-permute-start | bytes 352520 | tf_op jit(solution)/shard_map/ppermute | solution.py:617
  641.6 7.0 %collective-permute-start.55 = (bf16[64,2432]{1,0:T(8,128)(2,1)S(1)}, bf16[64,2432]{1,0:T(8,128)(2,1)S(1)}, u32[]{:S(2)}, u32[]{:S(2)}) collective-permute-start(bf16[64,2432]{1,0:T(8,128)(2,1)S(1)} %add_convert_fusion.5), channel_id=1, source_target_pairs={{0,8},{8,0},{16,24},{24,16},{1,9},{9,1},{17,25},{25,17},{2,10},{10... | collective-permute-start | bytes 933896 | tf_op jit(solution)/shard_map/ppermute | solution.py:617
  (170 other events, 1640.3 us)
Sparse Core Ops, SparseCore 0:
  10.5 43.6 all-gather.8
  56.6 37.4 all-gather.10
  96.0 58.3 all-gather.12
  156.1 37.4 all-gather.14
  195.3 36.7 all-gather.16
  266.1 59.7 reduce-scatter.2
  329.6 56.9 reduce-scatter.4
  523.2 67.7 all-reduce.4

commit v3 on v2

--- a/solution.py
+++ b/solution.py
@@ -105,7 +105,8 @@
 
 def state_kernel(
     v_ref, halo_ref, bc_ref, bchalo_ref, dt_ref, taps_ref, shift_ref, bctaps_ref, bcshift_ref,
-    prm_ref, f_ref, tot_ref, x_ref, p_ref, p3_ref, b_ref, c_ref, bt_ref, ct_ref, ext,
+    prm_ref, f_ref, tot_ref, x_ref, p_ref, p3_ref, b_ref, c_ref, bt_ref, ct_ref, ext, sumw,
+    dtw, wxw,
 ):
     i = pl.program_id(0)
     blocks = v_ref.shape[0] // T
@@ -143,22 +144,22 @@
     fill(ext, halo_ref, v_ref)
     steps = head_lanes(L_STEP, i)
     sums = head_lanes(L_CUMF, i)
-    tot = dot(p3_ref[pl.ds(blocks * T - 16, 16), :], sums)[15:16, :]
-    total = jnp.zeros((N, WB), F32)
+    heads = p3_ref[...]
+    sumw[...] = dot(heads, sums)
+    dtw[...] = dot(heads, steps)
+    tot = sumw[blocks * T - 8 :, :][7:8, :]
     for c in range(blocks):
         rows = pl.ds(c * T, T)
         conv = conv_block(ext, taps_ref, shift_ref, c)
         x = conv * sigmoid(conv)
         x_ref[rows, :] = x
-        heads = p3_ref[rows, :]
-        wx = (x * (jnp.exp(tot - dot(heads, sums)) * dot(heads, steps))).astype(BF16)
-        total = total + dot(bt_ref[:, rows], wx)
-    f_ref[...] = total.astype(BF16)
+        wxw[rows, :] = (x * (jnp.exp(tot - sumw[rows, :]) * dtw[rows, :])).astype(BF16)
+    f_ref[...] = dot(bt_ref[...], wxw[...]).astype(BF16)
     tot_ref[...] = jnp.broadcast_to(jnp.exp(tot), (8, WB))
 
 
 def scan_kernel(
-    x_ref, skip_ref, p3_ref, b_ref, c_ref, bt_ref, y_ref, cb,
+    x_ref, skip_ref, p3_ref, b_ref, c_ref, bt_ref, y_ref, cb, cumw, dtw,
 ):
     i = pl.program_id(0)
     blocks = x_ref.shape[0] // T
@@ -172,14 +173,16 @@
 
     steps = head_lanes(L_STEP, i)
     sums = head_tiles(L_CUM, i)
+    cumw[...] = dot(p3_ref[...], sums)
+    dtw[...] = dot(p3_ref[...], steps)
+    turned_all = head_rows(p3_ref[...], i)
     state = None
     for c in range(blocks):
         rows = pl.ds(c * T, T)
         x = x_ref[rows, :]
-        heads = p3_ref[rows, :]
-        cums = dot(heads, sums)
-        turned = head_rows(heads, i)
-        xd = x * dot(heads, steps)
+        cums = cumw[rows, :]
+        turned = turned_all[:, c * T : (c + 1) * T]
+        xd = x * dtw[rows, :]
         parts = []
         for p in range(HB // 2):
             weights = []
@@ -263,26 +266,32 @@
 
 
 def conv_back(ext, dext, taps_ref, dv_ref, tail_ref, head_ref, stats_ref, blocks):
-    sums = [jnp.zeros((1, WB), F32) for _ in range(5)]
+    early = dext[0:8, :]
+    before = ext[HALO - 8 : HALO, :]
+    sums = []
+    for k in range(5):
+        sums.append(jnp.zeros((1, WB), F32))
+        for j in range(3 - k):
+            sums[k] = sums[k] + early[j : j + 1, :] * before[5 + k + j : 6 + k + j, :]
     for c in range(blocks):
-        d = dext[pl.ds(c * T, T), :]
-        total = taps_ref[3:4, :] * d
-        for k in range(3):
-            total = total + taps_ref[k : k + 1, :] * dext[pl.ds(c * T + 3 - k, T), :]
+        v = ext[pl.ds(HALO + c * T, T), :]
+        total = None
+        for k in (3, 2, 1, 0):
+            d = dext[pl.ds(c * T + 3 - k, T), :]
+            total = taps_ref[k : k + 1, :] * d if total is None else total + taps_ref[k : k + 1, :] * d
+            sums[k] = sums[k] + jnp.sum(d * v, axis=0, keepdims=True)
+            if k == 3:
+                sums[4] = sums[4] + jnp.sum(d, axis=0, keepdims=True)
         dv_ref[pl.ds(c * T, T), :] = total.astype(BF16)
         if c == blocks - 1:
             tail_ref[...] = total[T - 8 :, :]
-        for k in range(4):
-            v = ext[pl.ds(HALO - 3 + k + c * T, T), :]
-            sums[k] = sums[k] + jnp.sum(d * v, axis=0, keepdims=True)
-        sums[4] = sums[4] + jnp.sum(d, axis=0, keepdims=True)
     head_ref[...] = dext[0:8, :]
     for k in range(5):
         stats_ref[k : k + 1, :] = sums[k]
 
 
 def back_inside_kernel(
-    x_ref, p3_ref, b_ref, c_ref, dy_ref, dxd_ref, dcbt_ref, cbt, first,
+    x_ref, p3_ref, b_ref, c_ref, dy_ref, dxd_ref, dcbt_ref, cbt, cumw, dtw, first,
 ):
     i = pl.program_id(0) + first
     blocks = x_ref.shape[0] // T
@@ -297,12 +306,14 @@
 
     steps = head_lanes(L_STEP, i)
     sums = head_tiles(L_CUM, i)
+    cumw[...] = dot(p3_ref[...], sums)
+    dtw[...] = dot(p3_ref[...], steps)
+    turned_all = head_rows(p3_ref[...], i)
     for c in range(blocks):
         rows = pl.ds(c * T, T)
-        heads = p3_ref[rows, :]
-        cums = dot(heads, sums)
-        turned = head_rows(heads, i)
-        xd = x_ref[rows, :] * dot(heads, steps)
+        cums = cumw[rows, :]
+        turned = turned_all[:, c * T : (c + 1) * T]
+        xd = x_ref[rows, :] * dtw[rows, :]
         dyb = dy_ref[rows, :]
         dy = dyb.astype(F32)
         dcb = jnp.zeros((T, T), F32)
@@ -325,11 +336,10 @@
 def back_kernel(
     v_ref, halo_ref, bc_ref, bchalo_ref, taps_ref, shift_ref, bctaps_ref, bcshift_ref, skip_ref,
     prm_ref, p_ref, p3_ref, b_ref, c_ref, bt_ref, ct_ref, s_ref, gin_ref, dy_ref, y_ref,
-    inside_ref,
-    low_ref, high_ref,
+    inside_low_ref, inside_high_ref, low_ref, high_ref,
     dv_ref, tail_ref, head_ref, stats_ref, bdv_ref, btail_ref, bhead_ref, bstats_ref,
     ddt_ref, dtstats_ref,
-    ext, dext, convs, sigs, cumw, dtw, acc, dbacc, dcacc,
+    ext, dext, convs, sigs, cumw, dtw, prods, acc, dbacc, dcacc,
 ):
     i = pl.program_id(0)
     blocks = v_ref.shape[0] // T
@@ -345,6 +355,8 @@
     dext[length:, :] = jnp.zeros((8, WB), F32)
     steps = head_lanes(L_STEP, i)
     sums = head_lanes(L_CUM, i)
+    cumw[...] = dot(p3_ref[...], sums)
+    dtw[...] = dot(p3_ref[...], steps)
     states = [s_ref[...].astype(F32)]
     for c in range(blocks):
         rows = pl.ds(c * T, T)
@@ -352,11 +364,7 @@
         sig = sigmoid(conv)
         convs[rows, :] = conv
         sigs[rows, :] = sig
-        heads = p3_ref[rows, :]
-        cumx = dot(heads, sums)
-        dt = dot(heads, steps)
-        cumw[rows, :] = cumx
-        dtw[rows, :] = dt
+        cumx, dt = cumw[rows, :], dtw[rows, :]
         tot = cumx[T - 1 : T, :]
         wx = (jnp.exp(tot - cumx) * (conv * sig * dt)).astype(BF16)
         states.append(states[-1] * jnp.exp(tot) + dot(bt_ref[:, rows], wx))
@@ -365,6 +373,7 @@
     seg1 = (lane_iota(WB) == HB * i + ch).astype(BF16)
     seg2 = (lane_iota(WB) == 32 + HB * i + ch).astype(BF16)
     final = row_iota(T, WB) == T - 1
+    lower = jnp.full((T, WB), i, jnp.int32) < STEPS // 2
     grad = gin_ref[...].astype(F32)
     skip_sum = jnp.zeros((1, WB), F32)
     for c in reversed(range(blocks)):
@@ -379,7 +388,8 @@
         dy = dyb.astype(F32)
         gb = grad.astype(BF16)
         w = jnp.exp(tot - cumx)
-        dxd = inside_ref[rows, :] + w * dot(b_ref[rows, :], gb)
+        inside = jnp.where(lower, inside_low_ref[rows, :], inside_high_ref[rows, :])
+        dxd = inside + w * dot(b_ref[rows, :], gb)
         ey = (jnp.exp(cumx) * dy).astype(BF16)
         wx = (w * xd).astype(BF16)
         dcacc[rows, :] += dot_nt(ey, states[c].astype(BF16))
@@ -391,13 +401,14 @@
         p2 = x * dxd
         p1h = p1.astype(BF16)
         p2h = p2.astype(BF16)
-        acc[rows, :] += (
-            dot(p1h, seg1) + dot((p1 - p1h.astype(F32)).astype(BF16), seg1)
-        ) + (dot(p2h, seg2) + dot((p2 - p2h.astype(F32)).astype(BF16), seg2))
+        sides = (p1h, (p1 - p1h.astype(F32)).astype(BF16), p2h, (p2 - p2h.astype(F32)).astype(BF16))
+        for k, side in enumerate(sides):
+            prods[rows, k * WB : (k + 1) * WB] = side
         skip_sum = skip_sum + jnp.sum(x * dy, axis=0, keepdims=True)
         dx = dt * dxd + skip * dy
         dext[rows, :] = dx * (sig * (1.0 + conv * (1.0 - sig)))
         grad = grad * jnp.exp(tot) + dot(ct_ref[:, rows], ey)
+    acc[...] += dot(prods[...], jnp.concatenate([seg1, seg1, seg2, seg2], axis=0))
     conv_back(ext, dext, taps_ref, dv_ref, tail_ref, head_ref, stats_ref, blocks)
     stats_ref[5:6, :] = skip_sum
 
@@ -479,7 +490,10 @@
             shape_of((length, N), BF16), shape_of((length, N), BF16),
             shape_of((N, length), BF16), shape_of((N, length), BF16),
         ],
-        scratch_shapes=[pltpu.VMEM((HALO + length, WB), F32)],
+        scratch_shapes=[
+            pltpu.VMEM((HALO + length, WB), F32), pltpu.VMEM((length, WB), F32),
+            pltpu.VMEM((length, WB), F32), pltpu.VMEM((length, WB), BF16),
+        ],
         compiler_params=params(),
         cost_estimate=cost(4e9, 8e6),
     )(r_low, halo, r_low, halo, r_low, taps, shift, taps, shift, prm)
@@ -497,7 +511,10 @@
         ],
         out_specs=wide(length),
         out_shape=shape_of((length, DI), F32),
-        scratch_shapes=[pltpu.VMEM((length // T, T, T), F32)],
+        scratch_shapes=[
+            pltpu.VMEM((length // T, T, T), F32), pltpu.VMEM((length, HB * 128), F32),
+            pltpu.VMEM((length, WB), F32),
+        ],
         compiler_params=params(),
         cost_estimate=cost(1.5e10, 8e6),
     )(x, skip, p3, b, c, bt)
@@ -555,7 +572,10 @@
         ],
         out_specs=[wide(length), whole((blocks, T, T))],
         out_shape=[shape_of((length, DI // 2), F32), shape_of((blocks, T, T), F32)],
-        scratch_shapes=[pltpu.VMEM((blocks, T, T), F32)],
+        scratch_shapes=[
+            pltpu.VMEM((blocks, T, T), F32), pltpu.VMEM((length, HB * 128), F32),
+            pltpu.VMEM((length, WB), F32),
+        ],
         compiler_params=params(),
         cost_estimate=cost(1e10, 6e6),
     )(x, p3, b, c, dy)
@@ -566,7 +586,6 @@
 ):
     length = r_low.shape[0]
     blocks = length // T
-    inside = jnp.concatenate([low[0], high[0]], axis=1)
     return pl.pallas_call(
         back_kernel,
         name="scan_backward",
@@ -576,7 +595,9 @@
             wide(4), wide(1), bc_block(4), bc_block(1), wide(1), whole((8, 128)),
             whole((length, 128)), whole((length, 384)), whole((length, N)), whole((length, N)),
             whole((N, length)), whole((N, length)), wide(N), wide(N), wide(length), wide(length),
-            wide(length), whole((blocks, T, T)), whole((blocks, T, T)),
+            pl.BlockSpec((length, WB), lambda i: (0, jnp.minimum(i, STEPS // 2 - 1))),
+            pl.BlockSpec((length, WB), lambda i: (0, jnp.maximum(i - STEPS // 2, 0))),
+            whole((blocks, T, T)), whole((blocks, T, T)),
         ],
         out_specs=[
             wide(length), wide(8), wide(8), wide(8),
@@ -597,6 +618,7 @@
             pltpu.VMEM((length, WB), F32),
             pltpu.VMEM((length, WB), F32),
             pltpu.VMEM((length, WB), F32),
+            pltpu.VMEM((length, 4 * WB), BF16),
             pltpu.VMEM((length, 128), F32),
             pltpu.VMEM((length, 128), F32),
             pltpu.VMEM((length, 128), F32),
@@ -605,7 +627,7 @@
         cost_estimate=cost(3e10, 16e6),
     )(
         r_low, halo, r_low, halo, taps, shift, taps, shift, skip, prm, p, p3, b, c, bt, ct,
-        s_in, g_in, dy, y, inside, low[1], high[1],
+        s_in, g_in, dy, y, low[0], high[0], low[1], high[1],
     )
 
 
@@ -643,14 +665,6 @@
     for item in work:
         done.append(item())
     return state, done
-
-
-def gather_pieces(w):
-    n = lax.axis_size("fsdp")
-    pieces = [w, swap(w, "fsdp", 1)]
-    for piece in [swap(w, "fsdp", 2 * d) for d in range(1, n // 2)]:
-        pieces += [piece, swap(piece, "fsdp", 1)]
-    return pieces
 
 
 def pieces_kernel(order_ref, left_ref, base_ref, *refs):
@@ -833,6 +847,29 @@
     return a
 
 
+def turn_kernel(*refs):
+    out_ref = refs[-1]
+    for k in range(len(refs) // 2):
+        row = 0
+        for ref in refs[2 * k : 2 * k + 2]:
+            for j in range(0, ref.shape[1], 128):
+                rows = min(128, out_ref.shape[1] - row)
+                tile = ref[:, j : j + 128].astype(F32).T
+                out_ref[k, row : row + rows, :] = tile[:rows, :]
+                row += rows
+
+
+def in_weight_rows(pieces, in_width):
+    flat = [piece for pair in pieces for piece in pair]
+    return pl.pallas_call(
+        turn_kernel,
+        name="in_weight_rows",
+        out_shape=shape_of((len(pieces), in_width, flat[0].shape[0]), F32),
+        compiler_params=params(),
+        cost_estimate=cost(0, 7e6),
+    )(*flat)
+
+
 def on_device(
     hidden_in, cotangent, norm_gain, input_projection_weight, conv_weight, conv_bias, dt_bias,
     a_log, skip, gate_gain, output_projection_weight,
@@ -857,6 +894,7 @@
         unpacked.append(piece.reshape(a.shape[:-1] + (shards * a.shape[-1],)))
     gains, taps_all, shift_all, bias_all, rate_all, skip_all, gate_all = unpacked
 
+    by_pieces = output_projection_weight.shape[1] % 128 == 0
     weights = []
     for layer in range(layers):
         w = input_projection_weight[layer]
@@ -864,12 +902,15 @@
         rest = lax.all_gather(rest, "fsdp", axis=0, tiled=True)
         if layer == 0:
             rest, first_out = tie(rest, output_projection_weight[0])
+            if by_pieces:
+                near = swap(first_out, "fsdp", 1)
+                arrived = [swap(first_out, "fsdp", 2 * d) for d in range(1, shards // 2)]
         weights.append(
             (
                 rest,
                 lax.all_gather(w[:, :DI], "fsdp", axis=0, tiled=True),
-                gather_pieces(first_out)
-                if layer == 0 and first_out.shape[0] % 128 == 0
+                None
+                if layer == 0 and by_pieces
                 else lax.all_gather(output_projection_weight[layer], "fsdp", axis=0, tiled=True),
             )
         )
@@ -889,15 +930,24 @@
         prm = prm.at[0].set(jnp.tile(bias_all[layer], 4))
         prm = prm.at[1].set(jnp.tile(-jnp.exp(rate_all[layer]), 4))
         f, decay, x, p, p3, b, c, bt, ct = local_state(r_low, halo, taps, shift, prm)
-        s_in, (y, gate) = pass_along(
-            f,
-            decay[0:1],
-            True,
-            [
-                lambda: local_scan(x, skip_wide, p3, b, c, bt),
-                lambda: dot(normed, w_gate),
-            ],
-        )
+        state = hop_to(f, None, 0, True)
+        y = local_scan(x, skip_wide, p3, b, c, bt)
+        state, y = tie(state, y)
+        if w_out is None:
+            y, arrived = tie(y, arrived)
+            swapped = [swap(piece, "fsdp", 1) for piece in arrived]
+        for hop in range(1, seq_parts - 1):
+            state = hop_to(message_of(f, decay[0:1], state), state, hop, True)
+            if hop == 1:
+                gate = dot(normed, w_gate)
+                state, gate = tie(state, gate)
+                if w_out is None:
+                    gate, swapped = tie(gate, swapped)
+                    w_out = [first_out, near]
+                    for pair in zip(arrived, swapped):
+                        w_out += pair
+                    weights[layer] = (w_rest, w_gate, w_out)
+        s_in = state
         y, gate_low = gate_forward(y, gate, p, c, s_in, gate_all[layer][None, :])
         stored.append(
             (
@@ -980,9 +1030,12 @@
             low, high,
         )
         if layer == 0:
-            back, out_sent, above = tie(back, out_sent, above)
+            back, out_sent, gate_sent, above, big[layer + 1] = tie(
+                back, out_sent, gate_sent, above, big[layer + 1]
+            )
             big[layer + 1].append(seq_join(*above))
             out_seq = seq_first(gather_sum(out_mine, out_sent))
+            gate_sum = gather_sum(gate_mine, gate_sent)
         dv, tail, head, stats, bdv, btail, bhead, bstats, ddt, dtstats = back
         heads_in = lax.ppermute(jnp.concatenate([head, bhead], axis=1), "seq", down)
         tail = jnp.concatenate([tail, btail], axis=1)
@@ -994,30 +1047,34 @@
         d_rest = lax.dynamic_update_slice(
             d_rest, jnp.concatenate(fix, axis=0).astype(BF16), (d_rest.shape[0] - 8, 0)
         )
-        got = swap(product_give(normed_give, d_rest), "fsdp", 1)
+        give = product_give(normed_give, d_rest)
+        if layer == 0:
+            give, out_seq = tie(give, out_seq)
+            out_seq = seq_across(*out_seq)
+            gate_seq = seq_first(gate_sum)
+        got = swap(give, "fsdp", 1)
         d_normed = dot_nt(dgate, w_gate)
         got, d_normed = tie(got, d_normed)
-        if layer == 0:
-            got, out_seq, gate_sent = tie(got, out_seq, gate_sent)
-            out_seq = seq_across(*out_seq)
-            gate_seq = seq_first(gather_sum(gate_mine, gate_sent))
-        parts = product_own(normed_own, d_rest, got)
-        parts, d_rest = tie(parts, d_rest)
-        rest_mine, rest_sent = send_chips(parts)
+        if layer > 0:
+            parts = product_own(normed_own, d_rest, got)
+            parts, d_rest = tie(parts, d_rest)
+            rest_mine, rest_sent = send_chips(parts)
         d_normed = d_normed + dot_nt(d_rest, w_rest)
         q = hidden * r_in
         dq = d_normed * gains[layer][None, :]
         gain_in_grad = jnp.sum(d_normed * q, axis=0)
         grad = grad + r_in * (dq - q * jnp.mean(dq * q, axis=1, keepdims=True))
         if layer == 0:
-            grad, gain_in_grad, out_seq, gate_seq, rest_sent = tie(
-                grad, gain_in_grad, out_seq, gate_seq, rest_sent
-            )
+            grad, gain_in_grad, got = tie(grad, gain_in_grad, got)
+            parts = product_own(normed_own, d_rest, got)
+            parts, out_seq, gate_seq = tie(parts, out_seq, gate_seq)
+            rest_mine, rest_sent = send_chips(parts)
             out_seq = seq_back(*out_seq)
             gate_seq = seq_across(*gate_seq)
+            out_seq, gate_seq, rest_sent = tie(out_seq, gate_seq, rest_sent)
+            gate_seq = seq_back(*gate_seq)
             rest_seq = seq_first(gather_sum(rest_mine, rest_sent))
-            out_seq, gate_seq, rest_seq = tie(out_seq, gate_seq, rest_seq)
-            gate_seq = seq_back(*gate_seq)
+            rest_seq, gate_seq = tie(rest_seq, gate_seq)
             rest_seq = seq_back(*seq_across(*rest_seq))
             big[layer] = [seq_join(*out_seq), seq_join(*gate_seq), seq_join(*rest_seq)]
         waiting = layer
@@ -1037,17 +1094,16 @@
         full = jnp.stack([vectors[layer][member] for layer in range(layers)])
         full = full.reshape(a.shape[:-1] + (shards, a.shape[-1]))
         rows.append(jnp.moveaxis(full, -2, 0).reshape(shards, -1))
-    summed = sum_over(jnp.concatenate(rows, axis=1), "fsdp", "seq")
+    vector, rest_sent = tie(jnp.concatenate(rows, axis=1), rest_sent)
+    summed = sum_over(vector, "fsdp", "seq")
     mine = lax.dynamic_index_in_dim(summed, lax.axis_index("fsdp"), 0, keepdims=False)
     outs = []
     start = 0
     for a in small:
         outs.append(mine[start : start + a.size].reshape(a.shape))
         start += a.size
-    rest_width = in_width - DI
-    in_w = jnp.stack(
-        [jnp.concatenate([big[k][1], big[k][2][:, :rest_width]], axis=1) for k in range(layers)]
-    ).astype(F32)
+    in_w = in_weight_rows([big[k][1:] for k in range(layers)], in_width)
+    in_w = jnp.swapaxes(in_w, 1, 2)
     out_w = jnp.stack([big[k][0] for k in range(layers)]).astype(F32)
     return (
         block_out, grad[None], outs[0], in_w, outs[1], outs[2], outs[3], outs[4], outs[5],

time: 674 us -> 667 us (0.990)
  waiting for transfers between devices: 146 us -> 173 us
  Pallas kernels: 233 us -> 215 us
  other arithmetic: 60.9 us -> 50.9 us
  local copies, waits for them, and re-layouts: 59.7 us -> 52.2 us
    ppermute x12, waiting for transfers between devices: 26.2 us -> 42.7 us  [hop_to(): got = lax.ppermute(message, 'seq', [pair])]
    all_gather x2, waiting for transfers between devices: 0.02 us -> 11.4 us  [on_device(): lax.all_gather(w[:, :DI], 'fsdp', axis=0, tiled=True)]
    pallas_call x2, Pallas kernels: 63.2 us -> 55.4 us  [scan_backward(): pl.pallas_call(back_kernel, name='scan_backward', grid=(STEPS,), in_specs...]
    unnamed x346 -> x311, local copies, waits for them, and re-layouts: 31.2 us -> 25.5 us
  transfers between devices with their start and end apart: 64 -> 64, of which waited for: 23 -> 21; matrix products, arithmetic and copies ran while one was open for 21% -> 19% of each run, Pallas kernels for 33% -> 31%
where the time goes in v3:
time: 667 us; the launch traced here: 656 us
  Pallas kernels  215 us (32%)
  waiting for transfers between devices  173 us (26%)
  starting transfers between devices  72 us (11%)
  matrix products  65.6 us (10%)
  local copies, waits for them, and re-layouts  52.2 us (8%)
  other arithmetic  50.9 us (8%)
  between operations  16.7 us (3%)
  blocking collectives  10.7 us (2%)
    ppermute x40, waiting for transfers between devices, swap(): lax.ppermute(a, axis, [(k, k ^ bit) for k in range(lax.axis_size(axis))])  72.4 us
    pallas_call x2, Pallas kernels, scan_backward(): pl.pallas_call(back_kernel, name='scan_backward', grid=(STEPS,), in_specs...  55.4 us
    ppermute x12, waiting for transfers between devices, hop_to(): got = lax.ppermute(message, 'seq', [pair])  42.7 us
    ppermute x40, starting transfers between devices, swap(): lax.ppermute(a, axis, [(k, k ^ bit) for k in range(lax.axis_size(axis))])  37.6 us
    dot_general x5, matrix products, dot(): return jnp.dot(a, b, preferred_element_type=F32)  32.3 us
    all_gather x2, waiting for transfers between devices, on_device(): rest = lax.all_gather(rest, 'fsdp', axis=0, tiled=True)  31.3 us
    unnamed x311, local copies, waits for them, and re-layouts  25.5 us
    pallas_call x2, Pallas kernels, local_state(): pl.pallas_call(state_kernel, name='local_state', grid=(STEPS,), in_specs=...  24.9 us
  transfers between devices with their start and end apart: 64, of which 21 were waited for; matrix products, arithmetic and copies ran while one was open for 19% of the time, Pallas kernels for 31%

profile of v3, /device:TPU:0, one launch (start us, length us, event | category | flops | bytes accessed | tf_op | source)
XLA Modules:
  0.0 655.9 jit_solution(11192678139846543112)
XLA Ops:
  14.1 10.7 %all-gather.2 = bf16[8,2,1836]{2,1,0:T(2,128)(2,1)S(1)} all-gather(bf16[1,2,1836]{2,1,0:T(2,128)(2,1)S(1)} %bitcast.148), channel_id=2, replica_groups=mesh['seq'=4,'fsdp'=8] {'fsdp'}, dimensions={0}, use_global_device_ids=true | all-gather | bytes 66096 | tf_op jit(solution)/shard_map/all_gather | solution.py:885
  28.2 25.9 %all-gather.9.cloned.1.call-done = bf16[1024,2432]{0,1:T(8,128)(2,1)} async-done(((bf16[128,2432]{0,1:T(8,128)(2,1)}), bf16[1024,2432]{0,1:T(8,128)(2,1)}) %all-gather.9.cloned.1.call-update) | async-done | bytes 4980752 | tf_op jit(solution)/shard_map/all_gather | solution.py:902
  54.2 5.5 convolution_convert_fusion.1.v_ref.bc_ref.dt_ref
  59.8 3.4 collective-permute-start
  67.8 12.4 %local_state.2 = (bf16[128,2048]{1,0:T(8,128)(2,1)S(1)}, f32[8,2048]{1,0:T(8,128)S(1)}, f32[512,2048]{1,0:T(8,128)}, f32[512,128]{1,0:T(8,128)S(1)}, bf16[512,38...) custom-call(bf16[512,2432]{1,0:T(8,128)(2,1)} %copy-done.140, ...), custom_call_target="tpu_custom_call" | custom-call | flops 4000000000 | bytes 8000000 | tf_op jit(solution)/shard_map/local_state/pallas_call | solution.py:474
  80.3 3.4 collective-permute-start.1
  83.7 11.5 %local_scan.2.y_ref = f32[512,2048]{1,0:T(8,128)} custom-call(f32[512,2048]{1,0:T(8,128)} %get-tuple-element.250.x_ref, f32[1,2048]{1,0:T(1,128)S(1)} %broadcast_in_dim_reshape.6.skip_ref, bf16[512,384]{1,0:T(8,128)(2,1)S(1)} %get-tuple-element.251.p3_ref, bf16[512,128]{1,0:T(8,128)(2,1)S(1)} %get-tuple-element.252.b_ref, ...), custom_call_target="tpu_custom_call" | custom-call | flops 15000000512 | bytes 8000000 | tf_op jit(solution)/shard_map/local_scan/pallas_call | solution.py:504
  98.5 11.3 %all-gather.11.cloned.1.call-done = bf16[1024,2048]{0,1:T(8,128)(2,1)} async-done(((bf16[128,2048]{0,1:T(8,128)(2,1)}), bf16[1024,2048]{0,1:T(8,128)(2,1)}) %all-gather.11.cloned.1.call-update) | async-done | bytes 4194320 | tf_op jit(solution)/shard_map/all_gather | solution.py:911
  109.9 6.9 %fusion.41.gate_ref = f32[512,2048]{1,0:T(8,128)} fusion(bf16[512,1024]{1,0:T(8,128)(2,1)} %copy-done.89, bf16[1024,2048]{0,1:T(8,128)(2,1)} %all-gather.11.cloned.1.call-done), kind=kOutput, calls=%fused_computation.182 | convolution fusion | flops 2147483648 | bytes 9437184 | tf_op jit(solution)/shard_map/dot_general | solution.py:30
  121.6 2.8 bitcast_convert_fusion.base_ref
  126.0 7.1 %gate_forward.2 = (f32[512,2048]{1,0:T(8,128)}, bf16[512,2048]{1,0:T(8,128)(2,1)S(1)}) custom-call(f32[512,2048]{1,0:T(8,128)} %local_scan.2.y_ref, f32[512,2048]{1,0:T(8,128)} %fusion.41.gate_ref, f32[512,128]{1,0:T(8,128)S(1)} %get-tuple-element.265.p_ref, bf16[512,128]{1,0:T(8,128)(2,1)S(1)} %get-tuple-element.253.c_ref, ...), custom_call_target="tpu_custom_call" | custom-call | flops 5000000000 | bytes 15000000 | tf_op jit(solution)/shard_map/gate_forward/pallas_call | solution.py:526
  134.4 9.3 %add_product.1 = f32[512,1024]{1,0:T(8,128)} custom-call(s32[8]{0:T(128)S(1)} %iota_xor_fusion.order_ref, bf16[512,2048]{1,0:T(8,128)(2,1)} %copy-done, f32[512,1024]{1,0:T(8,128)} %bitcast_convert_fusion.base_ref, bf16[256,1024]{1,0:T(8,128)(2,1)S(1)} %get-tuple-element.256.refs_0_, bf16[256,1024]{1,0:T(8,128)(2,1)S(1)} %collective-permute-done.10.refs_1_, ...), custom_call_target="tpu_custom_call" | custom-call | flops 2000000000 | bytes 10000000 | tf_op jit(solution)/shard_map/add_product/pallas_call | solution.py:701
  147.3 5.4 all-gather.13.cloned.1.call-done
  152.7 5.6 convolution_convert_fusion.v_ref.bc_ref.dt_ref
  158.4 3.4 collective-permute-start.11
  163.7 12.4 %local_state.3 = (bf16[128,2048]{1,0:T(8,128)(2,1)S(1)}, f32[8,2048]{1,0:T(8,128)S(1)}, f32[512,2048]{1,0:T(8,128)}, f32[512,128]{1,0:T(8,128)S(1)}, bf16[512,38...) custom-call(bf16[512,2432]{1,0:T(8,128)(2,1)} %copy-done.141, ...), custom_call_target="tpu_custom_call" | custom-call | flops 4000000000 | bytes 8000000 | tf_op jit(solution)/shard_map/local_state/pallas_call | solution.py:474
  176.9 8.4 %collective-permute-start.12 = (bf16[128,2048]{1,0:T(8,128)(2,1)S(1)}, bf16[128,2048]{1,0:T(8,128)(2,1)S(1)}, u32[]{:S(2)}, u32[]{:S(2)}) collective-permute-start(bf16[128,2048]{1,0:T(8,128)(2,1)S(1)} %get-tuple-element.271), channel_id=1, source_target_pairs={{0,8},{1,9},{2,10},{3,11},{4,12},{5,13},{6,14},{7,15}} | collective-permute-start | bytes 1572872 | tf_op jit(solution)/shard_map/ppermute | solution.py:645
  185.3 11.5 %local_scan.3.y_ref = f32[512,2048]{1,0:T(8,128)} custom-call(f32[512,2048]{1,0:T(8,128)} %get-tuple-element.272.x_ref, f32[1,2048]{1,0:T(1,128)S(1)} %broadcast_in_dim_reshape.7.skip_ref, bf16[512,384]{1,0:T(8,128)(2,1)S(1)} %get-tuple-element.273.p3_ref, bf16[512,128]{1,0:T(8,128)(2,1)S(1)} %get-tuple-element.274.b_ref, ...), custom_call_target="tpu_custom_call" | custom-call | flops 15000000512 | bytes 8000000 | tf_op jit(solution)/shard_map/local_scan/pallas_call | solution.py:504
  200.5 7.2 %fusion.42.gate_ref = f32[512,2048]{1,0:T(8,128)} fusion(bf16[512,1024]{1,0:T(8,128)(2,1)} %multiply_convert_fusion, bf16[1024,2048]{0,1:T(8,128)(2,1)} %all-gather.15.cloned.1.call-done), kind=kOutput, calls=%fused_computation.183 | convolution fusion | flops 2147483648 | bytes 9437184 | tf_op jit(solution)/shard_map/dot_general | solution.py:30
  210.0 7.0 %gate_forward.3 = (f32[512,2048]{1,0:T(8,128)}, bf16[512,2048]{1,0:T(8,128)(2,1)S(1)}) custom-call(f32[512,2048]{1,0:T(8,128)} %local_scan.3.y_ref, f32[512,2048]{1,0:T(8,128)} %fusion.42.gate_ref, f32[512,128]{1,0:T(8,128)S(1)} %copy-done.44, bf16[512,128]{1,0:T(8,128)(2,1)S(1)} %copy-done.61, bf16[128,2048]{1,0:T(8,128)(2,1)S(1)} %add.306.s_ref, ...), custom_call_target="tpu_custom_call" | custom-call | flops 5000000000 | bytes 15000000 | tf_op jit(solution)/shard_map/gate_forward/pallas_call | solution.py:526
  219.2 11.2 %all-gather.17.cloned.1.call-done = bf16[1,2048,1024]{2,1,0:T(8,128)(2,1)} async-done(((bf16[1,256,1024]{2,1,0:T(8,128)(2,1)}), bf16[1,2048,1024]{2,1,0:T(8,128)(2,1)}) %all-gather.17.cloned.1.call-update) | async-done | bytes 4194320 | tf_op jit(solution)/shard_map/all_gather | solution.py:914
  230.4 6.9 %fusion.6 = bf16[1,512,1024]{2,1,0:T(8,128)(2,1)} fusion(f32[512,1024]{1,0:T(8,128)} %add_product.1, bf16[512,2048]{1,0:T(8,128)(2,1)} %copy-done.31, bf16[1,2048,1024]{2,1,0:T(8,128)(2,1)} %all-gather.17.cloned.1.call-done), kind=kOutput, calls=%fused_computation.21 | convolution fusion | flops 2148532224 | bytes 9437184 | tf_op jit(solution)/shard_map/dot_general | solution.py:30
  237.3 4.3 fusion.dgn_ref
  241.6 10.0 %gate_backward.2 = (bf16[512,2048]{1,0:T(8,128)(2,1)S(1)}, bf16[512,2048]{1,0:T(8,128)(2,1)}, f32[8,2048]{1,0:T(8,128)S(1)}, bf16[128,2048]{1,0:T(8,128)(2,1)S(1)}) custom-call(f32[512,2048]{1,0:T(8,128)} %get-tuple-element.287.y_ref, f32[512,2048]{1,0:T(8,128)} %fusion.42.gate_ref, f32[512,2048]{1,0:T(8,128)} %fusion.dgn_ref, f32[512,128]{1,0:T(8,128)S(1)} %copy-done.45, ...), custom_call_target="tpu_custom_call" | custom-call | flops 10000000000 | bytes 17000000 | tf_op jit(solution)/shard_map/gate_backward/pallas_call | solution.py:542
  254.6 4.3 convolution_convert_fusion.3
  259.0 6.4 convolution_convert_fusion.2
  268.9 2.2 constant_dynamic-slice_fusion.27
  273.9 5.8 scan_inside.4
  283.7 5.8 scan_inside.5
  291.6 11.6 %collective-permute-done.17 = bf16[128,2048]{1,0:T(8,128)(2,1)} collective-permute-done((bf16[128,2048]{1,0:T(8,128)(2,1)}, bf16[128,2048]{1,0:T(8,128)(2,1)}, u32[]{:S(2)}, u32[]{:S(2)}) %collective-permute-start.17) | collective-permute-done | bytes 524320 | tf_op jit(solution)/shard_map/ppermute | solution.py:645
  312.0 27.7 %scan_backward.2 = (bf16[512,2048]{1,0:T(8,128)(2,1)}, f32[8,2048]{1,0:T(8,128)S(1)}, f32[8,2048]{1,0:T(8,128)S(1)}, f32[8,2048]{1,0:T(8,128)S(1)}, bf16[512,256...) custom-call(bf16[512,2432]{1,0:T(8,128)(2,1)} %copy-done.141, ...), custom_call_target="tpu_custom_call" | custom-call | flops 30000001024 | bytes 16000000 | tf_op jit(solution)/shard_map/scan_backward/pallas_call | solution.py:589
  343.4 2.6 collective-permute-done.18
  347.6 4.8 product_give.4
  361.5 3.7 fusion.43
  367.9 5.4 product_own.4
  376.9 5.7 multiply_reduce_fusion
  382.6 2.4 fusion.33
  385.0 8.0 %product_back.1.dgn_ref = f32[512,2048]{1,0:T(8,128)} custom-call(s32[8]{0:T(128)S(1)} %iota_xor_fusion.order_ref, bf16[512,1024]{1,0:T(8,128)(2,1)} %get-tuple-element.454.left_ref.right_ref, bf16[256,1024]{1,0:T(8,128)(2,1)S(1)} %get-tuple-element.256.refs_0_, bf16[256,1024]{1,0:T(8,128)(2,1)S(1)} %copy-done.4, ...), custom_call_target="tpu_custom_call" | custom-call | flops 2000000000 | bytes 10000000 | tf_op jit(solution)/shard_map/product_back/pallas_call | solution.py:724
  393.1 9.9 %gate_backward.3 = (bf16[512,2048]{1,0:T(8,128)(2,1)S(1)}, bf16[512,2048]{1,0:T(8,128)(2,1)}, f32[8,2048]{1,0:T(8,128)S(1)}, bf16[128,2048]{1,0:T(8,128)(2,1)S(1)}) custom-call(f32[512,2048]{1,0:T(8,128)} %get-tuple-element.319.y_ref, f32[512,2048]{1,0:T(8,128)} %fusion.41.gate_ref, f32[512,2048]{1,0:T(8,128)} %product_back.1.dgn_ref, ...), custom_call_target="tpu_custom_call" | custom-call | flops 10000000000 | bytes 17000000 | tf_op jit(solution)/shard_map/gate_backward/pallas_call | solution.py:542
  405.2 5.9 scan_inside.6
  411.9 2.7 product_give.5
  417.9 5.8 scan_inside.7
  425.0 3.9 product_give.6
  429.4 3.7 fusion.44
  436.2 5.4 collective-permute-start.29
  442.2 3.8 product_own.5
  446.1 31.1 %collective-permute-done.27 = bf16[128,2048]{1,0:T(8,128)(2,1)} collective-permute-done((bf16[128,2048]{1,0:T(8,128)(2,1)}, bf16[128,2048]{1,0:T(8,128)(2,1)}, u32[]{:S(2)}, u32[]{:S(2)}) %collective-permute-start.27) | collective-permute-done | bytes 524320 | tf_op jit(solution)/shard_map/ppermute | solution.py:645
  482.0 4.1 product_own.6
  489.3 4.0 collective-permute-done.30
  494.6 9.4 %collective-permute-done.31 = bf16[256,1024]{1,0:T(8,128)(2,1)S(1)} collective-permute-done((bf16[256,1024]{1,0:T(8,128)(2,1)S(1)}, bf16[256,1024]{1,0:T(8,128)(2,1)S(1)}, u32[]{:S(2)}, u32[]{:S(2)}) %collective-permute-start.31) | collective-permute-done | bytes 524320 | tf_op jit(solution)/shard_map/ppermute | solution.py:639
  505.7 27.7 %scan_backward.3 = (bf16[512,2048]{1,0:T(8,128)(2,1)}, f32[8,2048]{1,0:T(8,128)S(1)}, f32[8,2048]{1,0:T(8,128)S(1)}, f32[8,2048]{1,0:T(8,128)S(1)}, bf16[512,256...) custom-call(bf16[512,2432]{1,0:T(8,128)(2,1)} %copy-done.140, ...), custom_call_target="tpu_custom_call" | custom-call | flops 30000001024 | bytes 16000000 | tf_op jit(solution)/shard_map/scan_backward/pallas_call | solution.py:589
  536.9 2.7 collective-permute-start.38
  541.5 4.7 product_give.7
  551.4 5.2 multiply_reduce_fusion.1
  558.6 4.8 product_own.7
  563.4 2.3 collective-permute-done.40
  572.7 9.3 %collective-permute-done.43 = bf16[64,2048]{1,0:T(8,128)(2,1)} collective-permute-done((bf16[64,2048]{1,0:T(8,128)(2,1)S(1)}, bf16[64,2048]{1,0:T(8,128)(2,1)}, u32[]{:S(2)}, u32[]{:S(2)}) %collective-permute-start.43) | collective-permute-done | bytes 262176 | tf_op jit(solution)/shard_map/ppermute | solution.py:639
  583.0 12.8 %collective-permute-done.46 = bf16[128,2432]{1,0:T(8,128)(2,1)} collective-permute-done((bf16[128,2432]{1,0:T(8,128)(2,1)S(1)}, bf16[128,2432]{1,0:T(8,128)(2,1)}, u32[]{:S(2)}, u32[]{:S(2)}) %collective-permute-start.46) | collective-permute-done | bytes 622624 | tf_op jit(solution)/shard_map/ppermute | solution.py:639
  602.6 3.3 collective-permute-done.48
  607.9 5.1 collective-permute-done.53
  615.5 3.8 collective-permute-done.50
  619.9 15.2 %collective-permute-done.51 = f32[8,3672]{1,0:T(8,128)S(1)} collective-permute-done((f32[8,3672]{1,0:T(8,128)S(1)}, f32[8,3672]{1,0:T(8,128)S(1)}, u32[]{:S(2)}, u32[]{:S(2)}) %collective-permute-start.51) | collective-permute-done | bytes 117536 | tf_op jit(solution)/shard_map/ppermute | solution.py:639
  639.9 6.1 collective-permute-done.55
  646.1 2.8 in_weight_rows.1
  (611 shorter events, 143.4 us)
Async XLA Ops:
  7.2 47.0 %all-gather.9.cloned.1.call-start = ((), (), s32[]{:S(2)}) async-start(), calls=%async_computation.2 | async-start | bytes 5603328 | tf_op jit(solution)/shard_map/all_gather | solution.py:902
  9.9 100.0 %all-gather.11.cloned.1.call-start = ((), (), s32[]{:S(2)}) async-start(), calls=%async_computation.3 | async-start | bytes 4718592 | tf_op jit(solution)/shard_map/all_gather | solution.py:911
  10.8 141.9 %all-gather.13.cloned.1.call-start = ((), (), s32[]{:S(2)}) async-start(), calls=%async_computation.4 | async-start | bytes 5603328 | tf_op jit(solution)/shard_map/all_gather | solution.py:902
  11.9 188.6 %all-gather.15.cloned.1.call-start = ((), (), s32[]{:S(2)}) async-start(), calls=%async_computation.5 | async-start | bytes 4718592 | tf_op jit(solution)/shard_map/all_gather | solution.py:911
  12.8 217.6 %all-gather.17.cloned.1.call-start = ((), (), s32[]{:S(2)}) async-start(), calls=%async_computation.8 | async-start | bytes 4718592 | tf_op jit(solution)/shard_map/all_gather | solution.py:914
  13.8 390.5 %reduce-scatter.3.cloned.1.call-start = ((), (), s32[]{:S(2)}) async-start(), calls=%async_computation.6 | async-start | bytes 4718592 | tf_op jit(solution)/shard_map/reduce_scatter | solution.py:1025
  59.8 8.0 %collective-permute-start = (bf16[16,2304]{1,0:T(8,128)(2,1)S(1)}, bf16[16,2304]{1,0:T(8,128)(2,1)S(1)}, u32[]{:S(2)}, u32[]{:S(2)}) collective-permute-start(bf16[16,2304]{1,0:T(8,128)(2,1)S(1)} %slice.456), channel_id=1, source_target_pairs={{0,8},{8,16},{16,24},{1,9},{9,17},{17,25},{2,10},{10,18},{18,26},{... | collective-permute-start | bytes 221192 | tf_op jit(solution)/shard_map/ppermute | solution.py:925
  64.2 52.6 %collective-permute-start.4 = (bf16[256,1024]{1,0:T(8,128)(2,1)S(1)}, bf16[256,1024]{1,0:T(8,128)(2,1)S(1)}, u32[]{:S(2)}, u32[]{:S(2)}) collective-permute-start(bf16[256,1024]{1,0:T(8,128)(2,1)S(1)} %get-tuple-element.256.refs_0_), channel_id=1, source_target_pairs={{0,6},{1,7},{2,4},{3,5},{4,2},{5,3},{6,0},{7,1},{8,14},{9,15},{10,... | collective-permute-start | bytes 1572872 | tf_op jit(solution)/shard_map/ppermute | solution.py:639
  65.7 51.1 %collective-permute-start.3 = (bf16[256,1024]{1,0:T(8,128)(2,1)S(1)}, bf16[256,1024]{1,0:T(8,128)(2,1)S(1)}, u32[]{:S(2)}, u32[]{:S(2)}) collective-permute-start(bf16[256,1024]{1,0:T(8,128)(2,1)S(1)} %get-tuple-element.256.refs_0_), channel_id=1, source_target_pairs={{0,4},{1,5},{2,6},{3,7},{4,0},{5,1},{6,2},{7,3},{8,12},{9,13},{10,... | collective-permute-start | bytes 1572872 | tf_op jit(solution)/shard_map/ppermute | solution.py:639
  67.2 49.6 %collective-permute-start.2 = (bf16[256,1024]{1,0:T(8,128)(2,1)S(1)}, bf16[256,1024]{1,0:T(8,128)(2,1)S(1)}, u32[]{:S(2)}, u32[]{:S(2)}) collective-permute-start(bf16[256,1024]{1,0:T(8,128)(2,1)S(1)} %get-tuple-element.256.refs_0_), channel_id=1, source_target_pairs={{0,2},{1,3},{2,0},{3,1},{4,6},{5,7},{6,4},{7,5},{8,10},{9,11},{10,... | collective-permute-start | bytes 1572872 | tf_op jit(solution)/shard_map/ppermute | solution.py:639
  80.3 15.0 %collective-permute-start.1 = (bf16[128,2048]{1,0:T(8,128)(2,1)S(1)}, bf16[128,2048]{1,0:T(8,128)(2,1)S(1)}, u32[]{:S(2)}, u32[]{:S(2)}) collective-permute-start(bf16[128,2048]{1,0:T(8,128)(2,1)S(1)} %get-tuple-element.249), channel_id=1, source_target_pairs={{0,8},{1,9},{2,10},{3,11},{4,12},{5,13},{6,14},{7,15}} | collective-permute-start | bytes 1572872 | tf_op jit(solution)/shard_map/ppermute | solution.py:645
  97.1 20.6 %collective-permute-start.5 = (bf16[128,2048]{1,0:T(8,128)(2,1)}, bf16[128,2048]{1,0:T(8,128)(2,1)}, u32[]{:S(2)}, u32[]{:S(2)}) collective-permute-start(bf16[128,2048]{1,0:T(8,128)(2,1)} %fusion.9), channel_id=1, source_target_pairs={{8,16},{9,17},{10,18},{11,19},{12,20},{13,21},{14,22},{15,23}} | collective-permute-start | bytes 1572872 | tf_op jit(solution)/shard_map/ppermute | solution.py:645
  116.8 7.9 %collective-permute-start.6 = (bf16[256,1024]{1,0:T(8,128)(2,1)S(1)}, bf16[256,1024]{1,0:T(8,128)(2,1)S(1)}, u32[]{:S(2)}, u32[]{:S(2)}) collective-permute-start(bf16[256,1024]{1,0:T(8,128)(2,1)S(1)} %collective-permute-done.2.refs_2_), channel_id=1, source_target_pairs={{0,1},{1,0},{2,3},{3,2},{4,5},{5,4},{6,7},{7,6},{8,9},{9,8},{10,11... | collective-permute-start | bytes 1572872 | tf_op jit(solution)/shard_map/ppermute | solution.py:639
  117.2 7.6 %collective-permute-start.7 = (bf16[256,1024]{1,0:T(8,128)(2,1)S(1)}, bf16[256,1024]{1,0:T(8,128)(2,1)}, u32[]{:S(2)}, u32[]{:S(2)}) collective-permute-start(bf16[256,1024]{1,0:T(8,128)(2,1)S(1)} %collective-permute-done.3.refs_4_), channel_id=1, source_target_pairs={{0,1},{1,0},{2,3},{3,2},{4,5},{5,4},{6,7},{7,6},{8,9},{9,8},{10,11... | collective-permute-start | bytes 1572872 | tf_op jit(solution)/shard_map/ppermute | solution.py:639
  117.4 7.3 %collective-permute-start.8 = (bf16[256,1024]{1,0:T(8,128)(2,1)S(1)}, bf16[256,1024]{1,0:T(8,128)(2,1)}, u32[]{:S(2)}, u32[]{:S(2)}) collective-permute-start(bf16[256,1024]{1,0:T(8,128)(2,1)S(1)} %collective-permute-done.4.refs_6_), channel_id=1, source_target_pairs={{0,1},{1,0},{2,3},{3,2},{4,5},{5,4},{6,7},{7,6},{8,9},{9,8},{10,11... | collective-permute-start | bytes 1572872 | tf_op jit(solution)/shard_map/ppermute | solution.py:639
  119.9 4.8 collective-permute-start.9
  124.5 10.0 %collective-permute-start.10 = (bf16[256,1024]{1,0:T(8,128)(2,1)S(1)}, bf16[256,1024]{1,0:T(8,128)(2,1)S(1)}, u32[]{:S(2)}, u32[]{:S(2)}) collective-permute-start(bf16[256,1024]{1,0:T(8,128)(2,1)S(1)} %get-tuple-element.256.refs_0_), channel_id=1, source_target_pairs={{0,1},{1,0},{2,3},{3,2},{4,5},{5,4},{6,7},{7,6},{8,9},{9,8},{10,11... | collective-permute-start | bytes 1572872 | tf_op jit(solution)/shard_map/ppermute | solution.py:639
  158.4 5.4 collective-permute-start.11
  176.9 19.9 %collective-permute-start.12 = (bf16[128,2048]{1,0:T(8,128)(2,1)S(1)}, bf16[128,2048]{1,0:T(8,128)(2,1)S(1)}, u32[]{:S(2)}, u32[]{:S(2)}) collective-permute-start(bf16[128,2048]{1,0:T(8,128)(2,1)S(1)} %get-tuple-element.271), channel_id=1, source_target_pairs={{0,8},{1,9},{2,10},{3,11},{4,12},{5,13},{6,14},{7,15}} | collective-permute-start | bytes 1572872 | tf_op jit(solution)/shard_map/ppermute | solution.py:645
  198.6 9.1 %collective-permute-start.13 = (bf16[128,2048]{1,0:T(8,128)(2,1)}, bf16[128,2048]{1,0:T(8,128)(2,1)}, u32[]{:S(2)}, u32[]{:S(2)}) collective-permute-start(bf16[128,2048]{1,0:T(8,128)(2,1)} %fusion.11), channel_id=1, source_target_pairs={{8,16},{9,17},{10,18},{11,19},{12,20},{13,21},{14,22},{15,23}} | collective-permute-start | bytes 1572872 | tf_op jit(solution)/shard_map/ppermute | solution.py:645
  209.1 0.7 collective-permute-start.14
  253.0 12.3 %collective-permute-start.15 = (bf16[128,2048]{1,0:T(8,128)(2,1)S(1)}, bf16[128,2048]{1,0:T(8,128)(2,1)}, u32[]{:S(2)}, u32[]{:S(2)}) collective-permute-start(bf16[128,2048]{1,0:T(8,128)(2,1)S(1)} %get-tuple-element.288), channel_id=1, source_target_pairs={{24,16},{25,17},{26,18},{27,19},{28,20},{29,21},{30,22},{31,23}} | collective-permute-start | bytes 1572872 | tf_op jit(solution)/shard_map/ppermute | solution.py:645
  265.4 139.0 %reduce-scatter.5.cloned.1.call-start = ((), (), s32[]{:S(2)}) async-start(), calls=%async_computation.7 | async-start | bytes 4718592 | tf_op jit(solution)/shard_map/reduce_scatter | solution.py:1025
  273.1 6.6 %collective-permute-start.16 = (bf16[128,2048]{1,0:T(8,128)(2,1)S(1)}, bf16[128,2048]{1,0:T(8,128)(2,1)S(1)}, u32[]{:S(2)}, u32[]{:S(2)}) collective-permute-start(bf16[128,2048]{1,0:T(8,128)(2,1)S(1)} %fusion.13), channel_id=1, source_target_pairs={{16,8},{17,9},{18,10},{19,11},{20,12},{21,13},{22,14},{23,15}} | collective-permute-start | bytes 1572872 | tf_op jit(solution)/shard_map/ppermute | solution.py:645
  282.4 20.8 %collective-permute-start.17 = (bf16[128,2048]{1,0:T(8,128)(2,1)}, bf16[128,2048]{1,0:T(8,128)(2,1)}, u32[]{:S(2)}, u32[]{:S(2)}) collective-permute-start(bf16[128,2048]{1,0:T(8,128)(2,1)} %fusion.14), channel_id=1, source_target_pairs={{8,0},{9,1},{10,2},{11,3},{12,4},{13,5},{14,6},{15,7}} | collective-permute-start | bytes 1572872 | tf_op jit(solution)/shard_map/ppermute | solution.py:645
  291.6 241.8 %all-reduce.5.cloned.1.call-start = ((), (), s32[]{:S(2)}) async-start(), calls=%async_computation.9 | async-start | bytes 2097152 | tf_op jit(solution)/shard_map/psum | solution.py:980
  339.7 6.2 collective-permute-start.18
  352.4 15.6 %collective-permute-start.19 = (bf16[512,2432]{1,0:T(8,128)(2,1)}, bf16[512,2432]{1,0:T(8,128)(2,1)}, u32[]{:S(2)}, u32[]{:S(2)}) collective-permute-start(bf16[512,2432]{1,0:T(8,128)(2,1)} %product_give.4), channel_id=1, source_target_pairs={{0,1},{1,0},{2,3},{3,2},{4,5},{5,4},{6,7},{7,6},{8,9},{9,8},{10,11... | collective-permute-start | bytes 7471112 | tf_op jit(solution)/shard_map/ppermute | solution.py:639
  373.4 41.2 %collective-permute-start.21 = (bf16[128,2432]{1,0:T(8,128)(2,1)}, bf16[128,2432]{1,0:T(8,128)(2,1)}, u32[]{:S(2)}, u32[]{:S(2)}) collective-permute-start(bf16[128,2432]{1,0:T(8,128)(2,1)} %get-tuple-element.325), channel_id=1, source_target_pairs={{0,2},{1,3},{2,0},{3,1},{4,6},{5,7},{6,4},{7,5},{8,10},{9,11},{10,... | collective-permute-start | bytes 1867784 | tf_op jit(solution)/shard_map/ppermute | solution.py:639
  375.1 39.4 %collective-permute-start.22 = (bf16[128,2432]{1,0:T(8,128)(2,1)}, bf16[128,2432]{1,0:T(8,128)(2,1)}, u32[]{:S(2)}, u32[]{:S(2)}) collective-permute-start(bf16[128,2432]{1,0:T(8,128)(2,1)} %get-tuple-element.326), channel_id=1, source_target_pairs={{0,4},{1,5},{2,6},{3,7},{4,0},{5,1},{6,2},{7,3},{8,12},{9,13},{10,... | collective-permute-start | bytes 1867784 | tf_op jit(solution)/shard_map/ppermute | solution.py:639
  375.8 38.8 %collective-permute-start.23 = (bf16[128,2432]{1,0:T(8,128)(2,1)}, bf16[128,2432]{1,0:T(8,128)(2,1)}, u32[]{:S(2)}, u32[]{:S(2)}) collective-permute-start(bf16[128,2432]{1,0:T(8,128)(2,1)} %get-tuple-element.327), channel_id=1, source_target_pairs={{0,6},{1,7},{2,4},{3,5},{4,2},{5,3},{6,0},{7,1},{8,14},{9,15},{10,... | collective-permute-start | bytes 1867784 | tf_op jit(solution)/shard_map/ppermute | solution.py:639
  404.3 10.2 %collective-permute-start.20 = (bf16[128,2048]{1,0:T(8,128)(2,1)S(1)}, bf16[128,2048]{1,0:T(8,128)(2,1)S(1)}, u32[]{:S(2)}, u32[]{:S(2)}) collective-permute-start(bf16[128,2048]{1,0:T(8,128)(2,1)S(1)} %get-tuple-element.321), channel_id=1, source_target_pairs={{24,16},{25,17},{26,18},{27,19},{28,20},{29,21},{30,22},{31,23}} | collective-permute-start | bytes 1572872 | tf_op jit(solution)/shard_map/ppermute | solution.py:645
  414.5 14.5 %collective-permute-start.25 = (bf16[1024,1024]{1,0:T(8,128)(2,1)}, bf16[1024,1024]{1,0:T(8,128)(2,1)}, u32[]{:S(2)}, u32[]{:S(2)}) collective-permute-start(bf16[1024,1024]{1,0:T(8,128)(2,1)} %product_give.5), channel_id=1, source_target_pairs={{0,1},{1,0},{2,3},{3,2},{4,5},{5,4},{6,7},{7,6},{8,9},{9,8},{10,11... | collective-permute-start | bytes 6291464 | tf_op jit(solution)/shard_map/ppermute | solution.py:639
  416.5 12.6 %collective-permute-start.26 = (bf16[64,2432]{1,0:T(8,128)(2,1)S(1)}, bf16[64,2432]{1,0:T(8,128)(2,1)S(1)}, u32[]{:S(2)}, u32[]{:S(2)}) collective-permute-start(bf16[64,2432]{1,0:T(8,128)(2,1)S(1)} %get-tuple-element.486), channel_id=1, source_target_pairs={{0,8},{8,0},{16,24},{24,16},{1,9},{9,1},{17,25},{25,17},{2,10},{10... | collective-permute-start | bytes 933896 | tf_op jit(solution)/shard_map/ppermute | solution.py:639
  417.1 11.9 %collective-permute-start.24 = (bf16[128,2048]{1,0:T(8,128)(2,1)S(1)}, bf16[128,2048]{1,0:T(8,128)(2,1)S(1)}, u32[]{:S(2)}, u32[]{:S(2)}) collective-permute-start(bf16[128,2048]{1,0:T(8,128)(2,1)S(1)} %fusion.15), channel_id=1, source_target_pairs={{16,8},{17,9},{18,10},{19,11},{20,12},{21,13},{22,14},{23,15}} | collective-permute-start | bytes 1572872 | tf_op jit(solution)/shard_map/ppermute | solution.py:645
  429.1 52.9 %collective-permute-start.28 = (bf16[512,2048]{1,0:T(8,128)(2,1)}, bf16[512,2048]{1,0:T(8,128)(2,1)}, u32[]{:S(2)}, u32[]{:S(2)}) collective-permute-start(bf16[512,2048]{1,0:T(8,128)(2,1)} %product_give.6), channel_id=1, source_target_pairs={{0,1},{1,0},{2,3},{3,2},{4,5},{5,4},{6,7},{7,6},{8,9},{9,8},{10,11... | collective-permute-start | bytes 6291464 | tf_op jit(solution)/shard_map/ppermute | solution.py:639
  434.0 43.1 %collective-permute-start.27 = (bf16[128,2048]{1,0:T(8,128)(2,1)}, bf16[128,2048]{1,0:T(8,128)(2,1)}, u32[]{:S(2)}, u32[]{:S(2)}) collective-permute-start(bf16[128,2048]{1,0:T(8,128)(2,1)} %fusion.16), channel_id=1, source_target_pairs={{8,0},{9,1},{10,2},{11,3},{12,4},{13,5},{14,6},{15,7}} | collective-permute-start | bytes 1572872 | tf_op jit(solution)/shard_map/ppermute | solution.py:645
  436.2 45.8 %collective-permute-start.29 = (bf16[64,2432]{1,0:T(8,128)(2,1)}, bf16[64,2432]{1,0:T(8,128)(2,1)}, u32[]{:S(2)}, u32[]{:S(2)}) collective-permute-start(bf16[64,2432]{1,0:T(8,128)(2,1)} %add_convert_fusion.8), channel_id=1, source_target_pairs={{0,16},{8,24},{16,0},{24,8},{1,17},{9,25},{17,1},{25,9},{2,18},{10... | collective-permute-start | bytes 933896 | tf_op jit(solution)/shard_map/ppermute | solution.py:639
  478.4 14.9 %collective-permute-start.30 = (bf16[256,1024]{1,0:T(8,128)(2,1)S(1)}, bf16[256,1024]{1,0:T(8,128)(2,1)S(1)}, u32[]{:S(2)}, u32[]{:S(2)}) collective-permute-start(bf16[256,1024]{1,0:T(8,128)(2,1)S(1)} %get-tuple-element.368), channel_id=1, source_target_pairs={{0,2},{1,3},{2,0},{3,1},{4,6},{5,7},{6,4},{7,5},{8,10},{9,11},{10,... | collective-permute-start | bytes 1572872 | tf_op jit(solution)/shard_map/ppermute | solution.py:639
  479.8 24.2 %collective-permute-start.31 = (bf16[256,1024]{1,0:T(8,128)(2,1)S(1)}, bf16[256,1024]{1,0:T(8,128)(2,1)S(1)}, u32[]{:S(2)}, u32[]{:S(2)}) collective-permute-start(bf16[256,1024]{1,0:T(8,128)(2,1)S(1)} %get-tuple-element.369), channel_id=1, source_target_pairs={{0,4},{1,5},{2,6},{3,7},{4,0},{5,1},{6,2},{7,3},{8,12},{9,13},{10,... | collective-permute-start | bytes 1572872 | tf_op jit(solution)/shard_map/ppermute | solution.py:639
  479.9 53.5 %collective-permute-start.32 = (bf16[256,1024]{1,0:T(8,128)(2,1)}, bf16[256,1024]{1,0:T(8,128)(2,1)}, u32[]{:S(2)}, u32[]{:S(2)}) collective-permute-start(bf16[256,1024]{1,0:T(8,128)(2,1)} %get-tuple-element.370), channel_id=1, source_target_pairs={{0,6},{1,7},{2,4},{3,5},{4,2},{5,3},{6,0},{7,1},{8,14},{9,15},{10,... | collective-permute-start | bytes 1572872 | tf_op jit(solution)/shard_map/ppermute | solution.py:639
  488.0 45.5 %collective-permute-start.36 = (bf16[64,2432]{1,0:T(8,128)(2,1)}, bf16[64,2432]{1,0:T(8,128)(2,1)}, u32[]{:S(2)}, u32[]{:S(2)}) collective-permute-start(bf16[64,2432]{1,0:T(8,128)(2,1)} %add_convert_fusion.7), channel_id=1, source_target_pairs={{0,8},{8,0},{16,24},{24,16},{1,9},{9,1},{17,25},{25,17},{2,10},{10... | collective-permute-start | bytes 933896 | tf_op jit(solution)/shard_map/ppermute | solution.py:639
  488.0 45.5 %collective-permute-start.33 = (bf16[128,2048]{1,0:T(8,128)(2,1)}, bf16[128,2048]{1,0:T(8,128)(2,1)}, u32[]{:S(2)}, u32[]{:S(2)}) collective-permute-start(bf16[128,2048]{1,0:T(8,128)(2,1)} %get-tuple-element.371), channel_id=1, source_target_pairs={{0,2},{1,3},{2,0},{3,1},{4,6},{5,7},{6,4},{7,5},{8,10},{9,11},{10,... | collective-permute-start | bytes 1572872 | tf_op jit(solution)/shard_map/ppermute | solution.py:639
  493.3 40.1 %collective-permute-start.34 = (bf16[128,2048]{1,0:T(8,128)(2,1)}, bf16[128,2048]{1,0:T(8,128)(2,1)}, u32[]{:S(2)}, u32[]{:S(2)}) collective-permute-start(bf16[128,2048]{1,0:T(8,128)(2,1)} %get-tuple-element.372), channel_id=1, source_target_pairs={{0,4},{1,5},{2,6},{3,7},{4,0},{5,1},{6,2},{7,3},{8,12},{9,13},{10,... | collective-permute-start | bytes 1572872 | tf_op jit(solution)/shard_map/ppermute | solution.py:639
  504.0 29.4 %collective-permute-start.35 = (bf16[128,2048]{1,0:T(8,128)(2,1)}, bf16[128,2048]{1,0:T(8,128)(2,1)}, u32[]{:S(2)}, u32[]{:S(2)}) collective-permute-start(bf16[128,2048]{1,0:T(8,128)(2,1)} %get-tuple-element.373), channel_id=1, source_target_pairs={{0,6},{1,7},{2,4},{3,5},{4,2},{5,3},{6,0},{7,1},{8,14},{9,15},{10,... | collective-permute-start | bytes 1572872 | tf_op jit(solution)/shard_map/ppermute | solution.py:639
  533.5 6.4 collective-permute-start.37
  536.9 9.3 %collective-permute-start.38 = (bf16[128,1024]{1,0:T(8,128)(2,1)S(1)}, bf16[128,1024]{1,0:T(8,128)(2,1)S(1)}, u32[]{:S(2)}, u32[]{:S(2)}) collective-permute-start(bf16[128,1024]{1,0:T(8,128)(2,1)S(1)} %get-tuple-element.490), channel_id=1, source_target_pairs={{0,8},{8,0},{16,24},{24,16},{1,9},{9,1},{17,25},{25,17},{2,10},{10... | collective-permute-start | bytes 786440 | tf_op jit(solution)/shard_map/ppermute | solution.py:639
  546.3 5.1 collective-permute-start.39
  548.6 14.8 %collective-permute-start.41 = (bf16[64,2048]{1,0:T(8,128)(2,1)S(1)}, bf16[64,2048]{1,0:T(8,128)(2,1)S(1)}, u32[]{:S(2)}, u32[]{:S(2)}) collective-permute-start(bf16[64,2048]{1,0:T(8,128)(2,1)S(1)} %get-tuple-element.488), channel_id=1, source_target_pairs={{0,8},{8,0},{16,24},{24,16},{1,9},{9,1},{17,25},{25,17},{2,10},{10... | collective-permute-start | bytes 786440 | tf_op jit(solution)/shard_map/ppermute | solution.py:639
  550.6 15.1 %collective-permute-start.40 = (bf16[128,1024]{1,0:T(8,128)(2,1)S(1)}, bf16[128,1024]{1,0:T(8,128)(2,1)S(1)}, u32[]{:S(2)}, u32[]{:S(2)}) collective-permute-start(bf16[128,1024]{1,0:T(8,128)(2,1)S(1)} %add_convert_fusion.12), channel_id=1, source_target_pairs={{0,16},{8,24},{16,0},{24,8},{1,17},{9,25},{17,1},{25,9},{2,18},{10... | collective-permute-start | bytes 786440 | tf_op jit(solution)/shard_map/ppermute | solution.py:639
  565.7 17.3 %collective-permute-start.44 = (bf16[128,2432]{1,0:T(8,128)(2,1)}, bf16[128,2432]{1,0:T(8,128)(2,1)}, u32[]{:S(2)}, u32[]{:S(2)}) collective-permute-start(bf16[128,2432]{1,0:T(8,128)(2,1)} %get-tuple-element.417), channel_id=1, source_target_pairs={{0,2},{1,3},{2,0},{3,1},{4,6},{5,7},{6,4},{7,5},{8,10},{9,11},{10,... | collective-permute-start | bytes 1867784 | tf_op jit(solution)/shard_map/ppermute | solution.py:639
  566.6 16.4 %collective-permute-start.45 = (bf16[128,2432]{1,0:T(8,128)(2,1)S(1)}, bf16[128,2432]{1,0:T(8,128)(2,1)}, u32[]{:S(2)}, u32[]{:S(2)}) collective-permute-start(bf16[128,2432]{1,0:T(8,128)(2,1)S(1)} %get-tuple-element.418), channel_id=1, source_target_pairs={{0,4},{1,5},{2,6},{3,7},{4,0},{5,1},{6,2},{7,3},{8,12},{9,13},{10,... | collective-permute-start | bytes 1867784 | tf_op jit(solution)/shard_map/ppermute | solution.py:639
  567.7 28.1 %collective-permute-start.46 = (bf16[128,2432]{1,0:T(8,128)(2,1)S(1)}, bf16[128,2432]{1,0:T(8,128)(2,1)}, u32[]{:S(2)}, u32[]{:S(2)}) collective-permute-start(bf16[128,2432]{1,0:T(8,128)(2,1)S(1)} %get-tuple-element.419), channel_id=1, source_target_pairs={{0,6},{1,7},{2,4},{3,5},{4,2},{5,3},{6,0},{7,1},{8,14},{9,15},{10,... | collective-permute-start | bytes 1867784 | tf_op jit(solution)/shard_map/ppermute | solution.py:639
  569.3 12.7 %collective-permute-start.43 = (bf16[64,2048]{1,0:T(8,128)(2,1)S(1)}, bf16[64,2048]{1,0:T(8,128)(2,1)}, u32[]{:S(2)}, u32[]{:S(2)}) collective-permute-start(bf16[64,2048]{1,0:T(8,128)(2,1)S(1)} %add_convert_fusion.10), channel_id=1, source_target_pairs={{0,16},{8,24},{16,0},{24,8},{1,17},{9,25},{17,1},{25,9},{2,18},{10... | collective-permute-start | bytes 786440 | tf_op jit(solution)/shard_map/ppermute | solution.py:639
  569.4 12.8 %collective-permute-start.42 = (bf16[128,1024]{1,0:T(8,128)(2,1)S(1)}, bf16[128,1024]{1,0:T(8,128)(2,1)}, u32[]{:S(2)}, u32[]{:S(2)}) collective-permute-start(bf16[128,1024]{1,0:T(8,128)(2,1)S(1)} %add_convert_fusion.11), channel_id=1, source_target_pairs={{0,8},{8,0},{16,24},{24,16},{1,9},{9,1},{17,25},{25,17},{2,10},{10... | collective-permute-start | bytes 786440 | tf_op jit(solution)/shard_map/ppermute | solution.py:639
  597.6 3.3 collective-permute-start.47
  597.7 15.4 %collective-permute-start.52 = (bf16[64,2432]{1,0:T(8,128)(2,1)S(1)}, bf16[64,2432]{1,0:T(8,128)(2,1)S(1)}, u32[]{:S(2)}, u32[]{:S(2)}) collective-permute-start(bf16[64,2432]{1,0:T(8,128)(2,1)S(1)} %get-tuple-element.484), channel_id=1, source_target_pairs={{0,8},{8,0},{16,24},{24,16},{1,9},{9,1},{17,25},{25,17},{2,10},{10... | collective-permute-start | bytes 933896 | tf_op jit(solution)/shard_map/ppermute | solution.py:639
  598.8 14.3 %collective-permute-start.53 = (bf16[64,2048]{1,0:T(8,128)(2,1)S(1)}, bf16[64,2048]{1,0:T(8,128)(2,1)S(1)}, u32[]{:S(2)}, u32[]{:S(2)}) collective-permute-start(bf16[64,2048]{1,0:T(8,128)(2,1)S(1)} %add_convert_fusion.9), channel_id=1, source_target_pairs={{0,8},{8,0},{16,24},{24,16},{1,9},{9,1},{17,25},{25,17},{2,10},{10... | collective-permute-start | bytes 786440 | tf_op jit(solution)/shard_map/ppermute | solution.py:639
  600.9 5.1 collective-permute-start.48
  606.0 7.1 %collective-permute-start.49 = (f32[8,3672]{1,0:T(8,128)S(1)}, f32[8,3672]{1,0:T(8,128)S(1)}, u32[]{:S(2)}, u32[]{:S(2)}) collective-permute-start(f32[8,3672]{1,0:T(8,128)S(1)} %add.368), channel_id=1, source_target_pairs={{0,4},{1,5},{2,6},{3,7},{4,0},{5,1},{6,2},{7,3},{8,12},{9,13},{10,... | collective-permute-start | bytes 352520 | tf_op jit(solution)/shard_map/ppermute | solution.py:639
  613.1 6.2 collective-permute-start.50
  613.5 24.2 %collective-permute-start.54 = (bf16[64,2432]{1,0:T(8,128)(2,1)S(1)}, bf16[64,2432]{1,0:T(8,128)(2,1)S(1)}, u32[]{:S(2)}, u32[]{:S(2)}) collective-permute-start(bf16[64,2432]{1,0:T(8,128)(2,1)S(1)} %add_convert_fusion.6), channel_id=1, source_target_pairs={{0,16},{8,24},{16,0},{24,8},{1,17},{9,25},{17,1},{25,9},{2,18},{10... | collective-permute-start | bytes 933896 | tf_op jit(solution)/shard_map/ppermute | solution.py:639
  619.3 15.7 %collective-permute-start.51 = (f32[8,3672]{1,0:T(8,128)S(1)}, f32[8,3672]{1,0:T(8,128)S(1)}, u32[]{:S(2)}, u32[]{:S(2)}) collective-permute-start(f32[8,3672]{1,0:T(8,128)S(1)} %add.370), channel_id=1, source_target_pairs={{0,16},{8,24},{16,0},{24,8},{1,17},{9,25},{17,1},{25,9},{2,18},{10... | collective-permute-start | bytes 352520 | tf_op jit(solution)/shard_map/ppermute | solution.py:639
  637.8 8.2 %collective-permute-start.55 = (bf16[64,2432]{1,0:T(8,128)(2,1)S(1)}, bf16[64,2432]{1,0:T(8,128)(2,1)S(1)}, u32[]{:S(2)}, u32[]{:S(2)}) collective-permute-start(bf16[64,2432]{1,0:T(8,128)(2,1)S(1)} %add_convert_fusion.5), channel_id=1, source_target_pairs={{0,8},{8,0},{16,24},{24,16},{1,9},{9,1},{17,25},{25,17},{2,10},{10... | collective-permute-start | bytes 933896 | tf_op jit(solution)/shard_map/ppermute | solution.py:639
  (153 other events, 1547.8 us)
Sparse Core Ops, SparseCore 0:
  10.5 43.6 all-gather.8
  56.6 53.2 all-gather.10
  111.7 40.8 all-gather.12
  154.4 37.4 all-gather.14
  193.6 36.7 all-gather.16
  265.5 55.9 reduce-scatter.2
  325.2 51.3 reduce-scatter.4
  442.3 67.1 all-reduce.4

commit v4 on v3

--- a/solution.py
+++ b/solution.py
@@ -1030,12 +1030,9 @@
             low, high,
         )
         if layer == 0:
-            back, out_sent, gate_sent, above, big[layer + 1] = tie(
-                back, out_sent, gate_sent, above, big[layer + 1]
-            )
+            back, out_sent, above, big[layer + 1] = tie(back, out_sent, above, big[layer + 1])
             big[layer + 1].append(seq_join(*above))
             out_seq = seq_first(gather_sum(out_mine, out_sent))
-            gate_sum = gather_sum(gate_mine, gate_sent)
         dv, tail, head, stats, bdv, btail, bhead, bstats, ddt, dtstats = back
         heads_in = lax.ppermute(jnp.concatenate([head, bhead], axis=1), "seq", down)
         tail = jnp.concatenate([tail, btail], axis=1)
@@ -1047,15 +1044,13 @@
         d_rest = lax.dynamic_update_slice(
             d_rest, jnp.concatenate(fix, axis=0).astype(BF16), (d_rest.shape[0] - 8, 0)
         )
-        give = product_give(normed_give, d_rest)
-        if layer == 0:
-            give, out_seq = tie(give, out_seq)
-            out_seq = seq_across(*out_seq)
-            gate_seq = seq_first(gate_sum)
-        got = swap(give, "fsdp", 1)
+        got = swap(product_give(normed_give, d_rest), "fsdp", 1)
         d_normed = dot_nt(dgate, w_gate)
         got, d_normed = tie(got, d_normed)
-        if layer > 0:
+        if layer == 0:
+            out_seq, d_rest = tie(out_seq, d_rest)
+            out_seq = seq_across(*out_seq)
+        else:
             parts = product_own(normed_own, d_rest, got)
             parts, d_rest = tie(parts, d_rest)
             rest_mine, rest_sent = send_chips(parts)
@@ -1067,14 +1062,15 @@
         if layer == 0:
             grad, gain_in_grad, got = tie(grad, gain_in_grad, got)
             parts = product_own(normed_own, d_rest, got)
-            parts, out_seq, gate_seq = tie(parts, out_seq, gate_seq)
+            parts, gate_sent = tie(parts, gate_sent)
             rest_mine, rest_sent = send_chips(parts)
+            gate_seq = seq_first(gather_sum(gate_mine, gate_sent))
+            out_seq, gate_seq = tie(out_seq, gate_seq)
             out_seq = seq_back(*out_seq)
             gate_seq = seq_across(*gate_seq)
             out_seq, gate_seq, rest_sent = tie(out_seq, gate_seq, rest_sent)
+            rest_seq = seq_first(gather_sum(rest_mine, rest_sent))
             gate_seq = seq_back(*gate_seq)
-            rest_seq = seq_first(gather_sum(rest_mine, rest_sent))
-            rest_seq, gate_seq = tie(rest_seq, gate_seq)
             rest_seq = seq_back(*seq_across(*rest_seq))
             big[layer] = [seq_join(*out_seq), seq_join(*gate_seq), seq_join(*rest_seq)]
         waiting = layer

time: 667 us -> 663 us (level)
  waiting for transfers between devices: 173 us -> 161 us
    ppermute x40, waiting for transfers between devices: 72.4 us -> 58 us  [swap(): lax.ppermute(a, axis, [(k, k ^ bit) for k in range(lax.axis_size(axis))])]
    unnamed x311 -> x303, local copies, waits for them, and re-layouts: 25.5 us -> 26.6 us
  transfers between devices with their start and end apart: 64 -> 64, of which waited for: 21 -> 19; matrix products, arithmetic and copies ran while one was open for 19% -> 20% of each run, Pallas kernels for 31% -> 30%
where the time goes in v4:
time: 663 us; the launch traced here: 653 us
  Pallas kernels  216 us (33%)
  waiting for transfers between devices  161 us (24%)
  starting transfers between devices  75.9 us (11%)
  matrix products  65.9 us (10%)
  local copies, waits for them, and re-layouts  53.7 us (8%)
  other arithmetic  53.3 us (8%)
  between operations  17 us (3%)
  blocking collectives  10.7 us (2%)
    ppermute x40, waiting for transfers between devices, swap(): lax.ppermute(a, axis, [(k, k ^ bit) for k in range(lax.axis_size(axis))])  58 us
    pallas_call x2, Pallas kernels, scan_backward(): pl.pallas_call(back_kernel, name='scan_backward', grid=(STEPS,), in_specs...  55.4 us
    ppermute x40, starting transfers between devices, swap(): lax.ppermute(a, axis, [(k, k ^ bit) for k in range(lax.axis_size(axis))])  41.7 us
    ppermute x12, waiting for transfers between devices, hop_to(): got = lax.ppermute(message, 'seq', [pair])  40.3 us
    all_gather x2, waiting for transfers between devices, on_device(): rest = lax.all_gather(rest, 'fsdp', axis=0, tiled=True)  32.5 us
    dot_general x5, matrix products, dot(): return jnp.dot(a, b, preferred_element_type=F32)  32.3 us
    unnamed x303, local copies, waits for them, and re-layouts  26.6 us
    pallas_call x2, Pallas kernels, local_state(): pl.pallas_call(state_kernel, name='local_state', grid=(STEPS,), in_specs=...  24.9 us
  transfers between devices with their start and end apart: 64, of which 19 were waited for; matrix products, arithmetic and copies ran while one was open for 20% of the time, Pallas kernels for 30%

profile of v4, /device:TPU:0, one launch (start us, length us, event | category | flops | bytes accessed | tf_op | source)
XLA Modules:
  0.0 653.2 jit_solution(9718300731593993579)
XLA Ops:
  14.1 10.7 %all-gather.2 = bf16[8,2,1836]{2,1,0:T(2,128)(2,1)S(1)} all-gather(bf16[1,2,1836]{2,1,0:T(2,128)(2,1)S(1)} %bitcast.148), channel_id=2, replica_groups=mesh['seq'=4,'fsdp'=8] {'fsdp'}, dimensions={0}, use_global_device_ids=true | all-gather | bytes 66096 | tf_op jit(solution)/shard_map/all_gather | solution.py:885
  27.1 27.1 %all-gather.9.cloned.1.call-done = bf16[1024,2432]{0,1:T(8,128)(2,1)} async-done(((bf16[128,2432]{0,1:T(8,128)(2,1)}), bf16[1024,2432]{0,1:T(8,128)(2,1)}) %all-gather.9.cloned.1.call-update) | async-done | bytes 4980752 | tf_op jit(solution)/shard_map/all_gather | solution.py:902
  54.2 5.5 convolution_convert_fusion.1.v_ref.bc_ref.dt_ref
  59.8 3.4 collective-permute-start
  67.2 12.4 %local_state.2 = (bf16[128,2048]{1,0:T(8,128)(2,1)S(1)}, f32[8,2048]{1,0:T(8,128)S(1)}, f32[512,2048]{1,0:T(8,128)}, f32[512,128]{1,0:T(8,128)S(1)}, bf16[512,38...) custom-call(bf16[512,2432]{1,0:T(8,128)(2,1)} %copy-done.137, ...), custom_call_target="tpu_custom_call" | custom-call | flops 4000000000 | bytes 8000000 | tf_op jit(solution)/shard_map/local_state/pallas_call | solution.py:474
  79.7 3.4 collective-permute-start.1
  83.2 11.5 %local_scan.2.y_ref = f32[512,2048]{1,0:T(8,128)} custom-call(f32[512,2048]{1,0:T(8,128)} %get-tuple-element.246.x_ref, f32[1,2048]{1,0:T(1,128)S(1)} %broadcast_in_dim_reshape.6.skip_ref, bf16[512,384]{1,0:T(8,128)(2,1)S(1)} %get-tuple-element.247.p3_ref, bf16[512,128]{1,0:T(8,128)(2,1)S(1)} %get-tuple-element.248.b_ref, ...), custom_call_target="tpu_custom_call" | custom-call | flops 15000000512 | bytes 8000000 | tf_op jit(solution)/shard_map/local_scan/pallas_call | solution.py:504
  98.0 11.9 %all-gather.11.cloned.1.call-done = bf16[1024,2048]{0,1:T(8,128)(2,1)} async-done(((bf16[128,2048]{0,1:T(8,128)(2,1)}), bf16[1024,2048]{0,1:T(8,128)(2,1)}) %all-gather.11.cloned.1.call-update) | async-done | bytes 4194320 | tf_op jit(solution)/shard_map/all_gather | solution.py:911
  109.9 6.9 %fusion.41.gate_ref = f32[512,2048]{1,0:T(8,128)} fusion(bf16[512,1024]{1,0:T(8,128)(2,1)} %copy-done.92, bf16[1024,2048]{0,1:T(8,128)(2,1)} %all-gather.11.cloned.1.call-done), kind=kOutput, calls=%fused_computation.181 | convolution fusion | flops 2147483648 | bytes 9437184 | tf_op jit(solution)/shard_map/dot_general | solution.py:30
  121.6 2.9 bitcast_convert_fusion.base_ref
  126.0 7.1 %gate_forward.2 = (f32[512,2048]{1,0:T(8,128)}, bf16[512,2048]{1,0:T(8,128)(2,1)S(1)}) custom-call(f32[512,2048]{1,0:T(8,128)} %local_scan.2.y_ref, f32[512,2048]{1,0:T(8,128)} %fusion.41.gate_ref, f32[512,128]{1,0:T(8,128)S(1)} %get-tuple-element.261.p_ref, bf16[512,128]{1,0:T(8,128)(2,1)S(1)} %copy-done.51, bf16[128,2048]{1,0:T(8,128)(2,1)S(1)} %add.301.s_ref, ...), custom_call_target="tpu_custom_call" | custom-call | flops 5000000000 | bytes 15000000 | tf_op jit(solution)/shard_map/gate_forward/pallas_call | solution.py:526
  134.5 9.3 %add_product.1 = f32[512,1024]{1,0:T(8,128)} custom-call(s32[8]{0:T(128)S(1)} %iota_xor_fusion.order_ref, bf16[512,2048]{1,0:T(8,128)(2,1)} %copy-done, f32[512,1024]{1,0:T(8,128)} %bitcast_convert_fusion.base_ref, bf16[256,1024]{1,0:T(8,128)(2,1)S(1)} %get-tuple-element.252.refs_0_, bf16[256,1024]{1,0:T(8,128)(2,1)S(1)} %collective-permute-done.10.refs_1_, ...), custom_call_target="tpu_custom_call" | custom-call | flops 2000000000 | bytes 10000000 | tf_op jit(solution)/shard_map/add_product/pallas_call | solution.py:701
  147.3 5.4 all-gather.13.cloned.1.call-done
  152.7 5.6 convolution_convert_fusion.v_ref.bc_ref.dt_ref
  158.4 3.4 collective-permute-start.11
  163.8 12.4 %local_state.3 = (bf16[128,2048]{1,0:T(8,128)(2,1)S(1)}, f32[8,2048]{1,0:T(8,128)S(1)}, f32[512,2048]{1,0:T(8,128)}, f32[512,128]{1,0:T(8,128)S(1)}, bf16[512,38...) custom-call(bf16[512,2432]{1,0:T(8,128)(2,1)} %copy-done.138, ...), custom_call_target="tpu_custom_call" | custom-call | flops 4000000000 | bytes 8000000 | tf_op jit(solution)/shard_map/local_state/pallas_call | solution.py:474
  177.0 8.3 %collective-permute-start.12 = (bf16[128,2048]{1,0:T(8,128)(2,1)S(1)}, bf16[128,2048]{1,0:T(8,128)(2,1)S(1)}, u32[]{:S(2)}, u32[]{:S(2)}) collective-permute-start(bf16[128,2048]{1,0:T(8,128)(2,1)S(1)} %get-tuple-element.267), channel_id=1, source_target_pairs={{0,8},{1,9},{2,10},{3,11},{4,12},{5,13},{6,14},{7,15}} | collective-permute-start | bytes 1572872 | tf_op jit(solution)/shard_map/ppermute | solution.py:645
  185.3 11.5 %local_scan.3.y_ref = f32[512,2048]{1,0:T(8,128)} custom-call(f32[512,2048]{1,0:T(8,128)} %get-tuple-element.268.x_ref, f32[1,2048]{1,0:T(1,128)S(1)} %broadcast_in_dim_reshape.7.skip_ref, bf16[512,384]{1,0:T(8,128)(2,1)S(1)} %get-tuple-element.269.p3_ref, bf16[512,128]{1,0:T(8,128)(2,1)S(1)} %get-tuple-element.270.b_ref, ...), custom_call_target="tpu_custom_call" | custom-call | flops 15000000512 | bytes 8000000 | tf_op jit(solution)/shard_map/local_scan/pallas_call | solution.py:504
  200.3 7.3 %fusion.42.gate_ref = f32[512,2048]{1,0:T(8,128)} fusion(bf16[512,1024]{1,0:T(8,128)(2,1)} %multiply_convert_fusion, bf16[1024,2048]{0,1:T(8,128)(2,1)} %all-gather.15.cloned.1.call-done), kind=kOutput, calls=%fused_computation.182 | convolution fusion | flops 2147483648 | bytes 9437184 | tf_op jit(solution)/shard_map/dot_general | solution.py:30
  209.9 7.1 %gate_forward.3 = (f32[512,2048]{1,0:T(8,128)}, bf16[512,2048]{1,0:T(8,128)(2,1)S(1)}) custom-call(f32[512,2048]{1,0:T(8,128)} %local_scan.3.y_ref, f32[512,2048]{1,0:T(8,128)} %fusion.42.gate_ref, f32[512,128]{1,0:T(8,128)S(1)} %copy-done.45, bf16[512,128]{1,0:T(8,128)(2,1)S(1)} %copy-done.62, bf16[128,2048]{1,0:T(8,128)(2,1)S(1)} %add.306.s_ref, ...), custom_call_target="tpu_custom_call" | custom-call | flops 5000000000 | bytes 15000000 | tf_op jit(solution)/shard_map/gate_forward/pallas_call | solution.py:526
  219.1 11.3 %all-gather.17.cloned.1.call-done = bf16[1,2048,1024]{2,1,0:T(8,128)(2,1)} async-done(((bf16[1,256,1024]{2,1,0:T(8,128)(2,1)}), bf16[1,2048,1024]{2,1,0:T(8,128)(2,1)}) %all-gather.17.cloned.1.call-update) | async-done | bytes 4194320 | tf_op jit(solution)/shard_map/all_gather | solution.py:914
  230.4 6.9 %fusion.6 = bf16[1,512,1024]{2,1,0:T(8,128)(2,1)} fusion(f32[512,1024]{1,0:T(8,128)} %add_product.1, bf16[512,2048]{1,0:T(8,128)(2,1)} %copy-done.31, bf16[1,2048,1024]{2,1,0:T(8,128)(2,1)} %all-gather.17.cloned.1.call-done), kind=kOutput, calls=%fused_computation.21 | convolution fusion | flops 2148532224 | bytes 9437184 | tf_op jit(solution)/shard_map/dot_general | solution.py:30
  237.4 4.3 fusion.dgn_ref
  241.7 10.0 %gate_backward.2 = (bf16[512,2048]{1,0:T(8,128)(2,1)S(1)}, bf16[512,2048]{1,0:T(8,128)(2,1)}, f32[8,2048]{1,0:T(8,128)S(1)}, bf16[128,2048]{1,0:T(8,128)(2,1)S(1)}) custom-call(f32[512,2048]{1,0:T(8,128)} %get-tuple-element.283.y_ref, f32[512,2048]{1,0:T(8,128)} %fusion.42.gate_ref, f32[512,2048]{1,0:T(8,128)} %fusion.dgn_ref, f32[512,128]{1,0:T(8,128)S(1)} %copy-done.46, ...), custom_call_target="tpu_custom_call" | custom-call | flops 10000000000 | bytes 17000000 | tf_op jit(solution)/shard_map/gate_backward/pallas_call | solution.py:542
  254.9 4.4 convolution_convert_fusion.3
  259.3 6.4 convolution_convert_fusion.2
  270.6 2.2 constant_dynamic-slice_fusion.26
  275.6 5.8 scan_inside.4
  285.4 5.8 scan_inside.5
  293.3 11.8 %collective-permute-done.17 = bf16[128,2048]{1,0:T(8,128)(2,1)} collective-permute-done((bf16[128,2048]{1,0:T(8,128)(2,1)}, bf16[128,2048]{1,0:T(8,128)(2,1)}, u32[]{:S(2)}, u32[]{:S(2)}) %collective-permute-start.17) | collective-permute-done | bytes 524320 | tf_op jit(solution)/shard_map/ppermute | solution.py:645
  314.0 27.6 %scan_backward.2 = (bf16[512,2048]{1,0:T(8,128)(2,1)}, f32[8,2048]{1,0:T(8,128)S(1)}, f32[8,2048]{1,0:T(8,128)S(1)}, f32[8,2048]{1,0:T(8,128)S(1)}, bf16[512,256...) custom-call(bf16[512,2432]{1,0:T(8,128)(2,1)} %copy-done.138, ...), custom_call_target="tpu_custom_call" | custom-call | flops 30000001024 | bytes 16000000 | tf_op jit(solution)/shard_map/scan_backward/pallas_call | solution.py:589
  345.1 2.8 collective-permute-done.18
  349.5 4.7 product_give.4
  363.3 2.4 fusion.43
  366.4 5.7 product_own.4
  375.6 5.1 multiply_reduce_fusion
  380.8 2.4 fusion.33
  383.2 8.1 %product_back.1.dgn_ref = f32[512,2048]{1,0:T(8,128)} custom-call(s32[8]{0:T(128)S(1)} %iota_xor_fusion.order_ref, bf16[512,1024]{1,0:T(8,128)(2,1)} %get-tuple-element.446.left_ref.right_ref, bf16[256,1024]{1,0:T(8,128)(2,1)S(1)} %get-tuple-element.252.refs_0_, bf16[256,1024]{1,0:T(8,128)(2,1)S(1)} %copy-done.4, ...), custom_call_target="tpu_custom_call" | custom-call | flops 2000000000 | bytes 10000000 | tf_op jit(solution)/shard_map/product_back/pallas_call | solution.py:724
  391.3 9.9 %gate_backward.3 = (bf16[512,2048]{1,0:T(8,128)(2,1)S(1)}, bf16[512,2048]{1,0:T(8,128)(2,1)}, f32[8,2048]{1,0:T(8,128)S(1)}, bf16[128,2048]{1,0:T(8,128)(2,1)S(1)}) custom-call(f32[512,2048]{1,0:T(8,128)} %get-tuple-element.315.y_ref, f32[512,2048]{1,0:T(8,128)} %fusion.41.gate_ref, f32[512,2048]{1,0:T(8,128)} %product_back.1.dgn_ref, ...), custom_call_target="tpu_custom_call" | custom-call | flops 10000000000 | bytes 17000000 | tf_op jit(solution)/shard_map/gate_backward/pallas_call | solution.py:542
  403.6 5.9 scan_inside.6
  410.9 2.6 product_give.5
  417.2 5.8 scan_inside.7
  424.3 3.9 product_give.6
  435.4 5.4 collective-permute-start.29
  441.5 4.0 product_own.5
  445.5 28.5 %collective-permute-done.27 = bf16[128,2048]{1,0:T(8,128)(2,1)} collective-permute-done((bf16[128,2048]{1,0:T(8,128)(2,1)}, bf16[128,2048]{1,0:T(8,128)(2,1)}, u32[]{:S(2)}, u32[]{:S(2)}) %collective-permute-start.27) | collective-permute-done | bytes 524320 | tf_op jit(solution)/shard_map/ppermute | solution.py:645
  476.7 2.1 collective-permute-start.32
  478.9 4.0 product_own.6
  484.9 27.8 %scan_backward.3 = (bf16[512,2048]{1,0:T(8,128)(2,1)}, f32[8,2048]{1,0:T(8,128)S(1)}, f32[8,2048]{1,0:T(8,128)S(1)}, f32[8,2048]{1,0:T(8,128)S(1)}, bf16[512,256...) custom-call(bf16[512,2432]{1,0:T(8,128)(2,1)} %copy-done.137, ...), custom_call_target="tpu_custom_call" | custom-call | flops 30000001024 | bytes 16000000 | tf_op jit(solution)/shard_map/scan_backward/pallas_call | solution.py:589
  516.2 2.9 collective-permute-done.34
  520.7 4.9 product_give.7
  525.6 5.8 fusion.44
  540.8 4.7 collective-permute-done.36
  546.6 5.2 multiply_reduce_fusion.1
  553.8 5.0 product_own.7
  572.7 8.0 %collective-permute-done.43 = bf16[64,2048]{1,0:T(8,128)(2,1)} collective-permute-done((bf16[64,2048]{1,0:T(8,128)(2,1)S(1)}, bf16[64,2048]{1,0:T(8,128)(2,1)}, u32[]{:S(2)}, u32[]{:S(2)}) %collective-permute-start.43) | collective-permute-done | bytes 262176 | tf_op jit(solution)/shard_map/ppermute | solution.py:639
  580.7 10.7 %collective-permute-done.45 = bf16[128,2432]{1,0:T(8,128)(2,1)} collective-permute-done((bf16[128,2432]{1,0:T(8,128)(2,1)}, bf16[128,2432]{1,0:T(8,128)(2,1)}, u32[]{:S(2)}, u32[]{:S(2)}) %collective-permute-start.45) | collective-permute-done | bytes 622624 | tf_op jit(solution)/shard_map/ppermute | solution.py:639
  598.8 2.7 collective-permute-done.48
  607.1 5.1 collective-permute-done.50
  612.1 2.1 collective-permute-start.51
  615.3 11.8 %collective-permute-done.51 = f32[8,3672]{1,0:T(8,128)S(1)} collective-permute-done((f32[8,3672]{1,0:T(8,128)S(1)}, f32[8,3672]{1,0:T(8,128)S(1)}, u32[]{:S(2)}, u32[]{:S(2)}) %collective-permute-start.51) | collective-permute-done | bytes 117536 | tf_op jit(solution)/shard_map/ppermute | solution.py:639
  629.7 3.9 collective-permute-done.54
  635.8 7.2 %collective-permute-done.55 = bf16[64,2432]{1,0:T(8,128)(2,1)S(1)} collective-permute-done((bf16[64,2432]{1,0:T(8,128)(2,1)S(1)}, bf16[64,2432]{1,0:T(8,128)(2,1)S(1)}, u32[]{:S(2)}, u32[]{:S(2)}) %collective-permute-start.55) | collective-permute-done | bytes 311328 | tf_op jit(solution)/shard_map/ppermute | solution.py:639
  643.1 2.8 in_weight_rows.1
  (603 shorter events, 152.5 us)
Async XLA Ops:
  7.2 47.0 %all-gather.9.cloned.1.call-start = ((), (), s32[]{:S(2)}) async-start(), calls=%async_computation.2 | async-start | bytes 5603328 | tf_op jit(solution)/shard_map/all_gather | solution.py:902
  9.9 100.0 %all-gather.11.cloned.1.call-start = ((), (), s32[]{:S(2)}) async-start(), calls=%async_computation.3 | async-start | bytes 4718592 | tf_op jit(solution)/shard_map/all_gather | solution.py:911
  10.8 141.9 %all-gather.13.cloned.1.call-start = ((), (), s32[]{:S(2)}) async-start(), calls=%async_computation.4 | async-start | bytes 5603328 | tf_op jit(solution)/shard_map/all_gather | solution.py:902
  11.9 188.4 %all-gather.15.cloned.1.call-start = ((), (), s32[]{:S(2)}) async-start(), calls=%async_computation.5 | async-start | bytes 4718592 | tf_op jit(solution)/shard_map/all_gather | solution.py:911
  12.8 217.6 %all-gather.17.cloned.1.call-start = ((), (), s32[]{:S(2)}) async-start(), calls=%async_computation.8 | async-start | bytes 4718592 | tf_op jit(solution)/shard_map/all_gather | solution.py:914
  13.8 388.8 %reduce-scatter.3.cloned.1.call-start = ((), (), s32[]{:S(2)}) async-start(), calls=%async_computation.6 | async-start | bytes 4718592 | tf_op jit(solution)/shard_map/reduce_scatter | solution.py:1025
  59.8 7.5 %collective-permute-start = (bf16[16,2304]{1,0:T(8,128)(2,1)S(1)}, bf16[16,2304]{1,0:T(8,128)(2,1)S(1)}, u32[]{:S(2)}, u32[]{:S(2)}) collective-permute-start(bf16[16,2304]{1,0:T(8,128)(2,1)S(1)} %slice.456), channel_id=1, source_target_pairs={{0,8},{8,16},{16,24},{1,9},{9,17},{17,25},{2,10},{10,18},{18,26},{... | collective-permute-start | bytes 221192 | tf_op jit(solution)/shard_map/ppermute | solution.py:925
  63.7 53.2 %collective-permute-start.4 = (bf16[256,1024]{1,0:T(8,128)(2,1)S(1)}, bf16[256,1024]{1,0:T(8,128)(2,1)S(1)}, u32[]{:S(2)}, u32[]{:S(2)}) collective-permute-start(bf16[256,1024]{1,0:T(8,128)(2,1)S(1)} %get-tuple-element.252.refs_0_), channel_id=1, source_target_pairs={{0,6},{1,7},{2,4},{3,5},{4,2},{5,3},{6,0},{7,1},{8,14},{9,15},{10,... | collective-permute-start | bytes 1572872 | tf_op jit(solution)/shard_map/ppermute | solution.py:639
  65.2 51.7 %collective-permute-start.3 = (bf16[256,1024]{1,0:T(8,128)(2,1)S(1)}, bf16[256,1024]{1,0:T(8,128)(2,1)S(1)}, u32[]{:S(2)}, u32[]{:S(2)}) collective-permute-start(bf16[256,1024]{1,0:T(8,128)(2,1)S(1)} %get-tuple-element.252.refs_0_), channel_id=1, source_target_pairs={{0,4},{1,5},{2,6},{3,7},{4,0},{5,1},{6,2},{7,3},{8,12},{9,13},{10,... | collective-permute-start | bytes 1572872 | tf_op jit(solution)/shard_map/ppermute | solution.py:639
  66.7 50.2 %collective-permute-start.2 = (bf16[256,1024]{1,0:T(8,128)(2,1)S(1)}, bf16[256,1024]{1,0:T(8,128)(2,1)S(1)}, u32[]{:S(2)}, u32[]{:S(2)}) collective-permute-start(bf16[256,1024]{1,0:T(8,128)(2,1)S(1)} %get-tuple-element.252.refs_0_), channel_id=1, source_target_pairs={{0,2},{1,3},{2,0},{3,1},{4,6},{5,7},{6,4},{7,5},{8,10},{9,11},{10,... | collective-permute-start | bytes 1572872 | tf_op jit(solution)/shard_map/ppermute | solution.py:639
  79.7 15.0 %collective-permute-start.1 = (bf16[128,2048]{1,0:T(8,128)(2,1)S(1)}, bf16[128,2048]{1,0:T(8,128)(2,1)S(1)}, u32[]{:S(2)}, u32[]{:S(2)}) collective-permute-start(bf16[128,2048]{1,0:T(8,128)(2,1)S(1)} %get-tuple-element.245), channel_id=1, source_target_pairs={{0,8},{1,9},{2,10},{3,11},{4,12},{5,13},{6,14},{7,15}} | collective-permute-start | bytes 1572872 | tf_op jit(solution)/shard_map/ppermute | solution.py:645
  96.5 21.2 %collective-permute-start.5 = (bf16[128,2048]{1,0:T(8,128)(2,1)}, bf16[128,2048]{1,0:T(8,128)(2,1)}, u32[]{:S(2)}, u32[]{:S(2)}) collective-permute-start(bf16[128,2048]{1,0:T(8,128)(2,1)} %fusion.9), channel_id=1, source_target_pairs={{8,16},{9,17},{10,18},{11,19},{12,20},{13,21},{14,22},{15,23}} | collective-permute-start | bytes 1572872 | tf_op jit(solution)/shard_map/ppermute | solution.py:645
  116.9 7.9 %collective-permute-start.6 = (bf16[256,1024]{1,0:T(8,128)(2,1)S(1)}, bf16[256,1024]{1,0:T(8,128)(2,1)S(1)}, u32[]{:S(2)}, u32[]{:S(2)}) collective-permute-start(bf16[256,1024]{1,0:T(8,128)(2,1)S(1)} %collective-permute-done.2.refs_2_), channel_id=1, source_target_pairs={{0,1},{1,0},{2,3},{3,2},{4,5},{5,4},{6,7},{7,6},{8,9},{9,8},{10,11... | collective-permute-start | bytes 1572872 | tf_op jit(solution)/shard_map/ppermute | solution.py:639
  117.2 7.5 %collective-permute-start.7 = (bf16[256,1024]{1,0:T(8,128)(2,1)S(1)}, bf16[256,1024]{1,0:T(8,128)(2,1)}, u32[]{:S(2)}, u32[]{:S(2)}) collective-permute-start(bf16[256,1024]{1,0:T(8,128)(2,1)S(1)} %collective-permute-done.3.refs_4_), channel_id=1, source_target_pairs={{0,1},{1,0},{2,3},{3,2},{4,5},{5,4},{6,7},{7,6},{8,9},{9,8},{10,11... | collective-permute-start | bytes 1572872 | tf_op jit(solution)/shard_map/ppermute | solution.py:639
  117.4 7.3 %collective-permute-start.8 = (bf16[256,1024]{1,0:T(8,128)(2,1)S(1)}, bf16[256,1024]{1,0:T(8,128)(2,1)}, u32[]{:S(2)}, u32[]{:S(2)}) collective-permute-start(bf16[256,1024]{1,0:T(8,128)(2,1)S(1)} %collective-permute-done.4.refs_6_), channel_id=1, source_target_pairs={{0,1},{1,0},{2,3},{3,2},{4,5},{5,4},{6,7},{7,6},{8,9},{9,8},{10,11... | collective-permute-start | bytes 1572872 | tf_op jit(solution)/shard_map/ppermute | solution.py:639
  119.9 4.8 collective-permute-start.9
  124.5 10.0 %collective-permute-start.10 = (bf16[256,1024]{1,0:T(8,128)(2,1)S(1)}, bf16[256,1024]{1,0:T(8,128)(2,1)S(1)}, u32[]{:S(2)}, u32[]{:S(2)}) collective-permute-start(bf16[256,1024]{1,0:T(8,128)(2,1)S(1)} %get-tuple-element.252.refs_0_), channel_id=1, source_target_pairs={{0,1},{1,0},{2,3},{3,2},{4,5},{5,4},{6,7},{7,6},{8,9},{9,8},{10,11... | collective-permute-start | bytes 1572872 | tf_op jit(solution)/shard_map/ppermute | solution.py:639
  158.4 5.4 collective-permute-start.11
  177.0 19.9 %collective-permute-start.12 = (bf16[128,2048]{1,0:T(8,128)(2,1)S(1)}, bf16[128,2048]{1,0:T(8,128)(2,1)S(1)}, u32[]{:S(2)}, u32[]{:S(2)}) collective-permute-start(bf16[128,2048]{1,0:T(8,128)(2,1)S(1)} %get-tuple-element.267), channel_id=1, source_target_pairs={{0,8},{1,9},{2,10},{3,11},{4,12},{5,13},{6,14},{7,15}} | collective-permute-start | bytes 1572872 | tf_op jit(solution)/shard_map/ppermute | solution.py:645
  198.6 9.0 %collective-permute-start.13 = (bf16[128,2048]{1,0:T(8,128)(2,1)}, bf16[128,2048]{1,0:T(8,128)(2,1)}, u32[]{:S(2)}, u32[]{:S(2)}) collective-permute-start(bf16[128,2048]{1,0:T(8,128)(2,1)} %fusion.11), channel_id=1, source_target_pairs={{8,16},{9,17},{10,18},{11,19},{12,20},{13,21},{14,22},{15,23}} | collective-permute-start | bytes 1572872 | tf_op jit(solution)/shard_map/ppermute | solution.py:645
  209.0 0.7 collective-permute-start.14
  253.1 12.6 %collective-permute-start.15 = (bf16[128,2048]{1,0:T(8,128)(2,1)S(1)}, bf16[128,2048]{1,0:T(8,128)(2,1)}, u32[]{:S(2)}, u32[]{:S(2)}) collective-permute-start(bf16[128,2048]{1,0:T(8,128)(2,1)S(1)} %get-tuple-element.284), channel_id=1, source_target_pairs={{24,16},{25,17},{26,18},{27,19},{28,20},{29,21},{30,22},{31,23}} | collective-permute-start | bytes 1572872 | tf_op jit(solution)/shard_map/ppermute | solution.py:645
  265.7 137.0 %reduce-scatter.5.cloned.1.call-start = ((), (), s32[]{:S(2)}) async-start(), calls=%async_computation.7 | async-start | bytes 4718592 | tf_op jit(solution)/shard_map/reduce_scatter | solution.py:1025
  274.9 6.6 %collective-permute-start.16 = (bf16[128,2048]{1,0:T(8,128)(2,1)S(1)}, bf16[128,2048]{1,0:T(8,128)(2,1)S(1)}, u32[]{:S(2)}, u32[]{:S(2)}) collective-permute-start(bf16[128,2048]{1,0:T(8,128)(2,1)S(1)} %fusion.13), channel_id=1, source_target_pairs={{16,8},{17,9},{18,10},{19,11},{20,12},{21,13},{22,14},{23,15}} | collective-permute-start | bytes 1572872 | tf_op jit(solution)/shard_map/ppermute | solution.py:645
  284.1 21.0 %collective-permute-start.17 = (bf16[128,2048]{1,0:T(8,128)(2,1)}, bf16[128,2048]{1,0:T(8,128)(2,1)}, u32[]{:S(2)}, u32[]{:S(2)}) collective-permute-start(bf16[128,2048]{1,0:T(8,128)(2,1)} %fusion.14), channel_id=1, source_target_pairs={{8,0},{9,1},{10,2},{11,3},{12,4},{13,5},{14,6},{15,7}} | collective-permute-start | bytes 1572872 | tf_op jit(solution)/shard_map/ppermute | solution.py:645
  293.3 219.3 %all-reduce.5.cloned.1.call-start = ((), (), s32[]{:S(2)}) async-start(), calls=%async_computation.9 | async-start | bytes 2097152 | tf_op jit(solution)/shard_map/psum | solution.py:980
  341.7 6.2 collective-permute-start.18
  354.1 12.2 %collective-permute-start.19 = (bf16[512,2432]{1,0:T(8,128)(2,1)}, bf16[512,2432]{1,0:T(8,128)(2,1)}, u32[]{:S(2)}, u32[]{:S(2)}) collective-permute-start(bf16[512,2432]{1,0:T(8,128)(2,1)} %product_give.4), channel_id=1, source_target_pairs={{0,1},{1,0},{2,3},{3,2},{4,5},{5,4},{6,7},{7,6},{8,9},{9,8},{10,11... | collective-permute-start | bytes 7471112 | tf_op jit(solution)/shard_map/ppermute | solution.py:639
  372.1 41.4 %collective-permute-start.21 = (bf16[128,2432]{1,0:T(8,128)(2,1)}, bf16[128,2432]{1,0:T(8,128)(2,1)}, u32[]{:S(2)}, u32[]{:S(2)}) collective-permute-start(bf16[128,2432]{1,0:T(8,128)(2,1)} %get-tuple-element.321), channel_id=1, source_target_pairs={{0,2},{1,3},{2,0},{3,1},{4,6},{5,7},{6,4},{7,5},{8,10},{9,11},{10,... | collective-permute-start | bytes 1867784 | tf_op jit(solution)/shard_map/ppermute | solution.py:639
  373.5 40.0 %collective-permute-start.22 = (bf16[128,2432]{1,0:T(8,128)(2,1)}, bf16[128,2432]{1,0:T(8,128)(2,1)}, u32[]{:S(2)}, u32[]{:S(2)}) collective-permute-start(bf16[128,2432]{1,0:T(8,128)(2,1)} %get-tuple-element.322), channel_id=1, source_target_pairs={{0,4},{1,5},{2,6},{3,7},{4,0},{5,1},{6,2},{7,3},{8,12},{9,13},{10,... | collective-permute-start | bytes 1867784 | tf_op jit(solution)/shard_map/ppermute | solution.py:639
  373.9 39.6 %collective-permute-start.23 = (bf16[128,2432]{1,0:T(8,128)(2,1)}, bf16[128,2432]{1,0:T(8,128)(2,1)}, u32[]{:S(2)}, u32[]{:S(2)}) collective-permute-start(bf16[128,2432]{1,0:T(8,128)(2,1)} %get-tuple-element.323), channel_id=1, source_target_pairs={{0,6},{1,7},{2,4},{3,5},{4,2},{5,3},{6,0},{7,1},{8,14},{9,15},{10,... | collective-permute-start | bytes 1867784 | tf_op jit(solution)/shard_map/ppermute | solution.py:639
  402.6 10.9 %collective-permute-start.20 = (bf16[128,2048]{1,0:T(8,128)(2,1)S(1)}, bf16[128,2048]{1,0:T(8,128)(2,1)S(1)}, u32[]{:S(2)}, u32[]{:S(2)}) collective-permute-start(bf16[128,2048]{1,0:T(8,128)(2,1)S(1)} %get-tuple-element.317), channel_id=1, source_target_pairs={{24,16},{25,17},{26,18},{27,19},{28,20},{29,21},{30,22},{31,23}} | collective-permute-start | bytes 1572872 | tf_op jit(solution)/shard_map/ppermute | solution.py:645
  413.5 14.8 %collective-permute-start.25 = (bf16[1024,1024]{1,0:T(8,128)(2,1)}, bf16[1024,1024]{1,0:T(8,128)(2,1)S(1)}, u32[]{:S(2)}, u32[]{:S(2)}) collective-permute-start(bf16[1024,1024]{1,0:T(8,128)(2,1)} %product_give.5), channel_id=1, source_target_pairs={{0,1},{1,0},{2,3},{3,2},{4,5},{5,4},{6,7},{7,6},{8,9},{9,8},{10,11... | collective-permute-start | bytes 6291464 | tf_op jit(solution)/shard_map/ppermute | solution.py:639
  416.2 12.1 %collective-permute-start.26 = (bf16[64,2432]{1,0:T(8,128)(2,1)S(1)}, bf16[64,2432]{1,0:T(8,128)(2,1)S(1)}, u32[]{:S(2)}, u32[]{:S(2)}) collective-permute-start(bf16[64,2432]{1,0:T(8,128)(2,1)S(1)} %get-tuple-element.476), channel_id=1, source_target_pairs={{0,8},{8,0},{16,24},{24,16},{1,9},{9,1},{17,25},{25,17},{2,10},{10... | collective-permute-start | bytes 933896 | tf_op jit(solution)/shard_map/ppermute | solution.py:639
  416.3 11.8 %collective-permute-start.24 = (bf16[128,2048]{1,0:T(8,128)(2,1)S(1)}, bf16[128,2048]{1,0:T(8,128)(2,1)S(1)}, u32[]{:S(2)}, u32[]{:S(2)}) collective-permute-start(bf16[128,2048]{1,0:T(8,128)(2,1)S(1)} %fusion.15), channel_id=1, source_target_pairs={{16,8},{17,9},{18,10},{19,11},{20,12},{21,13},{22,14},{23,15}} | collective-permute-start | bytes 1572872 | tf_op jit(solution)/shard_map/ppermute | solution.py:645
  428.3 50.5 %collective-permute-start.28 = (bf16[512,2048]{1,0:T(8,128)(2,1)}, bf16[512,2048]{1,0:T(8,128)(2,1)}, u32[]{:S(2)}, u32[]{:S(2)}) collective-permute-start(bf16[512,2048]{1,0:T(8,128)(2,1)} %product_give.6), channel_id=1, source_target_pairs={{0,1},{1,0},{2,3},{3,2},{4,5},{5,4},{6,7},{7,6},{8,9},{9,8},{10,11... | collective-permute-start | bytes 6291464 | tf_op jit(solution)/shard_map/ppermute | solution.py:639
  432.3 41.7 %collective-permute-start.27 = (bf16[128,2048]{1,0:T(8,128)(2,1)}, bf16[128,2048]{1,0:T(8,128)(2,1)}, u32[]{:S(2)}, u32[]{:S(2)}) collective-permute-start(bf16[128,2048]{1,0:T(8,128)(2,1)} %fusion.16), channel_id=1, source_target_pairs={{8,0},{9,1},{10,2},{11,3},{12,4},{13,5},{14,6},{15,7}} | collective-permute-start | bytes 1572872 | tf_op jit(solution)/shard_map/ppermute | solution.py:645
  435.4 43.5 %collective-permute-start.29 = (bf16[64,2432]{1,0:T(8,128)(2,1)}, bf16[64,2432]{1,0:T(8,128)(2,1)}, u32[]{:S(2)}, u32[]{:S(2)}) collective-permute-start(bf16[64,2432]{1,0:T(8,128)(2,1)} %add_convert_fusion.8), channel_id=1, source_target_pairs={{0,16},{8,24},{16,0},{24,8},{1,17},{9,25},{17,1},{25,9},{2,18},{10... | collective-permute-start | bytes 933896 | tf_op jit(solution)/shard_map/ppermute | solution.py:639
  475.3 37.3 %collective-permute-start.30 = (bf16[256,1024]{1,0:T(8,128)(2,1)}, bf16[256,1024]{1,0:T(8,128)(2,1)}, u32[]{:S(2)}, u32[]{:S(2)}) collective-permute-start(bf16[256,1024]{1,0:T(8,128)(2,1)} %get-tuple-element.364), channel_id=1, source_target_pairs={{0,2},{1,3},{2,0},{3,1},{4,6},{5,7},{6,4},{7,5},{8,10},{9,11},{10,... | collective-permute-start | bytes 1572872 | tf_op jit(solution)/shard_map/ppermute | solution.py:639
  476.7 35.9 %collective-permute-start.31 = (bf16[256,1024]{1,0:T(8,128)(2,1)}, bf16[256,1024]{1,0:T(8,128)(2,1)}, u32[]{:S(2)}, u32[]{:S(2)}) collective-permute-start(bf16[256,1024]{1,0:T(8,128)(2,1)} %get-tuple-element.365), channel_id=1, source_target_pairs={{0,4},{1,5},{2,6},{3,7},{4,0},{5,1},{6,2},{7,3},{8,12},{9,13},{10,... | collective-permute-start | bytes 1572872 | tf_op jit(solution)/shard_map/ppermute | solution.py:639
  476.7 35.9 %collective-permute-start.32 = (bf16[256,1024]{1,0:T(8,128)(2,1)}, bf16[256,1024]{1,0:T(8,128)(2,1)}, u32[]{:S(2)}, u32[]{:S(2)}) collective-permute-start(bf16[256,1024]{1,0:T(8,128)(2,1)} %get-tuple-element.366), channel_id=1, source_target_pairs={{0,6},{1,7},{2,4},{3,5},{4,2},{5,3},{6,0},{7,1},{8,14},{9,15},{10,... | collective-permute-start | bytes 1572872 | tf_op jit(solution)/shard_map/ppermute | solution.py:639
  484.8 27.9 %collective-permute-start.33 = (bf16[64,2432]{1,0:T(8,128)(2,1)}, bf16[64,2432]{1,0:T(8,128)(2,1)}, u32[]{:S(2)}, u32[]{:S(2)}) collective-permute-start(bf16[64,2432]{1,0:T(8,128)(2,1)} %add_convert_fusion.7), channel_id=1, source_target_pairs={{0,8},{8,0},{16,24},{24,16},{1,9},{9,1},{17,25},{25,17},{2,10},{10... | collective-permute-start | bytes 933896 | tf_op jit(solution)/shard_map/ppermute | solution.py:639
  512.7 6.4 collective-permute-start.34
  525.6 21.0 %collective-permute-start.35 = (bf16[512,2432]{1,0:T(8,128)(2,1)}, bf16[512,2432]{1,0:T(8,128)(2,1)}, u32[]{:S(2)}, u32[]{:S(2)}) collective-permute-start(bf16[512,2432]{1,0:T(8,128)(2,1)} %product_give.7), channel_id=1, source_target_pairs={{0,1},{1,0},{2,3},{3,2},{4,5},{5,4},{6,7},{7,6},{8,9},{9,8},{10,11... | collective-permute-start | bytes 7471112 | tf_op jit(solution)/shard_map/ppermute | solution.py:639
  531.4 27.4 %collective-permute-start.38 = (bf16[128,2048]{1,0:T(8,128)(2,1)}, bf16[128,2048]{1,0:T(8,128)(2,1)}, u32[]{:S(2)}, u32[]{:S(2)}) collective-permute-start(bf16[128,2048]{1,0:T(8,128)(2,1)} %get-tuple-element.403), channel_id=1, source_target_pairs={{0,2},{1,3},{2,0},{3,1},{4,6},{5,7},{6,4},{7,5},{8,10},{9,11},{10,... | collective-permute-start | bytes 1572872 | tf_op jit(solution)/shard_map/ppermute | solution.py:639
  532.8 26.0 %collective-permute-start.39 = (bf16[128,2048]{1,0:T(8,128)(2,1)}, bf16[128,2048]{1,0:T(8,128)(2,1)}, u32[]{:S(2)}, u32[]{:S(2)}) collective-permute-start(bf16[128,2048]{1,0:T(8,128)(2,1)} %get-tuple-element.404), channel_id=1, source_target_pairs={{0,4},{1,5},{2,6},{3,7},{4,0},{5,1},{6,2},{7,3},{8,12},{9,13},{10,... | collective-permute-start | bytes 1572872 | tf_op jit(solution)/shard_map/ppermute | solution.py:639
  532.9 26.0 %collective-permute-start.40 = (bf16[128,2048]{1,0:T(8,128)(2,1)}, bf16[128,2048]{1,0:T(8,128)(2,1)}, u32[]{:S(2)}, u32[]{:S(2)}) collective-permute-start(bf16[128,2048]{1,0:T(8,128)(2,1)} %get-tuple-element.405), channel_id=1, source_target_pairs={{0,6},{1,7},{2,4},{3,5},{4,2},{5,3},{6,0},{7,1},{8,14},{9,15},{10,... | collective-permute-start | bytes 1572872 | tf_op jit(solution)/shard_map/ppermute | solution.py:639
  537.3 8.2 %collective-permute-start.36 = (bf16[128,1024]{1,0:T(8,128)(2,1)S(1)}, bf16[128,1024]{1,0:T(8,128)(2,1)S(1)}, u32[]{:S(2)}, u32[]{:S(2)}) collective-permute-start(bf16[128,1024]{1,0:T(8,128)(2,1)S(1)} %get-tuple-element.480), channel_id=1, source_target_pairs={{0,8},{8,0},{16,24},{24,16},{1,9},{9,1},{17,25},{25,17},{2,10},{10... | collective-permute-start | bytes 786440 | tf_op jit(solution)/shard_map/ppermute | solution.py:639
  545.5 20.3 %collective-permute-start.37 = (bf16[128,1024]{1,0:T(8,128)(2,1)S(1)}, bf16[128,1024]{1,0:T(8,128)(2,1)S(1)}, u32[]{:S(2)}, u32[]{:S(2)}) collective-permute-start(bf16[128,1024]{1,0:T(8,128)(2,1)S(1)} %add_convert_fusion.12), channel_id=1, source_target_pairs={{0,16},{8,24},{16,0},{24,8},{1,17},{9,25},{17,1},{25,9},{2,18},{10... | collective-permute-start | bytes 786440 | tf_op jit(solution)/shard_map/ppermute | solution.py:639
  560.6 7.2 %collective-permute-start.41 = (bf16[64,2048]{1,0:T(8,128)(2,1)S(1)}, bf16[64,2048]{1,0:T(8,128)(2,1)S(1)}, u32[]{:S(2)}, u32[]{:S(2)}) collective-permute-start(bf16[64,2048]{1,0:T(8,128)(2,1)S(1)} %get-tuple-element.478), channel_id=1, source_target_pairs={{0,8},{8,0},{16,24},{24,16},{1,9},{9,1},{17,25},{25,17},{2,10},{10... | collective-permute-start | bytes 786440 | tf_op jit(solution)/shard_map/ppermute | solution.py:639
  562.3 18.4 %collective-permute-start.44 = (bf16[128,2432]{1,0:T(8,128)(2,1)}, bf16[128,2432]{1,0:T(8,128)(2,1)S(1)}, u32[]{:S(2)}, u32[]{:S(2)}) collective-permute-start(bf16[128,2432]{1,0:T(8,128)(2,1)} %get-tuple-element.413), channel_id=1, source_target_pairs={{0,2},{1,3},{2,0},{3,1},{4,6},{5,7},{6,4},{7,5},{8,10},{9,11},{10,... | collective-permute-start | bytes 1867784 | tf_op jit(solution)/shard_map/ppermute | solution.py:639
  563.1 28.4 %collective-permute-start.45 = (bf16[128,2432]{1,0:T(8,128)(2,1)}, bf16[128,2432]{1,0:T(8,128)(2,1)}, u32[]{:S(2)}, u32[]{:S(2)}) collective-permute-start(bf16[128,2432]{1,0:T(8,128)(2,1)} %get-tuple-element.414), channel_id=1, source_target_pairs={{0,4},{1,5},{2,6},{3,7},{4,0},{5,1},{6,2},{7,3},{8,12},{9,13},{10,... | collective-permute-start | bytes 1867784 | tf_op jit(solution)/shard_map/ppermute | solution.py:639
  564.1 27.3 %collective-permute-start.46 = (bf16[128,2432]{1,0:T(8,128)(2,1)S(1)}, bf16[128,2432]{1,0:T(8,128)(2,1)}, u32[]{:S(2)}, u32[]{:S(2)}) collective-permute-start(bf16[128,2432]{1,0:T(8,128)(2,1)S(1)} %get-tuple-element.415), channel_id=1, source_target_pairs={{0,6},{1,7},{2,4},{3,5},{4,2},{5,3},{6,0},{7,1},{8,14},{9,15},{10,... | collective-permute-start | bytes 1867784 | tf_op jit(solution)/shard_map/ppermute | solution.py:639
  567.8 12.9 %collective-permute-start.43 = (bf16[64,2048]{1,0:T(8,128)(2,1)S(1)}, bf16[64,2048]{1,0:T(8,128)(2,1)}, u32[]{:S(2)}, u32[]{:S(2)}) collective-permute-start(bf16[64,2048]{1,0:T(8,128)(2,1)S(1)} %add_convert_fusion.10), channel_id=1, source_target_pairs={{0,16},{8,24},{16,0},{24,8},{1,17},{9,25},{17,1},{25,9},{2,18},{10... | collective-permute-start | bytes 786440 | tf_op jit(solution)/shard_map/ppermute | solution.py:639
  569.9 10.8 %collective-permute-start.42 = (bf16[128,1024]{1,0:T(8,128)(2,1)S(1)}, bf16[128,1024]{1,0:T(8,128)(2,1)}, u32[]{:S(2)}, u32[]{:S(2)}) collective-permute-start(bf16[128,1024]{1,0:T(8,128)(2,1)S(1)} %add_convert_fusion.11), channel_id=1, source_target_pairs={{0,8},{8,0},{16,24},{24,16},{1,9},{9,1},{17,25},{25,17},{2,10},{10... | collective-permute-start | bytes 786440 | tf_op jit(solution)/shard_map/ppermute | solution.py:639
  593.0 3.3 collective-permute-start.47
  594.2 12.8 %collective-permute-start.52 = (bf16[64,2048]{1,0:T(8,128)(2,1)S(1)}, bf16[64,2048]{1,0:T(8,128)(2,1)S(1)}, u32[]{:S(2)}, u32[]{:S(2)}) collective-permute-start(bf16[64,2048]{1,0:T(8,128)(2,1)S(1)} %add_convert_fusion.9), channel_id=1, source_target_pairs={{0,8},{8,0},{16,24},{24,16},{1,9},{9,1},{17,25},{25,17},{2,10},{10... | collective-permute-start | bytes 786440 | tf_op jit(solution)/shard_map/ppermute | solution.py:639
  594.7 19.5 %collective-permute-start.53 = (bf16[64,2432]{1,0:T(8,128)(2,1)S(1)}, bf16[64,2432]{1,0:T(8,128)(2,1)S(1)}, u32[]{:S(2)}, u32[]{:S(2)}) collective-permute-start(bf16[64,2432]{1,0:T(8,128)(2,1)S(1)} %constant_dynamic-slice_fusion), channel_id=1, source_target_pairs={{0,8},{8,0},{16,24},{24,16},{1,9},{9,1},{17,25},{25,17},{2,10},{10... | collective-permute-start | bytes 933896 | tf_op jit(solution)/shard_map/ppermute | solution.py:639
  596.4 5.1 collective-permute-start.48
  601.5 4.9 collective-permute-start.49
  606.4 5.7 collective-permute-start.50
  612.1 14.9 %collective-permute-start.51 = (f32[8,3672]{1,0:T(8,128)S(1)}, f32[8,3672]{1,0:T(8,128)S(1)}, u32[]{:S(2)}, u32[]{:S(2)}) collective-permute-start(f32[8,3672]{1,0:T(8,128)S(1)} %add.370), channel_id=1, source_target_pairs={{0,16},{8,24},{16,0},{24,8},{1,17},{9,25},{17,1},{25,9},{2,18},{10... | collective-permute-start | bytes 352520 | tf_op jit(solution)/shard_map/ppermute | solution.py:639
  614.3 19.3 %collective-permute-start.54 = (bf16[64,2432]{1,0:T(8,128)(2,1)S(1)}, bf16[64,2432]{1,0:T(8,128)(2,1)S(1)}, u32[]{:S(2)}, u32[]{:S(2)}) collective-permute-start(bf16[64,2432]{1,0:T(8,128)(2,1)S(1)} %add_convert_fusion.6), channel_id=1, source_target_pairs={{0,16},{8,24},{16,0},{24,8},{1,17},{9,25},{17,1},{25,9},{2,18},{10... | collective-permute-start | bytes 933896 | tf_op jit(solution)/shard_map/ppermute | solution.py:639
  633.7 9.3 %collective-permute-start.55 = (bf16[64,2432]{1,0:T(8,128)(2,1)S(1)}, bf16[64,2432]{1,0:T(8,128)(2,1)S(1)}, u32[]{:S(2)}, u32[]{:S(2)}) collective-permute-start(bf16[64,2432]{1,0:T(8,128)(2,1)S(1)} %add_convert_fusion.5), channel_id=1, source_target_pairs={{0,8},{8,0},{16,24},{24,16},{1,9},{9,1},{17,25},{25,17},{2,10},{10... | collective-permute-start | bytes 933896 | tf_op jit(solution)/shard_map/ppermute | solution.py:639
  (149 other events, 1464.0 us)
Sparse Core Ops, SparseCore 0:
  10.5 43.6 all-gather.8
  56.6 53.2 all-gather.10
  111.8 40.8 all-gather.12
  154.5 37.4 all-gather.14
  193.7 36.7 all-gather.16
  265.8 55.8 reduce-scatter.2
  325.4 51.5 reduce-scatter.4
  441.6 65.6 all-reduce.4

commit v5 on v4

--- a/solution.py
+++ b/solution.py
@@ -985,25 +985,22 @@
             out_give = product_give(shard_columns(gate_low, 1), d_branch)
             state = hop_to(g_local, None, 0, False)
             low = inside(0)
-            state, out_give, low, rest_sent = tie(state, out_give, low, rest_sent)
-            above = seq_first(gather_sum(rest_mine, rest_sent))
+            state, out_give, low = tie(state, out_give, low)
             for hop in range(1, seq_parts - 1):
                 state = hop_to(message_of(g_local, decay[0:1], state), state, hop, False)
                 if hop == 1:
                     out_got = swap(out_give, "fsdp", 1)
                     gate_give = product_give(normed_give, dgate)
                     high = inside(STEPS // 2)
-                    state, out_got, gate_give, high, above = tie(
-                        state, out_got, gate_give, high, above
-                    )
-                    above = seq_across(*above)
+                    state, gate_give, high, rest_sent = tie(state, gate_give, high, rest_sent)
+                    above = seq_first(gather_sum(rest_mine, rest_sent))
                     gate_got = swap(gate_give, "fsdp", 1)
                     out_parts = product_own(shard_columns(gate_low, 0), d_branch, out_got)
                 elif hop == 2:
                     out_parts, state = tie(out_parts, state)
                     out_mine, out_sent = send_chips(out_parts)
                     state, gate_got, above = tie(state, gate_got, above)
-                    above = seq_back(*above)
+                    above = seq_across(*above)
                     gate_parts = product_own(normed_own, dgate, gate_got)
                     state, gate_parts = tie(state, gate_parts)
                     gate_mine, gate_sent = send_chips(gate_parts)
@@ -1031,7 +1028,7 @@
         )
         if layer == 0:
             back, out_sent, above, big[layer + 1] = tie(back, out_sent, above, big[layer + 1])
-            big[layer + 1].append(seq_join(*above))
+            big[layer + 1].append(seq_join(*seq_back(*above)))
             out_seq = seq_first(gather_sum(out_mine, out_sent))
         dv, tail, head, stats, bdv, btail, bhead, bstats, ddt, dtstats = back
         heads_in = lax.ppermute(jnp.concatenate([head, bhead], axis=1), "seq", down)

time: 663 us -> 654 us (0.986)
  waiting for transfers between devices: 161 us -> 170 us
  local copies, waits for them, and re-layouts: 53.7 us -> 44.9 us
    ppermute x40, waiting for transfers between devices: 58 us -> 78.4 us  [swap(): lax.ppermute(a, axis, [(k, k ^ bit) for k in range(lax.axis_size(axis))])]
    ppermute x40, starting transfers between devices: 41.7 us -> 33.3 us  [swap(): lax.ppermute(a, axis, [(k, k ^ bit) for k in range(lax.axis_size(axis))])]
    all_gather x1, waiting for transfers between devices: 11.3 us -> 4.64 us  [on_device(): lax.all_gather(output_projection_weight[layer], 'fsdp', axis=0, tiled=True)]
  transfers between devices with their start and end apart: 64 -> 64, of which waited for: 19 -> 26; matrix products, arithmetic and copies ran while one was open for 20% -> 20% of each run, Pallas kernels for 30% -> 30%
where the time goes in v5:
time: 654 us; the launch traced here: 644 us
  Pallas kernels  212 us (32%)
  waiting for transfers between devices  170 us (26%)
  starting transfers between devices  69.7 us (11%)
  matrix products  68.3 us (10%)
  other arithmetic  51.2 us (8%)
  local copies, waits for them, and re-layouts  44.9 us (7%)
  between operations  16.9 us (3%)
  blocking collectives  10.7 us (2%)
    ppermute x40, waiting for transfers between devices, swap(): lax.ppermute(a, axis, [(k, k ^ bit) for k in range(lax.axis_size(axis))])  78.4 us
    pallas_call x2, Pallas kernels, scan_backward(): pl.pallas_call(back_kernel, name='scan_backward', grid=(STEPS,), in_specs...  55.7 us
    ppermute x12, waiting for transfers between devices, hop_to(): got = lax.ppermute(message, 'seq', [pair])  34.1 us
    ppermute x40, starting transfers between devices, swap(): lax.ppermute(a, axis, [(k, k ^ bit) for k in range(lax.axis_size(axis))])  33.3 us
    all_gather x2, waiting for transfers between devices, on_device(): rest = lax.all_gather(rest, 'fsdp', axis=0, tiled=True)  33 us
    dot_general x5, matrix products, dot(): return jnp.dot(a, b, preferred_element_type=F32)  32.3 us
    ppermute x12, starting transfers between devices, hop_to(): got = lax.ppermute(message, 'seq', [pair])  26 us
    dot_general x5, matrix products, dot_nt(): lax.dot_general(a, b, (((1,), (1,)), ((), ())), preferred_element_type=F32)  25.3 us
  transfers between devices with their start and end apart: 64, of which 26 were waited for; matrix products, arithmetic and copies ran while one was open for 20% of the time, Pallas kernels for 30%

profile of v5, /device:TPU:0, one launch (start us, length us, event | category | flops | bytes accessed | tf_op | source)
XLA Modules:
  0.0 643.7 jit_solution(8870199234047679582)
XLA Ops:
  14.1 10.7 %all-gather.2 = bf16[8,2,1836]{2,1,0:T(2,128)(2,1)S(1)} all-gather(bf16[1,2,1836]{2,1,0:T(2,128)(2,1)S(1)} %bitcast.148), channel_id=2, replica_groups=mesh['seq'=4,'fsdp'=8] {'fsdp'}, dimensions={0}, use_global_device_ids=true | all-gather | bytes 66096 | tf_op jit(solution)/shard_map/all_gather | solution.py:885
  26.5 27.7 %all-gather.9.cloned.1.call-done = bf16[1024,2432]{0,1:T(8,128)(2,1)} async-done(((bf16[128,2432]{0,1:T(8,128)(2,1)}), bf16[1024,2432]{0,1:T(8,128)(2,1)}) %all-gather.9.cloned.1.call-update) | async-done | bytes 4980752 | tf_op jit(solution)/shard_map/all_gather | solution.py:902
  54.2 5.5 convolution_convert_fusion.1.v_ref.bc_ref.dt_ref
  59.8 3.4 collective-permute-start
  67.2 12.4 %local_state.2 = (bf16[128,2048]{1,0:T(8,128)(2,1)S(1)}, f32[8,2048]{1,0:T(8,128)S(1)}, f32[512,2048]{1,0:T(8,128)}, f32[512,128]{1,0:T(8,128)S(1)}, bf16[512,38...) custom-call(bf16[512,2432]{1,0:T(8,128)(2,1)} %copy-done.137, ...), custom_call_target="tpu_custom_call" | custom-call | flops 4000000000 | bytes 8000000 | tf_op jit(solution)/shard_map/local_state/pallas_call | solution.py:474
  79.7 3.4 collective-permute-start.1
  83.2 11.5 %local_scan.2.y_ref = f32[512,2048]{1,0:T(8,128)} custom-call(f32[512,2048]{1,0:T(8,128)} %get-tuple-element.243.x_ref, f32[1,2048]{1,0:T(1,128)S(1)} %broadcast_in_dim_reshape.6.skip_ref, bf16[512,384]{1,0:T(8,128)(2,1)S(1)} %get-tuple-element.244.p3_ref, bf16[512,128]{1,0:T(8,128)(2,1)S(1)} %get-tuple-element.245.b_ref, ...), custom_call_target="tpu_custom_call" | custom-call | flops 15000000512 | bytes 8000000 | tf_op jit(solution)/shard_map/local_scan/pallas_call | solution.py:504
  98.0 11.9 %all-gather.11.cloned.1.call-done = bf16[1024,2048]{0,1:T(8,128)(2,1)} async-done(((bf16[128,2048]{0,1:T(8,128)(2,1)}), bf16[1024,2048]{0,1:T(8,128)(2,1)}) %all-gather.11.cloned.1.call-update) | async-done | bytes 4194320 | tf_op jit(solution)/shard_map/all_gather | solution.py:911
  109.9 6.9 %fusion.41.gate_ref = f32[512,2048]{1,0:T(8,128)} fusion(bf16[512,1024]{1,0:T(8,128)(2,1)} %copy-done.97, bf16[1024,2048]{0,1:T(8,128)(2,1)} %all-gather.11.cloned.1.call-done), kind=kOutput, calls=%fused_computation.181 | convolution fusion | flops 2147483648 | bytes 9437184 | tf_op jit(solution)/shard_map/dot_general | solution.py:30
  121.7 2.9 bitcast_convert_fusion.base_ref
  126.0 7.2 %gate_forward.2 = (f32[512,2048]{1,0:T(8,128)}, bf16[512,2048]{1,0:T(8,128)(2,1)S(1)}) custom-call(f32[512,2048]{1,0:T(8,128)} %local_scan.2.y_ref, f32[512,2048]{1,0:T(8,128)} %fusion.41.gate_ref, f32[512,128]{1,0:T(8,128)S(1)} %get-tuple-element.258.p_ref, bf16[512,128]{1,0:T(8,128)(2,1)S(1)} %copy-done.58, bf16[128,2048]{1,0:T(8,128)(2,1)S(1)} %add.301.s_ref, ...), custom_call_target="tpu_custom_call" | custom-call | flops 5000000000 | bytes 15000000 | tf_op jit(solution)/shard_map/gate_forward/pallas_call | solution.py:526
  134.5 9.3 %add_product.1 = f32[512,1024]{1,0:T(8,128)} custom-call(s32[8]{0:T(128)S(1)} %iota_xor_fusion.order_ref, bf16[512,2048]{1,0:T(8,128)(2,1)} %copy-done, f32[512,1024]{1,0:T(8,128)} %bitcast_convert_fusion.base_ref, bf16[256,1024]{1,0:T(8,128)(2,1)S(1)} %get-tuple-element.249.refs_0_, bf16[256,1024]{1,0:T(8,128)(2,1)S(1)} %collective-permute-done.10.refs_1_, ...), custom_call_target="tpu_custom_call" | custom-call | flops 2000000000 | bytes 10000000 | tf_op jit(solution)/shard_map/add_product/pallas_call | solution.py:701
  147.4 5.3 all-gather.13.cloned.1.call-done
  152.7 5.6 convolution_convert_fusion.v_ref.bc_ref.dt_ref
  158.4 3.4 collective-permute-start.11
  163.8 12.4 %local_state.3 = (bf16[128,2048]{1,0:T(8,128)(2,1)S(1)}, f32[8,2048]{1,0:T(8,128)S(1)}, f32[512,2048]{1,0:T(8,128)}, f32[512,128]{1,0:T(8,128)S(1)}, bf16[512,38...) custom-call(bf16[512,2432]{1,0:T(8,128)(2,1)} %copy-done.138, ...), custom_call_target="tpu_custom_call" | custom-call | flops 4000000000 | bytes 8000000 | tf_op jit(solution)/shard_map/local_state/pallas_call | solution.py:474
  176.9 8.4 %collective-permute-start.12 = (bf16[128,2048]{1,0:T(8,128)(2,1)S(1)}, bf16[128,2048]{1,0:T(8,128)(2,1)S(1)}, u32[]{:S(2)}, u32[]{:S(2)}) collective-permute-start(bf16[128,2048]{1,0:T(8,128)(2,1)S(1)} %get-tuple-element.264), channel_id=1, source_target_pairs={{0,8},{1,9},{2,10},{3,11},{4,12},{5,13},{6,14},{7,15}} | collective-permute-start | bytes 1572872 | tf_op jit(solution)/shard_map/ppermute | solution.py:645
  185.3 11.5 %local_scan.3.y_ref = f32[512,2048]{1,0:T(8,128)} custom-call(f32[512,2048]{1,0:T(8,128)} %get-tuple-element.265.x_ref, f32[1,2048]{1,0:T(1,128)S(1)} %broadcast_in_dim_reshape.7.skip_ref, bf16[512,384]{1,0:T(8,128)(2,1)S(1)} %get-tuple-element.266.p3_ref, bf16[512,128]{1,0:T(8,128)(2,1)S(1)} %get-tuple-element.267.b_ref, ...), custom_call_target="tpu_custom_call" | custom-call | flops 15000000512 | bytes 8000000 | tf_op jit(solution)/shard_map/local_scan/pallas_call | solution.py:504
  200.5 7.3 %fusion.42.gate_ref = f32[512,2048]{1,0:T(8,128)} fusion(bf16[512,1024]{1,0:T(8,128)(2,1)} %multiply_convert_fusion, bf16[1024,2048]{0,1:T(8,128)(2,1)} %all-gather.15.cloned.1.call-done), kind=kOutput, calls=%fused_computation.182 | convolution fusion | flops 2147483648 | bytes 9437184 | tf_op jit(solution)/shard_map/dot_general | solution.py:30
  216.6 7.0 %gate_forward.3 = (f32[512,2048]{1,0:T(8,128)}, bf16[512,2048]{1,0:T(8,128)(2,1)S(1)}) custom-call(f32[512,2048]{1,0:T(8,128)} %local_scan.3.y_ref, f32[512,2048]{1,0:T(8,128)} %fusion.42.gate_ref, f32[512,128]{1,0:T(8,128)S(1)} %copy-done.51, bf16[512,128]{1,0:T(8,128)(2,1)S(1)} %copy-done.70, bf16[128,2048]{1,0:T(8,128)(2,1)S(1)} %add.306.s_ref, ...), custom_call_target="tpu_custom_call" | custom-call | flops 5000000000 | bytes 15000000 | tf_op jit(solution)/shard_map/gate_forward/pallas_call | solution.py:526
  225.8 4.6 all-gather.17.cloned.1.call-done
  230.4 6.9 %fusion.6 = bf16[1,512,1024]{2,1,0:T(8,128)(2,1)} fusion(f32[512,1024]{1,0:T(8,128)} %add_product.1, bf16[512,2048]{1,0:T(8,128)(2,1)} %copy-done.38, bf16[1,2048,1024]{2,1,0:T(8,128)(2,1)} %all-gather.17.cloned.1.call-done), kind=kOutput, calls=%fused_computation.21 | convolution fusion | flops 2148532224 | bytes 9437184 | tf_op jit(solution)/shard_map/dot_general | solution.py:30
  237.4 4.3 fusion.dgn_ref
  241.7 10.0 %gate_backward.2 = (bf16[512,2048]{1,0:T(8,128)(2,1)S(1)}, bf16[512,2048]{1,0:T(8,128)(2,1)}, f32[8,2048]{1,0:T(8,128)S(1)}, bf16[128,2048]{1,0:T(8,128)(2,1)S(1)}) custom-call(f32[512,2048]{1,0:T(8,128)} %get-tuple-element.280.y_ref, f32[512,2048]{1,0:T(8,128)} %fusion.42.gate_ref, f32[512,2048]{1,0:T(8,128)} %fusion.dgn_ref, f32[512,128]{1,0:T(8,128)S(1)} %copy-done.52, ...), custom_call_target="tpu_custom_call" | custom-call | flops 10000000000 | bytes 17000000 | tf_op jit(solution)/shard_map/gate_backward/pallas_call | solution.py:542
  254.7 4.3 convolution_convert_fusion.3
  259.1 6.4 convolution_convert_fusion.2
  271.7 5.7 scan_inside.4
  282.9 5.7 scan_inside.5
  289.9 7.4 %collective-permute-done.17 = bf16[128,2048]{1,0:T(8,128)(2,1)S(1)} collective-permute-done((bf16[128,2048]{1,0:T(8,128)(2,1)S(1)}, bf16[128,2048]{1,0:T(8,128)(2,1)S(1)}, u32[]{:S(2)}, u32[]{:S(2)}) %collective-permute-start.17) | collective-permute-done | bytes 524320 | tf_op jit(solution)/shard_map/ppermute | solution.py:645
  297.5 27.9 %scan_backward.2 = (bf16[512,2048]{1,0:T(8,128)(2,1)}, f32[8,2048]{1,0:T(8,128)S(1)}, f32[8,2048]{1,0:T(8,128)S(1)}, f32[8,2048]{1,0:T(8,128)S(1)}, bf16[512,256...) custom-call(bf16[512,2432]{1,0:T(8,128)(2,1)} %copy-done.138, ...), custom_call_target="tpu_custom_call" | custom-call | flops 30000001024 | bytes 16000000 | tf_op jit(solution)/shard_map/scan_backward/pallas_call | solution.py:589
  328.6 3.0 collective-permute-done.18
  333.2 4.8 product_give.4
  348.0 3.7 fusion.43
  353.8 4.3 product_own.4
  358.5 6.2 multiply_reduce_fusion
  367.2 8.1 %product_back.1.dgn_ref = f32[512,2048]{1,0:T(8,128)} custom-call(s32[8]{0:T(128)S(1)} %iota_xor_fusion.order_ref, bf16[512,1024]{1,0:T(8,128)(2,1)} %get-tuple-element.440.left_ref.right_ref, bf16[256,1024]{1,0:T(8,128)(2,1)S(1)} %get-tuple-element.249.refs_0_, bf16[256,1024]{1,0:T(8,128)(2,1)S(1)} %copy-done.4, ...), custom_call_target="tpu_custom_call" | custom-call | flops 2000000000 | bytes 10000000 | tf_op jit(solution)/shard_map/product_back/pallas_call | solution.py:724
  375.4 10.0 %gate_backward.3 = (bf16[512,2048]{1,0:T(8,128)(2,1)S(1)}, bf16[512,2048]{1,0:T(8,128)(2,1)}, f32[8,2048]{1,0:T(8,128)S(1)}, bf16[128,2048]{1,0:T(8,128)(2,1)S(1)}) custom-call(f32[512,2048]{1,0:T(8,128)} %get-tuple-element.312.y_ref, f32[512,2048]{1,0:T(8,128)} %fusion.41.gate_ref, f32[512,2048]{1,0:T(8,128)} %product_back.1.dgn_ref, ...), custom_call_target="tpu_custom_call" | custom-call | flops 10000000000 | bytes 17000000 | tf_op jit(solution)/shard_map/gate_backward/pallas_call | solution.py:542
  386.7 5.7 scan_inside.7
  394.9 5.9 scan_inside.6
  408.0 5.9 fusion.44
  414.0 3.7 product_give.6
  417.9 13.9 %collective-permute-done.24 = bf16[128,2432]{1,0:T(8,128)(2,1)S(1)} collective-permute-done((bf16[128,2432]{1,0:T(8,128)(2,1)S(1)}, bf16[128,2432]{1,0:T(8,128)(2,1)S(1)}, u32[]{:S(2)}, u32[]{:S(2)}) %collective-permute-start.24) | collective-permute-done | bytes 622624 | tf_op jit(solution)/shard_map/ppermute | solution.py:639
  435.5 2.7 collective-permute-start.28
  438.2 26.7 %collective-permute-done.26 = bf16[128,2048]{1,0:T(8,128)(2,1)S(1)} collective-permute-done((bf16[128,2048]{1,0:T(8,128)(2,1)}, bf16[128,2048]{1,0:T(8,128)(2,1)S(1)}, u32[]{:S(2)}, u32[]{:S(2)}) %collective-permute-start.26) | collective-permute-done | bytes 524320 | tf_op jit(solution)/shard_map/ppermute | solution.py:645
  465.1 3.8 product_own.5
  473.2 4.2 product_own.6
  479.3 27.8 %scan_backward.3 = (bf16[512,2048]{1,0:T(8,128)(2,1)}, f32[8,2048]{1,0:T(8,128)S(1)}, f32[8,2048]{1,0:T(8,128)S(1)}, f32[8,2048]{1,0:T(8,128)S(1)}, bf16[512,256...) custom-call(bf16[512,2432]{1,0:T(8,128)(2,1)} %copy-done.137, ...), custom_call_target="tpu_custom_call" | custom-call | flops 30000001024 | bytes 16000000 | tf_op jit(solution)/shard_map/scan_backward/pallas_call | solution.py:589
  511.6 2.9 collective-permute-done.33
  516.1 3.4 product_give.7
  527.7 5.4 collective-permute-done.35
  535.8 5.2 multiply_reduce_fusion.1
  543.0 4.0 product_own.7
  556.7 5.2 collective-permute-done.40
  563.1 3.3 collective-permute-done.55
  566.6 6.0 collective-permute-done.42
  572.6 2.9 collective-permute-done.41
  575.5 6.5 %collective-permute-done.45 = bf16[128,2432]{1,0:T(8,128)(2,1)} collective-permute-done((bf16[128,2432]{1,0:T(8,128)(2,1)S(1)}, bf16[128,2432]{1,0:T(8,128)(2,1)}, u32[]{:S(2)}, u32[]{:S(2)}) %collective-permute-start.45) | collective-permute-done | bytes 622624 | tf_op jit(solution)/shard_map/ppermute | solution.py:639
  589.0 3.2 collective-permute-done.47
  594.4 2.8 collective-permute-done.48
  597.7 5.2 collective-permute-done.49
  606.1 11.6 %collective-permute-done.50 = f32[8,3672]{1,0:T(8,128)S(1)} collective-permute-done((f32[8,3672]{1,0:T(8,128)S(1)}, f32[8,3672]{1,0:T(8,128)S(1)}, u32[]{:S(2)}, u32[]{:S(2)}) %collective-permute-start.50) | collective-permute-done | bytes 117536 | tf_op jit(solution)/shard_map/ppermute | solution.py:639
  620.3 4.0 collective-permute-done.53
  626.5 7.2 %collective-permute-done.54 = bf16[64,2432]{1,0:T(8,128)(2,1)S(1)} collective-permute-done((bf16[64,2432]{1,0:T(8,128)(2,1)S(1)}, bf16[64,2432]{1,0:T(8,128)(2,1)S(1)}, u32[]{:S(2)}, u32[]{:S(2)}) %collective-permute-start.54) | collective-permute-done | bytes 311328 | tf_op jit(solution)/shard_map/ppermute | solution.py:639
  633.8 2.8 in_weight_rows.1
  (603 shorter events, 147.5 us)
Async XLA Ops:
  7.2 47.0 %all-gather.9.cloned.1.call-start = ((), (), s32[]{:S(2)}) async-start(), calls=%async_computation.2 | async-start | bytes 5603328 | tf_op jit(solution)/shard_map/all_gather | solution.py:902
  9.9 100.0 %all-gather.11.cloned.1.call-start = ((), (), s32[]{:S(2)}) async-start(), calls=%async_computation.3 | async-start | bytes 4718592 | tf_op jit(solution)/shard_map/all_gather | solution.py:911
  10.8 141.9 %all-gather.13.cloned.1.call-start = ((), (), s32[]{:S(2)}) async-start(), calls=%async_computation.4 | async-start | bytes 5603328 | tf_op jit(solution)/shard_map/all_gather | solution.py:902
  11.9 188.6 %all-gather.15.cloned.1.call-start = ((), (), s32[]{:S(2)}) async-start(), calls=%async_computation.5 | async-start | bytes 4718592 | tf_op jit(solution)/shard_map/all_gather | solution.py:911
  12.8 217.6 %all-gather.17.cloned.1.call-start = ((), (), s32[]{:S(2)}) async-start(), calls=%async_computation.8 | async-start | bytes 4718592 | tf_op jit(solution)/shard_map/all_gather | solution.py:914
  13.8 380.1 %reduce-scatter.3.cloned.1.call-start = ((), (), s32[]{:S(2)}) async-start(), calls=%async_computation.6 | async-start | bytes 4718592 | tf_op jit(solution)/shard_map/reduce_scatter | solution.py:1022
  59.8 7.5 %collective-permute-start = (bf16[16,2304]{1,0:T(8,128)(2,1)S(1)}, bf16[16,2304]{1,0:T(8,128)(2,1)S(1)}, u32[]{:S(2)}, u32[]{:S(2)}) collective-permute-start(bf16[16,2304]{1,0:T(8,128)(2,1)S(1)} %slice.456), channel_id=1, source_target_pairs={{0,8},{8,16},{16,24},{1,9},{9,17},{17,25},{2,10},{10,18},{18,26},{... | collective-permute-start | bytes 221192 | tf_op jit(solution)/shard_map/ppermute | solution.py:925
  63.7 53.2 %collective-permute-start.4 = (bf16[256,1024]{1,0:T(8,128)(2,1)S(1)}, bf16[256,1024]{1,0:T(8,128)(2,1)S(1)}, u32[]{:S(2)}, u32[]{:S(2)}) collective-permute-start(bf16[256,1024]{1,0:T(8,128)(2,1)S(1)} %get-tuple-element.249.refs_0_), channel_id=1, source_target_pairs={{0,6},{1,7},{2,4},{3,5},{4,2},{5,3},{6,0},{7,1},{8,14},{9,15},{10,... | collective-permute-start | bytes 1572872 | tf_op jit(solution)/shard_map/ppermute | solution.py:639
  65.2 51.7 %collective-permute-start.3 = (bf16[256,1024]{1,0:T(8,128)(2,1)S(1)}, bf16[256,1024]{1,0:T(8,128)(2,1)S(1)}, u32[]{:S(2)}, u32[]{:S(2)}) collective-permute-start(bf16[256,1024]{1,0:T(8,128)(2,1)S(1)} %get-tuple-element.249.refs_0_), channel_id=1, source_target_pairs={{0,4},{1,5},{2,6},{3,7},{4,0},{5,1},{6,2},{7,3},{8,12},{9,13},{10,... | collective-permute-start | bytes 1572872 | tf_op jit(solution)/shard_map/ppermute | solution.py:639
  66.7 50.2 %collective-permute-start.2 = (bf16[256,1024]{1,0:T(8,128)(2,1)S(1)}, bf16[256,1024]{1,0:T(8,128)(2,1)S(1)}, u32[]{:S(2)}, u32[]{:S(2)}) collective-permute-start(bf16[256,1024]{1,0:T(8,128)(2,1)S(1)} %get-tuple-element.249.refs_0_), channel_id=1, source_target_pairs={{0,2},{1,3},{2,0},{3,1},{4,6},{5,7},{6,4},{7,5},{8,10},{9,11},{10,... | collective-permute-start | bytes 1572872 | tf_op jit(solution)/shard_map/ppermute | solution.py:639
  79.7 15.0 %collective-permute-start.1 = (bf16[128,2048]{1,0:T(8,128)(2,1)S(1)}, bf16[128,2048]{1,0:T(8,128)(2,1)S(1)}, u32[]{:S(2)}, u32[]{:S(2)}) collective-permute-start(bf16[128,2048]{1,0:T(8,128)(2,1)S(1)} %get-tuple-element.242), channel_id=1, source_target_pairs={{0,8},{1,9},{2,10},{3,11},{4,12},{5,13},{6,14},{7,15}} | collective-permute-start | bytes 1572872 | tf_op jit(solution)/shard_map/ppermute | solution.py:645
  96.5 21.2 %collective-permute-start.5 = (bf16[128,2048]{1,0:T(8,128)(2,1)}, bf16[128,2048]{1,0:T(8,128)(2,1)}, u32[]{:S(2)}, u32[]{:S(2)}) collective-permute-start(bf16[128,2048]{1,0:T(8,128)(2,1)} %fusion.9), channel_id=1, source_target_pairs={{8,16},{9,17},{10,18},{11,19},{12,20},{13,21},{14,22},{15,23}} | collective-permute-start | bytes 1572872 | tf_op jit(solution)/shard_map/ppermute | solution.py:645
  116.9 7.9 %collective-permute-start.6 = (bf16[256,1024]{1,0:T(8,128)(2,1)S(1)}, bf16[256,1024]{1,0:T(8,128)(2,1)S(1)}, u32[]{:S(2)}, u32[]{:S(2)}) collective-permute-start(bf16[256,1024]{1,0:T(8,128)(2,1)S(1)} %collective-permute-done.2.refs_2_), channel_id=1, source_target_pairs={{0,1},{1,0},{2,3},{3,2},{4,5},{5,4},{6,7},{7,6},{8,9},{9,8},{10,11... | collective-permute-start | bytes 1572872 | tf_op jit(solution)/shard_map/ppermute | solution.py:639
  117.2 7.6 %collective-permute-start.7 = (bf16[256,1024]{1,0:T(8,128)(2,1)S(1)}, bf16[256,1024]{1,0:T(8,128)(2,1)}, u32[]{:S(2)}, u32[]{:S(2)}) collective-permute-start(bf16[256,1024]{1,0:T(8,128)(2,1)S(1)} %collective-permute-done.3.refs_4_), channel_id=1, source_target_pairs={{0,1},{1,0},{2,3},{3,2},{4,5},{5,4},{6,7},{7,6},{8,9},{9,8},{10,11... | collective-permute-start | bytes 1572872 | tf_op jit(solution)/shard_map/ppermute | solution.py:639
  117.5 7.3 %collective-permute-start.8 = (bf16[256,1024]{1,0:T(8,128)(2,1)S(1)}, bf16[256,1024]{1,0:T(8,128)(2,1)}, u32[]{:S(2)}, u32[]{:S(2)}) collective-permute-start(bf16[256,1024]{1,0:T(8,128)(2,1)S(1)} %collective-permute-done.4.refs_6_), channel_id=1, source_target_pairs={{0,1},{1,0},{2,3},{3,2},{4,5},{5,4},{6,7},{7,6},{8,9},{9,8},{10,11... | collective-permute-start | bytes 1572872 | tf_op jit(solution)/shard_map/ppermute | solution.py:639
  119.9 4.9 collective-permute-start.9
  124.5 10.0 %collective-permute-start.10 = (bf16[256,1024]{1,0:T(8,128)(2,1)S(1)}, bf16[256,1024]{1,0:T(8,128)(2,1)S(1)}, u32[]{:S(2)}, u32[]{:S(2)}) collective-permute-start(bf16[256,1024]{1,0:T(8,128)(2,1)S(1)} %get-tuple-element.249.refs_0_), channel_id=1, source_target_pairs={{0,1},{1,0},{2,3},{3,2},{4,5},{5,4},{6,7},{7,6},{8,9},{9,8},{10,11... | collective-permute-start | bytes 1572872 | tf_op jit(solution)/shard_map/ppermute | solution.py:639
  158.4 5.4 collective-permute-start.11
  176.9 19.9 %collective-permute-start.12 = (bf16[128,2048]{1,0:T(8,128)(2,1)S(1)}, bf16[128,2048]{1,0:T(8,128)(2,1)S(1)}, u32[]{:S(2)}, u32[]{:S(2)}) collective-permute-start(bf16[128,2048]{1,0:T(8,128)(2,1)S(1)} %get-tuple-element.264), channel_id=1, source_target_pairs={{0,8},{1,9},{2,10},{3,11},{4,12},{5,13},{6,14},{7,15}} | collective-permute-start | bytes 1572872 | tf_op jit(solution)/shard_map/ppermute | solution.py:645
  198.6 9.1 %collective-permute-start.13 = (bf16[128,2048]{1,0:T(8,128)(2,1)}, bf16[128,2048]{1,0:T(8,128)(2,1)}, u32[]{:S(2)}, u32[]{:S(2)}) collective-permute-start(bf16[128,2048]{1,0:T(8,128)(2,1)} %fusion.11), channel_id=1, source_target_pairs={{8,16},{9,17},{10,18},{11,19},{12,20},{13,21},{14,22},{15,23}} | collective-permute-start | bytes 1572872 | tf_op jit(solution)/shard_map/ppermute | solution.py:645
  209.9 5.5 collective-permute-start.14
  253.1 12.4 %collective-permute-start.15 = (bf16[128,2048]{1,0:T(8,128)(2,1)S(1)}, bf16[128,2048]{1,0:T(8,128)(2,1)}, u32[]{:S(2)}, u32[]{:S(2)}) collective-permute-start(bf16[128,2048]{1,0:T(8,128)(2,1)S(1)} %get-tuple-element.281), channel_id=1, source_target_pairs={{24,16},{25,17},{26,18},{27,19},{28,20},{29,21},{30,22},{31,23}} | collective-permute-start | bytes 1572872 | tf_op jit(solution)/shard_map/ppermute | solution.py:645
  267.5 12.1 %collective-permute-start.16 = (bf16[128,2048]{1,0:T(8,128)(2,1)}, bf16[128,2048]{1,0:T(8,128)(2,1)}, u32[]{:S(2)}, u32[]{:S(2)}) collective-permute-start(bf16[128,2048]{1,0:T(8,128)(2,1)} %fusion.13), channel_id=1, source_target_pairs={{16,8},{17,9},{18,10},{19,11},{20,12},{21,13},{22,14},{23,15}} | collective-permute-start | bytes 1572872 | tf_op jit(solution)/shard_map/ppermute | solution.py:645
  279.5 114.4 %reduce-scatter.5.cloned.1.call-start = ((), (), s32[]{:S(2)}) async-start(), calls=%async_computation.7 | async-start | bytes 4718592 | tf_op jit(solution)/shard_map/reduce_scatter | solution.py:1022
  281.2 16.1 %collective-permute-start.17 = (bf16[128,2048]{1,0:T(8,128)(2,1)S(1)}, bf16[128,2048]{1,0:T(8,128)(2,1)S(1)}, u32[]{:S(2)}, u32[]{:S(2)}) collective-permute-start(bf16[128,2048]{1,0:T(8,128)(2,1)S(1)} %fusion.14), channel_id=1, source_target_pairs={{8,0},{9,1},{10,2},{11,3},{12,4},{13,5},{14,6},{15,7}} | collective-permute-start | bytes 1572872 | tf_op jit(solution)/shard_map/ppermute | solution.py:645
  325.4 6.2 collective-permute-start.18
  338.0 15.8 %collective-permute-start.19 = (bf16[512,2432]{1,0:T(8,128)(2,1)}, bf16[512,2432]{1,0:T(8,128)(2,1)}, u32[]{:S(2)}, u32[]{:S(2)}) collective-permute-start(bf16[512,2432]{1,0:T(8,128)(2,1)} %product_give.4), channel_id=1, source_target_pairs={{0,1},{1,0},{2,3},{3,2},{4,5},{5,4},{6,7},{7,6},{8,9},{9,8},{10,11... | collective-permute-start | bytes 7471112 | tf_op jit(solution)/shard_map/ppermute | solution.py:639
  338.0 169.6 %all-reduce.5.cloned.1.call-start = ((), (), s32[]{:S(2)}) async-start(), calls=%async_computation.9 | async-start | bytes 2097152 | tf_op jit(solution)/shard_map/psum | solution.py:980
  393.9 13.2 %collective-permute-start.20 = (bf16[128,2048]{1,0:T(8,128)(2,1)S(1)}, bf16[128,2048]{1,0:T(8,128)(2,1)S(1)}, u32[]{:S(2)}, u32[]{:S(2)}) collective-permute-start(bf16[128,2048]{1,0:T(8,128)(2,1)S(1)} %get-tuple-element.314), channel_id=1, source_target_pairs={{24,16},{25,17},{26,18},{27,19},{28,20},{29,21},{30,22},{31,23}} | collective-permute-start | bytes 1572872 | tf_op jit(solution)/shard_map/ppermute | solution.py:645
  401.0 16.9 %collective-permute-start.23 = (bf16[128,2432]{1,0:T(8,128)(2,1)S(1)}, bf16[128,2432]{1,0:T(8,128)(2,1)S(1)}, u32[]{:S(2)}, u32[]{:S(2)}) collective-permute-start(bf16[128,2432]{1,0:T(8,128)(2,1)S(1)} %copy-done.33), channel_id=1, source_target_pairs={{0,2},{1,3},{2,0},{3,1},{4,6},{5,7},{6,4},{7,5},{8,10},{9,11},{10,... | collective-permute-start | bytes 1867784 | tf_op jit(solution)/shard_map/ppermute | solution.py:639
  402.5 29.4 %collective-permute-start.24 = (bf16[128,2432]{1,0:T(8,128)(2,1)S(1)}, bf16[128,2432]{1,0:T(8,128)(2,1)S(1)}, u32[]{:S(2)}, u32[]{:S(2)}) collective-permute-start(bf16[128,2432]{1,0:T(8,128)(2,1)S(1)} %copy-done.31), channel_id=1, source_target_pairs={{0,4},{1,5},{2,6},{3,7},{4,0},{5,1},{6,2},{7,3},{8,12},{9,13},{10,... | collective-permute-start | bytes 1867784 | tf_op jit(solution)/shard_map/ppermute | solution.py:639
  403.0 28.8 %collective-permute-start.25 = (bf16[128,2432]{1,0:T(8,128)(2,1)S(1)}, bf16[128,2432]{1,0:T(8,128)(2,1)S(1)}, u32[]{:S(2)}, u32[]{:S(2)}) collective-permute-start(bf16[128,2432]{1,0:T(8,128)(2,1)S(1)} %copy-done.29), channel_id=1, source_target_pairs={{0,6},{1,7},{2,4},{3,5},{4,2},{5,3},{6,0},{7,1},{8,14},{9,15},{10,... | collective-permute-start | bytes 1867784 | tf_op jit(solution)/shard_map/ppermute | solution.py:639
  407.3 10.4 %collective-permute-start.22 = (bf16[128,2048]{1,0:T(8,128)(2,1)S(1)}, bf16[128,2048]{1,0:T(8,128)(2,1)S(1)}, u32[]{:S(2)}, u32[]{:S(2)}) collective-permute-start(bf16[128,2048]{1,0:T(8,128)(2,1)S(1)} %fusion.15), channel_id=1, source_target_pairs={{16,8},{17,9},{18,10},{19,11},{20,12},{21,13},{22,14},{23,15}} | collective-permute-start | bytes 1572872 | tf_op jit(solution)/shard_map/ppermute | solution.py:645
  414.0 51.1 %collective-permute-start.21 = (bf16[1024,1024]{1,0:T(8,128)(2,1)}, bf16[1024,1024]{1,0:T(8,128)(2,1)}, u32[]{:S(2)}, u32[]{:S(2)}) collective-permute-start(bf16[1024,1024]{1,0:T(8,128)(2,1)} %product_give.5), channel_id=1, source_target_pairs={{0,1},{1,0},{2,3},{3,2},{4,5},{5,4},{6,7},{7,6},{8,9},{9,8},{10,11... | collective-permute-start | bytes 6291464 | tf_op jit(solution)/shard_map/ppermute | solution.py:639
  431.8 41.3 %collective-permute-start.27 = (bf16[512,2048]{1,0:T(8,128)(2,1)}, bf16[512,2048]{1,0:T(8,128)(2,1)}, u32[]{:S(2)}, u32[]{:S(2)}) collective-permute-start(bf16[512,2048]{1,0:T(8,128)(2,1)} %product_give.6), channel_id=1, source_target_pairs={{0,1},{1,0},{2,3},{3,2},{4,5},{5,4},{6,7},{7,6},{8,9},{9,8},{10,11... | collective-permute-start | bytes 6291464 | tf_op jit(solution)/shard_map/ppermute | solution.py:639
  432.8 32.1 %collective-permute-start.26 = (bf16[128,2048]{1,0:T(8,128)(2,1)}, bf16[128,2048]{1,0:T(8,128)(2,1)S(1)}, u32[]{:S(2)}, u32[]{:S(2)}) collective-permute-start(bf16[128,2048]{1,0:T(8,128)(2,1)} %fusion.16), channel_id=1, source_target_pairs={{8,0},{9,1},{10,2},{11,3},{12,4},{13,5},{14,6},{15,7}} | collective-permute-start | bytes 1572872 | tf_op jit(solution)/shard_map/ppermute | solution.py:645
  435.5 37.6 %collective-permute-start.28 = (bf16[64,2432]{1,0:T(8,128)(2,1)}, bf16[64,2432]{1,0:T(8,128)(2,1)}, u32[]{:S(2)}, u32[]{:S(2)}) collective-permute-start(bf16[64,2432]{1,0:T(8,128)(2,1)} %get-tuple-element.470), channel_id=1, source_target_pairs={{0,8},{8,0},{16,24},{24,16},{1,9},{9,1},{17,25},{25,17},{2,10},{10... | collective-permute-start | bytes 933896 | tf_op jit(solution)/shard_map/ppermute | solution.py:639
  468.9 38.7 %collective-permute-start.29 = (bf16[256,1024]{1,0:T(8,128)(2,1)}, bf16[256,1024]{1,0:T(8,128)(2,1)}, u32[]{:S(2)}, u32[]{:S(2)}) collective-permute-start(bf16[256,1024]{1,0:T(8,128)(2,1)} %get-tuple-element.358), channel_id=1, source_target_pairs={{0,2},{1,3},{2,0},{3,1},{4,6},{5,7},{6,4},{7,5},{8,10},{9,11},{10,... | collective-permute-start | bytes 1572872 | tf_op jit(solution)/shard_map/ppermute | solution.py:639
  468.9 38.7 %collective-permute-start.30 = (bf16[256,1024]{1,0:T(8,128)(2,1)}, bf16[256,1024]{1,0:T(8,128)(2,1)}, u32[]{:S(2)}, u32[]{:S(2)}) collective-permute-start(bf16[256,1024]{1,0:T(8,128)(2,1)} %get-tuple-element.359), channel_id=1, source_target_pairs={{0,4},{1,5},{2,6},{3,7},{4,0},{5,1},{6,2},{7,3},{8,12},{9,13},{10,... | collective-permute-start | bytes 1572872 | tf_op jit(solution)/shard_map/ppermute | solution.py:639
  469.9 37.8 %collective-permute-start.31 = (bf16[256,1024]{1,0:T(8,128)(2,1)S(1)}, bf16[256,1024]{1,0:T(8,128)(2,1)}, u32[]{:S(2)}, u32[]{:S(2)}) collective-permute-start(bf16[256,1024]{1,0:T(8,128)(2,1)S(1)} %get-tuple-element.360), channel_id=1, source_target_pairs={{0,6},{1,7},{2,4},{3,5},{4,2},{5,3},{6,0},{7,1},{8,14},{9,15},{10,... | collective-permute-start | bytes 1572872 | tf_op jit(solution)/shard_map/ppermute | solution.py:639
  479.2 28.9 %collective-permute-start.32 = (bf16[64,2432]{1,0:T(8,128)(2,1)}, bf16[64,2432]{1,0:T(8,128)(2,1)}, u32[]{:S(2)}, u32[]{:S(2)}) collective-permute-start(bf16[64,2432]{1,0:T(8,128)(2,1)} %add_convert_fusion.8), channel_id=1, source_target_pairs={{0,16},{8,24},{16,0},{24,8},{1,17},{9,25},{17,1},{25,9},{2,18},{10... | collective-permute-start | bytes 933896 | tf_op jit(solution)/shard_map/ppermute | solution.py:639
  508.2 6.4 collective-permute-start.33
  519.6 16.2 %collective-permute-start.34 = (bf16[512,2432]{1,0:T(8,128)(2,1)S(1)}, bf16[512,2432]{1,0:T(8,128)(2,1)}, u32[]{:S(2)}, u32[]{:S(2)}) collective-permute-start(bf16[512,2432]{1,0:T(8,128)(2,1)S(1)} %product_give.7), channel_id=1, source_target_pairs={{0,1},{1,0},{2,3},{3,2},{4,5},{5,4},{6,7},{7,6},{8,9},{9,8},{10,11... | collective-permute-start | bytes 7471112 | tf_op jit(solution)/shard_map/ppermute | solution.py:639
  519.6 27.4 %collective-permute-start.37 = (bf16[128,2048]{1,0:T(8,128)(2,1)}, bf16[128,2048]{1,0:T(8,128)(2,1)S(1)}, u32[]{:S(2)}, u32[]{:S(2)}) collective-permute-start(bf16[128,2048]{1,0:T(8,128)(2,1)} %get-tuple-element.397), channel_id=1, source_target_pairs={{0,2},{1,3},{2,0},{3,1},{4,6},{5,7},{6,4},{7,5},{8,10},{9,11},{10,... | collective-permute-start | bytes 1572872 | tf_op jit(solution)/shard_map/ppermute | solution.py:639
  521.2 25.8 %collective-permute-start.38 = (bf16[128,2048]{1,0:T(8,128)(2,1)}, bf16[128,2048]{1,0:T(8,128)(2,1)}, u32[]{:S(2)}, u32[]{:S(2)}) collective-permute-start(bf16[128,2048]{1,0:T(8,128)(2,1)} %get-tuple-element.398), channel_id=1, source_target_pairs={{0,4},{1,5},{2,6},{3,7},{4,0},{5,1},{6,2},{7,3},{8,12},{9,13},{10,... | collective-permute-start | bytes 1572872 | tf_op jit(solution)/shard_map/ppermute | solution.py:639
  522.7 24.4 %collective-permute-start.39 = (bf16[128,2048]{1,0:T(8,128)(2,1)}, bf16[128,2048]{1,0:T(8,128)(2,1)}, u32[]{:S(2)}, u32[]{:S(2)}) collective-permute-start(bf16[128,2048]{1,0:T(8,128)(2,1)} %get-tuple-element.399), channel_id=1, source_target_pairs={{0,6},{1,7},{2,4},{3,5},{4,2},{5,3},{6,0},{7,1},{8,14},{9,15},{10,... | collective-permute-start | bytes 1572872 | tf_op jit(solution)/shard_map/ppermute | solution.py:639
  525.2 7.9 %collective-permute-start.35 = (bf16[128,1024]{1,0:T(8,128)(2,1)S(1)}, bf16[128,1024]{1,0:T(8,128)(2,1)S(1)}, u32[]{:S(2)}, u32[]{:S(2)}) collective-permute-start(bf16[128,1024]{1,0:T(8,128)(2,1)S(1)} %get-tuple-element.474), channel_id=1, source_target_pairs={{0,8},{8,0},{16,24},{24,16},{1,9},{9,1},{17,25},{25,17},{2,10},{10... | collective-permute-start | bytes 786440 | tf_op jit(solution)/shard_map/ppermute | solution.py:639
  533.8 21.2 %collective-permute-start.36 = (bf16[128,1024]{1,0:T(8,128)(2,1)}, bf16[128,1024]{1,0:T(8,128)(2,1)}, u32[]{:S(2)}, u32[]{:S(2)}) collective-permute-start(bf16[128,1024]{1,0:T(8,128)(2,1)} %add_convert_fusion.12), channel_id=1, source_target_pairs={{0,16},{8,24},{16,0},{24,8},{1,17},{9,25},{17,1},{25,9},{2,18},{10... | collective-permute-start | bytes 786440 | tf_op jit(solution)/shard_map/ppermute | solution.py:639
  549.6 12.3 %collective-permute-start.40 = (bf16[64,2048]{1,0:T(8,128)(2,1)}, bf16[64,2048]{1,0:T(8,128)(2,1)S(1)}, u32[]{:S(2)}, u32[]{:S(2)}) collective-permute-start(bf16[64,2048]{1,0:T(8,128)(2,1)} %get-tuple-element.472), channel_id=1, source_target_pairs={{0,8},{8,0},{16,24},{24,16},{1,9},{9,1},{17,25},{25,17},{2,10},{10... | collective-permute-start | bytes 786440 | tf_op jit(solution)/shard_map/ppermute | solution.py:639
  551.4 15.0 %collective-permute-start.55 = (bf16[64,2432]{1,0:T(8,128)(2,1)S(1)}, bf16[64,2432]{1,0:T(8,128)(2,1)S(1)}, u32[]{:S(2)}, u32[]{:S(2)}) collective-permute-start(bf16[64,2432]{1,0:T(8,128)(2,1)S(1)} %copy-done.108), channel_id=1, source_target_pairs={{0,8},{8,0},{16,24},{24,16},{1,9},{9,1},{17,25},{25,17},{2,10},{10... | collective-permute-start | bytes 933896 | tf_op jit(solution)/shard_map/ppermute | solution.py:639
  553.2 22.4 %collective-permute-start.43 = (bf16[128,2432]{1,0:T(8,128)(2,1)}, bf16[128,2432]{1,0:T(8,128)(2,1)}, u32[]{:S(2)}, u32[]{:S(2)}) collective-permute-start(bf16[128,2432]{1,0:T(8,128)(2,1)} %copy-done.27), channel_id=1, source_target_pairs={{0,2},{1,3},{2,0},{3,1},{4,6},{5,7},{6,4},{7,5},{8,10},{9,11},{10,... | collective-permute-start | bytes 1867784 | tf_op jit(solution)/shard_map/ppermute | solution.py:639
  553.9 21.7 %collective-permute-start.44 = (bf16[128,2432]{1,0:T(8,128)(2,1)S(1)}, bf16[128,2432]{1,0:T(8,128)(2,1)}, u32[]{:S(2)}, u32[]{:S(2)}) collective-permute-start(bf16[128,2432]{1,0:T(8,128)(2,1)S(1)} %get-tuple-element.408), channel_id=1, source_target_pairs={{0,4},{1,5},{2,6},{3,7},{4,0},{5,1},{6,2},{7,3},{8,12},{9,13},{10,... | collective-permute-start | bytes 1867784 | tf_op jit(solution)/shard_map/ppermute | solution.py:639
  555.1 27.0 %collective-permute-start.45 = (bf16[128,2432]{1,0:T(8,128)(2,1)S(1)}, bf16[128,2432]{1,0:T(8,128)(2,1)}, u32[]{:S(2)}, u32[]{:S(2)}) collective-permute-start(bf16[128,2432]{1,0:T(8,128)(2,1)S(1)} %get-tuple-element.409), channel_id=1, source_target_pairs={{0,6},{1,7},{2,4},{3,5},{4,2},{5,3},{6,0},{7,1},{8,14},{9,15},{10,... | collective-permute-start | bytes 1867784 | tf_op jit(solution)/shard_map/ppermute | solution.py:639
  561.9 10.7 %collective-permute-start.42 = (bf16[64,2048]{1,0:T(8,128)(2,1)S(1)}, bf16[64,2048]{1,0:T(8,128)(2,1)}, u32[]{:S(2)}, u32[]{:S(2)}) collective-permute-start(bf16[64,2048]{1,0:T(8,128)(2,1)S(1)} %add_convert_fusion.10), channel_id=1, source_target_pairs={{0,16},{8,24},{16,0},{24,8},{1,17},{9,25},{17,1},{25,9},{2,18},{10... | collective-permute-start | bytes 786440 | tf_op jit(solution)/shard_map/ppermute | solution.py:639
  566.4 9.1 %collective-permute-start.41 = (bf16[128,1024]{1,0:T(8,128)(2,1)S(1)}, bf16[128,1024]{1,0:T(8,128)(2,1)}, u32[]{:S(2)}, u32[]{:S(2)}) collective-permute-start(bf16[128,1024]{1,0:T(8,128)(2,1)S(1)} %add_convert_fusion.11), channel_id=1, source_target_pairs={{0,8},{8,0},{16,24},{24,16},{1,9},{9,1},{17,25},{25,17},{2,10},{10... | collective-permute-start | bytes 786440 | tf_op jit(solution)/shard_map/ppermute | solution.py:639
  583.8 3.3 collective-permute-start.46
  585.0 12.7 %collective-permute-start.51 = (bf16[64,2048]{1,0:T(8,128)(2,1)S(1)}, bf16[64,2048]{1,0:T(8,128)(2,1)S(1)}, u32[]{:S(2)}, u32[]{:S(2)}) collective-permute-start(bf16[64,2048]{1,0:T(8,128)(2,1)S(1)} %add_convert_fusion.9), channel_id=1, source_target_pairs={{0,8},{8,0},{16,24},{24,16},{1,9},{9,1},{17,25},{25,17},{2,10},{10... | collective-permute-start | bytes 786440 | tf_op jit(solution)/shard_map/ppermute | solution.py:639
  585.4 18.5 %collective-permute-start.52 = (bf16[64,2432]{1,0:T(8,128)(2,1)S(1)}, bf16[64,2432]{1,0:T(8,128)(2,1)S(1)}, u32[]{:S(2)}, u32[]{:S(2)}) collective-permute-start(bf16[64,2432]{1,0:T(8,128)(2,1)S(1)} %constant_dynamic-slice_fusion), channel_id=1, source_target_pairs={{0,8},{8,0},{16,24},{24,16},{1,9},{9,1},{17,25},{25,17},{2,10},{10... | collective-permute-start | bytes 933896 | tf_op jit(solution)/shard_map/ppermute | solution.py:639
  587.2 5.1 collective-permute-start.47
  592.3 4.9 collective-permute-start.48
  597.2 5.7 collective-permute-start.49
  602.9 14.8 %collective-permute-start.50 = (f32[8,3672]{1,0:T(8,128)S(1)}, f32[8,3672]{1,0:T(8,128)S(1)}, u32[]{:S(2)}, u32[]{:S(2)}) collective-permute-start(f32[8,3672]{1,0:T(8,128)S(1)} %add.369), channel_id=1, source_target_pairs={{0,16},{8,24},{16,0},{24,8},{1,17},{9,25},{17,1},{25,9},{2,18},{10... | collective-permute-start | bytes 352520 | tf_op jit(solution)/shard_map/ppermute | solution.py:639
  604.0 20.2 %collective-permute-start.53 = (bf16[64,2432]{1,0:T(8,128)(2,1)S(1)}, bf16[64,2432]{1,0:T(8,128)(2,1)S(1)}, u32[]{:S(2)}, u32[]{:S(2)}) collective-permute-start(bf16[64,2432]{1,0:T(8,128)(2,1)S(1)} %add_convert_fusion.7), channel_id=1, source_target_pairs={{0,16},{8,24},{16,0},{24,8},{1,17},{9,25},{17,1},{25,9},{2,18},{10... | collective-permute-start | bytes 933896 | tf_op jit(solution)/shard_map/ppermute | solution.py:639
  624.3 9.3 %collective-permute-start.54 = (bf16[64,2432]{1,0:T(8,128)(2,1)S(1)}, bf16[64,2432]{1,0:T(8,128)(2,1)S(1)}, u32[]{:S(2)}, u32[]{:S(2)}) collective-permute-start(bf16[64,2432]{1,0:T(8,128)(2,1)S(1)} %add_convert_fusion.6), channel_id=1, source_target_pairs={{0,8},{8,0},{16,24},{24,16},{1,9},{9,1},{17,25},{25,17},{2,10},{10... | collective-permute-start | bytes 933896 | tf_op jit(solution)/shard_map/ppermute | solution.py:639
  (149 other events, 1238.7 us)
Sparse Core Ops, SparseCore 0:
  10.5 43.6 all-gather.8
  56.6 53.2 all-gather.10
  111.8 40.8 all-gather.12
  154.5 37.4 all-gather.14
  193.7 36.7 all-gather.16
  279.6 58.0 reduce-scatter.2
  341.5 51.3 reduce-scatter.4
  438.3 69.2 all-reduce.4
